TPU v7x, 32 devices: a whole 2x2x4 slice. The times are simulated.
32 devices in a mesh: ctx: 16 (over z, x, core), tp: 2 (over y).
Axes of the slice: x: 2, y: 2, z: 4, core: 2. Of those that a mesh axis runs over, the one named last changes fastest.
Arguments:
- query: bfloat16 [12288, 4096], P('ctx', 'tp'), may hold values from -36 to 36
- key: bfloat16 [12288, 1024], P('ctx', 'tp'), may hold values from -32 to 32
- value: bfloat16 [12288, 1024], P('ctx', 'tp'), may hold values from -6 to 6
- keep_rank: int32 [16, 768], P('ctx'), may hold values from 0 to 767, each once within a row
- kept_count: int32 [16], replicated, may hold values from 1 to 768, 6144 in all
- out_weight: bfloat16 [4096, 8192], P('tp'), may hold values from -0.09375 to 0.09375
Outputs:
- mixed: bfloat16 [6144, 8192], P('ctx', 'tp')
Inputs may be any that keep to these rules, and one draw needn't show every extreme that they name: `keep_rank`: each row is a permutation of 0 to 767. `kept_count`: the counts sum to 6144; the largest is exactly 768.
All inputs are finite; a program needn't handle non-finite values.
Results may differ from a plain program's by a relative error of at most 0.019.
The roundings to bfloat16 on the way count: a program that leaves them out, or rounds other values in their place, can miss the bound.
Values may be sent and summed in bfloat16 or wider, within the bound.
No kernel may reach another device: no remote copies, remote signals or barrier semaphores. Data moves between devices by JAX's collectives and lax.ppermute only.
A program may use at most 128 MiB of HBM per device.

v0:
```python
import math

import jax
import jax.numpy as jnp
from jax import lax
from jax.sharding import PartitionSpec as P

HD = 128
TOK_DEV = 384


rope_base = 1000000.0
masked_score = -1e30


def rotate(rows, positions):
    count_rows = rows.shape[0]
    heads = rows.shape[1] // HD
    half_dim = HD // 2
    as_float = rows.astype(jnp.float32).reshape(count_rows, heads, HD)
    inv_freq = rope_base ** (-(jnp.arange(half_dim, dtype=jnp.float32) * 2.0 / HD))
    angles = positions.astype(jnp.float32)[:, None] * inv_freq[None, :]
    cosine = jnp.cos(angles)[:, None, :]
    sine = jnp.sin(angles)[:, None, :]
    first_half = as_float[..., :half_dim]
    second_half = as_float[..., half_dim:]
    turned = jnp.concatenate(
        [first_half * cosine - second_half * sine, second_half * cosine + first_half * sine],
        axis=-1,
    )
    return turned.reshape(count_rows, heads * HD).astype(jnp.bfloat16)


def local(query, key, value, keep_rank, kept_count, out_weight):
    ctx_size = lax.axis_size("ctx")
    my_shard = lax.axis_index("ctx")
    orig_rows = query.shape[0]
    slot_cap = orig_rows // ctx_size
    rows_dev = TOK_DEV
    shard_ids = jnp.arange(ctx_size, dtype=jnp.int32)
    count_ends = jnp.cumsum(kept_count)
    count_starts = count_ends - kept_count
    my_count = jnp.sum(jnp.where(shard_ids == my_shard, kept_count, 0))
    my_start = jnp.sum(jnp.where(shard_ids == my_shard, count_starts, 0))
    local_rows = jnp.arange(orig_rows, dtype=jnp.int32)
    positions = my_shard * orig_rows + local_rows
    rot_query = rotate(query, positions)
    rot_key = rotate(key, positions)
    is_kept = keep_rank[0] < my_count
    kept_order = jnp.cumsum(is_kept.astype(jnp.int32)) - 1
    kept_rows = (
        jnp.zeros((orig_rows,), jnp.int32)
        .at[jnp.where(is_kept, kept_order, orig_rows)]
        .set(local_rows, mode="drop")
    )
    dest_ids = shard_ids[:, None]
    slot_ids = jnp.arange(slot_cap, dtype=jnp.int32)[None, :]
    first_slot = (my_start - dest_ids + ctx_size - 1) // ctx_size
    offsets = (first_slot + slot_ids) * ctx_size + dest_ids - my_start
    is_valid = (offsets < my_count).reshape(-1)
    picked = kept_rows[jnp.clip(offsets, 0, orig_rows - 1).reshape(-1)]

    def pack_rows(source_rows):
        return jnp.where(is_valid[:, None], source_rows[picked], jnp.zeros((), source_rows.dtype))

    got_query, got_key, got_value = (
        lax.all_to_all(pack_rows(rot_query), "ctx", split_axis=0, concat_axis=0, tiled=True),
        lax.all_to_all(pack_rows(rot_key), "ctx", split_axis=0, concat_axis=0, tiled=True),
        lax.all_to_all(pack_rows(value), "ctx", split_axis=0, concat_axis=0, tiled=True),
    )
    own_slots = jnp.arange(rows_dev, dtype=jnp.int32)
    query_glob = own_slots * ctx_size + my_shard
    sources = jnp.sum((count_ends[None, :] <= query_glob[:, None]).astype(jnp.int32), axis=1)
    source_start = jnp.sum(
        jnp.where(shard_ids[None, :] == sources[:, None], count_starts[None, :], 0), axis=1
    )
    slot_of = own_slots - (source_start - my_shard + ctx_size - 1) // ctx_size
    places = sources * slot_cap + slot_of
    query_local = got_query[places]
    key_local = got_key[places]
    value_local = got_value[places]
    heads_dev = query_local.shape[1] // HD
    kv_dev = key_local.shape[1] // HD
    group_size = heads_dev // kv_dev
    queries = query_local.reshape(rows_dev, kv_dev, group_size, HD)

    def absorb_block(state, key_block, value_block, first_row):
        run_max, run_sum, run_acc = state
        block_len = key_block.shape[0]
        whole_rows = first_row + jnp.arange(block_len, dtype=jnp.int32)
        key_glob = whole_rows % rows_dev * ctx_size + whole_rows // rows_dev
        allowed = key_glob[None, :] <= query_glob[:, None]
        key_heads = key_block.reshape(block_len, kv_dev, HD)
        value_heads = value_block.reshape(block_len, kv_dev, HD)
        scores = jnp.einsum(
            "rkgd,pkd->kgrp", queries, key_heads, preferred_element_type=jnp.float32
        ) / math.sqrt(HD)
        scores = jnp.where(allowed, scores, masked_score)
        new_max = jnp.maximum(run_max, jnp.max(scores, axis=-1))
        weights = jnp.where(allowed, jnp.exp(scores - new_max[..., None]), 0.0)
        rescale = jnp.exp(run_max - new_max)
        new_sum = run_sum * rescale + jnp.sum(weights, axis=-1)
        weights_b = weights.astype(jnp.bfloat16)
        new_acc = run_acc * rescale[..., None] + jnp.einsum(
            "kgrp,pkd->kgrd", weights_b, value_heads, preferred_element_type=jnp.float32
        )
        return (new_max, new_sum, new_acc)

    start_state = (
        jnp.full((kv_dev, group_size, rows_dev), masked_score, jnp.float32),
        jnp.zeros((kv_dev, group_size, rows_dev), jnp.float32),
        jnp.zeros((kv_dev, group_size, rows_dev, HD), jnp.float32),
    )
    state = start_state
    key_piece = lax.all_gather(key_local, "ctx", axis=0, tiled=True)
    value_piece = lax.all_gather(value_local, "ctx", axis=0, tiled=True)
    total_rows = key_piece.shape[0]
    step_rows = 512
    turns = total_rows // step_rows
    key_blocks = key_piece.reshape(turns, step_rows, key_piece.shape[1])
    value_blocks = value_piece.reshape(turns, step_rows, value_piece.shape[1])
    block_firsts = jnp.arange(turns, dtype=jnp.int32) * step_rows

    def one_turn(inner, item):
        key_block, value_block, block_first = item
        return (absorb_block(inner, key_block, value_block, block_first), None)

    state, _ = lax.scan(one_turn, state, (key_blocks, value_blocks, block_firsts))
    run_max, run_sum, run_acc = state
    attention = (
        jnp.transpose(run_acc / run_sum[..., None], (2, 0, 1, 3))
        .reshape(rows_dev, heads_dev * HD)
        .astype(jnp.bfloat16)
    )
    summed = lax.psum_scatter(
        lax.dot_general(
            out_weight, attention, (((0,), (1,)), ((), ())), preferred_element_type=jnp.float32
        ).astype(jnp.bfloat16),
        "tp",
        scatter_dimension=0,
        tiled=True,
    ).astype(jnp.float32)
    projected = jnp.transpose(summed).astype(jnp.bfloat16)
    received = lax.all_to_all(projected, "ctx", split_axis=0, concat_axis=0, tiled=True)
    return jnp.transpose(
        received.reshape(ctx_size, rows_dev // ctx_size, received.shape[1]), (1, 0, 2)
    ).reshape(rows_dev, received.shape[1])


def solution(mesh):
    placed = (P("ctx", "tp"), P("ctx", "tp"), P("ctx", "tp"), P("ctx", None), P(), P("tp", None))
    return jax.shard_map(
        local, mesh=mesh, in_specs=placed, out_specs=P("ctx", "tp"), check_vma=False
    )
```

profile of v0, /device:TPU:0, one launch (start us, length us, event | category | flops | bytes accessed | tf_op | source)
XLA Modules:
  0.0 612.3 jit_solution(16103817426042118524)
XLA Ops:
  32.8 7.4 %all-to-all-start.2 = ((bf16[16,48,512]{2,1,0:T(8,128)(2,1)}), bf16[16,48,512]{2,1,0:T(8,128)(2,1)S(1)}, u32[]{:S(2)}, u32[]{:S(2)}) async-start(bf16[16,48,512]{2,1,0:T(8,128)(2,1)} %get-tuple-element.216), calls=%async_computation.2 | async-start | bytes 1572864 | tf_op jit(solution)/shard_map/all_to_all | solution.py:69
  40.4 18.4 %all-to-all-done.2 = bf16[16,48,512]{2,1,0:T(8,128)(2,1)S(1)} async-done(((bf16[16,48,512]{2,1,0:T(8,128)(2,1)}), bf16[16,48,512]{2,1,0:T(8,128)(2,1)S(1)}, u32[]{:S(2)}, u32[]{:S(2)}) %all-to-all-start.2) | async-done | bytes 786464 | tf_op jit(solution)/shard_map/all_to_all | solution.py:69
  61.5 37.2 %all_to_all.36 = bf16[16,48,512]{2,1,0:T(8,128)(2,1)S(1)} all-to-all(bf16[16,48,512]{2,1,0:T(8,128)(2,1)S(1)} %get-tuple-element.217), channel_id=1, replica_groups=mesh['ctx'=16,'tp'=2] {'ctx'}, dimensions={0} | all-to-all | bytes 1572864 | tf_op jit(solution)/shard_map/all_to_all | solution.py:68
  111.1 4.2 gather_fusion.3
  115.3 3.9 broadcast_select_fusion
  119.2 4.9 all-to-all-start.1
  124.4 77.9 %all-to-all-done.1 = bf16[16,48,2048]{2,1,0:T(8,128)(2,1)S(1)} async-done(((bf16[16,48,2048]{2,1,0:T(8,128)(2,1)}), bf16[16,48,2048]{2,1,0:T(8,128)(2,1)S(1)}, u32[]{:S(2)}, u32[]{:S(2)}) %all-to-all-start.1) | async-done | bytes 3145760 | tf_op jit(solution)/shard_map/all_to_all | solution.py:67
  208.7 34.1 %all-gather.5.cloned.1.call-done = bf16[6144,512]{1,0:T(8,128)(2,1)} async-done(((bf16[384,512]{1,0:T(8,128)(2,1)}), bf16[6144,512]{1,0:T(8,128)(2,1)}) %all-gather.5.cloned.1.call-update) | async-done | bytes 6291472 | tf_op jit(solution)/shard_map/all_gather | solution.py:115
  242.8 182.7 %while.17 = (s32[]{:T(128)}, f32[4,4,384]{2,1,0:T(4,128)S(1)}, f32[4,4,384]{2,1,0:T(4,128)S(1)}, f32[4,4,384,128]{3,2,1,0:T(8,128)}, s32[12]{0:T(128)S(1)}, /*in...) while((s32[]{:T(128)}, f32[4,4,384]{2,1,0:T(4,128)S(1)}, ...), condition=%wide.region_11.12_spmd.clone, body=%wide.region_8.11_spmd.clone.sunk | while | flops 1654102272 | bytes 52042900 | solution.py:128
  251.2 5.6 fusion.56
  265.3 6.9 %fusion.56 = f32[4,4,384,128]{3,2,1,0:T(8,128)} fusion(f32[4,4,384,128]{3,2,1,0:T(8,128)} %get-tuple-element.302, bf16[512,4,128,1]{0,2,3,1:T(8,128)(2,1)S(1)} %bitcast.96, f32[4,512,384,4]{2,1,3,0:T(8,128)S(1)} %get-tuple-element.284, f32[4,4,384]{2,1,0:T(4,128)S(1)} %select_maximum_fusion.2, pred[384,512]{0,1:T(8,128)(4,1)S(1)} %broadcast_compare_fusion.2, ...), kind=kOutput, calls=%fused_computation.17.clone.1 | convolution fusion | flops 823394304 | bytes 19644416 | tf_op jit(solution)/shard_map/while/body/eval_jaxpr/kgrp,pkd->kgrd/dot_general | solution.py:104
  280.6 6.9 %fusion.56 = f32[4,4,384,128]{3,2,1,0:T(8,128)} fusion(f32[4,4,384,128]{3,2,1,0:T(8,128)} %get-tuple-element.302, bf16[512,4,128,1]{0,2,3,1:T(8,128)(2,1)S(1)} %bitcast.96, f32[4,512,384,4]{2,1,3,0:T(8,128)S(1)} %get-tuple-element.284, f32[4,4,384]{2,1,0:T(4,128)S(1)} %select_maximum_fusion.2, pred[384,512]{0,1:T(8,128)(4,1)S(1)} %broadcast_compare_fusion.2, ...), kind=kOutput, calls=%fused_computation.17.clone.1 | convolution fusion | flops 823394304 | bytes 19644416 | tf_op jit(solution)/shard_map/while/body/eval_jaxpr/kgrp,pkd->kgrd/dot_general | solution.py:104
  296.0 6.9 %fusion.56 = f32[4,4,384,128]{3,2,1,0:T(8,128)} fusion(f32[4,4,384,128]{3,2,1,0:T(8,128)} %get-tuple-element.302, bf16[512,4,128,1]{0,2,3,1:T(8,128)(2,1)S(1)} %bitcast.96, f32[4,512,384,4]{2,1,3,0:T(8,128)S(1)} %get-tuple-element.284, f32[4,4,384]{2,1,0:T(4,128)S(1)} %select_maximum_fusion.2, pred[384,512]{0,1:T(8,128)(4,1)S(1)} %broadcast_compare_fusion.2, ...), kind=kOutput, calls=%fused_computation.17.clone.1 | convolution fusion | flops 823394304 | bytes 19644416 | tf_op jit(solution)/shard_map/while/body/eval_jaxpr/kgrp,pkd->kgrd/dot_general | solution.py:104
  311.3 6.9 %fusion.56 = f32[4,4,384,128]{3,2,1,0:T(8,128)} fusion(f32[4,4,384,128]{3,2,1,0:T(8,128)} %get-tuple-element.302, bf16[512,4,128,1]{0,2,3,1:T(8,128)(2,1)S(1)} %bitcast.96, f32[4,512,384,4]{2,1,3,0:T(8,128)S(1)} %get-tuple-element.284, f32[4,4,384]{2,1,0:T(4,128)S(1)} %select_maximum_fusion.2, pred[384,512]{0,1:T(8,128)(4,1)S(1)} %broadcast_compare_fusion.2, ...), kind=kOutput, calls=%fused_computation.17.clone.1 | convolution fusion | flops 823394304 | bytes 19644416 | tf_op jit(solution)/shard_map/while/body/eval_jaxpr/kgrp,pkd->kgrd/dot_general | solution.py:104
  326.6 6.9 %fusion.56 = f32[4,4,384,128]{3,2,1,0:T(8,128)} fusion(f32[4,4,384,128]{3,2,1,0:T(8,128)} %get-tuple-element.302, bf16[512,4,128,1]{0,2,3,1:T(8,128)(2,1)S(1)} %bitcast.96, f32[4,512,384,4]{2,1,3,0:T(8,128)S(1)} %get-tuple-element.284, f32[4,4,384]{2,1,0:T(4,128)S(1)} %select_maximum_fusion.2, pred[384,512]{0,1:T(8,128)(4,1)S(1)} %broadcast_compare_fusion.2, ...), kind=kOutput, calls=%fused_computation.17.clone.1 | convolution fusion | flops 823394304 | bytes 19644416 | tf_op jit(solution)/shard_map/while/body/eval_jaxpr/kgrp,pkd->kgrd/dot_general | solution.py:104
  341.9 6.9 %fusion.56 = f32[4,4,384,128]{3,2,1,0:T(8,128)} fusion(f32[4,4,384,128]{3,2,1,0:T(8,128)} %get-tuple-element.302, bf16[512,4,128,1]{0,2,3,1:T(8,128)(2,1)S(1)} %bitcast.96, f32[4,512,384,4]{2,1,3,0:T(8,128)S(1)} %get-tuple-element.284, f32[4,4,384]{2,1,0:T(4,128)S(1)} %select_maximum_fusion.2, pred[384,512]{0,1:T(8,128)(4,1)S(1)} %broadcast_compare_fusion.2, ...), kind=kOutput, calls=%fused_computation.17.clone.1 | convolution fusion | flops 823394304 | bytes 19644416 | tf_op jit(solution)/shard_map/while/body/eval_jaxpr/kgrp,pkd->kgrd/dot_general | solution.py:104
  357.3 6.9 %fusion.56 = f32[4,4,384,128]{3,2,1,0:T(8,128)} fusion(f32[4,4,384,128]{3,2,1,0:T(8,128)} %get-tuple-element.302, bf16[512,4,128,1]{0,2,3,1:T(8,128)(2,1)S(1)} %bitcast.96, f32[4,512,384,4]{2,1,3,0:T(8,128)S(1)} %get-tuple-element.284, f32[4,4,384]{2,1,0:T(4,128)S(1)} %select_maximum_fusion.2, pred[384,512]{0,1:T(8,128)(4,1)S(1)} %broadcast_compare_fusion.2, ...), kind=kOutput, calls=%fused_computation.17.clone.1 | convolution fusion | flops 823394304 | bytes 19644416 | tf_op jit(solution)/shard_map/while/body/eval_jaxpr/kgrp,pkd->kgrd/dot_general | solution.py:104
  372.6 6.9 %fusion.56 = f32[4,4,384,128]{3,2,1,0:T(8,128)} fusion(f32[4,4,384,128]{3,2,1,0:T(8,128)} %get-tuple-element.302, bf16[512,4,128,1]{0,2,3,1:T(8,128)(2,1)S(1)} %bitcast.96, f32[4,512,384,4]{2,1,3,0:T(8,128)S(1)} %get-tuple-element.284, f32[4,4,384]{2,1,0:T(4,128)S(1)} %select_maximum_fusion.2, pred[384,512]{0,1:T(8,128)(4,1)S(1)} %broadcast_compare_fusion.2, ...), kind=kOutput, calls=%fused_computation.17.clone.1 | convolution fusion | flops 823394304 | bytes 19644416 | tf_op jit(solution)/shard_map/while/body/eval_jaxpr/kgrp,pkd->kgrd/dot_general | solution.py:104
  387.9 6.9 %fusion.56 = f32[4,4,384,128]{3,2,1,0:T(8,128)} fusion(f32[4,4,384,128]{3,2,1,0:T(8,128)} %get-tuple-element.302, bf16[512,4,128,1]{0,2,3,1:T(8,128)(2,1)S(1)} %bitcast.96, f32[4,512,384,4]{2,1,3,0:T(8,128)S(1)} %get-tuple-element.284, f32[4,4,384]{2,1,0:T(4,128)S(1)} %select_maximum_fusion.2, pred[384,512]{0,1:T(8,128)(4,1)S(1)} %broadcast_compare_fusion.2, ...), kind=kOutput, calls=%fused_computation.17.clone.1 | convolution fusion | flops 823394304 | bytes 19644416 | tf_op jit(solution)/shard_map/while/body/eval_jaxpr/kgrp,pkd->kgrd/dot_general | solution.py:104
  403.2 6.9 %fusion.56 = f32[4,4,384,128]{3,2,1,0:T(8,128)} fusion(f32[4,4,384,128]{3,2,1,0:T(8,128)} %get-tuple-element.302, bf16[512,4,128,1]{0,2,3,1:T(8,128)(2,1)S(1)} %bitcast.96, f32[4,512,384,4]{2,1,3,0:T(8,128)S(1)} %get-tuple-element.284, f32[4,4,384]{2,1,0:T(4,128)S(1)} %select_maximum_fusion.2, pred[384,512]{0,1:T(8,128)(4,1)S(1)} %broadcast_compare_fusion.2, ...), kind=kOutput, calls=%fused_computation.17.clone.1 | convolution fusion | flops 823394304 | bytes 19644416 | tf_op jit(solution)/shard_map/while/body/eval_jaxpr/kgrp,pkd->kgrd/dot_general | solution.py:104
  418.6 6.9 %fusion.56 = f32[4,4,384,128]{3,2,1,0:T(8,128)} fusion(f32[4,4,384,128]{3,2,1,0:T(8,128)} %get-tuple-element.302, bf16[512,4,128,1]{0,2,3,1:T(8,128)(2,1)S(1)} %bitcast.96, f32[4,512,384,4]{2,1,3,0:T(8,128)S(1)} %get-tuple-element.284, f32[4,4,384]{2,1,0:T(4,128)S(1)} %select_maximum_fusion.2, pred[384,512]{0,1:T(8,128)(4,1)S(1)} %broadcast_compare_fusion.2, ...), kind=kOutput, calls=%fused_computation.17.clone.1 | convolution fusion | flops 823394304 | bytes 19644416 | tf_op jit(solution)/shard_map/while/body/eval_jaxpr/kgrp,pkd->kgrd/dot_general | solution.py:104
  428.2 21.5 %fusion.22 = bf16[8192,384]{0,1:T(8,128)(2,1)} fusion(bf16[384,2048]{0,1:T(8,128)(2,1)S(1)} %bitcast.104, bf16[2048,8192]{1,0:T(8,128)(2,1)} %param.13), kind=kOutput, calls=%fused_computation.41 | convolution fusion | flops 12888047616 | bytes 41418752 | tf_op jit(solution)/shard_map/dot_general | solution.py:136
  449.7 77.3 %reduce-scatter.2.cloned.1.call-done = bf16[4096,384]{0,1:T(8,128)(2,1)} async-done(((bf16[8192,384]{0,1:T(8,128)(2,1)}), bf16[4096,384]{0,1:T(8,128)(2,1)}) %reduce-scatter.2.cloned.1.call-update) | async-done | bytes 3145744 | tf_op jit(solution)/shard_map/reduce_scatter | solution.py:135
  527.0 75.4 %all_to_all.37 = bf16[16,24,4096]{2,1,0:T(8,128)(2,1)S(1)} all-to-all(bf16[16,24,4096]{2,1,0:T(8,128)(2,1)} %bitcast.100), channel_id=1, replica_groups=mesh['ctx'=16,'tp'=2] {'ctx'}, dimensions={0} | all-to-all | bytes 6291456 | tf_op jit(solution)/shard_map/all_to_all | solution.py:144
  (212 shorter events, 155.1 us)
Async XLA Ops:
  6.5 19.8 %copy-start = (bf16[768,512]{1,0:T(8,128)(2,1)S(1)}, bf16[768,512]{1,0:T(8,128)(2,1)}, u32[]{:S(2)}) copy-start(bf16[768,512]{1,0:T(8,128)(2,1)} %param.10) | copy-start | bytes 2359300
  6.5 15.3 %copy-start.2 = (bf16[768,512]{1,0:T(8,128)(2,1)S(1)}, bf16[768,512]{1,0:T(8,128)(2,1)}, u32[]{:S(2)}) copy-start(bf16[768,512]{1,0:T(8,128)(2,1)} %param.9) | copy-start | bytes 2359300
  32.8 26.1 %all-to-all-start.2 = ((bf16[16,48,512]{2,1,0:T(8,128)(2,1)}), bf16[16,48,512]{2,1,0:T(8,128)(2,1)S(1)}, u32[]{:S(2)}, u32[]{:S(2)}) async-start(bf16[16,48,512]{2,1,0:T(8,128)(2,1)} %get-tuple-element.216), calls=%async_computation.2 | async-start | bytes 1572864 | tf_op jit(solution)/shard_map/all_to_all | solution.py:69
  40.1 168.5 %all-gather.7.cloned.1.call-start = ((), (), s32[]{:S(2)}) async-start(), calls=%async_computation.7 | async-start | bytes 6684672 | tf_op jit(solution)/shard_map/all_gather | solution.py:116
  61.4 181.3 %all-gather.5.cloned.1.call-start = ((), (), s32[]{:S(2)}) async-start(), calls=%async_computation.6 | async-start | bytes 6684672 | tf_op jit(solution)/shard_map/all_gather | solution.py:115
  119.2 83.1 %all-to-all-start.1 = ((bf16[16,48,2048]{2,1,0:T(8,128)(2,1)}), bf16[16,48,2048]{2,1,0:T(8,128)(2,1)S(1)}, u32[]{:S(2)}, u32[]{:S(2)}) async-start(bf16[16,48,2048]{2,1,0:T(8,128)(2,1)} %broadcast_select_fusion), calls=%async_computation.1 | async-start | bytes 6291456 | tf_op jit(solution)/shard_map/all_to_all | solution.py:67
  124.1 402.9 %reduce-scatter.2.cloned.1.call-start = ((), (), s32[]{:S(2)}) async-start(), calls=%async_computation.5 | async-start | bytes 9437184 | tf_op jit(solution)/shard_map/reduce_scatter | solution.py:135
  602.4 3.4 copy-start.1
Sparse Core Ops, SparseCore 0:
  61.6 96.0 all-gather.6
  159.9 82.8 all-gather.4
  449.8 77.1 reduce-scatter.1
where the time goes:
time: 614 us; the launch traced here: 612 us
  waiting for transfers between devices  208 us (34%)
  matrix products  129 us (21%)
  blocking collectives  113 us (18%)
  other arithmetic  70.3 us (11%)
  local copies, waits for them, and re-layouts  65.7 us (11%)
  between operations  13.4 us (2%)
  starting transfers between devices  12.6 us (2%)
    dot_general x12, matrix products, absorb_block(): jnp.einsum('kgrp,pkd->kgrd', weights_b, value_heads, preferred_element_ty...  81 us
    all_to_all x1, waiting for transfers between devices, local(): lax.all_to_all(pack_rows(rot_query), 'ctx', split_axis=0, concat_axis=0,...  77.9 us
    reduce_scatter x1, waiting for transfers between devices, local(): lax.psum_scatter(lax.dot_general(out_weight, attention, (((0,), (1,)), ((...  77.3 us
    all_to_all x1, blocking collectives, local(): lax.all_to_all(projected, 'ctx', split_axis=0, concat_axis=0, tiled=True)  75.4 us
    all_to_all x1, blocking collectives, local(): lax.all_to_all(pack_rows(rot_key), 'ctx', split_axis=0, concat_axis=0, ti...  37.2 us
    reduce_sum x12, other arithmetic, absorb_block(): new_sum = run_sum * rescale + jnp.sum(weights, axis=-1)  36.3 us
    all_gather x1, waiting for transfers between devices, local(): key_piece = lax.all_gather(key_local, 'ctx', axis=0, tiled=True)  34.1 us
    dynamic_slice x48, local copies, waits for them, and re-layouts, local(): lax.scan(one_turn, state, (key_blocks, value_blocks, block_firsts))  27.7 us
  transfers between devices with their start and end apart: 5, of which 4 were waited for; matrix products, arithmetic and copies ran while one was open for 4% of the time, Pallas kernels for 0%

commit v1 on v0

v1 whole, which is shorter than its diff:
```python
import functools
import math

import jax
import jax.numpy as jnp
from jax import lax
from jax.experimental import pallas as pl
from jax.experimental.pallas import tpu as pltpu
from jax.sharding import PartitionSpec as P

HD = 128
TOK_DEV = 384
TILE = 16
PAD = 128
CHUNKS = 2

rope_base = 1000000.0
masked_score = -1e30
exp2_scale = math.log2(math.e) / math.sqrt(HD)
VMEM_BYTES = 58 * 1024 * 1024


def whole_vmem():
    return pl.BlockSpec(memory_space=pltpu.VMEM)


def whole_smem():
    return pl.BlockSpec(memory_space=pltpu.SMEM)


def params():
    return pltpu.CompilerParams(vmem_limit_bytes=VMEM_BYTES)


def turn(rows, cosine, sine):
    as_float = rows.astype(jnp.float32)
    swapped = pltpu.roll(as_float, HD // 2, 1)
    return (as_float * cosine + swapped * sine).astype(jnp.bfloat16)


def one_hot(slots, count):
    ids = lax.broadcasted_iota(jnp.int32, (count, slots.shape[1]), 0)
    return (ids == slots).astype(jnp.float32).astype(jnp.bfloat16)


def pack_kv_kernel(slot_ref, cos_ref, sin_ref, key_ref, value_ref, out_ref, hot_ref):
    @pl.when(pl.program_id(0) == 0)
    def _():
        hot_ref[...] = one_hot(slot_ref[...], hot_ref.shape[0])

    both = jnp.concatenate([turn(key_ref[...], cos_ref[...], sin_ref[...]), value_ref[...]], axis=1)
    out_ref[0] = jnp.dot(hot_ref[...], both, preferred_element_type=jnp.float32).astype(jnp.bfloat16)


def pack_kv(slots, cosine, sine, key, value, cap):
    rows = key.shape[0]
    heads = key.shape[1] // HD
    fixed = lambda i: (0, 0)
    return pl.pallas_call(
        pack_kv_kernel,
        grid=(heads,),
        in_specs=[
            pl.BlockSpec((1, rows), fixed),
            pl.BlockSpec((rows, HD), fixed),
            pl.BlockSpec((rows, HD), fixed),
            pl.BlockSpec((rows, HD), lambda i: (0, i)),
            pl.BlockSpec((rows, HD), lambda i: (0, i)),
        ],
        out_specs=pl.BlockSpec((1, cap, 2 * HD), lambda i: (i, 0, 0)),
        out_shape=jax.ShapeDtypeStruct((heads, cap, 2 * HD), jnp.bfloat16),
        scratch_shapes=[pltpu.VMEM((cap, rows), jnp.bfloat16)],
        compiler_params=params(),
        cost_estimate=pl.CostEstimate(
            flops=2 * heads * cap * rows * 2 * HD, bytes_accessed=rows * heads * HD * 8, transcendentals=0
        ),
    )(slots, cosine, sine, key, value)


def pack_q_kernel(classes, cap, slot_ref, cos_ref, sin_ref, query_ref, *rest):
    out_refs, hot_ref = rest[:-1], rest[-1]

    @pl.when(pl.program_id(0) == 0)
    def _():
        hot_ref[...] = one_hot(slot_ref[...], hot_ref.shape[0])

    cosine, sine = cos_ref[...], sin_ref[...]
    both = jnp.concatenate(
        [turn(query_ref[:, :HD], cosine, sine), turn(query_ref[:, HD:], cosine, sine)], axis=1
    )
    for j, out_ref in enumerate(out_refs):
        for r in range(classes):
            first = (j * classes + r) * cap
            moved = jnp.dot(
                hot_ref[first : first + cap, :], both, preferred_element_type=jnp.float32
            ).astype(jnp.bfloat16)
            out_ref[0, r] = moved[:, :HD]
            out_ref[1, r] = moved[:, HD:]


def pack_q(slots, cosine, sine, query, chunks, classes, cap):
    rows = query.shape[0]
    heads = query.shape[1] // HD
    fixed = lambda i: (0, 0)
    total = chunks * classes * cap
    return pl.pallas_call(
        functools.partial(pack_q_kernel, classes, cap),
        grid=(heads // 2,),
        in_specs=[
            pl.BlockSpec((1, rows), fixed),
            pl.BlockSpec((rows, HD), fixed),
            pl.BlockSpec((rows, HD), fixed),
            pl.BlockSpec((rows, 2 * HD), lambda i: (0, i)),
        ],
        out_specs=[pl.BlockSpec((2, classes, cap, HD), lambda i: (i, 0, 0, 0))] * chunks,
        out_shape=[jax.ShapeDtypeStruct((heads, classes, cap, HD), jnp.bfloat16)] * chunks,
        scratch_shapes=[pltpu.VMEM((total, rows), jnp.bfloat16)],
        compiler_params=params(),
        cost_estimate=pl.CostEstimate(
            flops=2 * heads * total * rows * HD, bytes_accessed=rows * heads * HD * 4, transcendentals=0
        ),
    )(slots, cosine, sine, query)


def piece_rows(cap):
    return max(rows for rows in range(TILE, PAD + 1, TILE) if cap % rows == 0)


def merge_pieces(first_tile, pieces, piece, source, add):
    def one(i, carry):
        at = pl.multiple_of(first_tile * TILE + i * piece, TILE)
        add(at, source(pl.multiple_of(i * piece, TILE)))
        return carry

    lax.fori_loop(0, pieces, one, 0)


def compact_kv_kernel(per, total, tile_ref, piece_ref, *rest):
    parts, (key_out, value_out), (key_all, value_all) = rest[:-4], rest[-4:-2], rest[-2:]
    piece = piece_rows(parts[0].shape[1])
    key_all[...] = jnp.zeros_like(key_all)
    value_all[...] = jnp.zeros_like(value_all)

    def add(at, rows):
        key_all[pl.ds(at, piece), :] += rows[:, :HD]
        value_all[pl.ds(at, piece), :] += rows[:, HD:]

    for k, part in enumerate(parts):
        for z in range(per):
            entry = k * per + z
            merge_pieces(
                tile_ref[entry], piece_ref[entry], piece, lambda at: part[z, pl.ds(at, piece), :], add
            )
    key_out[...] = key_all[:total, :]
    value_out[:, :HD] = value_all[:total, :]
    value_out[:, HD:] = jnp.ones((total, HD), jnp.bfloat16)


def compact_kv(tiles, pieces, parts, total):
    per = parts[0].shape[0]
    return pl.pallas_call(
        functools.partial(compact_kv_kernel, per, total),
        in_specs=[whole_smem(), whole_smem()] + [whole_vmem()] * len(parts),
        out_specs=[whole_vmem()] * 2,
        out_shape=[
            jax.ShapeDtypeStruct((total, HD), jnp.bfloat16),
            jax.ShapeDtypeStruct((total, 2 * HD), jnp.bfloat16),
        ],
        scratch_shapes=[pltpu.VMEM((total + PAD, HD), jnp.bfloat16)] * 2,
        compiler_params=params(),
        cost_estimate=pl.CostEstimate(flops=total * HD * 8, bytes_accessed=total * HD * 16, transcendentals=0),
    )(tiles, pieces, *parts)


def attend_kernel(ctx_size, block, base_ref, tile_ref, piece_ref, got_ref, key_ref, value_ref, out_ref,
                  query_all, scores, run_max, run_acc):
    span = 2 * TOK_DEV
    pair = 2 * block
    piece = piece_rows(got_ref.shape[1])
    query_all[...] = jnp.zeros_like(query_all)

    def add(at, rows):
        query_all[pl.ds(at, piece), :] += rows

    for s in range(ctx_size):
        merge_pieces(tile_ref[s], piece_ref[s], piece, lambda at: got_ref[s, pl.ds(at, piece), :], add)

    def score(to, i, k):
        rows = query_all[pl.ds(pl.multiple_of(i * pair, TILE), pair), :]
        keys = key_ref[pl.ds(pl.multiple_of(k * span, TILE), span), :]
        scores[to] = lax.dot_general(
            rows, keys, (((1,), (1,)), ((), ())), preferred_element_type=jnp.float32
        )

    def absorb(found, k):
        before = run_max[...]
        after = jnp.maximum(before, jnp.max(found, axis=1, keepdims=True))
        weights = jnp.exp2((found - jnp.concatenate([after] * (span // HD), axis=1)) * exp2_scale)
        rescale = jnp.exp2((before - after) * exp2_scale)
        run_max[...] = after
        values = value_ref[pl.ds(pl.multiple_of(k * span, TILE), span), :]
        run_acc[...] = run_acc[...] * jnp.concatenate([rescale, rescale], axis=1) + jnp.dot(
            weights.astype(jnp.bfloat16), values, preferred_element_type=jnp.float32
        )

    supers = ctx_size // 2
    base = base_ref[0]
    score(0, 0, 0)

    def one_super(i, step):
        run_max[...] = jnp.full_like(run_max, masked_score)
        run_acc[...] = jnp.zeros_like(run_acc)

        def one_block(k, step):
            now = step % 2
            score(1 - now, i, k + 1)
            absorb(scores[now], k)
            return step + 1

        step = lax.fori_loop(0, i, one_block, step)
        now = step % 2
        score(1 - now, jnp.minimum(i + 1, supers - 1), 0)
        row = lax.broadcasted_iota(jnp.int32, (pair, span), 0)
        col = lax.broadcasted_iota(jnp.int32, (pair, span), 1)
        row = jnp.where(row >= block, row + (TOK_DEV - block), row) + base
        absorb(jnp.where(col <= row, scores[now], masked_score), i)
        result = (run_acc[:, :HD] / run_acc[:, HD:]).astype(jnp.bfloat16)
        out_ref[2 * i] = result[:block]
        out_ref[2 * i + 1] = result[block:]
        return step + 1

    lax.fori_loop(0, supers, one_super, 0)


def attend(base, tiles, pieces, got, keys, values, block):
    ctx_size = got.shape[0]
    total = keys.shape[0]
    pairs = total * ctx_size * block // 2
    return pl.pallas_call(
        functools.partial(attend_kernel, ctx_size, block),
        in_specs=[whole_smem()] * 3 + [whole_vmem()] * 3,
        out_specs=whole_vmem(),
        out_shape=jax.ShapeDtypeStruct((ctx_size, block, HD), jnp.bfloat16),
        scratch_shapes=[
            pltpu.VMEM((ctx_size * block + PAD, HD), jnp.bfloat16),
            pltpu.VMEM((2, 2 * block, 2 * TOK_DEV), jnp.float32),
            pltpu.VMEM((2 * block, HD), jnp.float32),
            pltpu.VMEM((2 * block, 2 * HD), jnp.float32),
        ],
        compiler_params=params(),
        cost_estimate=pl.CostEstimate(
            flops=pairs * 8 * HD, bytes_accessed=total * HD * 8, transcendentals=pairs
        ),
    )(base, tiles, pieces, got, keys, values)


def project_kernel(classes, column_ref, got_ref, weight_ref, out_ref, rows_ref):
    block = got_ref.shape[1]

    @pl.when(pl.program_id(0) == 0)
    def _():
        for d in range(got_ref.shape[0]):
            h, r = d // classes, d % classes
            rows_ref[r * block : (r + 1) * block, h * HD : (h + 1) * HD] = got_ref[d]

    out_ref[...] = jnp.dot(
        rows_ref[...], weight_ref[...], preferred_element_type=jnp.float32
    ).astype(jnp.bfloat16)


def project(first_column, got, weight, columns, classes):
    ctx_size, block, _ = got.shape
    rows, depth = classes * block, weight.shape[0]
    step = min(512, columns)
    return pl.pallas_call(
        functools.partial(project_kernel, classes),
        grid_spec=pltpu.PrefetchScalarGridSpec(
            num_scalar_prefetch=1,
            grid=(columns // step,),
            in_specs=[
                pl.BlockSpec((ctx_size, block, HD), lambda i, first: (0, 0, 0)),
                pl.BlockSpec((depth, step), lambda i, first: (0, first[0] + i)),
            ],
            out_specs=pl.BlockSpec((rows, step), lambda i, first: (0, i)),
            scratch_shapes=[pltpu.VMEM((rows, depth), jnp.bfloat16)],
        ),
        out_shape=jax.ShapeDtypeStruct((rows, columns), jnp.bfloat16),
        compiler_params=params(),
        cost_estimate=pl.CostEstimate(
            flops=2 * rows * depth * columns, bytes_accessed=2 * depth * columns, transcendentals=0
        ),
    )((first_column // step).astype(jnp.int32).reshape(1), got, weight)


def tables(query_rows):
    half_dim = HD // 2
    positions = lax.axis_index("ctx") * query_rows + jnp.arange(query_rows, dtype=jnp.int32)
    inv_freq = rope_base ** (-(jnp.arange(half_dim, dtype=jnp.float32) * 2.0 / HD))
    angles = positions.astype(jnp.float32)[:, None] * inv_freq[None, :]
    cosine, sine = jnp.cos(angles), jnp.sin(angles)
    return jnp.concatenate([cosine, cosine], axis=1), jnp.concatenate([-sine, sine], axis=1)


def rows_below(start, cls, block):
    return start // TOK_DEV * block + jnp.clip(start % TOK_DEV - cls * block, 0, block)


def piece_table(starts, ends, cls, block, cap):
    piece = piece_rows(cap)
    low, high = rows_below(starts, cls, block), rows_below(ends, cls, block)
    return low // TILE, jnp.where(high > low, (high - low + low % TILE + piece - 1) // piece, 0)


def local(query, key, value, keep_rank, kept_count, out_weight):
    ctx_size = lax.axis_size("ctx")
    tp_size = lax.axis_size("tp")
    me = lax.axis_index("ctx")
    tp_me = lax.axis_index("tp")
    orig_rows = query.shape[0]
    heads = query.shape[1] // HD
    kv_heads = key.shape[1] // HD
    members = ctx_size // kv_heads
    classes = ctx_size // heads
    chunks = CHUNKS if classes == 1 else 1
    block = TOK_DEV // (chunks * classes)
    total = ctx_size * TOK_DEV
    reach = orig_rows // TOK_DEV
    cap = reach * block + TILE
    cap_kv = orig_rows + TILE

    ends = jnp.cumsum(kept_count)
    starts = ends - kept_count
    ids = jnp.arange(ctx_size, dtype=jnp.int32)
    my_count = jnp.sum(jnp.where(ids == me, kept_count, 0))
    my_start = jnp.sum(jnp.where(ids == me, starts, 0))
    is_kept = keep_rank[0] < my_count
    order = jnp.cumsum(is_kept.astype(jnp.int32)) - 1
    place = my_start + order
    kv_slots = jnp.where(is_kept, order + my_start % TILE, -1)[None, :]
    within = place % TOK_DEV
    cls = within // block
    low = rows_below(my_start, cls, block)
    q_slots = jnp.where(
        is_kept, cls * cap + place // TOK_DEV * block + within % block - low + low % TILE, -1
    )[None, :]
    cosine, sine = tables(orig_rows)

    packed_kv = pack_kv(kv_slots, cosine, sine, key, value, cap_kv)
    if kv_heads > 1:
        across = [[z * members + m for z in range(kv_heads)] for m in range(members)]
        packed_kv = lax.all_to_all(
            packed_kv, "ctx", split_axis=0, concat_axis=0, tiled=True, axis_index_groups=across
        )
    parts = [packed_kv]
    bit = members // 2
    offsets = [0]
    while bit >= 1:
        swap = [(d, d ^ bit) for d in range(ctx_size)]
        parts = parts + [lax.ppermute(part, "ctx", swap) for part in parts]
        offsets = offsets + [offset ^ bit for offset in offsets]
        bit //= 2

    packed_q = pack_q(q_slots, cosine, sine, query, chunks, classes, cap)
    got_q = [
        lax.all_to_all(
            one.reshape(ctx_size, cap, HD), "ctx", split_axis=0, concat_axis=0, tiled=True
        )
        for one in packed_q
    ]

    member = me % members
    kv_sources = (
        ids[:kv_heads][None, :] * members + (member ^ jnp.array(offsets, jnp.int32))[:, None]
    ).reshape(-1)
    kv_starts = jnp.sum(jnp.where(kv_sources[:, None] == ids[None, :], starts[None, :], 0), axis=1)
    kv_ends = jnp.sum(jnp.where(kv_sources[:, None] == ids[None, :], ends[None, :], 0), axis=1)
    kv_tiles, kv_pieces = piece_table(kv_starts, kv_ends, 0, TOK_DEV, cap_kv)
    keys, values = compact_kv(kv_tiles, kv_pieces, parts, total)

    mine, other = [], []
    for j in range(chunks):
        cls_j = j * classes + me % classes
        tiles, pieces = piece_table(starts, ends, cls_j, block, cap)
        done = attend(
            (cls_j * block).reshape(1), tiles, pieces, got_q[j], keys, values, block
        )
        got = lax.all_to_all(done, "ctx", split_axis=0, concat_axis=0, tiled=True)
        columns = out_weight.shape[1] // tp_size
        if tp_size == 2:
            theirs = project((1 - tp_me) * columns, got, out_weight, columns, classes)
            other.append(lax.ppermute(theirs, "tp", [(0, 1), (1, 0)]))
            mine.append(project(tp_me * columns, got, out_weight, columns, classes))
        else:
            full = project(jnp.int32(0) * tp_me, got, out_weight, columns * tp_size, classes)
            split = jnp.transpose(full.reshape(full.shape[0], tp_size, columns), (1, 0, 2))
            swapped = lax.all_to_all(split, "tp", split_axis=0, concat_axis=0, tiled=True)
            mine.append(jnp.sum(swapped.astype(jnp.float32), axis=0))
            other.append(jnp.zeros((), jnp.float32))
    return jnp.concatenate(
        [
            (a.astype(jnp.float32) + b.astype(jnp.float32)).astype(jnp.bfloat16)
            for a, b in zip(mine, other)
        ],
        axis=0,
    )


def solution(mesh):
    placed = (P("ctx", "tp"), P("ctx", "tp"), P("ctx", "tp"), P("ctx", None), P(), P("tp", None))
    return jax.shard_map(
        local, mesh=mesh, in_specs=placed, out_specs=P("ctx", "tp"), check_vma=False
    )
```

time: 614 us -> 325 us (0.53)
  Pallas kernels: 0 us -> 153 us
  matrix products: 129 us -> 0 us
  blocking collectives: 113 us -> 0 us
  waiting for transfers between devices: 208 us -> 113 us
  local copies, waits for them, and re-layouts: 65.7 us -> 3.08 us
  other arithmetic: 70.3 us -> 16.3 us
  starting transfers between devices: 12.6 us -> 34.6 us
  between operations: 13.4 us -> 4.07 us
    pallas_call x0 -> x9, Pallas kernels: none -> 153 us  [the longest x2 87.3 us: attend(): pl.pallas_call(functools.partial(attend_kernel, ctx_size, block), in_spec...]
    dot_general x25 -> x0, matrix products: 129 us -> none  [the longest x12 81 us: absorb_block(): jnp.einsum('kgrp,pkd->kgrd', weights_b, value_heads, preferred_element_ty...]
    all_to_all x2 -> x0, blocking collectives: 113 us -> none  [the longest x1 75.4 us: local(): lax.all_to_all(projected, 'ctx', split_axis=0, concat_axis=0, tiled=True)]
    reduce_scatter x1 -> x0, waiting for transfers between devices: 77.3 us -> none  [local(): lax.psum_scatter(lax.dot_general(out_weight, attention, (((0,), (1,)), ((...]
    ppermute x0 -> x5, waiting for transfers between devices: none -> 46.4 us  [the longest x2 25 us: local(): other.append(lax.ppermute(theirs, 'tp', [(0, 1), (1, 0)]))]
    reduce_sum x15 -> x2, other arithmetic: 37.9 us -> 0.81 us  [the longest x1 0.63 us: local(): my_start = jnp.sum(jnp.where(ids == me, starts, 0))]
    all_gather x2 -> x0, waiting for transfers between devices: 34.1 us -> none  [the longest x1 34.1 us: local(): key_piece = lax.all_gather(key_local, 'ctx', axis=0, tiled=True)]
    all_to_all x2 -> x5, waiting for transfers between devices: 96.3 us -> 66.3 us  [the longest x2 31.4 us: local(): lax.all_to_all(one.reshape(ctx_size, cap, HD), 'ctx', split_axis=0, conca...]
  transfers between devices with their start and end apart: 5 -> 10, of which waited for: 4 -> 6; matrix products, arithmetic and copies ran while one was open for 4% -> 1% of each run, Pallas kernels for 0% -> 46%
where the time goes in v1:
time: 325 us; the launch traced here: 324 us
  Pallas kernels  153 us (47%)
  waiting for transfers between devices  113 us (35%)
  starting transfers between devices  34.6 us (11%)
  other arithmetic  16.3 us (5%)
  between operations  4.07 us (1%)
    pallas_call x2, Pallas kernels, attend(): pl.pallas_call(functools.partial(attend_kernel, ctx_size, block), in_spec...  87.3 us
    pallas_call x4, Pallas kernels, project(): pl.pallas_call(functools.partial(project_kernel, classes), grid_spec=pltp...  44.9 us
    all_to_all x2, waiting for transfers between devices, local(): lax.all_to_all(one.reshape(ctx_size, cap, HD), 'ctx', split_axis=0, conca...  31.4 us
    all_to_all x1, waiting for transfers between devices, local(): lax.all_to_all(packed_kv, 'ctx', split_axis=0, concat_axis=0, tiled=True,...  29 us
    ppermute x2, waiting for transfers between devices, local(): other.append(lax.ppermute(theirs, 'tp', [(0, 1), (1, 0)]))  25 us
    ppermute x3, waiting for transfers between devices, local(): parts = parts + [lax.ppermute(part, 'ctx', swap) for part in parts]  21.4 us
    all_to_all x2, starting transfers between devices, local(): lax.all_to_all(one.reshape(ctx_size, cap, HD), 'ctx', split_axis=0, conca...  13.2 us
    all_to_all x2, starting transfers between devices, local(): got = lax.all_to_all(done, 'ctx', split_axis=0, concat_axis=0, tiled=True)  9.59 us
  transfers between devices with their start and end apart: 10, of which 6 were waited for; matrix products, arithmetic and copies ran while one was open for 1% of the time, Pallas kernels for 46%

profile of v1, /device:TPU:0, one launch (start us, length us, event | category | flops | bytes accessed | tf_op | source)
XLA Modules:
  0.0 323.7 jit_solution(2335558508383383048)
XLA Ops:
  0.9 1.9 compare_select_fusion.4
  14.6 5.2 %shard_map.74 = bf16[4,784,256]{2,1,0:T(8,128)(2,1)} custom-call(s32[1,768]{1,0:T(1,128)} %get-tuple-element.28.slot_ref, f32[768,128]{1,0:T(8,128)} %get-tuple-element.34.cos_ref, f32[768,128]{1,0:T(8,128)} %get-tuple-element.35.sin_ref, bf16[768,512]{1,0:T(8,128)(2,1)} %key_ref.1, bf16[768,512]{1,0:T(8,128)(2,1)} %value_ref.1), custom_call_target="tpu_custom_call" | custom-call | flops 1233125376 | bytes 3145728 | tf_op jit(solution)/shard_map/pallas_call | solution.py:59
  19.8 6.3 %all-to-all-start.1 = ((bf16[4,784,256]{2,1,0:T(8,128)(2,1)}), bf16[4,784,256]{2,1,0:T(8,128)(2,1)S(1)}, u32[]{:S(2)}, u32[]{:S(2)}) async-start(bf16[4,784,256]{2,1,0:T(8,128)(2,1)} %shard_map.74), calls=%async_computation.1 | async-start | bytes 3211264 | tf_op jit(solution)/shard_map/all_to_all | solution.py:350
  26.1 8.7 %shard_map.73 = (bf16[16,1,400,128]{3,2,1,0:T(8,128)(2,1)}, bf16[16,1,400,128]{3,2,1,0:T(8,128)(2,1)}) custom-call(s32[1,768]{1,0:T(1,128)} %get-tuple-element.29.slot_ref, f32[768,128]{1,0:T(8,128)} %get-tuple-element.34.cos_ref, f32[768,128]{1,0:T(8,128)} %get-tuple-element.35.sin_ref, bf16[768,2048]{1,0:T(8,128)(2,1)} %query_ref.1), custom_call_target="tpu_custom_call" | custom-call | flops 2516582400 | bytes 6291456 | tf_op jit(solution)/shard_map/pallas_call | solution.py:105
  34.8 29.0 %all-to-all-done.1.rest_0_ = bf16[4,784,256]{2,1,0:T(8,128)(2,1)S(1)} async-done(((bf16[4,784,256]{2,1,0:T(8,128)(2,1)}), bf16[4,784,256]{2,1,0:T(8,128)(2,1)S(1)}, u32[]{:S(2)}, u32[]{:S(2)}) %all-to-all-start.1) | async-done | bytes 1605664 | tf_op jit(solution)/shard_map/all_to_all | solution.py:350
  63.8 3.8 %all-to-all-start.3 = ((bf16[16,400,128]{2,1,0:T(8,128)(2,1)}), bf16[16,400,128]{2,1,0:T(8,128)(2,1)S(1)}, u32[]{:S(2)}, u32[]{:S(2)}) async-start(bf16[16,400,128]{2,1,0:T(8,128)(2,1)} %bitcast.37), calls=%async_computation.3 | async-start | bytes 3276800 | tf_op jit(solution)/shard_map/all_to_all | solution.py:364
  67.6 1.9 collective-permute-start
  69.5 31.4 %all-to-all-done.3.got_ref = bf16[16,400,128]{2,1,0:T(8,128)(2,1)S(1)} async-done(((bf16[16,400,128]{2,1,0:T(8,128)(2,1)}), bf16[16,400,128]{2,1,0:T(8,128)(2,1)S(1)}, u32[]{:S(2)}, u32[]{:S(2)}) %all-to-all-start.3) | async-done | bytes 1638432 | tf_op jit(solution)/shard_map/all_to_all | solution.py:364
  102.1 9.4 %all-to-all-start = ((bf16[16,400,128]{2,1,0:T(8,128)(2,1)}), bf16[16,400,128]{2,1,0:T(8,128)(2,1)S(1)}, u32[]{:S(2)}, u32[]{:S(2)}) async-start(bf16[16,400,128]{2,1,0:T(8,128)(2,1)} %bitcast.2), calls=%async_computation | async-start | bytes 3276800 | tf_op jit(solution)/shard_map/all_to_all | solution.py:364
  111.9 19.8 %collective-permute-done.rest_1_ = bf16[4,784,256]{2,1,0:T(8,128)(2,1)} collective-permute-done((bf16[4,784,256]{2,1,0:T(8,128)(2,1)S(1)}, bf16[4,784,256]{2,1,0:T(8,128)(2,1)}, u32[]{:S(2)}, u32[]{:S(2)}) %collective-permute-start) | collective-permute-done | bytes 1605664 | tf_op jit(solution)/shard_map/ppermute | solution.py:358
  133.9 1.6 collective-permute-done.2.rest_3_
  135.5 6.8 %shard_map.75 = (bf16[6144,128]{1,0:T(8,128)(2,1)}, bf16[6144,256]{1,0:T(8,128)(2,1)}) custom-call(s32[16]{0:T(128)} %and_select_fusion.11.tile_ref, s32[16]{0:T(128)} %get-tuple-element.20.piece_ref, bf16[4,784,256]{2,1,0:T(8,128)(2,1)} %copy-done.2, bf16[4,784,256]{2,1,0:T(8,128)(2,1)} %collective-permute-done.rest_1_, ...), custom_call_target="tpu_custom_call" | custom-call | flops 6291456 | bytes 12582912 | tf_op jit(solution)/shard_map/pallas_call | solution.py:160
  142.3 43.7 %shard_map.79 = bf16[16,192,128]{2,1,0:T(8,128)(2,1)} custom-call(s32[1]{0:T(128)} %constant.243.clone.1.base_ref, s32[16]{0:T(128)} %get-tuple-element.32.tile_ref, s32[16]{0:T(128)} %get-tuple-element.31.piece_ref, bf16[16,400,128]{2,1,0:T(8,128)(2,1)} %copy-done.5, bf16[6144,128]{1,0:T(8,128)(2,1)} %get-tuple-element.10.key_ref, ...), custom_call_target="tpu_custom_call" | custom-call | flops 9663676416 | bytes 6291456 | tf_op jit(solution)/shard_map/pallas_call | solution.py:238
  186.0 3.6 %all-to-all-start.4 = ((bf16[16,192,128]{2,1,0:T(8,128)(2,1)}), bf16[16,192,128]{2,1,0:T(8,128)(2,1)S(1)}, u32[]{:S(2)}, u32[]{:S(2)}) async-start(bf16[16,192,128]{2,1,0:T(8,128)(2,1)} %shard_map.79), calls=%async_computation.4 | async-start | bytes 1572864 | tf_op jit(solution)/shard_map/all_to_all | solution.py:386
  189.6 43.7 %shard_map.76 = bf16[16,192,128]{2,1,0:T(8,128)(2,1)} custom-call(s32[1]{0:T(128)} %constant.227.clone.1.base_ref, s32[16]{0:T(128)} %get-tuple-element.30.tile_ref, s32[16]{0:T(128)} %get-tuple-element.15.piece_ref, bf16[16,400,128]{2,1,0:T(8,128)(2,1)} %copy-done.4, bf16[6144,128]{1,0:T(8,128)(2,1)} %get-tuple-element.10.key_ref, ...), custom_call_target="tpu_custom_call" | custom-call | flops 9663676416 | bytes 6291456 | tf_op jit(solution)/shard_map/pallas_call | solution.py:238
  233.3 6.0 %all-to-all-start.2 = ((bf16[16,192,128]{2,1,0:T(8,128)(2,1)}), bf16[16,192,128]{2,1,0:T(8,128)(2,1)S(1)}, u32[]{:S(2)}, u32[]{:S(2)}) async-start(bf16[16,192,128]{2,1,0:T(8,128)(2,1)} %shard_map.76), calls=%async_computation.2 | async-start | bytes 1572864 | tf_op jit(solution)/shard_map/all_to_all | solution.py:386
  239.3 11.2 %shard_map.81 = bf16[192,4096]{1,0:T(8,128)(2,1)} custom-call(s32[1]{0:T(128)} %bitcast.3.column_ref, bf16[16,192,128]{2,1,0:T(8,128)(2,1)} %copy-done, bf16[2048,8192]{1,0:T(8,128)(2,1)} %weight_ref.7), custom_call_target="tpu_custom_call" | custom-call | flops 3221225472 | bytes 16777216 | tf_op jit(solution)/shard_map/pallas_call | solution.py:274
  252.1 5.9 %all-to-all-done.2.got_ref = bf16[16,192,128]{2,1,0:T(8,128)(2,1)S(1)} async-done(((bf16[16,192,128]{2,1,0:T(8,128)(2,1)}), bf16[16,192,128]{2,1,0:T(8,128)(2,1)S(1)}, u32[]{:S(2)}, u32[]{:S(2)}) %all-to-all-start.2) | async-done | bytes 786464 | tf_op jit(solution)/shard_map/all_to_all | solution.py:386
  258.9 11.2 %shard_map.78 = bf16[192,4096]{1,0:T(8,128)(2,1)} custom-call(s32[1]{0:T(128)} %bitcast.3.column_ref, bf16[16,192,128]{2,1,0:T(8,128)(2,1)} %copy-done.1, bf16[2048,8192]{1,0:T(8,128)(2,1)} %weight_ref.7), custom_call_target="tpu_custom_call" | custom-call | flops 3221225472 | bytes 16777216 | tf_op jit(solution)/shard_map/pallas_call | solution.py:274
  271.6 11.2 %shard_map.77 = bf16[192,4096]{1,0:T(8,128)(2,1)} custom-call(s32[1]{0:T(128)} %bitcast.column_ref, bf16[16,192,128]{2,1,0:T(8,128)(2,1)} %copy-done.1, bf16[2048,8192]{1,0:T(8,128)(2,1)} %weight_ref.7), custom_call_target="tpu_custom_call" | custom-call | flops 3221225472 | bytes 16777216 | tf_op jit(solution)/shard_map/pallas_call | solution.py:274
  282.9 11.2 %shard_map.80 = bf16[192,4096]{1,0:T(8,128)(2,1)} custom-call(s32[1]{0:T(128)} %bitcast.column_ref, bf16[16,192,128]{2,1,0:T(8,128)(2,1)} %copy-done, bf16[2048,8192]{1,0:T(8,128)(2,1)} %weight_ref.7), custom_call_target="tpu_custom_call" | custom-call | flops 3221225472 | bytes 16777216 | tf_op jit(solution)/shard_map/pallas_call | solution.py:274
  294.1 2.1 add_convert_fusion
  296.2 25.0 %collective-permute-done.3 = bf16[192,4096]{1,0:T(8,128)(2,1)S(1)} collective-permute-done((bf16[192,4096]{1,0:T(8,128)(2,1)}, bf16[192,4096]{1,0:T(8,128)(2,1)S(1)}, u32[]{:S(2)}, u32[]{:S(2)}) %collective-permute-start.3) | collective-permute-done | bytes 1572896 | tf_op jit(solution)/shard_map/ppermute | solution.py:390
  321.7 2.0 pad_maximum_fusion
  (49 shorter events, 17.0 us)
Async XLA Ops:
  9.1 4.2 %copy-start.6 = (s32[1,768]{1,0:T(1,128)S(1)}, s32[1,768]{1,0:T(1,128)}, u32[]{:S(2)}) copy-start(s32[1,768]{1,0:T(1,128)} %param.10) | copy-start | bytes 9220
  19.8 44.0 %all-to-all-start.1 = ((bf16[4,784,256]{2,1,0:T(8,128)(2,1)}), bf16[4,784,256]{2,1,0:T(8,128)(2,1)S(1)}, u32[]{:S(2)}, u32[]{:S(2)}) async-start(bf16[4,784,256]{2,1,0:T(8,128)(2,1)} %shard_map.74), calls=%async_computation.1 | async-start | bytes 3211264 | tf_op jit(solution)/shard_map/all_to_all | solution.py:350
  63.8 47.7 %copy-start.2 = (bf16[4,784,256]{2,1,0:T(8,128)(2,1)}, bf16[4,784,256]{2,1,0:T(8,128)(2,1)S(1)}, u32[]{:S(2)}) copy-start(bf16[4,784,256]{2,1,0:T(8,128)(2,1)S(1)} %all-to-all-done.1.rest_0_) | copy-start | bytes 4816900
  63.8 37.1 %all-to-all-start.3 = ((bf16[16,400,128]{2,1,0:T(8,128)(2,1)}), bf16[16,400,128]{2,1,0:T(8,128)(2,1)S(1)}, u32[]{:S(2)}, u32[]{:S(2)}) async-start(bf16[16,400,128]{2,1,0:T(8,128)(2,1)} %bitcast.37), calls=%async_computation.3 | async-start | bytes 3276800 | tf_op jit(solution)/shard_map/all_to_all | solution.py:364
  67.6 64.1 %collective-permute-start = (bf16[4,784,256]{2,1,0:T(8,128)(2,1)S(1)}, bf16[4,784,256]{2,1,0:T(8,128)(2,1)}, u32[]{:S(2)}, u32[]{:S(2)}) collective-permute-start(bf16[4,784,256]{2,1,0:T(8,128)(2,1)S(1)} %all-to-all-done.1.rest_0_), channel_id=1, source_target_pairs={{0,4},{2,6},{4,0},{6,2},{8,12},{10,14},{12,8},{14,10},{16,20},{18,... | collective-permute-start | bytes 4816904 | tf_op jit(solution)/shard_map/ppermute | solution.py:358
  100.9 1.2 copy-start.5
  100.9 30.8 %copy-start.7 = (s32[4]{0:T(128)S(1)}, s32[4]{0:T(128)}, u32[]{:S(2)}) copy-start(s32[4]{0:T(128)} %constant.245.clone) | copy-start | bytes 52
  102.1 84.0 %all-to-all-start = ((bf16[16,400,128]{2,1,0:T(8,128)(2,1)}), bf16[16,400,128]{2,1,0:T(8,128)(2,1)S(1)}, u32[]{:S(2)}, u32[]{:S(2)}) async-start(bf16[16,400,128]{2,1,0:T(8,128)(2,1)} %bitcast.2), calls=%async_computation | async-start | bytes 3276800 | tf_op jit(solution)/shard_map/all_to_all | solution.py:364
  111.5 22.4 %collective-permute-start.1 = (bf16[4,784,256]{2,1,0:T(8,128)(2,1)S(1)}, bf16[4,784,256]{2,1,0:T(8,128)(2,1)}, u32[]{:S(2)}, u32[]{:S(2)}) collective-permute-start(bf16[4,784,256]{2,1,0:T(8,128)(2,1)S(1)} %all-to-all-done.1.rest_0_), channel_id=1, source_target_pairs={{0,2},{2,0},{4,6},{6,4},{8,10},{10,8},{12,14},{14,12},{16,18},{18,... | collective-permute-start | bytes 4816904 | tf_op jit(solution)/shard_map/ppermute | solution.py:358
  131.7 3.8 %collective-permute-start.2 = (bf16[4,784,256]{2,1,0:T(8,128)(2,1)}, bf16[4,784,256]{2,1,0:T(8,128)(2,1)}, u32[]{:S(2)}, u32[]{:S(2)}) collective-permute-start(bf16[4,784,256]{2,1,0:T(8,128)(2,1)} %collective-permute-done.rest_1_), channel_id=1, source_target_pairs={{0,2},{2,0},{4,6},{6,4},{8,10},{10,8},{12,14},{14,12},{16,18},{18,... | collective-permute-start | bytes 4816904 | tf_op jit(solution)/shard_map/ppermute | solution.py:358
  186.0 3.6 %copy-start.4 = (bf16[16,400,128]{2,1,0:T(8,128)(2,1)}, bf16[16,400,128]{2,1,0:T(8,128)(2,1)S(1)}, u32[]{:S(2)}) copy-start(bf16[16,400,128]{2,1,0:T(8,128)(2,1)S(1)} %all-to-all-done.got_ref) | copy-start | bytes 4915204
  186.0 47.3 %all-to-all-start.4 = ((bf16[16,192,128]{2,1,0:T(8,128)(2,1)}), bf16[16,192,128]{2,1,0:T(8,128)(2,1)S(1)}, u32[]{:S(2)}, u32[]{:S(2)}) async-start(bf16[16,192,128]{2,1,0:T(8,128)(2,1)} %shard_map.79), calls=%async_computation.4 | async-start | bytes 1572864 | tf_op jit(solution)/shard_map/all_to_all | solution.py:386
  233.3 6.0 %copy-start = (bf16[16,192,128]{2,1,0:T(8,128)(2,1)}, bf16[16,192,128]{2,1,0:T(8,128)(2,1)S(1)}, u32[]{:S(2)}) copy-start(bf16[16,192,128]{2,1,0:T(8,128)(2,1)S(1)} %all-to-all-done.4.got_ref) | copy-start | bytes 2359300
  233.3 24.7 %all-to-all-start.2 = ((bf16[16,192,128]{2,1,0:T(8,128)(2,1)}), bf16[16,192,128]{2,1,0:T(8,128)(2,1)S(1)}, u32[]{:S(2)}, u32[]{:S(2)}) async-start(bf16[16,192,128]{2,1,0:T(8,128)(2,1)} %shard_map.76), calls=%async_computation.2 | async-start | bytes 1572864 | tf_op jit(solution)/shard_map/all_to_all | solution.py:386
  250.5 43.6 %collective-permute-start.4 = (bf16[192,4096]{1,0:T(8,128)(2,1)}, bf16[192,4096]{1,0:T(8,128)(2,1)S(1)}, u32[]{:S(2)}, u32[]{:S(2)}) collective-permute-start(bf16[192,4096]{1,0:T(8,128)(2,1)} %shard_map.81), channel_id=1, source_target_pairs={{0,1},{1,0},{2,3},{3,2},{4,5},{5,4},{6,7},{7,6},{8,9},{9,8},{10,11... | collective-permute-start | bytes 4718600 | tf_op jit(solution)/shard_map/ppermute | solution.py:390
  258.0 0.9 copy-start.1
  270.1 51.0 %collective-permute-start.3 = (bf16[192,4096]{1,0:T(8,128)(2,1)}, bf16[192,4096]{1,0:T(8,128)(2,1)S(1)}, u32[]{:S(2)}, u32[]{:S(2)}) collective-permute-start(bf16[192,4096]{1,0:T(8,128)(2,1)} %shard_map.78), channel_id=1, source_target_pairs={{0,1},{1,0},{2,3},{3,2},{4,5},{5,4},{6,7},{7,6},{8,9},{9,8},{10,11... | collective-permute-start | bytes 4718600 | tf_op jit(solution)/shard_map/ppermute | solution.py:390
  294.1 27.0 %copy-start.3 = (bf16[192,4096]{1,0:T(8,128)(2,1)S(1)}, bf16[192,4096]{1,0:T(8,128)(2,1)}, u32[]{:S(2)}) copy-start(bf16[192,4096]{1,0:T(8,128)(2,1)} %shard_map.77) | copy-start | bytes 4718596

commit v2 on v1

v2 whole, which is shorter than its diff:
```python
import functools
import math

import jax
import jax.numpy as jnp
from jax import lax
from jax.experimental import pallas as pl
from jax.experimental.pallas import tpu as pltpu
from jax.sharding import PartitionSpec as P

HD = 128
TOK_DEV = 384
TILE = 16
PAD = 128
CHUNKS = 2

rope_base = 1000000.0
masked_score = -1e30
exp2_scale = math.log2(math.e) / math.sqrt(HD)
VMEM_BYTES = 58 * 1024 * 1024


def whole_vmem():
    return pl.BlockSpec(memory_space=pltpu.VMEM)


def whole_smem():
    return pl.BlockSpec(memory_space=pltpu.SMEM)


def params():
    return pltpu.CompilerParams(vmem_limit_bytes=VMEM_BYTES)


def turn(rows, cosine, sine):
    as_float = rows.astype(jnp.float32)
    swapped = pltpu.roll(as_float, HD // 2, 1)
    return (as_float * cosine + swapped * sine).astype(jnp.bfloat16)


def rows_below(start, cls, block):
    whole = lax.div(start, TOK_DEV)
    return whole * block + jnp.clip(start - whole * TOK_DEV - cls * block, 0, block)


def slots_kernel(reach, groups, block, cap, me_ref, count_ref, rank_ref, kv_out, q_out):
    me = me_ref[0]
    rows = rank_ref.shape[1]
    start = jnp.int32(0)
    for s in range(count_ref.shape[0]):
        start = start + jnp.where(s < me, count_ref[s], 0)
    kept = rank_ref[...] < count_ref[me]
    upper = lax.broadcasted_iota(jnp.int32, (rows, rows), 0) <= lax.broadcasted_iota(
        jnp.int32, (rows, rows), 1
    )
    flags = jnp.broadcast_to(kept.astype(jnp.float32), (8, rows)).astype(jnp.bfloat16)
    order = (
        jnp.dot(
            flags, upper.astype(jnp.float32).astype(jnp.bfloat16), preferred_element_type=jnp.float32
        )[:1].astype(jnp.int32)
        - 1
    )
    kv_out[...] = jnp.where(kept, order + (start & (TILE - 1)), -1)
    place = start + order
    first = lax.div(start, TOK_DEV)
    device = first + jnp.zeros_like(place)
    for step in range(1, reach + 1):
        device = device + (place >= (first + step) * TOK_DEV).astype(jnp.int32)
    within = place - device * TOK_DEV
    cls = jnp.zeros_like(place)
    for step in range(1, groups):
        cls = cls + (within >= step * block).astype(jnp.int32)
    low = first * block + jnp.clip(start - first * TOK_DEV - cls * block, 0, block)
    slot = cls * cap + device * block + within - cls * block - low + (low & (TILE - 1))
    q_out[...] = jnp.where(kept, slot, -1)


def find_slots(me, counts, ranks, reach, groups, block, cap):
    shape = jax.ShapeDtypeStruct(ranks.shape, jnp.int32)
    return pl.pallas_call(
        functools.partial(slots_kernel, reach, groups, block, cap),
        in_specs=[whole_smem(), whole_smem(), whole_vmem()],
        out_specs=[whole_vmem()] * 2,
        out_shape=[shape, shape],
        compiler_params=params(),
        cost_estimate=pl.CostEstimate(flops=2**20, bytes_accessed=2**14, transcendentals=0),
    )(me, counts, ranks)


def pack_kernel(turned, classes, cap, width, slot_ref, cos_ref, sin_ref, row_ref, *rest):
    out_refs, hot_ref = rest[:-1], rest[-1]

    @pl.when(pl.program_id(0) == 0)
    def _():
        ids = lax.broadcasted_iota(jnp.int32, hot_ref.shape, 0)
        hot_ref[...] = (ids == slot_ref[...]).astype(jnp.float32).astype(jnp.bfloat16)

    if turned:
        rows = jnp.concatenate(
            [
                turn(row_ref[:, h * HD : (h + 1) * HD], cos_ref[...], sin_ref[...])
                for h in range(width)
            ],
            axis=1,
        )
    else:
        rows = row_ref[...]
    for j, out_ref in enumerate(out_refs):
        for r in range(classes):
            first = (j * classes + r) * cap
            moved = jnp.dot(
                hot_ref[first : first + cap, :], rows, preferred_element_type=jnp.float32
            ).astype(jnp.bfloat16)
            for h in range(width):
                out_ref[h, r] = moved[:, h * HD : (h + 1) * HD]


def pack(slots, cosine, sine, rows, turned, chunks, classes, cap):
    count = rows.shape[0]
    heads = rows.shape[1] // HD
    width = min(2, heads)
    fixed = lambda i: (0, 0)
    total = chunks * classes * cap
    return pl.pallas_call(
        functools.partial(pack_kernel, turned, classes, cap, width),
        grid=(heads // width,),
        in_specs=[
            pl.BlockSpec((1, count), fixed),
            pl.BlockSpec((count, HD), fixed),
            pl.BlockSpec((count, HD), fixed),
            pl.BlockSpec((count, width * HD), lambda i: (0, i)),
        ],
        out_specs=[pl.BlockSpec((width, classes, cap, HD), lambda i: (i, 0, 0, 0))] * chunks,
        out_shape=[jax.ShapeDtypeStruct((heads, classes, cap, HD), jnp.bfloat16)] * chunks,
        scratch_shapes=[pltpu.VMEM((total, count), jnp.bfloat16)],
        compiler_params=params(),
        cost_estimate=pl.CostEstimate(
            flops=2 * heads * total * count * HD, bytes_accessed=count * heads * HD * 4, transcendentals=0
        ),
    )(slots, cosine, sine, rows)


def piece_rows(cap):
    return max(rows for rows in range(TILE, PAD + 1, TILE) if cap % rows == 0)


def merge_pieces(low, high, piece, source, add):
    shift = low & (TILE - 1)
    pieces = jnp.where(high > low, lax.div(high - low + shift + piece - 1, piece), 0)
    first = low - shift

    def one(i, carry):
        at = pl.multiple_of(first + i * piece, TILE)
        add(at, source(pl.multiple_of(i * piece, TILE)))
        return carry

    lax.fori_loop(0, pieces, one, 0)


def compact_kernel(offsets, per, total, doubled, member_ref, count_ref, *rest):
    parts, out, all_rows, starts = rest[:-3], rest[-3], rest[-2], rest[-1]
    members = len(parts)
    piece = piece_rows(parts[0].shape[1])
    all_rows[...] = jnp.zeros_like(all_rows)
    start = jnp.int32(0)
    for s in range(count_ref.shape[0]):
        starts[s] = start
        start = start + count_ref[s]

    def add(at, rows):
        all_rows[pl.ds(at, piece), :] += rows

    for part, offset in zip(parts, offsets):
        for z in range(per):
            source = z * members + (member_ref[0] ^ offset)
            low = starts[source]
            merge_pieces(
                low,
                low + count_ref[source],
                piece,
                lambda at: part[z, pl.ds(at, piece), :],
                add,
            )
    out[:, :HD] = all_rows[:total, :]
    out[:, HD:] = all_rows[:total, :] if doubled else jnp.ones((total, HD), jnp.bfloat16)


def compact(member, counts, parts, offsets, total, doubled):
    per = parts[0].shape[0]
    return pl.pallas_call(
        functools.partial(compact_kernel, offsets, per, total, doubled),
        in_specs=[whole_smem(), whole_smem()] + [whole_vmem()] * len(parts),
        out_specs=whole_vmem(),
        out_shape=jax.ShapeDtypeStruct((total, 2 * HD), jnp.bfloat16),
        scratch_shapes=[
            pltpu.VMEM((total + PAD, HD), jnp.bfloat16),
            pltpu.SMEM(counts.shape, jnp.int32),
        ],
        compiler_params=params(),
        cost_estimate=pl.CostEstimate(flops=total * HD * 8, bytes_accessed=total * HD * 8, transcendentals=0),
    )(member, counts, *parts)


def attend_kernel(ctx_size, block, cls_ref, count_ref, got_ref, key_ref, value_ref, out_ref,
                  query_all, query_two, scores_a, scores_b, top_a, top_b, run_max, run_acc):
    span = 2 * TOK_DEV
    pair = 2 * block
    supers = ctx_size // 2
    steps = supers * (supers + 1) // 2
    cls = cls_ref[0]
    piece = piece_rows(got_ref.shape[1])
    query_all[...] = jnp.zeros_like(query_all)

    def add(at, rows):
        query_all[pl.ds(at, piece), :] += rows

    start = jnp.int32(0)
    for s in range(ctx_size):
        end = start + count_ref[s]
        merge_pieces(
            rows_below(start, cls, block),
            rows_below(end, cls, block),
            piece,
            lambda at: got_ref[s, pl.ds(at, piece), :],
            add,
        )
        start = end

    def split(i, carry):
        rows = pl.ds(pl.multiple_of(i * pair, TILE), pair)
        scaled = query_all[rows, :].astype(jnp.float32) * exp2_scale
        high = scaled.astype(jnp.bfloat16)
        query_two[rows, :HD] = high
        query_two[rows, HD:] = (scaled - high.astype(jnp.float32)).astype(jnp.bfloat16)
        return carry

    lax.fori_loop(0, supers, split, 0)

    def row_top(found):
        return jnp.broadcast_to(jnp.max(found, axis=1, keepdims=True), (pair, HD))

    def score(scores, top, i, k):
        rows = query_two[pl.ds(pl.multiple_of(jnp.minimum(i, supers - 1) * pair, TILE), pair), :]
        keys = key_ref[pl.ds(pl.multiple_of(k * span, TILE), span), :]
        found = lax.dot_general(
            rows, keys, (((1,), (1,)), ((), ())), preferred_element_type=jnp.float32
        )
        scores[...] = found
        top[...] = row_top(found)

    def mask(scores, top):
        row = lax.broadcasted_iota(jnp.int32, (pair, span), 0)
        col = lax.broadcasted_iota(jnp.int32, (pair, span), 1)
        row = jnp.where(row >= block, row + (TOK_DEV - block), row) + cls * block
        found = jnp.where(col <= row, scores[...], masked_score)
        scores[...] = found
        top[...] = row_top(found)

    def absorb(scores, top, k):
        before = run_max[...]
        after = jnp.maximum(before, top[...])
        rescale = jnp.exp2(before - after)
        run_max[...] = after
        weights = jnp.exp2(scores[...] - jnp.concatenate([after] * (span // HD), axis=1))
        values = value_ref[pl.ds(pl.multiple_of(k * span, TILE), span), :]
        run_acc[...] = run_acc[...] * jnp.concatenate([rescale, rescale], axis=1) + jnp.dot(
            weights.astype(jnp.bfloat16), values, preferred_element_type=jnp.float32
        )

    def clear():
        run_max[...] = jnp.full_like(run_max, masked_score)
        run_acc[...] = jnp.zeros_like(run_acc)

    def one_step(now, later, i, k):
        last = k == i
        next_i = jnp.where(last, i + 1, i)
        next_k = jnp.where(last, 0, k + 1)
        score(*later, next_i, next_k)
        absorb(*now, k)

        @pl.when(last)
        def _():
            result = (run_acc[:, :HD] / run_acc[:, HD:]).astype(jnp.bfloat16)
            out_ref[2 * i] = result[:block]
            out_ref[2 * i + 1] = result[block:]
            clear()

        @pl.when(next_k == next_i)
        def _():
            mask(*later)

        return next_i, next_k

    buffers_a, buffers_b = (scores_a, top_a), (scores_b, top_b)
    clear()
    score(*buffers_a, 0, 0)
    mask(*buffers_a)

    def two_steps(t, at):
        at = one_step(buffers_a, buffers_b, *at)
        return one_step(buffers_b, buffers_a, *at)

    lax.fori_loop(0, steps // 2, two_steps, (jnp.int32(0), jnp.int32(0)))


def attend(cls, counts, got, keys, values, block):
    ctx_size = got.shape[0]
    total = keys.shape[0]
    pairs = total * ctx_size * block // 2
    return pl.pallas_call(
        functools.partial(attend_kernel, ctx_size, block),
        in_specs=[whole_smem()] * 2 + [whole_vmem()] * 3,
        out_specs=whole_vmem(),
        out_shape=jax.ShapeDtypeStruct((ctx_size, block, HD), jnp.bfloat16),
        scratch_shapes=[
            pltpu.VMEM((ctx_size * block + PAD, HD), jnp.bfloat16),
            pltpu.VMEM((ctx_size * block, 2 * HD), jnp.bfloat16),
            pltpu.VMEM((2 * block, 2 * TOK_DEV), jnp.float32),
            pltpu.VMEM((2 * block, 2 * TOK_DEV), jnp.float32),
            pltpu.VMEM((2 * block, HD), jnp.float32),
            pltpu.VMEM((2 * block, HD), jnp.float32),
            pltpu.VMEM((2 * block, HD), jnp.float32),
            pltpu.VMEM((2 * block, 2 * HD), jnp.float32),
        ],
        compiler_params=params(),
        cost_estimate=pl.CostEstimate(
            flops=pairs * 8 * HD, bytes_accessed=total * HD * 8, transcendentals=pairs
        ),
    )(cls, counts, got, keys, values)


def project_kernel(classes, column_ref, got_ref, weight_ref, out_ref, rows_ref):
    block = got_ref.shape[1]

    @pl.when(pl.program_id(0) == 0)
    def _():
        for d in range(got_ref.shape[0]):
            h, r = d // classes, d % classes
            rows_ref[r * block : (r + 1) * block, h * HD : (h + 1) * HD] = got_ref[d]

    out_ref[...] = jnp.dot(
        rows_ref[...], weight_ref[...], preferred_element_type=jnp.float32
    ).astype(jnp.bfloat16)


def project(first_column, got, weight, columns, classes):
    ctx_size, block, _ = got.shape
    rows, depth = classes * block, weight.shape[0]
    step = min(512, columns)
    return pl.pallas_call(
        functools.partial(project_kernel, classes),
        grid_spec=pltpu.PrefetchScalarGridSpec(
            num_scalar_prefetch=1,
            grid=(columns // step,),
            in_specs=[
                pl.BlockSpec((ctx_size, block, HD), lambda i, first: (0, 0, 0)),
                pl.BlockSpec((depth, step), lambda i, first: (0, first[0] + i)),
            ],
            out_specs=pl.BlockSpec((rows, step), lambda i, first: (0, i)),
            scratch_shapes=[pltpu.VMEM((rows, depth), jnp.bfloat16)],
        ),
        out_shape=jax.ShapeDtypeStruct((rows, columns), jnp.bfloat16),
        compiler_params=params(),
        cost_estimate=pl.CostEstimate(
            flops=2 * rows * depth * columns, bytes_accessed=2 * depth * columns, transcendentals=0
        ),
    )((first_column // step).astype(jnp.int32).reshape(1), got, weight)


def tables(query_rows):
    half_dim = HD // 2
    positions = lax.axis_index("ctx") * query_rows + jnp.arange(query_rows, dtype=jnp.int32)
    lane = jnp.arange(HD, dtype=jnp.int32)
    pair_id = jnp.where(lane < half_dim, lane, lane - half_dim)
    inv_freq = rope_base ** (-(pair_id.astype(jnp.float32) * 2.0 / HD))
    angles = positions.astype(jnp.float32)[:, None] * inv_freq[None, :]
    sine = jnp.sin(angles)
    return jnp.cos(angles), jnp.where(lane[None, :] < half_dim, -sine, sine)


def local(query, key, value, keep_rank, kept_count, out_weight):
    ctx_size = lax.axis_size("ctx")
    tp_size = lax.axis_size("tp")
    me = lax.axis_index("ctx")
    tp_me = lax.axis_index("tp")
    orig_rows = query.shape[0]
    heads = query.shape[1] // HD
    kv_heads = key.shape[1] // HD
    members = ctx_size // kv_heads
    classes = ctx_size // heads
    chunks = CHUNKS if classes == 1 else 1
    block = TOK_DEV // (chunks * classes)
    total = ctx_size * TOK_DEV
    reach = orig_rows // TOK_DEV
    cap = reach * block + TILE
    cap_kv = orig_rows + TILE
    columns = out_weight.shape[1] // tp_size

    kv_slots, q_slots = find_slots(
        me.reshape(1), kept_count, keep_rank, reach, chunks * classes, block, cap
    )
    cosine, sine = tables(orig_rows)

    across = [[z * members + m for z in range(kv_heads)] for m in range(members)]

    def spread(rows, turned):
        (packed,) = pack(kv_slots, cosine, sine, rows, turned, 1, 1, cap_kv)
        packed = packed.reshape(kv_heads, cap_kv, HD)
        if kv_heads > 1:
            packed = lax.all_to_all(
                packed, "ctx", split_axis=0, concat_axis=0, tiled=True, axis_index_groups=across
            )
        parts, offsets = [packed], [0]
        bit = members // 2
        while bit >= 1:
            swap = [(d, d ^ bit) for d in range(ctx_size)]
            parts = parts + [lax.ppermute(part, "ctx", swap) for part in parts]
            offsets = offsets + [offset ^ bit for offset in offsets]
            bit //= 2
        return compact((me & (members - 1)).reshape(1), kept_count, parts, offsets, total, turned)

    keys = spread(key, True)
    values = spread(value, False)
    packed_q = pack(q_slots, cosine, sine, query, True, chunks, classes, cap)
    got_q = [
        lax.all_to_all(
            one.reshape(ctx_size, cap, HD), "ctx", split_axis=0, concat_axis=0, tiled=True
        )
        for one in packed_q
    ]

    mine, other = [], []
    for j in range(chunks):
        cls_j = j * classes + (me & (classes - 1))
        done = attend(cls_j.reshape(1), kept_count, got_q[j], keys, values, block)
        got = lax.all_to_all(done, "ctx", split_axis=0, concat_axis=0, tiled=True)
        if tp_size == 2:
            theirs = project((1 - tp_me) * columns, got, out_weight, columns, classes)
            other.append(lax.ppermute(theirs, "tp", [(0, 1), (1, 0)]))
            mine.append(project(tp_me * columns, got, out_weight, columns, classes))
        else:
            full = project(jnp.int32(0) * tp_me, got, out_weight, columns * tp_size, classes)
            split = jnp.transpose(full.reshape(full.shape[0], tp_size, columns), (1, 0, 2))
            swapped = lax.all_to_all(split, "tp", split_axis=0, concat_axis=0, tiled=True)
            mine.append(jnp.sum(swapped.astype(jnp.float32), axis=0))
            other.append(jnp.zeros((), jnp.float32))
    return jnp.concatenate(
        [
            (a.astype(jnp.float32) + b.astype(jnp.float32)).astype(jnp.bfloat16)
            for a, b in zip(mine, other)
        ],
        axis=0,
    )


def solution(mesh):
    placed = (P("ctx", "tp"), P("ctx", "tp"), P("ctx", "tp"), P("ctx", None), P(), P("tp", None))
    return jax.shard_map(
        local, mesh=mesh, in_specs=placed, out_specs=P("ctx", "tp"), check_vma=False
    )
```

time: 325 us -> 326 us (level)
  blocking collectives: 0 us -> 44.2 us
  Pallas kernels: 153 us -> 131 us
  other arithmetic: 16.3 us -> 7.12 us
  starting transfers between devices: 34.6 us -> 30 us
  between operations: 4.07 us -> 0.12 us
    all_to_all x0 -> x1, blocking collectives: none -> 44.2 us  [local(): lax.all_to_all(one.reshape(ctx_size, cap, HD), 'ctx', split_axis=0, conca...]
    all_to_all x2 -> x1, waiting for transfers between devices: 31.4 us -> 0.01 us  [local(): lax.all_to_all(one.reshape(ctx_size, cap, HD), 'ctx', split_axis=0, conca...]
    ppermute x3 -> x6, waiting for transfers between devices: 21.4 us -> 52.5 us  [spread(): parts = parts + [lax.ppermute(part, 'ctx', swap) for part in parts]]
    pallas_call x2, Pallas kernels: 87.3 us -> 58.3 us  [attend(): pl.pallas_call(functools.partial(attend_kernel, ctx_size, block), in_spec...]
    all_to_all x2 -> x1, starting transfers between devices: 13.2 us -> 3.71 us  [local(): lax.all_to_all(one.reshape(ctx_size, cap, HD), 'ctx', split_axis=0, conca...]
    pallas_call x3 -> x6, Pallas kernels: 20.8 us -> 27.4 us  [the longest x3 15.4 us: pack(): pl.pallas_call(functools.partial(pack_kernel, turned, classes, cap, width...]
    all_to_all x1 -> x2, starting transfers between devices: 6.32 us -> 9.82 us  [spread(): lax.all_to_all(packed, 'ctx', split_axis=0, concat_axis=0, tiled=True, ax...]
    all_to_all x1 -> x2, waiting for transfers between devices: 29 us -> 28.2 us  [spread(): lax.all_to_all(packed, 'ctx', split_axis=0, concat_axis=0, tiled=True, ax...]
  transfers between devices with their start and end apart: 10 -> 13, of which waited for: 6 -> 6; matrix products, arithmetic and copies ran while one was open for 1% -> 1% of each run, Pallas kernels for 46% -> 39%
where the time goes in v2:
time: 326 us; the launch traced here: 324 us
  Pallas kernels  131 us (40%)
  waiting for transfers between devices  112 us (34%)
  blocking collectives  44.2 us (14%)
  starting transfers between devices  30 us (9%)
  other arithmetic  7.12 us (2%)
    pallas_call x2, Pallas kernels, attend(): pl.pallas_call(functools.partial(attend_kernel, ctx_size, block), in_spec...  58.3 us
    ppermute x6, waiting for transfers between devices, spread(): parts = parts + [lax.ppermute(part, 'ctx', swap) for part in parts]  52.5 us
    pallas_call x4, Pallas kernels, project(): pl.pallas_call(functools.partial(project_kernel, classes), grid_spec=pltp...  44.9 us
    all_to_all x1, blocking collectives, local(): lax.all_to_all(one.reshape(ctx_size, cap, HD), 'ctx', split_axis=0, conca...  44.2 us
    all_to_all x2, waiting for transfers between devices, spread(): lax.all_to_all(packed, 'ctx', split_axis=0, concat_axis=0, tiled=True, ax...  28.2 us
    ppermute x2, waiting for transfers between devices, local(): other.append(lax.ppermute(theirs, 'tp', [(0, 1), (1, 0)]))  25 us
    pallas_call x3, Pallas kernels, pack(): pl.pallas_call(functools.partial(pack_kernel, turned, classes, cap, width...  15.4 us
    all_to_all x2, starting transfers between devices, local(): got = lax.all_to_all(done, 'ctx', split_axis=0, concat_axis=0, tiled=True)  10.8 us
  transfers between devices with their start and end apart: 13, of which 6 were waited for; matrix products, arithmetic and copies ran while one was open for 1% of the time, Pallas kernels for 39%

profile of v2, /device:TPU:0, one launch (start us, length us, event | category | flops | bytes accessed | tf_op | source)
XLA Modules:
  0.0 324.5 jit_solution(11542994513965661590)
XLA Ops:
  1.6 2.5 negate_select_fusion
  4.1 3.2 shard_map.68
  7.3 6.3 %all-to-all-start.2 = ((bf16[4,784,128]{2,1,0:T(8,128)(2,1)}), bf16[4,784,128]{2,1,0:T(8,128)(2,1)S(1)}, u32[]{:S(2)}, u32[]{:S(2)}) async-start(bf16[4,784,128]{2,1,0:T(8,128)(2,1)} %bitcast.9), calls=%async_computation.2 | async-start | bytes 1605632 | tf_op jit(solution)/shard_map/all_to_all | solution.py:410
  13.6 3.5 %shard_map.66 = bf16[4,1,784,128]{3,2,1,0:T(8,128)(2,1)} custom-call(s32[1,768]{1,0:T(1,128)} %get-tuple-element.11.slot_ref, f32[768,128]{1,0:T(8,128)} %get-tuple-element.14.cos_ref, f32[768,128]{1,0:T(8,128)} %get-tuple-element.13.sin_ref, bf16[768,512]{1,0:T(8,128)(2,1)} %row_ref.4), custom_call_target="tpu_custom_call" | custom-call | flops 616562688 | bytes 1572864 | tf_op jit(solution)/shard_map/pallas_call | solution.py:124
  17.1 17.0 %all-to-all-done.2.rest_0_ = bf16[4,784,128]{2,1,0:T(8,128)(2,1)S(1)} async-done(((bf16[4,784,128]{2,1,0:T(8,128)(2,1)}), bf16[4,784,128]{2,1,0:T(8,128)(2,1)S(1)}, u32[]{:S(2)}, u32[]{:S(2)}) %all-to-all-start.2) | async-done | bytes 802848 | tf_op jit(solution)/shard_map/all_to_all | solution.py:410
  34.1 3.5 %all-to-all-start.1 = ((bf16[4,784,128]{2,1,0:T(8,128)(2,1)}), bf16[4,784,128]{2,1,0:T(8,128)(2,1)S(1)}, u32[]{:S(2)}, u32[]{:S(2)}) async-start(bf16[4,784,128]{2,1,0:T(8,128)(2,1)} %bitcast.8), calls=%async_computation.1 | async-start | bytes 1605632 | tf_op jit(solution)/shard_map/all_to_all | solution.py:410
  37.6 8.7 %shard_map.65 = (bf16[16,1,400,128]{3,2,1,0:T(8,128)(2,1)}, bf16[16,1,400,128]{3,2,1,0:T(8,128)(2,1)}) custom-call(s32[1,768]{1,0:T(1,128)} %get-tuple-element.9.slot_ref, f32[768,128]{1,0:T(8,128)} %get-tuple-element.14.cos_ref, f32[768,128]{1,0:T(8,128)} %get-tuple-element.13.sin_ref, bf16[768,2048]{1,0:T(8,128)(2,1)} %row_ref.3), custom_call_target="tpu_custom_call" | custom-call | flops 2516582400 | bytes 6291456 | tf_op jit(solution)/shard_map/pallas_call | solution.py:124
  46.3 11.2 %all-to-all-done.1.rest_0_ = bf16[4,784,128]{2,1,0:T(8,128)(2,1)S(1)} async-done(((bf16[4,784,128]{2,1,0:T(8,128)(2,1)}), bf16[4,784,128]{2,1,0:T(8,128)(2,1)S(1)}, u32[]{:S(2)}, u32[]{:S(2)}) %all-to-all-start.1) | async-done | bytes 802848 | tf_op jit(solution)/shard_map/all_to_all | solution.py:410
  57.5 44.2 %all_to_all.30.got_ref = bf16[16,400,128]{2,1,0:T(8,128)(2,1)} all-to-all(bf16[16,400,128]{2,1,0:T(8,128)(2,1)} %bitcast.10), channel_id=1, replica_groups=mesh['ctx'=16,'tp'=2] {'ctx'}, dimensions={0} | all-to-all | bytes 3276800 | tf_op jit(solution)/shard_map/all_to_all | solution.py:426
  101.6 3.7 %all-to-all-start = ((bf16[16,400,128]{2,1,0:T(8,128)(2,1)}), bf16[16,400,128]{2,1,0:T(8,128)(2,1)S(1)}, u32[]{:S(2)}, u32[]{:S(2)}) async-start(bf16[16,400,128]{2,1,0:T(8,128)(2,1)} %bitcast.2), calls=%async_computation | async-start | bytes 3276800 | tf_op jit(solution)/shard_map/all_to_all | solution.py:426
  107.5 36.3 %collective-permute-done.rest_1_ = bf16[4,784,128]{2,1,0:T(8,128)(2,1)} collective-permute-done((bf16[4,784,128]{2,1,0:T(8,128)(2,1)S(1)}, bf16[4,784,128]{2,1,0:T(8,128)(2,1)}, u32[]{:S(2)}, u32[]{:S(2)}) %collective-permute-start) | collective-permute-done | bytes 802848 | tf_op jit(solution)/shard_map/ppermute | solution.py:417
  144.2 16.2 %collective-permute-done.3.rest_1_ = bf16[4,784,128]{2,1,0:T(8,128)(2,1)} collective-permute-done((bf16[4,784,128]{2,1,0:T(8,128)(2,1)S(1)}, bf16[4,784,128]{2,1,0:T(8,128)(2,1)}, u32[]{:S(2)}, u32[]{:S(2)}) %collective-permute-start.3) | collective-permute-done | bytes 802848 | tf_op jit(solution)/shard_map/ppermute | solution.py:417
  160.5 5.3 %shard_map.67.key_ref = bf16[6144,256]{1,0:T(8,128)(2,1)} custom-call(s32[1]{0:T(128)} %bitcast.3.member_ref, s32[16]{0:T(128)} %count_ref.9, bf16[4,784,128]{2,1,0:T(8,128)(2,1)} %copy-done.4, bf16[4,784,128]{2,1,0:T(8,128)(2,1)} %collective-permute-done.rest_1_, bf16[4,784,128]{2,1,0:T(8,128)(2,1)} %collective-permute-done.1.rest_2_, ...), custom_call_target="tpu_custom_call" | custom-call | flops 6291456 | bytes 6291456 | tf_op jit(solution)/shard_map/pallas_call | solution.py:190
  165.7 5.2 %shard_map.69.value_ref = bf16[6144,256]{1,0:T(8,128)(2,1)} custom-call(s32[1]{0:T(128)} %bitcast.3.member_ref, s32[16]{0:T(128)} %count_ref.9, bf16[4,784,128]{2,1,0:T(8,128)(2,1)} %copy-done.3, bf16[4,784,128]{2,1,0:T(8,128)(2,1)} %collective-permute-done.3.rest_1_, bf16[4,784,128]{2,1,0:T(8,128)(2,1)} %collective-permute-done.4.rest_2_, ...), custom_call_target="tpu_custom_call" | custom-call | flops 6291456 | bytes 6291456 | tf_op jit(solution)/shard_map/pallas_call | solution.py:190
  170.9 29.0 %shard_map.73 = bf16[16,192,128]{2,1,0:T(8,128)(2,1)} custom-call(s32[1]{0:T(128)} %constant.57.clone.1.cls_ref, s32[16]{0:T(128)} %count_ref.9, bf16[16,400,128]{2,1,0:T(8,128)(2,1)} %all_to_all.30.got_ref, bf16[6144,256]{1,0:T(8,128)(2,1)} %shard_map.67.key_ref, bf16[6144,256]{1,0:T(8,128)(2,1)} %shard_map.69.value_ref), custom_call_target="tpu_custom_call" | custom-call | flops 9663676416 | bytes 6291456 | tf_op jit(solution)/shard_map/pallas_call | solution.py:310
  199.9 4.8 %all-to-all-start.5 = ((bf16[16,192,128]{2,1,0:T(8,128)(2,1)}), bf16[16,192,128]{2,1,0:T(8,128)(2,1)S(1)}, u32[]{:S(2)}, u32[]{:S(2)}) async-start(bf16[16,192,128]{2,1,0:T(8,128)(2,1)} %shard_map.73), calls=%async_computation.5 | async-start | bytes 1572864 | tf_op jit(solution)/shard_map/all_to_all | solution.py:436
  204.8 29.2 %shard_map.70 = bf16[16,192,128]{2,1,0:T(8,128)(2,1)} custom-call(s32[1]{0:T(128)} %constant.49.clone.1.cls_ref, s32[16]{0:T(128)} %count_ref.9, bf16[16,400,128]{2,1,0:T(8,128)(2,1)} %copy-done.5, bf16[6144,256]{1,0:T(8,128)(2,1)} %shard_map.67.key_ref, bf16[6144,256]{1,0:T(8,128)(2,1)} %shard_map.69.value_ref), custom_call_target="tpu_custom_call" | custom-call | flops 9663676416 | bytes 6291456 | tf_op jit(solution)/shard_map/pallas_call | solution.py:310
  234.0 6.0 %all-to-all-start.3 = ((bf16[16,192,128]{2,1,0:T(8,128)(2,1)}), bf16[16,192,128]{2,1,0:T(8,128)(2,1)S(1)}, u32[]{:S(2)}, u32[]{:S(2)}) async-start(bf16[16,192,128]{2,1,0:T(8,128)(2,1)} %shard_map.70), calls=%async_computation.3 | async-start | bytes 1572864 | tf_op jit(solution)/shard_map/all_to_all | solution.py:436
  240.1 11.2 %shard_map.75 = bf16[192,4096]{1,0:T(8,128)(2,1)} custom-call(s32[1]{0:T(128)} %bitcast.6.column_ref, bf16[16,192,128]{2,1,0:T(8,128)(2,1)} %copy-done, bf16[2048,8192]{1,0:T(8,128)(2,1)} %weight_ref.7), custom_call_target="tpu_custom_call" | custom-call | flops 3221225472 | bytes 16777216 | tf_op jit(solution)/shard_map/pallas_call | solution.py:350
  252.8 5.9 %all-to-all-done.3.got_ref = bf16[16,192,128]{2,1,0:T(8,128)(2,1)S(1)} async-done(((bf16[16,192,128]{2,1,0:T(8,128)(2,1)}), bf16[16,192,128]{2,1,0:T(8,128)(2,1)S(1)}, u32[]{:S(2)}, u32[]{:S(2)}) %all-to-all-start.3) | async-done | bytes 786464 | tf_op jit(solution)/shard_map/all_to_all | solution.py:436
  259.7 11.2 %shard_map.72 = bf16[192,4096]{1,0:T(8,128)(2,1)} custom-call(s32[1]{0:T(128)} %bitcast.6.column_ref, bf16[16,192,128]{2,1,0:T(8,128)(2,1)} %copy-done.1, bf16[2048,8192]{1,0:T(8,128)(2,1)} %weight_ref.7), custom_call_target="tpu_custom_call" | custom-call | flops 3221225472 | bytes 16777216 | tf_op jit(solution)/shard_map/pallas_call | solution.py:350
  272.4 11.2 %shard_map.71 = bf16[192,4096]{1,0:T(8,128)(2,1)} custom-call(s32[1]{0:T(128)} %bitcast.column_ref, bf16[16,192,128]{2,1,0:T(8,128)(2,1)} %copy-done.1, bf16[2048,8192]{1,0:T(8,128)(2,1)} %weight_ref.7), custom_call_target="tpu_custom_call" | custom-call | flops 3221225472 | bytes 16777216 | tf_op jit(solution)/shard_map/pallas_call | solution.py:350
  283.6 11.2 %shard_map.74 = bf16[192,4096]{1,0:T(8,128)(2,1)} custom-call(s32[1]{0:T(128)} %bitcast.column_ref, bf16[16,192,128]{2,1,0:T(8,128)(2,1)} %copy-done, bf16[2048,8192]{1,0:T(8,128)(2,1)} %weight_ref.7), custom_call_target="tpu_custom_call" | custom-call | flops 3221225472 | bytes 16777216 | tf_op jit(solution)/shard_map/pallas_call | solution.py:350
  296.9 25.0 %collective-permute-done.6 = bf16[192,4096]{1,0:T(8,128)(2,1)S(1)} collective-permute-done((bf16[192,4096]{1,0:T(8,128)(2,1)}, bf16[192,4096]{1,0:T(8,128)(2,1)S(1)}, u32[]{:S(2)}, u32[]{:S(2)}) %collective-permute-start.6) | collective-permute-done | bytes 1572896 | tf_op jit(solution)/shard_map/ppermute | solution.py:439
  (34 shorter events, 12.8 us)
Async XLA Ops:
  7.3 26.8 %all-to-all-start.2 = ((bf16[4,784,128]{2,1,0:T(8,128)(2,1)}), bf16[4,784,128]{2,1,0:T(8,128)(2,1)S(1)}, u32[]{:S(2)}, u32[]{:S(2)}) async-start(bf16[4,784,128]{2,1,0:T(8,128)(2,1)} %bitcast.9), calls=%async_computation.2 | async-start | bytes 1605632 | tf_op jit(solution)/shard_map/all_to_all | solution.py:410
  34.0 109.7 %copy-start.3 = (bf16[4,784,128]{2,1,0:T(8,128)(2,1)}, bf16[4,784,128]{2,1,0:T(8,128)(2,1)S(1)}, u32[]{:S(2)}) copy-start(bf16[4,784,128]{2,1,0:T(8,128)(2,1)S(1)} %all-to-all-done.2.rest_0_) | copy-start | bytes 2408452
  34.1 23.4 %all-to-all-start.1 = ((bf16[4,784,128]{2,1,0:T(8,128)(2,1)}), bf16[4,784,128]{2,1,0:T(8,128)(2,1)S(1)}, u32[]{:S(2)}, u32[]{:S(2)}) async-start(bf16[4,784,128]{2,1,0:T(8,128)(2,1)} %bitcast.8), calls=%async_computation.1 | async-start | bytes 1605632 | tf_op jit(solution)/shard_map/all_to_all | solution.py:410
  57.5 50.0 %copy-start.4 = (bf16[4,784,128]{2,1,0:T(8,128)(2,1)}, bf16[4,784,128]{2,1,0:T(8,128)(2,1)S(1)}, u32[]{:S(2)}) copy-start(bf16[4,784,128]{2,1,0:T(8,128)(2,1)S(1)} %all-to-all-done.1.rest_0_) | copy-start | bytes 2408452
  101.6 98.3 %all-to-all-start = ((bf16[16,400,128]{2,1,0:T(8,128)(2,1)}), bf16[16,400,128]{2,1,0:T(8,128)(2,1)S(1)}, u32[]{:S(2)}, u32[]{:S(2)}) async-start(bf16[16,400,128]{2,1,0:T(8,128)(2,1)} %bitcast.2), calls=%async_computation | async-start | bytes 3276800 | tf_op jit(solution)/shard_map/all_to_all | solution.py:426
  105.4 38.4 %collective-permute-start = (bf16[4,784,128]{2,1,0:T(8,128)(2,1)S(1)}, bf16[4,784,128]{2,1,0:T(8,128)(2,1)}, u32[]{:S(2)}, u32[]{:S(2)}) collective-permute-start(bf16[4,784,128]{2,1,0:T(8,128)(2,1)S(1)} %all-to-all-done.1.rest_0_), channel_id=1, source_target_pairs={{0,4},{2,6},{4,0},{6,2},{8,12},{10,14},{12,8},{14,10},{16,20},{18,... | collective-permute-start | bytes 2408456 | tf_op jit(solution)/shard_map/ppermute | solution.py:417
  107.2 53.3 %collective-permute-start.3 = (bf16[4,784,128]{2,1,0:T(8,128)(2,1)S(1)}, bf16[4,784,128]{2,1,0:T(8,128)(2,1)}, u32[]{:S(2)}, u32[]{:S(2)}) collective-permute-start(bf16[4,784,128]{2,1,0:T(8,128)(2,1)S(1)} %all-to-all-done.2.rest_0_), channel_id=1, source_target_pairs={{0,4},{2,6},{4,0},{6,2},{8,12},{10,14},{12,8},{14,10},{16,20},{18,... | collective-permute-start | bytes 2408456 | tf_op jit(solution)/shard_map/ppermute | solution.py:417
  107.5 53.0 %collective-permute-start.1 = (bf16[4,784,128]{2,1,0:T(8,128)(2,1)S(1)}, bf16[4,784,128]{2,1,0:T(8,128)(2,1)}, u32[]{:S(2)}, u32[]{:S(2)}) collective-permute-start(bf16[4,784,128]{2,1,0:T(8,128)(2,1)S(1)} %all-to-all-done.1.rest_0_), channel_id=1, source_target_pairs={{0,2},{2,0},{4,6},{6,4},{8,10},{10,8},{12,14},{14,12},{16,18},{18,... | collective-permute-start | bytes 2408456 | tf_op jit(solution)/shard_map/ppermute | solution.py:417
  143.7 16.7 %collective-permute-start.2 = (bf16[4,784,128]{2,1,0:T(8,128)(2,1)}, bf16[4,784,128]{2,1,0:T(8,128)(2,1)}, u32[]{:S(2)}, u32[]{:S(2)}) collective-permute-start(bf16[4,784,128]{2,1,0:T(8,128)(2,1)} %collective-permute-done.rest_1_), channel_id=1, source_target_pairs={{0,2},{2,0},{4,6},{6,4},{8,10},{10,8},{12,14},{14,12},{16,18},{18,... | collective-permute-start | bytes 2408456 | tf_op jit(solution)/shard_map/ppermute | solution.py:417
  143.7 22.0 %collective-permute-start.4 = (bf16[4,784,128]{2,1,0:T(8,128)(2,1)S(1)}, bf16[4,784,128]{2,1,0:T(8,128)(2,1)}, u32[]{:S(2)}, u32[]{:S(2)}) collective-permute-start(bf16[4,784,128]{2,1,0:T(8,128)(2,1)S(1)} %all-to-all-done.2.rest_0_), channel_id=1, source_target_pairs={{0,2},{2,0},{4,6},{6,4},{8,10},{10,8},{12,14},{14,12},{16,18},{18,... | collective-permute-start | bytes 2408456 | tf_op jit(solution)/shard_map/ppermute | solution.py:417
  160.4 5.3 %collective-permute-start.5 = (bf16[4,784,128]{2,1,0:T(8,128)(2,1)}, bf16[4,784,128]{2,1,0:T(8,128)(2,1)}, u32[]{:S(2)}, u32[]{:S(2)}) collective-permute-start(bf16[4,784,128]{2,1,0:T(8,128)(2,1)} %collective-permute-done.3.rest_1_), channel_id=1, source_target_pairs={{0,2},{2,0},{4,6},{6,4},{8,10},{10,8},{12,14},{14,12},{16,18},{18,... | collective-permute-start | bytes 2408456 | tf_op jit(solution)/shard_map/ppermute | solution.py:417
  199.9 4.8 %copy-start.5 = (bf16[16,400,128]{2,1,0:T(8,128)(2,1)}, bf16[16,400,128]{2,1,0:T(8,128)(2,1)S(1)}, u32[]{:S(2)}) copy-start(bf16[16,400,128]{2,1,0:T(8,128)(2,1)S(1)} %all-to-all-done.got_ref) | copy-start | bytes 4915204
  199.9 34.1 %all-to-all-start.5 = ((bf16[16,192,128]{2,1,0:T(8,128)(2,1)}), bf16[16,192,128]{2,1,0:T(8,128)(2,1)S(1)}, u32[]{:S(2)}, u32[]{:S(2)}) async-start(bf16[16,192,128]{2,1,0:T(8,128)(2,1)} %shard_map.73), calls=%async_computation.5 | async-start | bytes 1572864 | tf_op jit(solution)/shard_map/all_to_all | solution.py:436
  234.0 6.0 %copy-start = (bf16[16,192,128]{2,1,0:T(8,128)(2,1)}, bf16[16,192,128]{2,1,0:T(8,128)(2,1)S(1)}, u32[]{:S(2)}) copy-start(bf16[16,192,128]{2,1,0:T(8,128)(2,1)S(1)} %all-to-all-done.5.got_ref) | copy-start | bytes 2359300
  234.0 24.7 %all-to-all-start.3 = ((bf16[16,192,128]{2,1,0:T(8,128)(2,1)}), bf16[16,192,128]{2,1,0:T(8,128)(2,1)S(1)}, u32[]{:S(2)}, u32[]{:S(2)}) async-start(bf16[16,192,128]{2,1,0:T(8,128)(2,1)} %shard_map.70), calls=%async_computation.3 | async-start | bytes 1572864 | tf_op jit(solution)/shard_map/all_to_all | solution.py:436
  251.3 43.6 %collective-permute-start.7 = (bf16[192,4096]{1,0:T(8,128)(2,1)}, bf16[192,4096]{1,0:T(8,128)(2,1)S(1)}, u32[]{:S(2)}, u32[]{:S(2)}) collective-permute-start(bf16[192,4096]{1,0:T(8,128)(2,1)} %shard_map.75), channel_id=1, source_target_pairs={{0,1},{1,0},{2,3},{3,2},{4,5},{5,4},{6,7},{7,6},{8,9},{9,8},{10,11... | collective-permute-start | bytes 4718600 | tf_op jit(solution)/shard_map/ppermute | solution.py:439
  258.8 0.9 copy-start.1
  270.9 51.0 %collective-permute-start.6 = (bf16[192,4096]{1,0:T(8,128)(2,1)}, bf16[192,4096]{1,0:T(8,128)(2,1)S(1)}, u32[]{:S(2)}, u32[]{:S(2)}) collective-permute-start(bf16[192,4096]{1,0:T(8,128)(2,1)} %shard_map.72), channel_id=1, source_target_pairs={{0,1},{1,0},{2,3},{3,2},{4,5},{5,4},{6,7},{7,6},{8,9},{9,8},{10,11... | collective-permute-start | bytes 4718600 | tf_op jit(solution)/shard_map/ppermute | solution.py:439
  294.9 27.1 %copy-start.2 = (bf16[192,4096]{1,0:T(8,128)(2,1)S(1)}, bf16[192,4096]{1,0:T(8,128)(2,1)}, u32[]{:S(2)}) copy-start(bf16[192,4096]{1,0:T(8,128)(2,1)} %shard_map.71) | copy-start | bytes 4718596

commit v3 on v2

--- a/solution.py
+++ b/solution.py
@@ -403,31 +403,54 @@
 
     across = [[z * members + m for z in range(kv_heads)] for m in range(members)]
 
-    def spread(rows, turned):
+    member = (me & (members - 1)).reshape(1)
+
+    def pack_shared(rows, turned):
         (packed,) = pack(kv_slots, cosine, sine, rows, turned, 1, 1, cap_kv)
-        packed = packed.reshape(kv_heads, cap_kv, HD)
-        if kv_heads > 1:
-            packed = lax.all_to_all(
-                packed, "ctx", split_axis=0, concat_axis=0, tiled=True, axis_index_groups=across
-            )
-        parts, offsets = [packed], [0]
-        bit = members // 2
-        while bit >= 1:
-            swap = [(d, d ^ bit) for d in range(ctx_size)]
-            parts = parts + [lax.ppermute(part, "ctx", swap) for part in parts]
-            offsets = offsets + [offset ^ bit for offset in offsets]
-            bit //= 2
-        return compact((me & (members - 1)).reshape(1), kept_count, parts, offsets, total, turned)
-
-    keys = spread(key, True)
-    values = spread(value, False)
-    packed_q = pack(q_slots, cosine, sine, query, True, chunks, classes, cap)
-    got_q = [
-        lax.all_to_all(
-            one.reshape(ctx_size, cap, HD), "ctx", split_axis=0, concat_axis=0, tiled=True
-        )
-        for one in packed_q
-    ]
+        return packed.reshape(kv_heads, cap_kv, HD)
+
+    def send_across(packed):
+        if kv_heads == 1:
+            return packed
+        return lax.all_to_all(
+            packed, "ctx", split_axis=0, concat_axis=0, tiled=True, axis_index_groups=across
+        )
+
+    def swap(parts, bit):
+        pairs = [(d, d ^ bit) for d in range(ctx_size)]
+        return parts + [lax.ppermute(part, "ctx", pairs) for part in parts]
+
+    bits = [members >> n for n in range(1, members.bit_length())]
+    offsets = [0]
+    for bit in bits:
+        offsets = offsets + [offset ^ bit for offset in offsets]
+
+    def send_query(packed):
+        return lax.all_to_all(
+            packed.reshape(ctx_size, cap, HD), "ctx", split_axis=0, concat_axis=0, tiled=True
+        )
+
+    key_parts = [send_across(pack_shared(key, True))]
+    value_packed, key_parts = lax.optimization_barrier((pack_shared(value, False), key_parts))
+    key_parts = swap(key_parts, bits[0])
+    value_parts = [send_across(value_packed)]
+    packed_q = list(pack(q_slots, cosine, sine, query, True, chunks, classes, cap))
+    packed_q[0], key_parts, value_parts = lax.optimization_barrier(
+        (packed_q[0], key_parts, value_parts)
+    )
+    got_q = [send_query(packed_q[0])]
+    value_parts = swap(value_parts, bits[0])
+    for bit in bits[1:]:
+        key_parts = swap(key_parts, bit)
+    if chunks > 1:
+        packed_q[1], key_parts, value_parts = lax.optimization_barrier(
+            (packed_q[1], key_parts, value_parts)
+        )
+    for bit in bits[1:]:
+        value_parts = swap(value_parts, bit)
+    got_q = got_q + [send_query(packed) for packed in packed_q[1:]]
+    keys = compact(member, kept_count, key_parts, offsets, total, True)
+    values = compact(member, kept_count, value_parts, offsets, total, False)
 
     mine, other = [], []
     for j in range(chunks):

time: 326 us -> 276 us (0.85)
  blocking collectives: 44.2 us -> 0 us
  waiting for transfers between devices: 112 us -> 94.8 us
  starting transfers between devices: 30 us -> 39 us
  local copies, waits for them, and re-layouts: 0.9 us -> 4.85 us
    all_to_all x1 -> x0, blocking collectives: 44.2 us -> none  [local(): lax.all_to_all(one.reshape(ctx_size, cap, HD), 'ctx', split_axis=0, conca...]
    all_to_all x3 -> x4, waiting for transfers between devices: 28.2 us -> 18.2 us  [the longest x2 18.2 us: send_across(): lax.all_to_all(packed, 'ctx', split_axis=0, concat_axis=0, tiled=True, ax...]
    ppermute x6, waiting for transfers between devices: 52.5 us -> 44.2 us  [swap(): return parts + [lax.ppermute(part, 'ctx', pairs) for part in parts]]
    all_to_all x3 -> x4, starting transfers between devices: 13.5 us -> 19.4 us  [the longest x2 9.82 us: send_across(): lax.all_to_all(packed, 'ctx', split_axis=0, concat_axis=0, tiled=True, ax...]
    unnamed x12 -> x26, local copies, waits for them, and re-layouts: 0.9 us -> 4.85 us
  transfers between devices with their start and end apart: 13 -> 14, of which waited for: 6 -> 7; matrix products, arithmetic and copies ran while one was open for 1% -> 0% of each run, Pallas kernels for 39% -> 46%
where the time goes in v3:
time: 276 us; the launch traced here: 275 us
  Pallas kernels  131 us (47%)
  waiting for transfers between devices  94.8 us (34%)
  starting transfers between devices  39 us (14%)
  other arithmetic  5.64 us (2%)
  local copies, waits for them, and re-layouts  4.85 us (2%)
    pallas_call x2, Pallas kernels, attend(): pl.pallas_call(functools.partial(attend_kernel, ctx_size, block), in_spec...  58.3 us
    pallas_call x4, Pallas kernels, project(): pl.pallas_call(functools.partial(project_kernel, classes), grid_spec=pltp...  45 us
    ppermute x6, waiting for transfers between devices, swap(): return parts + [lax.ppermute(part, 'ctx', pairs) for part in parts]  44.2 us
    ppermute x2, waiting for transfers between devices, local(): other.append(lax.ppermute(theirs, 'tp', [(0, 1), (1, 0)]))  26.5 us
    all_to_all x2, waiting for transfers between devices, send_across(): lax.all_to_all(packed, 'ctx', split_axis=0, concat_axis=0, tiled=True, ax...  18.2 us
    pallas_call x3, Pallas kernels, pack(): pl.pallas_call(functools.partial(pack_kernel, turned, classes, cap, width...  15.4 us
    all_to_all x2, starting transfers between devices, local(): got = lax.all_to_all(done, 'ctx', split_axis=0, concat_axis=0, tiled=True)  12 us
    pallas_call x2, Pallas kernels, compact(): pl.pallas_call(functools.partial(compact_kernel, offsets, per, total, dou...  10.4 us
  transfers between devices with their start and end apart: 14, of which 7 were waited for; matrix products, arithmetic and copies ran while one was open for 0% of the time, Pallas kernels for 46%

profile of v3, /device:TPU:0, one launch (start us, length us, event | category | flops | bytes accessed | tf_op | source)
XLA Modules:
  0.0 275.0 jit_solution(12863259048981603405)
XLA Ops:
  1.6 2.5 negate_select_fusion
  4.1 3.5 %shard_map.67 = bf16[4,1,784,128]{3,2,1,0:T(8,128)(2,1)} custom-call(s32[1,768]{1,0:T(1,128)} %get-tuple-element.24.slot_ref, f32[768,128]{1,0:T(8,128)} %get-tuple-element.40.cos_ref, f32[768,128]{1,0:T(8,128)} %get-tuple-element.39.sin_ref, bf16[768,512]{1,0:T(8,128)(2,1)} %row_ref.5), custom_call_target="tpu_custom_call" | custom-call | flops 616562688 | bytes 1572864 | tf_op jit(solution)/shard_map/pallas_call | solution.py:124
  7.6 6.3 %all-to-all-start = ((bf16[4,784,128]{2,1,0:T(8,128)(2,1)}), bf16[4,784,128]{2,1,0:T(8,128)(2,1)S(1)}, u32[]{:S(2)}, u32[]{:S(2)}) async-start(bf16[4,784,128]{2,1,0:T(8,128)(2,1)} %bitcast.9), calls=%async_computation | async-start | bytes 1605632 | tf_op jit(solution)/shard_map/all_to_all | solution.py:415
  13.9 3.2 %shard_map.66 = bf16[4,1,784,128]{3,2,1,0:T(8,128)(2,1)} custom-call(s32[1,768]{1,0:T(1,128)} %get-tuple-element.24.slot_ref, f32[768,128]{1,0:T(8,128)} %get-tuple-element.40.cos_ref, f32[768,128]{1,0:T(8,128)} %get-tuple-element.39.sin_ref, bf16[768,512]{1,0:T(8,128)(2,1)} %row_ref.4), custom_call_target="tpu_custom_call" | custom-call | flops 616562688 | bytes 1572864 | tf_op jit(solution)/shard_map/pallas_call | solution.py:124
  17.1 17.3 %all-to-all-done.rest_0_ = bf16[4,784,128]{2,1,0:T(8,128)(2,1)S(1)} async-done(((bf16[4,784,128]{2,1,0:T(8,128)(2,1)}), bf16[4,784,128]{2,1,0:T(8,128)(2,1)S(1)}, u32[]{:S(2)}, u32[]{:S(2)}) %all-to-all-start) | async-done | bytes 802848 | tf_op jit(solution)/shard_map/all_to_all | solution.py:415
  34.4 3.5 %all-to-all-start.1 = ((bf16[4,784,128]{2,1,0:T(8,128)(2,1)}), bf16[4,784,128]{2,1,0:T(8,128)(2,1)S(1)}, u32[]{:S(2)}, u32[]{:S(2)}) async-start(bf16[4,784,128]{2,1,0:T(8,128)(2,1)} %bitcast.8), calls=%async_computation.1 | async-start | bytes 1605632 | tf_op jit(solution)/shard_map/all_to_all | solution.py:415
  39.4 8.7 %shard_map.65 = (bf16[16,1,400,128]{3,2,1,0:T(8,128)(2,1)}, bf16[16,1,400,128]{3,2,1,0:T(8,128)(2,1)}) custom-call(s32[1,768]{1,0:T(1,128)} %get-tuple-element.22.slot_ref, f32[768,128]{1,0:T(8,128)} %get-tuple-element.40.cos_ref, f32[768,128]{1,0:T(8,128)} %get-tuple-element.39.sin_ref, bf16[768,2048]{1,0:T(8,128)(2,1)} %row_ref.3), custom_call_target="tpu_custom_call" | custom-call | flops 2516582400 | bytes 6291456 | tf_op jit(solution)/shard_map/pallas_call | solution.py:124
  48.1 8.8 %collective-permute-done.rest_1_ = bf16[4,784,128]{2,1,0:T(8,128)(2,1)} collective-permute-done((bf16[4,784,128]{2,1,0:T(8,128)(2,1)S(1)}, bf16[4,784,128]{2,1,0:T(8,128)(2,1)}, u32[]{:S(2)}, u32[]{:S(2)}) %collective-permute-start) | collective-permute-done | bytes 802848 | tf_op jit(solution)/shard_map/ppermute | solution.py:421
  57.8 4.9 %all-to-all-start.2 = ((bf16[16,400,128]{2,1,0:T(8,128)(2,1)}), bf16[16,400,128]{2,1,0:T(8,128)(2,1)S(1)}, u32[]{:S(2)}, u32[]{:S(2)}) async-start(bf16[16,400,128]{2,1,0:T(8,128)(2,1)} %bitcast.10), calls=%async_computation.2 | async-start | bytes 3276800 | tf_op jit(solution)/shard_map/all_to_all | solution.py:429
  66.4 34.1 %collective-permute-done.3.rest_1_ = bf16[4,784,128]{2,1,0:T(8,128)(2,1)S(1)} collective-permute-done((bf16[4,784,128]{2,1,0:T(8,128)(2,1)S(1)}, bf16[4,784,128]{2,1,0:T(8,128)(2,1)S(1)}, u32[]{:S(2)}, u32[]{:S(2)}) %collective-permute-start.3) | collective-permute-done | bytes 802848 | tf_op jit(solution)/shard_map/ppermute | solution.py:421
  102.7 4.7 %all-to-all-start.4 = ((bf16[16,400,128]{2,1,0:T(8,128)(2,1)}), bf16[16,400,128]{2,1,0:T(8,128)(2,1)}, u32[]{:S(2)}, u32[]{:S(2)}) async-start(bf16[16,400,128]{2,1,0:T(8,128)(2,1)} %bitcast.7), calls=%async_computation.4 | async-start | bytes 3276800 | tf_op jit(solution)/shard_map/all_to_all | solution.py:429
  108.0 5.3 %shard_map.68.key_ref = bf16[6144,256]{1,0:T(8,128)(2,1)} custom-call(s32[1]{0:T(128)} %bitcast.5.member_ref, s32[16]{0:T(128)} %count_ref.9, bf16[4,784,128]{2,1,0:T(8,128)(2,1)} %copy-done.4, bf16[4,784,128]{2,1,0:T(8,128)(2,1)} %collective-permute-done.rest_1_, bf16[4,784,128]{2,1,0:T(8,128)(2,1)} %copy-done.9, bf16[4,784,128]{2,1,0:T(8,128)(2,1)} %copy-done.10), custom_call_target="tpu_custom_call" | custom-call | flops 6291456 | bytes 6291456 | tf_op jit(solution)/shard_map/pallas_call | solution.py:190
  115.0 5.2 %shard_map.69.value_ref = bf16[6144,256]{1,0:T(8,128)(2,1)} custom-call(s32[1]{0:T(128)} %bitcast.5.member_ref, s32[16]{0:T(128)} %count_ref.9, bf16[4,784,128]{2,1,0:T(8,128)(2,1)} %copy-done.5, bf16[4,784,128]{2,1,0:T(8,128)(2,1)} %copy-done.7, bf16[4,784,128]{2,1,0:T(8,128)(2,1)} %copy-done.11, bf16[4,784,128]{2,1,0:T(8,128)(2,1)} %copy-done.12), custom_call_target="tpu_custom_call" | custom-call | flops 6291456 | bytes 6291456 | tf_op jit(solution)/shard_map/pallas_call | solution.py:190
  120.2 29.1 %shard_map.70 = bf16[16,192,128]{2,1,0:T(8,128)(2,1)} custom-call(s32[1]{0:T(128)} %constant.49.clone.1.cls_ref, s32[16]{0:T(128)} %count_ref.9, bf16[16,400,128]{2,1,0:T(8,128)(2,1)} %copy-done.6, bf16[6144,256]{1,0:T(8,128)(2,1)} %shard_map.68.key_ref, bf16[6144,256]{1,0:T(8,128)(2,1)} %shard_map.69.value_ref), custom_call_target="tpu_custom_call" | custom-call | flops 9663676416 | bytes 6291456 | tf_op jit(solution)/shard_map/pallas_call | solution.py:310
  149.3 6.0 %all-to-all-start.3 = ((bf16[16,192,128]{2,1,0:T(8,128)(2,1)}), bf16[16,192,128]{2,1,0:T(8,128)(2,1)S(1)}, u32[]{:S(2)}, u32[]{:S(2)}) async-start(bf16[16,192,128]{2,1,0:T(8,128)(2,1)} %shard_map.70), calls=%async_computation.3 | async-start | bytes 1572864 | tf_op jit(solution)/shard_map/all_to_all | solution.py:459
  155.3 29.2 %shard_map.73 = bf16[16,192,128]{2,1,0:T(8,128)(2,1)} custom-call(s32[1]{0:T(128)} %constant.57.clone.1.cls_ref, s32[16]{0:T(128)} %count_ref.9, bf16[16,400,128]{2,1,0:T(8,128)(2,1)} %all-to-all-done.4.got_ref, bf16[6144,256]{1,0:T(8,128)(2,1)} %shard_map.68.key_ref, bf16[6144,256]{1,0:T(8,128)(2,1)} %shard_map.69.value_ref), custom_call_target="tpu_custom_call" | custom-call | flops 9663676416 | bytes 6291456 | tf_op jit(solution)/shard_map/pallas_call | solution.py:310
  184.5 6.0 %all-to-all-start.5 = ((bf16[16,192,128]{2,1,0:T(8,128)(2,1)}), bf16[16,192,128]{2,1,0:T(8,128)(2,1)S(1)}, u32[]{:S(2)}, u32[]{:S(2)}) async-start(bf16[16,192,128]{2,1,0:T(8,128)(2,1)} %shard_map.73), calls=%async_computation.5 | async-start | bytes 1572864 | tf_op jit(solution)/shard_map/all_to_all | solution.py:459
  190.5 11.2 %shard_map.72 = bf16[192,4096]{1,0:T(8,128)(2,1)} custom-call(s32[1]{0:T(128)} %bitcast.6.column_ref, bf16[16,192,128]{2,1,0:T(8,128)(2,1)} %copy-done, bf16[2048,8192]{1,0:T(8,128)(2,1)} %weight_ref.7), custom_call_target="tpu_custom_call" | custom-call | flops 3221225472 | bytes 16777216 | tf_op jit(solution)/shard_map/pallas_call | solution.py:350
  203.3 5.9 %all-to-all-done.5.got_ref = bf16[16,192,128]{2,1,0:T(8,128)(2,1)S(1)} async-done(((bf16[16,192,128]{2,1,0:T(8,128)(2,1)}), bf16[16,192,128]{2,1,0:T(8,128)(2,1)S(1)}, u32[]{:S(2)}, u32[]{:S(2)}) %all-to-all-start.5) | async-done | bytes 786464 | tf_op jit(solution)/shard_map/all_to_all | solution.py:459
  210.1 11.2 %shard_map.75 = bf16[192,4096]{1,0:T(8,128)(2,1)} custom-call(s32[1]{0:T(128)} %bitcast.6.column_ref, bf16[16,192,128]{2,1,0:T(8,128)(2,1)} %copy-done.1, bf16[2048,8192]{1,0:T(8,128)(2,1)} %weight_ref.7), custom_call_target="tpu_custom_call" | custom-call | flops 3221225472 | bytes 16777216 | tf_op jit(solution)/shard_map/pallas_call | solution.py:350
  222.8 11.2 %shard_map.71 = bf16[192,4096]{1,0:T(8,128)(2,1)} custom-call(s32[1]{0:T(128)} %bitcast.column_ref, bf16[16,192,128]{2,1,0:T(8,128)(2,1)} %copy-done, bf16[2048,8192]{1,0:T(8,128)(2,1)} %weight_ref.7), custom_call_target="tpu_custom_call" | custom-call | flops 3221225472 | bytes 16777216 | tf_op jit(solution)/shard_map/pallas_call | solution.py:350
  234.0 11.3 %shard_map.74 = bf16[192,4096]{1,0:T(8,128)(2,1)} custom-call(s32[1]{0:T(128)} %bitcast.column_ref, bf16[16,192,128]{2,1,0:T(8,128)(2,1)} %copy-done.1, bf16[2048,8192]{1,0:T(8,128)(2,1)} %weight_ref.7), custom_call_target="tpu_custom_call" | custom-call | flops 3221225472 | bytes 16777216 | tf_op jit(solution)/shard_map/pallas_call | solution.py:350
  245.9 26.5 %collective-permute-done.7 = bf16[192,4096]{1,0:T(8,128)(2,1)S(1)} collective-permute-done((bf16[192,4096]{1,0:T(8,128)(2,1)}, bf16[192,4096]{1,0:T(8,128)(2,1)S(1)}, u32[]{:S(2)}, u32[]{:S(2)}) %collective-permute-start.7) | collective-permute-done | bytes 1572896 | tf_op jit(solution)/shard_map/ppermute | solution.py:462
  272.9 2.0 pad_maximum_fusion
  (49 shorter events, 17.3 us)
Async XLA Ops:
  7.6 26.8 %all-to-all-start = ((bf16[4,784,128]{2,1,0:T(8,128)(2,1)}), bf16[4,784,128]{2,1,0:T(8,128)(2,1)S(1)}, u32[]{:S(2)}, u32[]{:S(2)}) async-start(bf16[4,784,128]{2,1,0:T(8,128)(2,1)} %bitcast.9), calls=%async_computation | async-start | bytes 1605632 | tf_op jit(solution)/shard_map/all_to_all | solution.py:415
  34.4 28.3 %copy-start.4 = (bf16[4,784,128]{2,1,0:T(8,128)(2,1)}, bf16[4,784,128]{2,1,0:T(8,128)(2,1)S(1)}, u32[]{:S(2)}) copy-start(bf16[4,784,128]{2,1,0:T(8,128)(2,1)S(1)} %all-to-all-done.rest_0_) | copy-start | bytes 2408452
  34.4 23.4 %all-to-all-start.1 = ((bf16[4,784,128]{2,1,0:T(8,128)(2,1)}), bf16[4,784,128]{2,1,0:T(8,128)(2,1)S(1)}, u32[]{:S(2)}, u32[]{:S(2)}) async-start(bf16[4,784,128]{2,1,0:T(8,128)(2,1)} %bitcast.8), calls=%async_computation.1 | async-start | bytes 1605632 | tf_op jit(solution)/shard_map/all_to_all | solution.py:415
  37.9 19.0 %collective-permute-start = (bf16[4,784,128]{2,1,0:T(8,128)(2,1)S(1)}, bf16[4,784,128]{2,1,0:T(8,128)(2,1)}, u32[]{:S(2)}, u32[]{:S(2)}) collective-permute-start(bf16[4,784,128]{2,1,0:T(8,128)(2,1)S(1)} %all-to-all-done.rest_0_), channel_id=1, source_target_pairs={{0,4},{2,6},{4,0},{6,2},{8,12},{10,14},{12,8},{14,10},{16,20},{18,... | collective-permute-start | bytes 2408456 | tf_op jit(solution)/shard_map/ppermute | solution.py:421
  57.8 49.6 %copy-start.5 = (bf16[4,784,128]{2,1,0:T(8,128)(2,1)}, bf16[4,784,128]{2,1,0:T(8,128)(2,1)S(1)}, u32[]{:S(2)}) copy-start(bf16[4,784,128]{2,1,0:T(8,128)(2,1)S(1)} %all-to-all-done.1.rest_0_) | copy-start | bytes 2408452
  57.8 43.7 %all-to-all-start.2 = ((bf16[16,400,128]{2,1,0:T(8,128)(2,1)}), bf16[16,400,128]{2,1,0:T(8,128)(2,1)S(1)}, u32[]{:S(2)}, u32[]{:S(2)}) async-start(bf16[16,400,128]{2,1,0:T(8,128)(2,1)} %bitcast.10), calls=%async_computation.2 | async-start | bytes 3276800 | tf_op jit(solution)/shard_map/all_to_all | solution.py:429
  62.7 2.5 collective-permute-start.1
  63.1 3.3 %collective-permute-start.2 = (bf16[4,784,128]{2,1,0:T(8,128)(2,1)}, bf16[4,784,128]{2,1,0:T(8,128)(2,1)S(1)}, u32[]{:S(2)}, u32[]{:S(2)}) collective-permute-start(bf16[4,784,128]{2,1,0:T(8,128)(2,1)} %collective-permute-done.rest_1_), channel_id=1, source_target_pairs={{0,2},{2,0},{4,6},{6,4},{8,10},{10,8},{12,14},{14,12},{16,18},{18,... | collective-permute-start | bytes 2408456 | tf_op jit(solution)/shard_map/ppermute | solution.py:421
  63.2 37.3 %collective-permute-start.3 = (bf16[4,784,128]{2,1,0:T(8,128)(2,1)S(1)}, bf16[4,784,128]{2,1,0:T(8,128)(2,1)S(1)}, u32[]{:S(2)}, u32[]{:S(2)}) collective-permute-start(bf16[4,784,128]{2,1,0:T(8,128)(2,1)S(1)} %all-to-all-done.1.rest_0_), channel_id=1, source_target_pairs={{0,4},{2,6},{4,0},{6,2},{8,12},{10,14},{12,8},{14,10},{16,20},{18,... | collective-permute-start | bytes 2408456 | tf_op jit(solution)/shard_map/ppermute | solution.py:421
  65.2 35.4 %copy-start.9 = (bf16[4,784,128]{2,1,0:T(8,128)(2,1)}, bf16[4,784,128]{2,1,0:T(8,128)(2,1)S(1)}, u32[]{:S(2)}) copy-start(bf16[4,784,128]{2,1,0:T(8,128)(2,1)S(1)} %collective-permute-done.1.rest_2_) | copy-start | bytes 2408452
  66.4 34.1 %copy-start.10 = (bf16[4,784,128]{2,1,0:T(8,128)(2,1)}, bf16[4,784,128]{2,1,0:T(8,128)(2,1)S(1)}, u32[]{:S(2)}) copy-start(bf16[4,784,128]{2,1,0:T(8,128)(2,1)S(1)} %collective-permute-done.2.rest_3_) | copy-start | bytes 2408452
  101.5 1.2 copy-start.6
  101.5 6.3 %copy-start.8 = (bf16[4,784,128]{2,1,0:T(8,128)(2,1)S(1)}, bf16[4,784,128]{2,1,0:T(8,128)(2,1)}, u32[]{:S(2)}) copy-start(bf16[4,784,128]{2,1,0:T(8,128)(2,1)} %copy-done.7) | copy-start | bytes 2408452
  102.7 46.6 %all-to-all-start.4 = ((bf16[16,400,128]{2,1,0:T(8,128)(2,1)}), bf16[16,400,128]{2,1,0:T(8,128)(2,1)}, u32[]{:S(2)}, u32[]{:S(2)}) async-start(bf16[16,400,128]{2,1,0:T(8,128)(2,1)} %bitcast.7), calls=%async_computation.4 | async-start | bytes 3276800 | tf_op jit(solution)/shard_map/all_to_all | solution.py:429
  107.4 5.8 %collective-permute-start.4 = (bf16[4,784,128]{2,1,0:T(8,128)(2,1)S(1)}, bf16[4,784,128]{2,1,0:T(8,128)(2,1)S(1)}, u32[]{:S(2)}, u32[]{:S(2)}) collective-permute-start(bf16[4,784,128]{2,1,0:T(8,128)(2,1)S(1)} %all-to-all-done.1.rest_0_), channel_id=1, source_target_pairs={{0,2},{2,0},{4,6},{6,4},{8,10},{10,8},{12,14},{14,12},{16,18},{18,... | collective-permute-start | bytes 2408456 | tf_op jit(solution)/shard_map/ppermute | solution.py:421
  107.8 5.4 %collective-permute-start.5 = (bf16[4,784,128]{2,1,0:T(8,128)(2,1)S(1)}, bf16[4,784,128]{2,1,0:T(8,128)(2,1)S(1)}, u32[]{:S(2)}, u32[]{:S(2)}) collective-permute-start(bf16[4,784,128]{2,1,0:T(8,128)(2,1)S(1)} %copy-done.8), channel_id=1, source_target_pairs={{0,2},{2,0},{4,6},{6,4},{8,10},{10,8},{12,14},{14,12},{16,18},{18,... | collective-permute-start | bytes 2408456 | tf_op jit(solution)/shard_map/ppermute | solution.py:421
  149.3 35.2 %all-to-all-start.3 = ((bf16[16,192,128]{2,1,0:T(8,128)(2,1)}), bf16[16,192,128]{2,1,0:T(8,128)(2,1)S(1)}, u32[]{:S(2)}, u32[]{:S(2)}) async-start(bf16[16,192,128]{2,1,0:T(8,128)(2,1)} %shard_map.70), calls=%async_computation.3 | async-start | bytes 1572864 | tf_op jit(solution)/shard_map/all_to_all | solution.py:459
  184.5 6.0 %copy-start = (bf16[16,192,128]{2,1,0:T(8,128)(2,1)}, bf16[16,192,128]{2,1,0:T(8,128)(2,1)S(1)}, u32[]{:S(2)}) copy-start(bf16[16,192,128]{2,1,0:T(8,128)(2,1)S(1)} %all-to-all-done.3.got_ref) | copy-start | bytes 2359300
  184.5 24.7 %all-to-all-start.5 = ((bf16[16,192,128]{2,1,0:T(8,128)(2,1)}), bf16[16,192,128]{2,1,0:T(8,128)(2,1)S(1)}, u32[]{:S(2)}, u32[]{:S(2)}) async-start(bf16[16,192,128]{2,1,0:T(8,128)(2,1)} %shard_map.73), calls=%async_computation.5 | async-start | bytes 1572864 | tf_op jit(solution)/shard_map/all_to_all | solution.py:459
  201.8 43.6 %collective-permute-start.6 = (bf16[192,4096]{1,0:T(8,128)(2,1)}, bf16[192,4096]{1,0:T(8,128)(2,1)S(1)}, u32[]{:S(2)}, u32[]{:S(2)}) collective-permute-start(bf16[192,4096]{1,0:T(8,128)(2,1)} %shard_map.72), channel_id=1, source_target_pairs={{0,1},{1,0},{2,3},{3,2},{4,5},{5,4},{6,7},{7,6},{8,9},{9,8},{10,11... | collective-permute-start | bytes 4718600 | tf_op jit(solution)/shard_map/ppermute | solution.py:462
  209.2 0.9 copy-start.1
  221.3 51.1 %collective-permute-start.7 = (bf16[192,4096]{1,0:T(8,128)(2,1)}, bf16[192,4096]{1,0:T(8,128)(2,1)S(1)}, u32[]{:S(2)}, u32[]{:S(2)}) collective-permute-start(bf16[192,4096]{1,0:T(8,128)(2,1)} %shard_map.75), channel_id=1, source_target_pairs={{0,1},{1,0},{2,3},{3,2},{4,5},{5,4},{6,7},{7,6},{8,9},{9,8},{10,11... | collective-permute-start | bytes 4718600 | tf_op jit(solution)/shard_map/ppermute | solution.py:462
  234.0 11.3 %copy-start.3 = (bf16[192,4096]{1,0:T(8,128)(2,1)S(1)}, bf16[192,4096]{1,0:T(8,128)(2,1)}, u32[]{:S(2)}) copy-start(bf16[192,4096]{1,0:T(8,128)(2,1)} %shard_map.71) | copy-start | bytes 4718596
  245.3 27.1 %copy-start.2 = (bf16[192,4096]{1,0:T(8,128)(2,1)S(1)}, bf16[192,4096]{1,0:T(8,128)(2,1)}, u32[]{:S(2)}) copy-start(bf16[192,4096]{1,0:T(8,128)(2,1)} %shard_map.74) | copy-start | bytes 4718596
  (3 other events, 2.7 us)

commit v4 on v3

--- a/solution.py
+++ b/solution.py
@@ -181,8 +181,14 @@
                 lambda at: part[z, pl.ds(at, piece), :],
                 add,
             )
-    out[:, :HD] = all_rows[:total, :]
-    out[:, HD:] = all_rows[:total, :] if doubled else jnp.ones((total, HD), jnp.bfloat16)
+    if doubled:
+        for first in range(0, total, 2 * TOK_DEV):
+            turned = jnp.transpose(all_rows[first : first + 2 * TOK_DEV, :])
+            out[:HD, first : first + 2 * TOK_DEV] = turned
+            out[HD:, first : first + 2 * TOK_DEV] = turned
+    else:
+        out[:, :HD] = all_rows[:total, :]
+        out[:, HD:] = jnp.ones((total, HD), jnp.bfloat16)
 
 
 def compact(member, counts, parts, offsets, total, doubled):
@@ -191,7 +197,9 @@
         functools.partial(compact_kernel, offsets, per, total, doubled),
         in_specs=[whole_smem(), whole_smem()] + [whole_vmem()] * len(parts),
         out_specs=whole_vmem(),
-        out_shape=jax.ShapeDtypeStruct((total, 2 * HD), jnp.bfloat16),
+        out_shape=jax.ShapeDtypeStruct(
+            (2 * HD, total) if doubled else (total, 2 * HD), jnp.bfloat16
+        ),
         scratch_shapes=[
             pltpu.VMEM((total + PAD, HD), jnp.bfloat16),
             pltpu.SMEM(counts.shape, jnp.int32),
@@ -241,10 +249,8 @@
 
     def score(scores, top, i, k):
         rows = query_two[pl.ds(pl.multiple_of(jnp.minimum(i, supers - 1) * pair, TILE), pair), :]
-        keys = key_ref[pl.ds(pl.multiple_of(k * span, TILE), span), :]
-        found = lax.dot_general(
-            rows, keys, (((1,), (1,)), ((), ())), preferred_element_type=jnp.float32
-        )
+        keys = key_ref[:, pl.ds(pl.multiple_of(k * span, HD), span)]
+        found = jnp.dot(rows, keys, preferred_element_type=jnp.float32)
         scores[...] = found
         top[...] = row_top(found)
 
@@ -305,7 +311,7 @@
 
 def attend(cls, counts, got, keys, values, block):
     ctx_size = got.shape[0]
-    total = keys.shape[0]
+    total = values.shape[0]
     pairs = total * ctx_size * block // 2
     return pl.pallas_call(
         functools.partial(attend_kernel, ctx_size, block),
@@ -329,14 +335,17 @@
     )(cls, counts, got, keys, values)
 
 
-def project_kernel(classes, column_ref, got_ref, weight_ref, out_ref, rows_ref):
-    block = got_ref.shape[1]
+def project_kernel(classes, chunks, column_ref, *rest):
+    got_refs, (weight_ref, out_ref, rows_ref) = rest[:chunks], rest[chunks:]
+    block = got_refs[0].shape[1]
 
     @pl.when(pl.program_id(0) == 0)
     def _():
-        for d in range(got_ref.shape[0]):
-            h, r = d // classes, d % classes
-            rows_ref[r * block : (r + 1) * block, h * HD : (h + 1) * HD] = got_ref[d]
+        for j, got_ref in enumerate(got_refs):
+            for d in range(got_ref.shape[0]):
+                h, r = d // classes, d % classes
+                first = (j * classes + r) * block
+                rows_ref[first : first + block, h * HD : (h + 1) * HD] = got_ref[d]
 
     out_ref[...] = jnp.dot(
         rows_ref[...], weight_ref[...], preferred_element_type=jnp.float32
@@ -344,18 +353,16 @@
 
 
 def project(first_column, got, weight, columns, classes):
-    ctx_size, block, _ = got.shape
-    rows, depth = classes * block, weight.shape[0]
+    ctx_size, block, _ = got[0].shape
+    rows, depth = len(got) * classes * block, weight.shape[0]
     step = min(512, columns)
     return pl.pallas_call(
-        functools.partial(project_kernel, classes),
+        functools.partial(project_kernel, classes, len(got)),
         grid_spec=pltpu.PrefetchScalarGridSpec(
             num_scalar_prefetch=1,
             grid=(columns // step,),
-            in_specs=[
-                pl.BlockSpec((ctx_size, block, HD), lambda i, first: (0, 0, 0)),
-                pl.BlockSpec((depth, step), lambda i, first: (0, first[0] + i)),
-            ],
+            in_specs=[pl.BlockSpec((ctx_size, block, HD), lambda i, first: (0, 0, 0))] * len(got)
+            + [pl.BlockSpec((depth, step), lambda i, first: (0, first[0] + i))],
             out_specs=pl.BlockSpec((rows, step), lambda i, first: (0, i)),
             scratch_shapes=[pltpu.VMEM((rows, depth), jnp.bfloat16)],
         ),
@@ -364,7 +371,59 @@
         cost_estimate=pl.CostEstimate(
             flops=2 * rows * depth * columns, bytes_accessed=2 * depth * columns, transcendentals=0
         ),
-    )((first_column // step).astype(jnp.int32).reshape(1), got, weight)
+    )((first_column // step).astype(jnp.int32).reshape(1), *got, weight)
+
+
+def join_kernel(chunks, parts, head_ref, *rest):
+    got_refs, weight_refs = rest[:chunks], rest[chunks : chunks + parts]
+    own_ref, out_ref, rows_ref = rest[chunks + parts :]
+    block = got_refs[0].shape[1]
+    depth = weight_refs[0].shape[0]
+
+    @pl.when(pl.program_id(0) == 0)
+    def _():
+        for j, got_ref in enumerate(got_refs):
+            for p in range(parts):
+                for n in range(depth // HD):
+                    at = p * depth + n * HD
+                    rows_ref[j * block : (j + 1) * block, at : at + HD] = got_ref[head_ref[p] + n]
+
+    total = jnp.zeros(out_ref.shape, jnp.float32)
+    for p, weight_ref in enumerate(weight_refs):
+        total = total + jnp.dot(
+            rows_ref[:, p * depth : (p + 1) * depth],
+            weight_ref[...],
+            preferred_element_type=jnp.float32,
+        )
+    theirs = total.astype(jnp.bfloat16).astype(jnp.float32)
+    out_ref[...] = (own_ref[...].astype(jnp.float32) + theirs).astype(jnp.bfloat16)
+
+
+def join(first_heads, got, weights, own):
+    ctx_size, block, _ = got[0].shape
+    rows, columns = own.shape
+    depth = weights[0].shape[0]
+    step = min(512, columns)
+    tile = pl.BlockSpec((rows, step), lambda i, first: (0, i))
+    return pl.pallas_call(
+        functools.partial(join_kernel, len(got), len(weights)),
+        grid_spec=pltpu.PrefetchScalarGridSpec(
+            num_scalar_prefetch=1,
+            grid=(columns // step,),
+            in_specs=[pl.BlockSpec((ctx_size, block, HD), lambda i, first: (0, 0, 0))] * len(got)
+            + [pl.BlockSpec((depth, step), lambda i, first: (0, i))] * len(weights)
+            + [tile],
+            out_specs=tile,
+            scratch_shapes=[pltpu.VMEM((rows, depth * len(weights)), jnp.bfloat16)],
+        ),
+        out_shape=jax.ShapeDtypeStruct((rows, columns), jnp.bfloat16),
+        compiler_params=params(),
+        cost_estimate=pl.CostEstimate(
+            flops=2 * rows * depth * len(weights) * columns,
+            bytes_accessed=2 * depth * len(weights) * columns,
+            transcendentals=0,
+        ),
+    )(first_heads, *got, *weights, own)
 
 
 def tables(query_rows):
@@ -430,50 +489,72 @@
             packed.reshape(ctx_size, cap, HD), "ctx", split_axis=0, concat_axis=0, tiled=True
         )
 
+    traded = tp_size == 2 and classes == 1
+    both = [(0, 1), (1, 0)]
+
+    def chip_swap(part, bit):
+        return lax.ppermute(part, "ctx", [(d, d ^ bit) for d in range(ctx_size)])
+
+    core, side = me & 1, (me >> 1) & 1
+    depth = out_weight.shape[0] // 8
+
+    def weight_rows(p):
+        first = core * (4 * depth) + jnp.where(side == 0, p, 3 - p) * depth
+        return lax.dynamic_slice(out_weight, (first, (1 - tp_me) * columns), (depth, columns))
+
     key_parts = [send_across(pack_shared(key, True))]
     value_packed, key_parts = lax.optimization_barrier((pack_shared(value, False), key_parts))
     key_parts = swap(key_parts, bits[0])
     value_parts = [send_across(value_packed)]
     packed_q = list(pack(q_slots, cosine, sine, query, True, chunks, classes, cap))
-    packed_q[0], key_parts, value_parts = lax.optimization_barrier(
-        (packed_q[0], key_parts, value_parts)
+    came = [lax.ppermute(weight_rows(0), "tp", both)] if traded else []
+    packed_q[0], key_parts, value_parts, came = lax.optimization_barrier(
+        (packed_q[0], key_parts, value_parts, came)
     )
     got_q = [send_query(packed_q[0])]
     value_parts = swap(value_parts, bits[0])
     for bit in bits[1:]:
         key_parts = swap(key_parts, bit)
+    if traded:
+        slice_1, came = lax.optimization_barrier((weight_rows(1), came))
+        came = came + [lax.ppermute(slice_1, "tp", both)]
     if chunks > 1:
-        packed_q[1], key_parts, value_parts = lax.optimization_barrier(
-            (packed_q[1], key_parts, value_parts)
-        )
+        packed_q[1], value_parts, came = lax.optimization_barrier((packed_q[1], value_parts, came))
     for bit in bits[1:]:
         value_parts = swap(value_parts, bit)
     got_q = got_q + [send_query(packed) for packed in packed_q[1:]]
     keys = compact(member, kept_count, key_parts, offsets, total, True)
     values = compact(member, kept_count, value_parts, offsets, total, False)
-
-    mine, other = [], []
+    crossed = []
+    if traded:
+        crossed = [chip_swap(part, 1) for part in came]
+        slice_2, came = lax.optimization_barrier((weight_rows(2), came))
+        came = came + [lax.ppermute(slice_2, "tp", both), chip_swap(came[0], 2)]
+
+    got, done = [], None
     for j in range(chunks):
         cls_j = j * classes + (me & (classes - 1))
+        if j > 0:
+            got_q[j], done = lax.optimization_barrier((got_q[j], done))
+            got.append(lax.all_to_all(done, "ctx", split_axis=0, concat_axis=0, tiled=True))
         done = attend(cls_j.reshape(1), kept_count, got_q[j], keys, values, block)
-        got = lax.all_to_all(done, "ctx", split_axis=0, concat_axis=0, tiled=True)
-        if tp_size == 2:
-            theirs = project((1 - tp_me) * columns, got, out_weight, columns, classes)
-            other.append(lax.ppermute(theirs, "tp", [(0, 1), (1, 0)]))
-            mine.append(project(tp_me * columns, got, out_weight, columns, classes))
-        else:
-            full = project(jnp.int32(0) * tp_me, got, out_weight, columns * tp_size, classes)
-            split = jnp.transpose(full.reshape(full.shape[0], tp_size, columns), (1, 0, 2))
-            swapped = lax.all_to_all(split, "tp", split_axis=0, concat_axis=0, tiled=True)
-            mine.append(jnp.sum(swapped.astype(jnp.float32), axis=0))
-            other.append(jnp.zeros((), jnp.float32))
-    return jnp.concatenate(
-        [
-            (a.astype(jnp.float32) + b.astype(jnp.float32)).astype(jnp.bfloat16)
-            for a, b in zip(mine, other)
-        ],
-        axis=0,
-    )
+    if traded:
+        done, came, crossed = lax.optimization_barrier((done, came, crossed))
+    got.append(lax.all_to_all(done, "ctx", split_axis=0, concat_axis=0, tiled=True))
+    if traded:
+        theirs = [lax.ppermute(one, "tp", both) for one in got]
+        came = came + crossed + [chip_swap(part, 1) for part in came[2:]]
+        own = project(tp_me * columns, got, out_weight, columns, classes)
+        per = depth // HD
+        order = [jnp.where(side == 0, p, 3 - p) for p in range(3)] + [jnp.where(side == 0, 3, 0)]
+        first_heads = jnp.stack(
+            [(c * 4 + p) * per for c in (core, 1 - core) for p in order]
+        ).astype(jnp.int32)
+        return join(first_heads, theirs, came, own)
+    full = project(jnp.int32(0) * tp_me, got, out_weight, columns * tp_size, classes)
+    split = jnp.transpose(full.reshape(full.shape[0], tp_size, columns), (1, 0, 2))
+    swapped = lax.all_to_all(split, "tp", split_axis=0, concat_axis=0, tiled=True)
+    return jnp.sum(swapped.astype(jnp.float32), axis=0).astype(jnp.bfloat16)
 
 
 def solution(mesh):

time: 276 us -> 271 us (0.982)
  Pallas kernels: 131 us -> 114 us
  starting transfers between devices: 39 us -> 45.2 us
  local copies, waits for them, and re-layouts: 4.85 us -> 9.58 us
  waiting for transfers between devices: 94.8 us -> 99 us
  other arithmetic: 5.64 us -> 2.55 us
    pallas_call x4 -> x2, Pallas kernels: 45 us -> 29 us  [the longest x1 15.1 us: join(): pl.pallas_call(functools.partial(join_kernel, len(got), len(weights)), gr...]
    all_to_all x2, waiting for transfers between devices: 5.93 us -> 17.6 us  [local(): lax.all_to_all(done, 'ctx', split_axis=0, concat_axis=0, tiled=True)]
    all_to_all x2, waiting for transfers between devices: 18.2 us -> 9.92 us  [send_across(): lax.all_to_all(packed, 'ctx', split_axis=0, concat_axis=0, tiled=True, ax...]
    dynamic_slice x0 -> x1, local copies, waits for them, and re-layouts: none -> 5.81 us  [weight_rows(): lax.dynamic_slice(out_weight, (first, (1 - tp_me) * columns), (depth, col...]
    ppermute x2 -> x10, starting transfers between devices: 3.02 us -> 8.58 us  [the longest x5 2.95 us: chip_swap(): return lax.ppermute(part, 'ctx', [(d, d ^ bit) for d in range(ctx_size)])]
    ppermute x6, waiting for transfers between devices: 44.2 us -> 47 us  [swap(): return parts + [lax.ppermute(part, 'ctx', pairs) for part in parts]]
    ppermute x2 -> x10, waiting for transfers between devices: 26.5 us -> 24.4 us  [the longest x1 10.4 us: local(): came = came + [lax.ppermute(slice_1, 'tp', both)]]
  transfers between devices with their start and end apart: 14 -> 22, of which waited for: 7 -> 9; matrix products, arithmetic and copies ran while one was open for 0% -> 2% of each run, Pallas kernels for 46% -> 35%
where the time goes in v4:
time: 271 us; the launch traced here: 270 us
  Pallas kernels  114 us (42%)
  waiting for transfers between devices  99 us (37%)
  starting transfers between devices  45.2 us (17%)
  local copies, waits for them, and re-layouts  9.58 us (4%)
    pallas_call x2, Pallas kernels, attend(): pl.pallas_call(functools.partial(attend_kernel, ctx_size, block), in_spec...  57.4 us
    ppermute x6, waiting for transfers between devices, swap(): return parts + [lax.ppermute(part, 'ctx', pairs) for part in parts]  47 us
    all_to_all x2, waiting for transfers between devices, local(): lax.all_to_all(done, 'ctx', split_axis=0, concat_axis=0, tiled=True)  17.6 us
    pallas_call x3, Pallas kernels, pack(): pl.pallas_call(functools.partial(pack_kernel, turned, classes, cap, width...  15.4 us
    pallas_call x1, Pallas kernels, join(): pl.pallas_call(functools.partial(join_kernel, len(got), len(weights)), gr...  15.1 us
    pallas_call x1, Pallas kernels, project(): pl.pallas_call(functools.partial(project_kernel, classes, len(got)), grid...  13.9 us
    all_to_all x2, starting transfers between devices, send_query(): lax.all_to_all(packed.reshape(ctx_size, cap, HD), 'ctx', split_axis=0, co...  11.7 us
    all_to_all x2, starting transfers between devices, local(): lax.all_to_all(done, 'ctx', split_axis=0, concat_axis=0, tiled=True)  10.7 us
  transfers between devices with their start and end apart: 22, of which 9 were waited for; matrix products, arithmetic and copies ran while one was open for 2% of the time, Pallas kernels for 35%

profile of v4, /device:TPU:0, one launch (start us, length us, event | category | flops | bytes accessed | tf_op | source)
XLA Modules:
  0.0 270.3 jit_solution(17287649840411567523)
XLA Ops:
  1.6 2.5 negate_select_fusion
  4.1 3.5 %shard_map.67 = bf16[4,1,784,128]{3,2,1,0:T(8,128)(2,1)} custom-call(s32[1,768]{1,0:T(1,128)} %get-tuple-element.38.slot_ref, f32[768,128]{1,0:T(8,128)} %get-tuple-element.69.cos_ref, f32[768,128]{1,0:T(8,128)} %get-tuple-element.68.sin_ref, bf16[768,512]{1,0:T(8,128)(2,1)} %row_ref.5), custom_call_target="tpu_custom_call" | custom-call | flops 616562688 | bytes 1572864 | tf_op jit(solution)/shard_map/pallas_call | solution.py:124
  7.6 6.3 %all-to-all-start = ((bf16[4,784,128]{2,1,0:T(8,128)(2,1)}), bf16[4,784,128]{2,1,0:T(8,128)(2,1)S(1)}, u32[]{:S(2)}, u32[]{:S(2)}) async-start(bf16[4,784,128]{2,1,0:T(8,128)(2,1)} %bitcast.15), calls=%async_computation | async-start | bytes 1605632 | tf_op jit(solution)/shard_map/all_to_all | solution.py:474
  13.9 5.8 %fusion.4 = (bf16[256,4096]{1,0:T(8,128)(2,1)}, bf16[256,4096]{1,0:T(8,128)(2,1)}, bf16[256,4096]{1,0:T(8,128)(2,1)}) fusion(bf16[2048,8192]{1,0:T(8,128)(2,1)} %rest_2_.1, s32[]{:T(128)S(6)} %select_n.56, s32[]{:T(128)S(6)} %select_n.54, s32[]{:T(128)S(6)} %select_n.55, s32[]{:T(128)S(6)} %select_n.53), kind=kLoop, calls=%fused_computation.11 | loop fusion | bytes 12582928 | tf_op jit(solution)/shard_map/dynamic_slice | solution.py:503
  21.2 3.2 %shard_map.66 = bf16[4,1,784,128]{3,2,1,0:T(8,128)(2,1)} custom-call(s32[1,768]{1,0:T(1,128)} %get-tuple-element.38.slot_ref, f32[768,128]{1,0:T(8,128)} %get-tuple-element.69.cos_ref, f32[768,128]{1,0:T(8,128)} %get-tuple-element.68.sin_ref, bf16[768,512]{1,0:T(8,128)(2,1)} %row_ref.4), custom_call_target="tpu_custom_call" | custom-call | flops 616562688 | bytes 1572864 | tf_op jit(solution)/shard_map/pallas_call | solution.py:124
  24.4 9.9 %all-to-all-done.rest_0_ = bf16[4,784,128]{2,1,0:T(8,128)(2,1)S(1)} async-done(((bf16[4,784,128]{2,1,0:T(8,128)(2,1)}), bf16[4,784,128]{2,1,0:T(8,128)(2,1)S(1)}, u32[]{:S(2)}, u32[]{:S(2)}) %all-to-all-start) | async-done | bytes 802848 | tf_op jit(solution)/shard_map/all_to_all | solution.py:474
  34.4 3.5 %all-to-all-start.1 = ((bf16[4,784,128]{2,1,0:T(8,128)(2,1)}), bf16[4,784,128]{2,1,0:T(8,128)(2,1)S(1)}, u32[]{:S(2)}, u32[]{:S(2)}) async-start(bf16[4,784,128]{2,1,0:T(8,128)(2,1)} %bitcast.16), calls=%async_computation.1 | async-start | bytes 1605632 | tf_op jit(solution)/shard_map/all_to_all | solution.py:474
  39.4 8.7 %shard_map.65 = (bf16[16,1,400,128]{3,2,1,0:T(8,128)(2,1)}, bf16[16,1,400,128]{3,2,1,0:T(8,128)(2,1)}) custom-call(s32[1,768]{1,0:T(1,128)} %get-tuple-element.35.slot_ref, f32[768,128]{1,0:T(8,128)} %get-tuple-element.69.cos_ref, f32[768,128]{1,0:T(8,128)} %get-tuple-element.68.sin_ref, bf16[768,2048]{1,0:T(8,128)(2,1)} %row_ref.3), custom_call_target="tpu_custom_call" | custom-call | flops 2516582400 | bytes 6291456 | tf_op jit(solution)/shard_map/pallas_call | solution.py:124
  48.1 8.7 %collective-permute-done.rest_1_ = bf16[4,784,128]{2,1,0:T(8,128)(2,1)S(1)} collective-permute-done((bf16[4,784,128]{2,1,0:T(8,128)(2,1)S(1)}, bf16[4,784,128]{2,1,0:T(8,128)(2,1)S(1)}, u32[]{:S(2)}, u32[]{:S(2)}) %collective-permute-start) | collective-permute-done | bytes 802848 | tf_op jit(solution)/shard_map/ppermute | solution.py:480
  57.7 9.4 %collective-permute-done.1.rest_2_ = bf16[256,4096]{1,0:T(8,128)(2,1)} collective-permute-done((bf16[256,4096]{1,0:T(8,128)(2,1)}, bf16[256,4096]{1,0:T(8,128)(2,1)}, u32[]{:S(2)}, u32[]{:S(2)}) %collective-permute-start.1) | collective-permute-done | bytes 2097184 | tf_op jit(solution)/shard_map/ppermute | solution.py:510
  67.1 5.9 %all-to-all-start.3 = ((bf16[16,400,128]{2,1,0:T(8,128)(2,1)}), bf16[16,400,128]{2,1,0:T(8,128)(2,1)S(1)}, u32[]{:S(2)}, u32[]{:S(2)}) async-start(bf16[16,400,128]{2,1,0:T(8,128)(2,1)} %bitcast.17), calls=%async_computation.3 | async-start | bytes 3276800 | tf_op jit(solution)/shard_map/all_to_all | solution.py:488
  76.4 34.4 %collective-permute-done.2.rest_1_ = bf16[4,784,128]{2,1,0:T(8,128)(2,1)S(1)} collective-permute-done((bf16[4,784,128]{2,1,0:T(8,128)(2,1)S(1)}, bf16[4,784,128]{2,1,0:T(8,128)(2,1)S(1)}, u32[]{:S(2)}, u32[]{:S(2)}) %collective-permute-start.2) | collective-permute-done | bytes 802848 | tf_op jit(solution)/shard_map/ppermute | solution.py:480
  110.9 10.4 %collective-permute-done.3.rest_3_ = bf16[256,4096]{1,0:T(8,128)(2,1)} collective-permute-done((bf16[256,4096]{1,0:T(8,128)(2,1)}, bf16[256,4096]{1,0:T(8,128)(2,1)}, u32[]{:S(2)}, u32[]{:S(2)}) %collective-permute-start.3) | collective-permute-done | bytes 2097184 | tf_op jit(solution)/shard_map/ppermute | solution.py:520
  121.3 5.8 %all-to-all-start.2 = ((bf16[16,400,128]{2,1,0:T(8,128)(2,1)}), bf16[16,400,128]{2,1,0:T(8,128)(2,1)}, u32[]{:S(2)}, u32[]{:S(2)}) async-start(bf16[16,400,128]{2,1,0:T(8,128)(2,1)} %bitcast.11), calls=%async_computation.2 | async-start | bytes 3276800 | tf_op jit(solution)/shard_map/all_to_all | solution.py:488
  132.1 5.2 %shard_map.68.key_ref = bf16[256,6144]{1,0:T(8,128)(2,1)} custom-call(s32[1]{0:T(128)} %bitcast.13.member_ref, s32[16]{0:T(128)} %count_ref.9, bf16[4,784,128]{2,1,0:T(8,128)(2,1)} %copy-done, bf16[4,784,128]{2,1,0:T(8,128)(2,1)} %copy-done.6, bf16[4,784,128]{2,1,0:T(8,128)(2,1)} %collective-permute-done.4.rest_2_, ...), custom_call_target="tpu_custom_call" | custom-call | flops 6291456 | bytes 6291456 | tf_op jit(solution)/shard_map/pallas_call | solution.py:196
  141.3 5.2 %shard_map.69.value_ref = bf16[6144,256]{1,0:T(8,128)(2,1)} custom-call(s32[1]{0:T(128)} %bitcast.13.member_ref, s32[16]{0:T(128)} %count_ref.9, bf16[4,784,128]{2,1,0:T(8,128)(2,1)} %copy-done.1, bf16[4,784,128]{2,1,0:T(8,128)(2,1)} %copy-done.7, bf16[4,784,128]{2,1,0:T(8,128)(2,1)} %collective-permute-done.6.rest_2_, ...), custom_call_target="tpu_custom_call" | custom-call | flops 6291456 | bytes 6291456 | tf_op jit(solution)/shard_map/pallas_call | solution.py:196
  146.4 28.6 %shard_map.70 = bf16[16,192,128]{2,1,0:T(8,128)(2,1)} custom-call(s32[1]{0:T(128)} %constant.55.clone.1.cls_ref, s32[16]{0:T(128)} %count_ref.9, bf16[16,400,128]{2,1,0:T(8,128)(2,1)} %copy-done.5, bf16[256,6144]{1,0:T(8,128)(2,1)} %shard_map.68.key_ref, bf16[6144,256]{1,0:T(8,128)(2,1)} %shard_map.69.value_ref), custom_call_target="tpu_custom_call" | custom-call | flops 9663676416 | bytes 6291456 | tf_op jit(solution)/shard_map/pallas_call | solution.py:316
  175.0 4.7 %all-to-all-start.4 = ((bf16[16,192,128]{2,1,0:T(8,128)(2,1)}), bf16[16,192,128]{2,1,0:T(8,128)(2,1)S(1)}, u32[]{:S(2)}, u32[]{:S(2)}) async-start(bf16[16,192,128]{2,1,0:T(8,128)(2,1)} %shard_map.70), calls=%async_computation.4 | async-start | bytes 1572864 | tf_op jit(solution)/shard_map/all_to_all | solution.py:539
  179.7 28.8 %shard_map.71 = bf16[16,192,128]{2,1,0:T(8,128)(2,1)} custom-call(s32[1]{0:T(128)} %constant.56.clone.1.cls_ref, s32[16]{0:T(128)} %count_ref.9, bf16[16,400,128]{2,1,0:T(8,128)(2,1)} %all-to-all-done.2.got_ref, bf16[256,6144]{1,0:T(8,128)(2,1)} %shard_map.68.key_ref, bf16[6144,256]{1,0:T(8,128)(2,1)} %shard_map.69.value_ref), custom_call_target="tpu_custom_call" | custom-call | flops 9663676416 | bytes 6291456 | tf_op jit(solution)/shard_map/pallas_call | solution.py:316
  209.8 6.0 %all-to-all-start.5 = ((bf16[16,192,128]{2,1,0:T(8,128)(2,1)}), bf16[16,192,128]{2,1,0:T(8,128)(2,1)S(1)}, u32[]{:S(2)}, u32[]{:S(2)}) async-start(bf16[16,192,128]{2,1,0:T(8,128)(2,1)} %shard_map.71), calls=%async_computation.5 | async-start | bytes 1572864 | tf_op jit(solution)/shard_map/all_to_all | solution.py:543
  216.9 17.6 %all-to-all-done.5.rest_1_ = bf16[16,192,128]{2,1,0:T(8,128)(2,1)S(1)} async-done(((bf16[16,192,128]{2,1,0:T(8,128)(2,1)}), bf16[16,192,128]{2,1,0:T(8,128)(2,1)S(1)}, u32[]{:S(2)}, u32[]{:S(2)}) %all-to-all-start.5) | async-done | bytes 786464 | tf_op jit(solution)/shard_map/all_to_all | solution.py:543
  235.7 13.9 %shard_map.72.rest_10_ = bf16[384,4096]{1,0:T(8,128)(2,1)} custom-call(s32[1]{0:T(128)} %bitcast.14.column_ref, bf16[16,192,128]{2,1,0:T(8,128)(2,1)} %copy-done.2, bf16[16,192,128]{2,1,0:T(8,128)(2,1)} %copy-done.3, bf16[2048,8192]{1,0:T(8,128)(2,1)} %rest_2_.1), custom_call_target="tpu_custom_call" | custom-call | flops 6442450944 | bytes 16777216 | tf_op jit(solution)/shard_map/pallas_call | solution.py:359
  249.7 4.6 %collective-permute-done.13.rest_1_ = bf16[16,192,128]{2,1,0:T(8,128)(2,1)S(1)} collective-permute-done((bf16[16,192,128]{2,1,0:T(8,128)(2,1)S(1)}, bf16[16,192,128]{2,1,0:T(8,128)(2,1)S(1)}, u32[]{:S(2)}, u32[]{:S(2)}) %collective-permute-start.13) | collective-permute-done | bytes 786464 | tf_op jit(solution)/shard_map/ppermute | solution.py:545
  255.2 15.1 %shard_map.73 = bf16[384,4096]{1,0:T(8,128)(2,1)} custom-call(s32[8]{0:T(128)} %stack.35.head_ref, bf16[16,192,128]{2,1,0:T(8,128)(2,1)} %copy-done.8, bf16[16,192,128]{2,1,0:T(8,128)(2,1)} %copy-done.9, bf16[256,4096]{1,0:T(8,128)(2,1)} %collective-permute-done.1.rest_2_, bf16[256,4096]{1,0:T(8,128)(2,1)} %collective-permute-done.3.rest_3_, ...), custom_call_target="tpu_custom_call" | custom-call | flops 6442450944 | bytes 16777216 | tf_op jit(solution)/shard_map/pallas_call | solution.py:408
  (56 shorter events, 22.4 us)
Async XLA Ops:
  7.6 26.8 %all-to-all-start = ((bf16[4,784,128]{2,1,0:T(8,128)(2,1)}), bf16[4,784,128]{2,1,0:T(8,128)(2,1)S(1)}, u32[]{:S(2)}, u32[]{:S(2)}) async-start(bf16[4,784,128]{2,1,0:T(8,128)(2,1)} %bitcast.15), calls=%async_computation | async-start | bytes 1605632 | tf_op jit(solution)/shard_map/all_to_all | solution.py:474
  19.7 47.4 %collective-permute-start.1 = (bf16[256,4096]{1,0:T(8,128)(2,1)}, bf16[256,4096]{1,0:T(8,128)(2,1)}, u32[]{:S(2)}, u32[]{:S(2)}) collective-permute-start(bf16[256,4096]{1,0:T(8,128)(2,1)} %get-tuple-element.67), channel_id=1, source_target_pairs={{0,1},{1,0},{2,3},{3,2},{4,5},{5,4},{6,7},{7,6},{8,9},{9,8},{10,11... | collective-permute-start | bytes 6291464 | tf_op jit(solution)/shard_map/ppermute | solution.py:510
  34.4 92.7 %copy-start = (bf16[4,784,128]{2,1,0:T(8,128)(2,1)}, bf16[4,784,128]{2,1,0:T(8,128)(2,1)S(1)}, u32[]{:S(2)}) copy-start(bf16[4,784,128]{2,1,0:T(8,128)(2,1)S(1)} %all-to-all-done.rest_0_) | copy-start | bytes 2408452
  34.4 32.8 %all-to-all-start.1 = ((bf16[4,784,128]{2,1,0:T(8,128)(2,1)}), bf16[4,784,128]{2,1,0:T(8,128)(2,1)S(1)}, u32[]{:S(2)}, u32[]{:S(2)}) async-start(bf16[4,784,128]{2,1,0:T(8,128)(2,1)} %bitcast.16), calls=%async_computation.1 | async-start | bytes 1605632 | tf_op jit(solution)/shard_map/all_to_all | solution.py:474
  37.9 18.9 %collective-permute-start = (bf16[4,784,128]{2,1,0:T(8,128)(2,1)S(1)}, bf16[4,784,128]{2,1,0:T(8,128)(2,1)S(1)}, u32[]{:S(2)}, u32[]{:S(2)}) collective-permute-start(bf16[4,784,128]{2,1,0:T(8,128)(2,1)S(1)} %all-to-all-done.rest_0_), channel_id=1, source_target_pairs={{0,4},{2,6},{4,0},{6,2},{8,12},{10,14},{12,8},{14,10},{16,20},{18,... | collective-permute-start | bytes 2408456 | tf_op jit(solution)/shard_map/ppermute | solution.py:480
  67.1 60.5 %copy-start.1 = (bf16[4,784,128]{2,1,0:T(8,128)(2,1)}, bf16[4,784,128]{2,1,0:T(8,128)(2,1)S(1)}, u32[]{:S(2)}) copy-start(bf16[4,784,128]{2,1,0:T(8,128)(2,1)S(1)} %all-to-all-done.1.rest_0_) | copy-start | bytes 2408452
  67.1 54.1 %all-to-all-start.3 = ((bf16[16,400,128]{2,1,0:T(8,128)(2,1)}), bf16[16,400,128]{2,1,0:T(8,128)(2,1)S(1)}, u32[]{:S(2)}, u32[]{:S(2)}) async-start(bf16[16,400,128]{2,1,0:T(8,128)(2,1)} %bitcast.17), calls=%async_computation.3 | async-start | bytes 3276800 | tf_op jit(solution)/shard_map/all_to_all | solution.py:488
  73.0 48.3 %collective-permute-start.3 = (bf16[256,4096]{1,0:T(8,128)(2,1)}, bf16[256,4096]{1,0:T(8,128)(2,1)}, u32[]{:S(2)}, u32[]{:S(2)}) collective-permute-start(bf16[256,4096]{1,0:T(8,128)(2,1)} %get-tuple-element.44), channel_id=1, source_target_pairs={{0,1},{1,0},{2,3},{3,2},{4,5},{5,4},{6,7},{7,6},{8,9},{9,8},{10,11... | collective-permute-start | bytes 6291464 | tf_op jit(solution)/shard_map/ppermute | solution.py:520
  74.6 36.3 %collective-permute-start.2 = (bf16[4,784,128]{2,1,0:T(8,128)(2,1)S(1)}, bf16[4,784,128]{2,1,0:T(8,128)(2,1)S(1)}, u32[]{:S(2)}, u32[]{:S(2)}) collective-permute-start(bf16[4,784,128]{2,1,0:T(8,128)(2,1)S(1)} %all-to-all-done.1.rest_0_), channel_id=1, source_target_pairs={{0,4},{2,6},{4,0},{6,2},{8,12},{10,14},{12,8},{14,10},{16,20},{18,... | collective-permute-start | bytes 2408456 | tf_op jit(solution)/shard_map/ppermute | solution.py:480
  121.3 53.8 %all-to-all-start.2 = ((bf16[16,400,128]{2,1,0:T(8,128)(2,1)}), bf16[16,400,128]{2,1,0:T(8,128)(2,1)}, u32[]{:S(2)}, u32[]{:S(2)}) async-start(bf16[16,400,128]{2,1,0:T(8,128)(2,1)} %bitcast.11), calls=%async_computation.2 | async-start | bytes 3276800 | tf_op jit(solution)/shard_map/all_to_all | solution.py:488
  127.1 2.5 collective-permute-start.4
  127.5 4.6 %collective-permute-start.5 = (bf16[4,784,128]{2,1,0:T(8,128)(2,1)}, bf16[4,784,128]{2,1,0:T(8,128)(2,1)}, u32[]{:S(2)}, u32[]{:S(2)}) collective-permute-start(bf16[4,784,128]{2,1,0:T(8,128)(2,1)} %copy-done.6), channel_id=1, source_target_pairs={{0,2},{2,0},{4,6},{6,4},{8,10},{10,8},{12,14},{14,12},{16,18},{18,... | collective-permute-start | bytes 2408456 | tf_op jit(solution)/shard_map/ppermute | solution.py:480
  127.7 11.7 %collective-permute-start.6 = (bf16[4,784,128]{2,1,0:T(8,128)(2,1)S(1)}, bf16[4,784,128]{2,1,0:T(8,128)(2,1)}, u32[]{:S(2)}, u32[]{:S(2)}) collective-permute-start(bf16[4,784,128]{2,1,0:T(8,128)(2,1)S(1)} %all-to-all-done.1.rest_0_), channel_id=1, source_target_pairs={{0,2},{2,0},{4,6},{6,4},{8,10},{10,8},{12,14},{14,12},{16,18},{18,... | collective-permute-start | bytes 2408456 | tf_op jit(solution)/shard_map/ppermute | solution.py:480
  128.0 13.2 %collective-permute-start.7 = (bf16[4,784,128]{2,1,0:T(8,128)(2,1)}, bf16[4,784,128]{2,1,0:T(8,128)(2,1)}, u32[]{:S(2)}, u32[]{:S(2)}) collective-permute-start(bf16[4,784,128]{2,1,0:T(8,128)(2,1)} %copy-done.7), channel_id=1, source_target_pairs={{0,2},{2,0},{4,6},{6,4},{8,10},{10,8},{12,14},{14,12},{16,18},{18,... | collective-permute-start | bytes 2408456 | tf_op jit(solution)/shard_map/ppermute | solution.py:480
  137.3 71.2 %collective-permute-start.11 = (bf16[256,4096]{1,0:T(8,128)(2,1)}, bf16[256,4096]{1,0:T(8,128)(2,1)}, u32[]{:S(2)}, u32[]{:S(2)}) collective-permute-start(bf16[256,4096]{1,0:T(8,128)(2,1)} %collective-permute-done.1.rest_2_), channel_id=1, source_target_pairs={{0,2},{2,0},{4,6},{6,4},{8,10},{10,8},{12,14},{14,12},{16,18},{18,... | collective-permute-start | bytes 6291464 | tf_op jit(solution)/shard_map/ppermute | solution.py:496
  137.7 70.8 %collective-permute-start.12 = (bf16[256,4096]{1,0:T(8,128)(2,1)}, bf16[256,4096]{1,0:T(8,128)(2,1)}, u32[]{:S(2)}, u32[]{:S(2)}) collective-permute-start(bf16[256,4096]{1,0:T(8,128)(2,1)} %collective-permute-done.3.rest_3_), channel_id=1, source_target_pairs={{0,2},{2,0},{4,6},{6,4},{8,10},{10,8},{12,14},{14,12},{16,18},{18,... | collective-permute-start | bytes 6291464 | tf_op jit(solution)/shard_map/ppermute | solution.py:496
  137.9 70.7 %collective-permute-start.9 = (bf16[256,4096]{1,0:T(8,128)(2,1)}, bf16[256,4096]{1,0:T(8,128)(2,1)}, u32[]{:S(2)}, u32[]{:S(2)}) collective-permute-start(bf16[256,4096]{1,0:T(8,128)(2,1)} %get-tuple-element.57), channel_id=1, source_target_pairs={{0,1},{1,0},{2,3},{3,2},{4,5},{5,4},{6,7},{7,6},{8,9},{9,8},{10,11... | collective-permute-start | bytes 6291464 | tf_op jit(solution)/shard_map/ppermute | solution.py:532
  139.4 69.1 %collective-permute-start.10 = (bf16[256,4096]{1,0:T(8,128)(2,1)}, bf16[256,4096]{1,0:T(8,128)(2,1)S(1)}, u32[]{:S(2)}, u32[]{:S(2)}) collective-permute-start(bf16[256,4096]{1,0:T(8,128)(2,1)} %collective-permute-done.1.rest_2_), channel_id=1, source_target_pairs={{0,4},{2,6},{4,0},{6,2},{8,12},{10,14},{12,8},{14,10},{16,20},{18,... | collective-permute-start | bytes 6291464 | tf_op jit(solution)/shard_map/ppermute | solution.py:496
  175.0 33.5 %all-to-all-start.4 = ((bf16[16,192,128]{2,1,0:T(8,128)(2,1)}), bf16[16,192,128]{2,1,0:T(8,128)(2,1)S(1)}, u32[]{:S(2)}, u32[]{:S(2)}) async-start(bf16[16,192,128]{2,1,0:T(8,128)(2,1)} %shard_map.70), calls=%async_computation.4 | async-start | bytes 1572864 | tf_op jit(solution)/shard_map/all_to_all | solution.py:539
  209.8 24.7 %all-to-all-start.5 = ((bf16[16,192,128]{2,1,0:T(8,128)(2,1)}), bf16[16,192,128]{2,1,0:T(8,128)(2,1)S(1)}, u32[]{:S(2)}, u32[]{:S(2)}) async-start(bf16[16,192,128]{2,1,0:T(8,128)(2,1)} %shard_map.71), calls=%async_computation.5 | async-start | bytes 1572864 | tf_op jit(solution)/shard_map/all_to_all | solution.py:543
  215.9 33.8 %collective-permute-start.14 = (bf16[256,4096]{1,0:T(8,128)(2,1)}, bf16[256,4096]{1,0:T(8,128)(2,1)}, u32[]{:S(2)}, u32[]{:S(2)}) collective-permute-start(bf16[256,4096]{1,0:T(8,128)(2,1)} %collective-permute-done.9.rest_4_), channel_id=1, source_target_pairs={{0,2},{2,0},{4,6},{6,4},{8,10},{10,8},{12,14},{14,12},{16,18},{18,... | collective-permute-start | bytes 6291464 | tf_op jit(solution)/shard_map/ppermute | solution.py:496
  216.3 33.4 %collective-permute-start.15 = (bf16[256,4096]{1,0:T(8,128)(2,1)}, bf16[256,4096]{1,0:T(8,128)(2,1)}, u32[]{:S(2)}, u32[]{:S(2)}) collective-permute-start(bf16[256,4096]{1,0:T(8,128)(2,1)} %copy-done.4), channel_id=1, source_target_pairs={{0,2},{2,0},{4,6},{6,4},{8,10},{10,8},{12,14},{14,12},{16,18},{18,... | collective-permute-start | bytes 6291464 | tf_op jit(solution)/shard_map/ppermute | solution.py:496
  216.4 33.2 %collective-permute-start.8 = (bf16[16,192,128]{2,1,0:T(8,128)(2,1)S(1)}, bf16[16,192,128]{2,1,0:T(8,128)(2,1)S(1)}, u32[]{:S(2)}, u32[]{:S(2)}) collective-permute-start(bf16[16,192,128]{2,1,0:T(8,128)(2,1)S(1)} %all-to-all-done.4.rest_0_), channel_id=1, source_target_pairs={{0,1},{1,0},{2,3},{3,2},{4,5},{5,4},{6,7},{7,6},{8,9},{9,8},{10,11... | collective-permute-start | bytes 2359304 | tf_op jit(solution)/shard_map/ppermute | solution.py:545
  234.6 19.7 %collective-permute-start.13 = (bf16[16,192,128]{2,1,0:T(8,128)(2,1)S(1)}, bf16[16,192,128]{2,1,0:T(8,128)(2,1)S(1)}, u32[]{:S(2)}, u32[]{:S(2)}) collective-permute-start(bf16[16,192,128]{2,1,0:T(8,128)(2,1)S(1)} %all-to-all-done.5.rest_1_), channel_id=1, source_target_pairs={{0,1},{1,0},{2,3},{3,2},{4,5},{5,4},{6,7},{7,6},{8,9},{9,8},{10,11... | collective-permute-start | bytes 2359304 | tf_op jit(solution)/shard_map/ppermute | solution.py:545
  (8 other events, 62.5 us)

commit v5 on v4

--- a/solution.py
+++ b/solution.py
@@ -212,9 +212,9 @@
 def attend_kernel(ctx_size, block, cls_ref, count_ref, got_ref, key_ref, value_ref, out_ref,
                   query_all, query_two, scores_a, scores_b, top_a, top_b, run_max, run_acc):
     span = 2 * TOK_DEV
-    pair = 2 * block
-    supers = ctx_size // 2
-    steps = supers * (supers + 1) // 2
+    pair = 4 * block
+    supers = ctx_size // 4
+    steps = supers * (supers + 1)
     cls = cls_ref[0]
     piece = piece_rows(got_ref.shape[1])
     query_all[...] = jnp.zeros_like(query_all)
@@ -254,11 +254,15 @@
         scores[...] = found
         top[...] = row_top(found)
 
-    def mask(scores, top):
-        row = lax.broadcasted_iota(jnp.int32, (pair, span), 0)
+    def mask(scores, top, first):
+        row_ids = lax.broadcasted_iota(jnp.int32, (pair, HD), 0)
+        row = row_ids + cls * block - first
+        for n in range(1, 4):
+            row = row + jnp.where(row_ids >= n * block, TOK_DEV - block, 0)
         col = lax.broadcasted_iota(jnp.int32, (pair, span), 1)
-        row = jnp.where(row >= block, row + (TOK_DEV - block), row) + cls * block
-        found = jnp.where(col <= row, scores[...], masked_score)
+        found = jnp.where(
+            col <= jnp.concatenate([row] * (span // HD), axis=1), scores[...], masked_score
+        )
         scores[...] = found
         top[...] = row_top(found)
 
@@ -278,7 +282,7 @@
         run_acc[...] = jnp.zeros_like(run_acc)
 
     def one_step(now, later, i, k):
-        last = k == i
+        last = k == 2 * i + 1
         next_i = jnp.where(last, i + 1, i)
         next_k = jnp.where(last, 0, k + 1)
         score(*later, next_i, next_k)
@@ -287,20 +291,20 @@
         @pl.when(last)
         def _():
             result = (run_acc[:, :HD] / run_acc[:, HD:]).astype(jnp.bfloat16)
-            out_ref[2 * i] = result[:block]
-            out_ref[2 * i + 1] = result[block:]
+            for n in range(4):
+                out_ref[4 * i + n] = result[n * block : (n + 1) * block]
             clear()
 
-        @pl.when(next_k == next_i)
+        @pl.when(next_k >= 2 * next_i)
         def _():
-            mask(*later)
+            mask(*later, (next_k - 2 * next_i) * span)
 
         return next_i, next_k
 
     buffers_a, buffers_b = (scores_a, top_a), (scores_b, top_b)
     clear()
     score(*buffers_a, 0, 0)
-    mask(*buffers_a)
+    mask(*buffers_a, 0)
 
     def two_steps(t, at):
         at = one_step(buffers_a, buffers_b, *at)
@@ -321,12 +325,12 @@
         scratch_shapes=[
             pltpu.VMEM((ctx_size * block + PAD, HD), jnp.bfloat16),
             pltpu.VMEM((ctx_size * block, 2 * HD), jnp.bfloat16),
-            pltpu.VMEM((2 * block, 2 * TOK_DEV), jnp.float32),
-            pltpu.VMEM((2 * block, 2 * TOK_DEV), jnp.float32),
-            pltpu.VMEM((2 * block, HD), jnp.float32),
-            pltpu.VMEM((2 * block, HD), jnp.float32),
-            pltpu.VMEM((2 * block, HD), jnp.float32),
-            pltpu.VMEM((2 * block, 2 * HD), jnp.float32),
+            pltpu.VMEM((4 * block, 2 * TOK_DEV), jnp.float32),
+            pltpu.VMEM((4 * block, 2 * TOK_DEV), jnp.float32),
+            pltpu.VMEM((4 * block, HD), jnp.float32),
+            pltpu.VMEM((4 * block, HD), jnp.float32),
+            pltpu.VMEM((4 * block, HD), jnp.float32),
+            pltpu.VMEM((4 * block, 2 * HD), jnp.float32),
         ],
         compiler_params=params(),
         cost_estimate=pl.CostEstimate(
@@ -507,29 +511,23 @@
     key_parts = swap(key_parts, bits[0])
     value_parts = [send_across(value_packed)]
     packed_q = list(pack(q_slots, cosine, sine, query, True, chunks, classes, cap))
-    came = [lax.ppermute(weight_rows(0), "tp", both)] if traded else []
-    packed_q[0], key_parts, value_parts, came = lax.optimization_barrier(
-        (packed_q[0], key_parts, value_parts, came)
+    came = [lax.ppermute(weight_rows(p), "tp", both) for p in range(3)] if traded else []
+    packed_q[0], key_parts, value_parts = lax.optimization_barrier(
+        (packed_q[0], key_parts, value_parts)
     )
     got_q = [send_query(packed_q[0])]
     value_parts = swap(value_parts, bits[0])
     for bit in bits[1:]:
         key_parts = swap(key_parts, bit)
-    if traded:
-        slice_1, came = lax.optimization_barrier((weight_rows(1), came))
-        came = came + [lax.ppermute(slice_1, "tp", both)]
+    keys = compact(member, kept_count, key_parts, offsets, total, True)
     if chunks > 1:
-        packed_q[1], value_parts, came = lax.optimization_barrier((packed_q[1], value_parts, came))
+        packed_q[1], value_parts, keys = lax.optimization_barrier((packed_q[1], value_parts, keys))
     for bit in bits[1:]:
         value_parts = swap(value_parts, bit)
     got_q = got_q + [send_query(packed) for packed in packed_q[1:]]
-    keys = compact(member, kept_count, key_parts, offsets, total, True)
     values = compact(member, kept_count, value_parts, offsets, total, False)
-    crossed = []
     if traded:
-        crossed = [chip_swap(part, 1) for part in came]
-        slice_2, came = lax.optimization_barrier((weight_rows(2), came))
-        came = came + [lax.ppermute(slice_2, "tp", both), chip_swap(came[0], 2)]
+        came = came + [chip_swap(came[0], 2)]
 
     got, done = [], None
     for j in range(chunks):
@@ -539,11 +537,11 @@
             got.append(lax.all_to_all(done, "ctx", split_axis=0, concat_axis=0, tiled=True))
         done = attend(cls_j.reshape(1), kept_count, got_q[j], keys, values, block)
     if traded:
-        done, came, crossed = lax.optimization_barrier((done, came, crossed))
+        done, came = lax.optimization_barrier((done, came))
     got.append(lax.all_to_all(done, "ctx", split_axis=0, concat_axis=0, tiled=True))
     if traded:
         theirs = [lax.ppermute(one, "tp", both) for one in got]
-        came = came + crossed + [chip_swap(part, 1) for part in came[2:]]
+        came = came + [chip_swap(part, 1) for part in came]
         own = project(tp_me * columns, got, out_weight, columns, classes)
         per = depth // HD
         order = [jnp.where(side == 0, p, 3 - p) for p in range(3)] + [jnp.where(side == 0, 3, 0)]

time: 271 us -> 269 us (level)
  Pallas kernels: 114 us -> 111 us
  waiting for transfers between devices: 99 us -> 102 us
  starting transfers between devices: 45.2 us -> 42.3 us
    ppermute x6, waiting for transfers between devices: 47 us -> 30.8 us  [swap(): return parts + [lax.ppermute(part, 'ctx', pairs) for part in parts]]
    ppermute x3, waiting for transfers between devices: 19.8 us -> 32.5 us  [local(): lax.ppermute(weight_rows(p), 'tp', both)]
    all_to_all x2, waiting for transfers between devices: 9.92 us -> 18.3 us  [send_across(): lax.all_to_all(packed, 'ctx', split_axis=0, concat_axis=0, tiled=True, ax...]
  transfers between devices with their start and end apart: 22 -> 22, of which waited for: 9 -> 8; matrix products, arithmetic and copies ran while one was open for 2% -> 2% of each run, Pallas kernels for 35% -> 34%
where the time goes in v5:
time: 269 us; the launch traced here: 268 us
  Pallas kernels  111 us (41%)
  waiting for transfers between devices  102 us (38%)
  starting transfers between devices  42.3 us (16%)
  local copies, waits for them, and re-layouts  9.93 us (4%)
    pallas_call x2, Pallas kernels, attend(): pl.pallas_call(functools.partial(attend_kernel, ctx_size, block), in_spec...  54.8 us
    ppermute x3, waiting for transfers between devices, local(): lax.ppermute(weight_rows(p), 'tp', both)  32.5 us
    ppermute x6, waiting for transfers between devices, swap(): return parts + [lax.ppermute(part, 'ctx', pairs) for part in parts]  30.8 us
    all_to_all x2, waiting for transfers between devices, send_across(): lax.all_to_all(packed, 'ctx', split_axis=0, concat_axis=0, tiled=True, ax...  18.3 us
    all_to_all x2, waiting for transfers between devices, local(): lax.all_to_all(done, 'ctx', split_axis=0, concat_axis=0, tiled=True)  16.3 us
    pallas_call x3, Pallas kernels, pack(): pl.pallas_call(functools.partial(pack_kernel, turned, classes, cap, width...  15.4 us
    pallas_call x1, Pallas kernels, join(): pl.pallas_call(functools.partial(join_kernel, len(got), len(weights)), gr...  15.1 us
    pallas_call x1, Pallas kernels, project(): pl.pallas_call(functools.partial(project_kernel, classes, len(got)), grid...  13.8 us
  transfers between devices with their start and end apart: 22, of which 8 were waited for; matrix products, arithmetic and copies ran while one was open for 2% of the time, Pallas kernels for 34%

profile of v5, /device:TPU:0, one launch (start us, length us, event | category | flops | bytes accessed | tf_op | source)
XLA Modules:
  0.0 267.6 jit_solution(10120894950230419916)
XLA Ops:
  1.6 2.5 negate_select_fusion
  4.1 3.5 %shard_map.67 = bf16[4,1,784,128]{3,2,1,0:T(8,128)(2,1)} custom-call(s32[1,768]{1,0:T(1,128)} %get-tuple-element.29.slot_ref, f32[768,128]{1,0:T(8,128)} %get-tuple-element.51.cos_ref, f32[768,128]{1,0:T(8,128)} %get-tuple-element.50.sin_ref, bf16[768,512]{1,0:T(8,128)(2,1)} %row_ref.5), custom_call_target="tpu_custom_call" | custom-call | flops 616562688 | bytes 1572864 | tf_op jit(solution)/shard_map/pallas_call | solution.py:124
  7.5 6.3 %all-to-all-start = ((bf16[4,784,128]{2,1,0:T(8,128)(2,1)}), bf16[4,784,128]{2,1,0:T(8,128)(2,1)S(1)}, u32[]{:S(2)}, u32[]{:S(2)}) async-start(bf16[4,784,128]{2,1,0:T(8,128)(2,1)} %bitcast.16), calls=%async_computation | async-start | bytes 1605632 | tf_op jit(solution)/shard_map/all_to_all | solution.py:478
  13.9 3.2 %shard_map.66 = bf16[4,1,784,128]{3,2,1,0:T(8,128)(2,1)} custom-call(s32[1,768]{1,0:T(1,128)} %get-tuple-element.29.slot_ref, f32[768,128]{1,0:T(8,128)} %get-tuple-element.51.cos_ref, f32[768,128]{1,0:T(8,128)} %get-tuple-element.50.sin_ref, bf16[768,512]{1,0:T(8,128)(2,1)} %row_ref.4), custom_call_target="tpu_custom_call" | custom-call | flops 616562688 | bytes 1572864 | tf_op jit(solution)/shard_map/pallas_call | solution.py:124
  17.1 17.3 %all-to-all-done.rest_0_ = bf16[4,784,128]{2,1,0:T(8,128)(2,1)S(1)} async-done(((bf16[4,784,128]{2,1,0:T(8,128)(2,1)}), bf16[4,784,128]{2,1,0:T(8,128)(2,1)S(1)}, u32[]{:S(2)}, u32[]{:S(2)}) %all-to-all-start) | async-done | bytes 802848 | tf_op jit(solution)/shard_map/all_to_all | solution.py:478
  34.3 3.5 %all-to-all-start.1 = ((bf16[4,784,128]{2,1,0:T(8,128)(2,1)}), bf16[4,784,128]{2,1,0:T(8,128)(2,1)S(1)}, u32[]{:S(2)}, u32[]{:S(2)}) async-start(bf16[4,784,128]{2,1,0:T(8,128)(2,1)} %bitcast.15), calls=%async_computation.1 | async-start | bytes 1605632 | tf_op jit(solution)/shard_map/all_to_all | solution.py:478
  39.4 8.7 %shard_map.65 = (bf16[16,1,400,128]{3,2,1,0:T(8,128)(2,1)}, bf16[16,1,400,128]{3,2,1,0:T(8,128)(2,1)}) custom-call(s32[1,768]{1,0:T(1,128)} %get-tuple-element.26.slot_ref, f32[768,128]{1,0:T(8,128)} %get-tuple-element.51.cos_ref, f32[768,128]{1,0:T(8,128)} %get-tuple-element.50.sin_ref, bf16[768,2048]{1,0:T(8,128)(2,1)} %row_ref.3), custom_call_target="tpu_custom_call" | custom-call | flops 2516582400 | bytes 6291456 | tf_op jit(solution)/shard_map/pallas_call | solution.py:124
  48.1 8.7 %collective-permute-done.rest_1_ = bf16[4,784,128]{2,1,0:T(8,128)(2,1)S(1)} collective-permute-done((bf16[4,784,128]{2,1,0:T(8,128)(2,1)S(1)}, bf16[4,784,128]{2,1,0:T(8,128)(2,1)S(1)}, u32[]{:S(2)}, u32[]{:S(2)}) %collective-permute-start) | collective-permute-done | bytes 802848 | tf_op jit(solution)/shard_map/ppermute | solution.py:484
  57.8 4.8 %all-to-all-start.3 = ((bf16[16,400,128]{2,1,0:T(8,128)(2,1)}), bf16[16,400,128]{2,1,0:T(8,128)(2,1)}, u32[]{:S(2)}, u32[]{:S(2)}) async-start(bf16[16,400,128]{2,1,0:T(8,128)(2,1)} %bitcast.18), calls=%async_computation.3 | async-start | bytes 3276800 | tf_op jit(solution)/shard_map/all_to_all | solution.py:492
  65.0 5.7 %fusion.4 = (bf16[256,4096]{1,0:T(8,128)(2,1)}, bf16[256,4096]{1,0:T(8,128)(2,1)}, bf16[256,4096]{1,0:T(8,128)(2,1)}) fusion(bf16[2048,8192]{1,0:T(8,128)(2,1)} %rest_2_.1, s32[]{:T(128)S(6)} %select_n.56, s32[]{:T(128)S(6)} %select_n.54, s32[]{:T(128)S(6)} %select_n.55, s32[]{:T(128)S(6)} %select_n.53), kind=kLoop, calls=%fused_computation.11 | loop fusion | bytes 12582928 | tf_op jit(solution)/shard_map/dynamic_slice | solution.py:507
  73.1 5.2 %shard_map.68.key_ref = bf16[256,6144]{1,0:T(8,128)(2,1)} custom-call(s32[1]{0:T(128)} %bitcast.11.member_ref, s32[16]{0:T(128)} %count_ref.9, bf16[4,784,128]{2,1,0:T(8,128)(2,1)} %copy-done.1, bf16[4,784,128]{2,1,0:T(8,128)(2,1)} %copy-done.5, bf16[4,784,128]{2,1,0:T(8,128)(2,1)} %copy-done.8, bf16[4,784,128]{2,1,0:T(8,128)(2,1)} %collective-permute-done.3.rest_3_), custom_call_target="tpu_custom_call" | custom-call | flops 6291456 | bytes 6291456 | tf_op jit(solution)/shard_map/pallas_call | solution.py:196
  78.4 22.2 %collective-permute-done.1.rest_1_ = bf16[4,784,128]{2,1,0:T(8,128)(2,1)} collective-permute-done((bf16[4,784,128]{2,1,0:T(8,128)(2,1)S(1)}, bf16[4,784,128]{2,1,0:T(8,128)(2,1)}, u32[]{:S(2)}, u32[]{:S(2)}) %collective-permute-start.1) | collective-permute-done | bytes 802848 | tf_op jit(solution)/shard_map/ppermute | solution.py:484
  100.5 4.8 %all-to-all-start.2 = ((bf16[16,400,128]{2,1,0:T(8,128)(2,1)}), bf16[16,400,128]{2,1,0:T(8,128)(2,1)}, u32[]{:S(2)}, u32[]{:S(2)}) async-start(bf16[16,400,128]{2,1,0:T(8,128)(2,1)} %bitcast.17), calls=%async_computation.2 | async-start | bytes 3276800 | tf_op jit(solution)/shard_map/all_to_all | solution.py:492
  107.9 11.6 %collective-permute-done.7.rest_2_ = bf16[256,4096]{1,0:T(8,128)(2,1)} collective-permute-done((bf16[256,4096]{1,0:T(8,128)(2,1)}, bf16[256,4096]{1,0:T(8,128)(2,1)}, u32[]{:S(2)}, u32[]{:S(2)}) %collective-permute-start.7) | collective-permute-done | bytes 2097184 | tf_op jit(solution)/shard_map/ppermute | solution.py:514
  121.6 5.2 %shard_map.69.value_ref = bf16[6144,256]{1,0:T(8,128)(2,1)} custom-call(s32[1]{0:T(128)} %bitcast.11.member_ref, s32[16]{0:T(128)} %count_ref.9, bf16[4,784,128]{2,1,0:T(8,128)(2,1)} %copy-done, bf16[4,784,128]{2,1,0:T(8,128)(2,1)} %collective-permute-done.1.rest_1_, bf16[4,784,128]{2,1,0:T(8,128)(2,1)} %copy-done.6, bf16[4,784,128]{2,1,0:T(8,128)(2,1)} %copy-done.7), custom_call_target="tpu_custom_call" | custom-call | flops 6291456 | bytes 6291456 | tf_op jit(solution)/shard_map/pallas_call | solution.py:196
  126.8 27.3 %shard_map.70 = bf16[16,192,128]{2,1,0:T(8,128)(2,1)} custom-call(s32[1]{0:T(128)} %constant.50.clone.1.cls_ref, s32[16]{0:T(128)} %count_ref.9, bf16[16,400,128]{2,1,0:T(8,128)(2,1)} %all-to-all-done.3.got_ref, bf16[256,6144]{1,0:T(8,128)(2,1)} %shard_map.68.key_ref, bf16[6144,256]{1,0:T(8,128)(2,1)} %shard_map.69.value_ref), custom_call_target="tpu_custom_call" | custom-call | flops 9663676416 | bytes 6291456 | tf_op jit(solution)/shard_map/pallas_call | solution.py:320
  154.1 5.9 %all-to-all-start.4 = ((bf16[16,192,128]{2,1,0:T(8,128)(2,1)}), bf16[16,192,128]{2,1,0:T(8,128)(2,1)S(1)}, u32[]{:S(2)}, u32[]{:S(2)}) async-start(bf16[16,192,128]{2,1,0:T(8,128)(2,1)} %shard_map.70), calls=%async_computation.4 | async-start | bytes 1572864 | tf_op jit(solution)/shard_map/all_to_all | solution.py:537
  160.0 27.5 %shard_map.71 = bf16[16,192,128]{2,1,0:T(8,128)(2,1)} custom-call(s32[1]{0:T(128)} %constant.51.clone.1.cls_ref, s32[16]{0:T(128)} %count_ref.9, bf16[16,400,128]{2,1,0:T(8,128)(2,1)} %all-to-all-done.2.got_ref, bf16[256,6144]{1,0:T(8,128)(2,1)} %shard_map.68.key_ref, bf16[6144,256]{1,0:T(8,128)(2,1)} %shard_map.69.value_ref), custom_call_target="tpu_custom_call" | custom-call | flops 9663676416 | bytes 6291456 | tf_op jit(solution)/shard_map/pallas_call | solution.py:320
  187.5 21.0 %collective-permute-done.8.rest_3_ = bf16[256,4096]{1,0:T(8,128)(2,1)} collective-permute-done((bf16[256,4096]{1,0:T(8,128)(2,1)S(1)}, bf16[256,4096]{1,0:T(8,128)(2,1)}, u32[]{:S(2)}, u32[]{:S(2)}) %collective-permute-start.8) | collective-permute-done | bytes 2097184 | tf_op jit(solution)/shard_map/ppermute | solution.py:514
  208.5 4.7 %all-to-all-start.5 = ((bf16[16,192,128]{2,1,0:T(8,128)(2,1)}), bf16[16,192,128]{2,1,0:T(8,128)(2,1)S(1)}, u32[]{:S(2)}, u32[]{:S(2)}) async-start(bf16[16,192,128]{2,1,0:T(8,128)(2,1)} %shard_map.71), calls=%async_computation.5 | async-start | bytes 1572864 | tf_op jit(solution)/shard_map/all_to_all | solution.py:541
  215.6 16.3 %all-to-all-done.5.rest_1_ = bf16[16,192,128]{2,1,0:T(8,128)(2,1)S(1)} async-done(((bf16[16,192,128]{2,1,0:T(8,128)(2,1)}), bf16[16,192,128]{2,1,0:T(8,128)(2,1)S(1)}, u32[]{:S(2)}, u32[]{:S(2)}) %all-to-all-start.5) | async-done | bytes 786464 | tf_op jit(solution)/shard_map/all_to_all | solution.py:541
  234.1 13.8 %shard_map.72.rest_10_ = bf16[384,4096]{1,0:T(8,128)(2,1)} custom-call(s32[1]{0:T(128)} %bitcast.14.column_ref, bf16[16,192,128]{2,1,0:T(8,128)(2,1)} %copy-done.2, bf16[16,192,128]{2,1,0:T(8,128)(2,1)} %copy-done.3, bf16[2048,8192]{1,0:T(8,128)(2,1)} %rest_2_.1), custom_call_target="tpu_custom_call" | custom-call | flops 6442450944 | bytes 16777216 | tf_op jit(solution)/shard_map/pallas_call | solution.py:363
  247.9 3.7 %collective-permute-done.11.rest_1_ = bf16[16,192,128]{2,1,0:T(8,128)(2,1)S(1)} collective-permute-done((bf16[16,192,128]{2,1,0:T(8,128)(2,1)S(1)}, bf16[16,192,128]{2,1,0:T(8,128)(2,1)S(1)}, u32[]{:S(2)}, u32[]{:S(2)}) %collective-permute-start.11) | collective-permute-done | bytes 786464 | tf_op jit(solution)/shard_map/ppermute | solution.py:543
  252.5 15.1 %shard_map.73 = bf16[384,4096]{1,0:T(8,128)(2,1)} custom-call(s32[8]{0:T(128)} %stack.35.head_ref, bf16[16,192,128]{2,1,0:T(8,128)(2,1)} %copy-done.9, bf16[16,192,128]{2,1,0:T(8,128)(2,1)} %copy-done.10, bf16[256,4096]{1,0:T(8,128)(2,1)} %collective-permute-done.7.rest_2_, bf16[256,4096]{1,0:T(8,128)(2,1)} %collective-permute-done.8.rest_3_, ...), custom_call_target="tpu_custom_call" | custom-call | flops 6442450944 | bytes 16777216 | tf_op jit(solution)/shard_map/pallas_call | solution.py:412
  (58 shorter events, 19.1 us)
Async XLA Ops:
  7.5 26.8 %all-to-all-start = ((bf16[4,784,128]{2,1,0:T(8,128)(2,1)}), bf16[4,784,128]{2,1,0:T(8,128)(2,1)S(1)}, u32[]{:S(2)}, u32[]{:S(2)}) async-start(bf16[4,784,128]{2,1,0:T(8,128)(2,1)} %bitcast.16), calls=%async_computation | async-start | bytes 1605632 | tf_op jit(solution)/shard_map/all_to_all | solution.py:478
  34.3 30.1 %copy-start.1 = (bf16[4,784,128]{2,1,0:T(8,128)(2,1)}, bf16[4,784,128]{2,1,0:T(8,128)(2,1)S(1)}, u32[]{:S(2)}) copy-start(bf16[4,784,128]{2,1,0:T(8,128)(2,1)S(1)} %all-to-all-done.rest_0_) | copy-start | bytes 2408452
  34.3 23.4 %all-to-all-start.1 = ((bf16[4,784,128]{2,1,0:T(8,128)(2,1)}), bf16[4,784,128]{2,1,0:T(8,128)(2,1)S(1)}, u32[]{:S(2)}, u32[]{:S(2)}) async-start(bf16[4,784,128]{2,1,0:T(8,128)(2,1)} %bitcast.15), calls=%async_computation.1 | async-start | bytes 1605632 | tf_op jit(solution)/shard_map/all_to_all | solution.py:478
  37.8 18.9 %collective-permute-start = (bf16[4,784,128]{2,1,0:T(8,128)(2,1)S(1)}, bf16[4,784,128]{2,1,0:T(8,128)(2,1)S(1)}, u32[]{:S(2)}, u32[]{:S(2)}) collective-permute-start(bf16[4,784,128]{2,1,0:T(8,128)(2,1)S(1)} %all-to-all-done.rest_0_), channel_id=1, source_target_pairs={{0,4},{2,6},{4,0},{6,2},{8,12},{10,14},{12,8},{14,10},{16,20},{18,... | collective-permute-start | bytes 2408456 | tf_op jit(solution)/shard_map/ppermute | solution.py:484
  57.8 47.5 %copy-start = (bf16[4,784,128]{2,1,0:T(8,128)(2,1)}, bf16[4,784,128]{2,1,0:T(8,128)(2,1)S(1)}, u32[]{:S(2)}) copy-start(bf16[4,784,128]{2,1,0:T(8,128)(2,1)S(1)} %all-to-all-done.1.rest_0_) | copy-start | bytes 2408452
  57.8 42.8 %all-to-all-start.3 = ((bf16[16,400,128]{2,1,0:T(8,128)(2,1)}), bf16[16,400,128]{2,1,0:T(8,128)(2,1)}, u32[]{:S(2)}, u32[]{:S(2)}) async-start(bf16[16,400,128]{2,1,0:T(8,128)(2,1)} %bitcast.18), calls=%async_computation.3 | async-start | bytes 3276800 | tf_op jit(solution)/shard_map/all_to_all | solution.py:492
  62.6 37.9 %collective-permute-start.1 = (bf16[4,784,128]{2,1,0:T(8,128)(2,1)S(1)}, bf16[4,784,128]{2,1,0:T(8,128)(2,1)}, u32[]{:S(2)}, u32[]{:S(2)}) collective-permute-start(bf16[4,784,128]{2,1,0:T(8,128)(2,1)S(1)} %all-to-all-done.1.rest_0_), channel_id=1, source_target_pairs={{0,4},{2,6},{4,0},{6,2},{8,12},{10,14},{12,8},{14,10},{16,20},{18,... | collective-permute-start | bytes 2408456 | tf_op jit(solution)/shard_map/ppermute | solution.py:484
  64.5 7.7 %collective-permute-start.2 = (bf16[4,784,128]{2,1,0:T(8,128)(2,1)S(1)}, bf16[4,784,128]{2,1,0:T(8,128)(2,1)S(1)}, u32[]{:S(2)}, u32[]{:S(2)}) collective-permute-start(bf16[4,784,128]{2,1,0:T(8,128)(2,1)S(1)} %all-to-all-done.rest_0_), channel_id=1, source_target_pairs={{0,2},{2,0},{4,6},{6,4},{8,10},{10,8},{12,14},{14,12},{16,18},{18,... | collective-permute-start | bytes 2408456 | tf_op jit(solution)/shard_map/ppermute | solution.py:484
  64.5 7.7 %collective-permute-start.3 = (bf16[4,784,128]{2,1,0:T(8,128)(2,1)S(1)}, bf16[4,784,128]{2,1,0:T(8,128)(2,1)}, u32[]{:S(2)}, u32[]{:S(2)}) collective-permute-start(bf16[4,784,128]{2,1,0:T(8,128)(2,1)S(1)} %collective-permute-done.rest_1_), channel_id=1, source_target_pairs={{0,2},{2,0},{4,6},{6,4},{8,10},{10,8},{12,14},{14,12},{16,18},{18,... | collective-permute-start | bytes 2408456 | tf_op jit(solution)/shard_map/ppermute | solution.py:484
  70.7 48.8 %collective-permute-start.7 = (bf16[256,4096]{1,0:T(8,128)(2,1)}, bf16[256,4096]{1,0:T(8,128)(2,1)}, u32[]{:S(2)}, u32[]{:S(2)}) collective-permute-start(bf16[256,4096]{1,0:T(8,128)(2,1)} %get-tuple-element.49), channel_id=1, source_target_pairs={{0,1},{1,0},{2,3},{3,2},{4,5},{5,4},{6,7},{7,6},{8,9},{9,8},{10,11... | collective-permute-start | bytes 6291464 | tf_op jit(solution)/shard_map/ppermute | solution.py:514
  100.5 53.6 %all-to-all-start.2 = ((bf16[16,400,128]{2,1,0:T(8,128)(2,1)}), bf16[16,400,128]{2,1,0:T(8,128)(2,1)}, u32[]{:S(2)}, u32[]{:S(2)}) async-start(bf16[16,400,128]{2,1,0:T(8,128)(2,1)} %bitcast.17), calls=%async_computation.2 | async-start | bytes 3276800 | tf_op jit(solution)/shard_map/all_to_all | solution.py:492
  105.3 14.4 %collective-permute-start.4 = (bf16[4,784,128]{2,1,0:T(8,128)(2,1)S(1)}, bf16[4,784,128]{2,1,0:T(8,128)(2,1)S(1)}, u32[]{:S(2)}, u32[]{:S(2)}) collective-permute-start(bf16[4,784,128]{2,1,0:T(8,128)(2,1)S(1)} %all-to-all-done.1.rest_0_), channel_id=1, source_target_pairs={{0,2},{2,0},{4,6},{6,4},{8,10},{10,8},{12,14},{14,12},{16,18},{18,... | collective-permute-start | bytes 2408456 | tf_op jit(solution)/shard_map/ppermute | solution.py:484
  105.7 14.0 %collective-permute-start.5 = (bf16[4,784,128]{2,1,0:T(8,128)(2,1)}, bf16[4,784,128]{2,1,0:T(8,128)(2,1)S(1)}, u32[]{:S(2)}, u32[]{:S(2)}) collective-permute-start(bf16[4,784,128]{2,1,0:T(8,128)(2,1)} %collective-permute-done.1.rest_1_), channel_id=1, source_target_pairs={{0,2},{2,0},{4,6},{6,4},{8,10},{10,8},{12,14},{14,12},{16,18},{18,... | collective-permute-start | bytes 2408456 | tf_op jit(solution)/shard_map/ppermute | solution.py:484
  105.9 81.6 %collective-permute-start.9 = (bf16[256,4096]{1,0:T(8,128)(2,1)}, bf16[256,4096]{1,0:T(8,128)(2,1)}, u32[]{:S(2)}, u32[]{:S(2)}) collective-permute-start(bf16[256,4096]{1,0:T(8,128)(2,1)} %get-tuple-element.47), channel_id=1, source_target_pairs={{0,1},{1,0},{2,3},{3,2},{4,5},{5,4},{6,7},{7,6},{8,9},{9,8},{10,11... | collective-permute-start | bytes 6291464 | tf_op jit(solution)/shard_map/ppermute | solution.py:514
  107.4 101.0 %collective-permute-start.8 = (bf16[256,4096]{1,0:T(8,128)(2,1)S(1)}, bf16[256,4096]{1,0:T(8,128)(2,1)}, u32[]{:S(2)}, u32[]{:S(2)}) collective-permute-start(bf16[256,4096]{1,0:T(8,128)(2,1)S(1)} %copy-done.4), channel_id=1, source_target_pairs={{0,1},{1,0},{2,3},{3,2},{4,5},{5,4},{6,7},{7,6},{8,9},{9,8},{10,11... | collective-permute-start | bytes 6291464 | tf_op jit(solution)/shard_map/ppermute | solution.py:514
  119.5 88.9 %collective-permute-start.10 = (bf16[256,4096]{1,0:T(8,128)(2,1)}, bf16[256,4096]{1,0:T(8,128)(2,1)}, u32[]{:S(2)}, u32[]{:S(2)}) collective-permute-start(bf16[256,4096]{1,0:T(8,128)(2,1)} %collective-permute-done.7.rest_2_), channel_id=1, source_target_pairs={{0,4},{2,6},{4,0},{6,2},{8,12},{10,14},{12,8},{14,10},{16,20},{18,... | collective-permute-start | bytes 6291464 | tf_op jit(solution)/shard_map/ppermute | solution.py:500
  154.1 54.3 %all-to-all-start.4 = ((bf16[16,192,128]{2,1,0:T(8,128)(2,1)}), bf16[16,192,128]{2,1,0:T(8,128)(2,1)S(1)}, u32[]{:S(2)}, u32[]{:S(2)}) async-start(bf16[16,192,128]{2,1,0:T(8,128)(2,1)} %shard_map.70), calls=%async_computation.4 | async-start | bytes 1572864 | tf_op jit(solution)/shard_map/all_to_all | solution.py:537
  208.4 23.5 %collective-permute-start.12 = (bf16[256,4096]{1,0:T(8,128)(2,1)}, bf16[256,4096]{1,0:T(8,128)(2,1)}, u32[]{:S(2)}, u32[]{:S(2)}) collective-permute-start(bf16[256,4096]{1,0:T(8,128)(2,1)} %collective-permute-done.7.rest_2_), channel_id=1, source_target_pairs={{0,2},{2,0},{4,6},{6,4},{8,10},{10,8},{12,14},{14,12},{16,18},{18,... | collective-permute-start | bytes 6291464 | tf_op jit(solution)/shard_map/ppermute | solution.py:500
  208.5 23.5 %all-to-all-start.5 = ((bf16[16,192,128]{2,1,0:T(8,128)(2,1)}), bf16[16,192,128]{2,1,0:T(8,128)(2,1)S(1)}, u32[]{:S(2)}, u32[]{:S(2)}) async-start(bf16[16,192,128]{2,1,0:T(8,128)(2,1)} %shard_map.71), calls=%async_computation.5 | async-start | bytes 1572864 | tf_op jit(solution)/shard_map/all_to_all | solution.py:541
  213.2 34.7 %collective-permute-start.13 = (bf16[256,4096]{1,0:T(8,128)(2,1)}, bf16[256,4096]{1,0:T(8,128)(2,1)}, u32[]{:S(2)}, u32[]{:S(2)}) collective-permute-start(bf16[256,4096]{1,0:T(8,128)(2,1)} %collective-permute-done.8.rest_3_), channel_id=1, source_target_pairs={{0,2},{2,0},{4,6},{6,4},{8,10},{10,8},{12,14},{14,12},{16,18},{18,... | collective-permute-start | bytes 6291464 | tf_op jit(solution)/shard_map/ppermute | solution.py:500
  213.6 34.3 %collective-permute-start.14 = (bf16[256,4096]{1,0:T(8,128)(2,1)}, bf16[256,4096]{1,0:T(8,128)(2,1)}, u32[]{:S(2)}, u32[]{:S(2)}) collective-permute-start(bf16[256,4096]{1,0:T(8,128)(2,1)} %collective-permute-done.9.rest_4_), channel_id=1, source_target_pairs={{0,2},{2,0},{4,6},{6,4},{8,10},{10,8},{12,14},{14,12},{16,18},{18,... | collective-permute-start | bytes 6291464 | tf_op jit(solution)/shard_map/ppermute | solution.py:500
  213.8 34.1 %collective-permute-start.15 = (bf16[256,4096]{1,0:T(8,128)(2,1)}, bf16[256,4096]{1,0:T(8,128)(2,1)}, u32[]{:S(2)}, u32[]{:S(2)}) collective-permute-start(bf16[256,4096]{1,0:T(8,128)(2,1)} %collective-permute-done.10.rest_5_), channel_id=1, source_target_pairs={{0,2},{2,0},{4,6},{6,4},{8,10},{10,8},{12,14},{14,12},{16,18},{18,... | collective-permute-start | bytes 6291464 | tf_op jit(solution)/shard_map/ppermute | solution.py:500
  214.1 33.8 %collective-permute-start.6 = (bf16[16,192,128]{2,1,0:T(8,128)(2,1)S(1)}, bf16[16,192,128]{2,1,0:T(8,128)(2,1)S(1)}, u32[]{:S(2)}, u32[]{:S(2)}) collective-permute-start(bf16[16,192,128]{2,1,0:T(8,128)(2,1)S(1)} %all-to-all-done.4.rest_0_), channel_id=1, source_target_pairs={{0,1},{1,0},{2,3},{3,2},{4,5},{5,4},{6,7},{7,6},{8,9},{9,8},{10,11... | collective-permute-start | bytes 2359304 | tf_op jit(solution)/shard_map/ppermute | solution.py:543
  231.9 19.7 %collective-permute-start.11 = (bf16[16,192,128]{2,1,0:T(8,128)(2,1)S(1)}, bf16[16,192,128]{2,1,0:T(8,128)(2,1)S(1)}, u32[]{:S(2)}, u32[]{:S(2)}) collective-permute-start(bf16[16,192,128]{2,1,0:T(8,128)(2,1)S(1)} %all-to-all-done.5.rest_1_), channel_id=1, source_target_pairs={{0,1},{1,0},{2,3},{3,2},{4,5},{5,4},{6,7},{7,6},{8,9},{9,8},{10,11... | collective-permute-start | bytes 2359304 | tf_op jit(solution)/shard_map/ppermute | solution.py:543
  (9 other events, 78.0 us)

commit v6 on v5

--- a/solution.py
+++ b/solution.py
@@ -157,7 +157,7 @@
     lax.fori_loop(0, pieces, one, 0)
 
 
-def compact_kernel(offsets, per, total, doubled, member_ref, count_ref, *rest):
+def compact_kernel(offsets, per, total, as_keys, member_ref, count_ref, *rest):
     parts, out, all_rows, starts = rest[:-3], rest[-3], rest[-2], rest[-1]
     members = len(parts)
     piece = piece_rows(parts[0].shape[1])
@@ -181,24 +181,24 @@
                 lambda at: part[z, pl.ds(at, piece), :],
                 add,
             )
-    if doubled:
+    if as_keys:
         for first in range(0, total, 2 * TOK_DEV):
-            turned = jnp.transpose(all_rows[first : first + 2 * TOK_DEV, :])
-            out[:HD, first : first + 2 * TOK_DEV] = turned
-            out[HD:, first : first + 2 * TOK_DEV] = turned
+            out[:, first : first + 2 * TOK_DEV] = jnp.transpose(
+                all_rows[first : first + 2 * TOK_DEV, :]
+            )
     else:
         out[:, :HD] = all_rows[:total, :]
         out[:, HD:] = jnp.ones((total, HD), jnp.bfloat16)
 
 
-def compact(member, counts, parts, offsets, total, doubled):
+def compact(member, counts, parts, offsets, total, as_keys):
     per = parts[0].shape[0]
     return pl.pallas_call(
-        functools.partial(compact_kernel, offsets, per, total, doubled),
+        functools.partial(compact_kernel, offsets, per, total, as_keys),
         in_specs=[whole_smem(), whole_smem()] + [whole_vmem()] * len(parts),
         out_specs=whole_vmem(),
         out_shape=jax.ShapeDtypeStruct(
-            (2 * HD, total) if doubled else (total, 2 * HD), jnp.bfloat16
+            (HD, total) if as_keys else (total, 2 * HD), jnp.bfloat16
         ),
         scratch_shapes=[
             pltpu.VMEM((total + PAD, HD), jnp.bfloat16),
@@ -210,7 +210,7 @@
 
 
 def attend_kernel(ctx_size, block, cls_ref, count_ref, got_ref, key_ref, value_ref, out_ref,
-                  query_all, query_two, scores_a, scores_b, top_a, top_b, run_max, run_acc):
+                  query_all, scores_a, scores_b, top_a, top_b, run_max, run_acc):
     span = 2 * TOK_DEV
     pair = 4 * block
     supers = ctx_size // 4
@@ -234,21 +234,11 @@
         )
         start = end
 
-    def split(i, carry):
-        rows = pl.ds(pl.multiple_of(i * pair, TILE), pair)
-        scaled = query_all[rows, :].astype(jnp.float32) * exp2_scale
-        high = scaled.astype(jnp.bfloat16)
-        query_two[rows, :HD] = high
-        query_two[rows, HD:] = (scaled - high.astype(jnp.float32)).astype(jnp.bfloat16)
-        return carry
-
-    lax.fori_loop(0, supers, split, 0)
-
     def row_top(found):
         return jnp.broadcast_to(jnp.max(found, axis=1, keepdims=True), (pair, HD))
 
     def score(scores, top, i, k):
-        rows = query_two[pl.ds(pl.multiple_of(jnp.minimum(i, supers - 1) * pair, TILE), pair), :]
+        rows = query_all[pl.ds(pl.multiple_of(jnp.minimum(i, supers - 1) * pair, TILE), pair), :]
         keys = key_ref[:, pl.ds(pl.multiple_of(k * span, HD), span)]
         found = jnp.dot(rows, keys, preferred_element_type=jnp.float32)
         scores[...] = found
@@ -269,9 +259,11 @@
     def absorb(scores, top, k):
         before = run_max[...]
         after = jnp.maximum(before, top[...])
-        rescale = jnp.exp2(before - after)
+        rescale = jnp.exp2((before - after) * exp2_scale)
         run_max[...] = after
-        weights = jnp.exp2(scores[...] - jnp.concatenate([after] * (span // HD), axis=1))
+        weights = jnp.exp2(
+            (scores[...] - jnp.concatenate([after] * (span // HD), axis=1)) * exp2_scale
+        )
         values = value_ref[pl.ds(pl.multiple_of(k * span, TILE), span), :]
         run_acc[...] = run_acc[...] * jnp.concatenate([rescale, rescale], axis=1) + jnp.dot(
             weights.astype(jnp.bfloat16), values, preferred_element_type=jnp.float32
@@ -324,7 +316,6 @@
         out_shape=jax.ShapeDtypeStruct((ctx_size, block, HD), jnp.bfloat16),
         scratch_shapes=[
             pltpu.VMEM((ctx_size * block + PAD, HD), jnp.bfloat16),
-            pltpu.VMEM((ctx_size * block, 2 * HD), jnp.bfloat16),
             pltpu.VMEM((4 * block, 2 * TOK_DEV), jnp.float32),
             pltpu.VMEM((4 * block, 2 * TOK_DEV), jnp.float32),
             pltpu.VMEM((4 * block, HD), jnp.float32),
@@ -382,20 +373,20 @@
     got_refs, weight_refs = rest[:chunks], rest[chunks : chunks + parts]
     own_ref, out_ref, rows_ref = rest[chunks + parts :]
     block = got_refs[0].shape[1]
-    depth = weight_refs[0].shape[0]
+    firsts = [sum(ref.shape[0] for ref in weight_refs[:p]) for p in range(parts)]
 
     @pl.when(pl.program_id(0) == 0)
     def _():
         for j, got_ref in enumerate(got_refs):
             for p in range(parts):
-                for n in range(depth // HD):
-                    at = p * depth + n * HD
+                for n in range(weight_refs[p].shape[0] // HD):
+                    at = firsts[p] + n * HD
                     rows_ref[j * block : (j + 1) * block, at : at + HD] = got_ref[head_ref[p] + n]
 
     total = jnp.zeros(out_ref.shape, jnp.float32)
-    for p, weight_ref in enumerate(weight_refs):
+    for first, weight_ref in zip(firsts, weight_refs):
         total = total + jnp.dot(
-            rows_ref[:, p * depth : (p + 1) * depth],
+            rows_ref[:, first : first + weight_ref.shape[0]],
             weight_ref[...],
             preferred_element_type=jnp.float32,
         )
@@ -406,7 +397,7 @@
 def join(first_heads, got, weights, own):
     ctx_size, block, _ = got[0].shape
     rows, columns = own.shape
-    depth = weights[0].shape[0]
+    depth = sum(weight.shape[0] for weight in weights)
     step = min(512, columns)
     tile = pl.BlockSpec((rows, step), lambda i, first: (0, i))
     return pl.pallas_call(
@@ -415,16 +406,16 @@
             num_scalar_prefetch=1,
             grid=(columns // step,),
             in_specs=[pl.BlockSpec((ctx_size, block, HD), lambda i, first: (0, 0, 0))] * len(got)
-            + [pl.BlockSpec((depth, step), lambda i, first: (0, i))] * len(weights)
+            + [pl.BlockSpec((weight.shape[0], step), lambda i, first: (0, i)) for weight in weights]
             + [tile],
             out_specs=tile,
-            scratch_shapes=[pltpu.VMEM((rows, depth * len(weights)), jnp.bfloat16)],
+            scratch_shapes=[pltpu.VMEM((rows, depth), jnp.bfloat16)],
         ),
         out_shape=jax.ShapeDtypeStruct((rows, columns), jnp.bfloat16),
         compiler_params=params(),
         cost_estimate=pl.CostEstimate(
-            flops=2 * rows * depth * len(weights) * columns,
-            bytes_accessed=2 * depth * len(weights) * columns,
+            flops=2 * rows * depth * columns,
+            bytes_accessed=2 * depth * columns,
             transcendentals=0,
         ),
     )(first_heads, *got, *weights, own)
@@ -493,62 +484,78 @@
             packed.reshape(ctx_size, cap, HD), "ctx", split_axis=0, concat_axis=0, tiled=True
         )
 
-    traded = tp_size == 2 and classes == 1
+    traded = tp_size == 2 and classes == 1 and heads == 16 and chunks == 2
     both = [(0, 1), (1, 0)]
 
     def chip_swap(part, bit):
         return lax.ppermute(part, "ctx", [(d, d ^ bit) for d in range(ctx_size)])
 
     core, side = me & 1, (me >> 1) & 1
-    depth = out_weight.shape[0] // 8
+    sizes = [1, 1, 2, 2]
 
     def weight_rows(p):
-        first = core * (4 * depth) + jnp.where(side == 0, p, 3 - p) * depth
-        return lax.dynamic_slice(out_weight, (first, (1 - tp_me) * columns), (depth, columns))
+        low = sum(sizes[:p])
+        first = jnp.where(side == 0, low, 8 - low - sizes[p]) + core * 8
+        return lax.dynamic_slice(
+            out_weight, (first * HD, (1 - tp_me) * columns), (sizes[p] * HD, columns)
+        )
+
+    def trade(part):
+        return lax.ppermute(part, "tp", both)
 
     key_parts = [send_across(pack_shared(key, True))]
-    value_packed, key_parts = lax.optimization_barrier((pack_shared(value, False), key_parts))
+    slices = [weight_rows(p) for p in range(len(sizes))] if traded else []
+    value_packed, key_parts, slices = lax.optimization_barrier(
+        (pack_shared(value, False), key_parts, slices)
+    )
     key_parts = swap(key_parts, bits[0])
     value_parts = [send_across(value_packed)]
     packed_q = list(pack(q_slots, cosine, sine, query, True, chunks, classes, cap))
-    came = [lax.ppermute(weight_rows(p), "tp", both) for p in range(3)] if traded else []
-    packed_q[0], key_parts, value_parts = lax.optimization_barrier(
-        (packed_q[0], key_parts, value_parts)
+    came = [trade(slices[0])] if traded else []
+    packed_q[0], key_parts, value_parts, came, slices = lax.optimization_barrier(
+        (packed_q[0], key_parts, value_parts, came, slices)
     )
+    if traded:
+        came = came + [trade(slices[1])]
     got_q = [send_query(packed_q[0])]
     value_parts = swap(value_parts, bits[0])
     for bit in bits[1:]:
         key_parts = swap(key_parts, bit)
     keys = compact(member, kept_count, key_parts, offsets, total, True)
     if chunks > 1:
-        packed_q[1], value_parts, keys = lax.optimization_barrier((packed_q[1], value_parts, keys))
+        packed_q[1], value_parts, keys, came, slices = lax.optimization_barrier(
+            (packed_q[1], value_parts, keys, came, slices)
+        )
     for bit in bits[1:]:
         value_parts = swap(value_parts, bit)
     got_q = got_q + [send_query(packed) for packed in packed_q[1:]]
     values = compact(member, kept_count, value_parts, offsets, total, False)
     if traded:
-        came = came + [chip_swap(came[0], 2)]
+        came = came + [trade(slices[2])]
+        aside = [chip_swap(part, 2) for part in came[:2]]
 
     got, done = [], None
     for j in range(chunks):
         cls_j = j * classes + (me & (classes - 1))
         if j > 0:
-            got_q[j], done = lax.optimization_barrier((got_q[j], done))
+            got_q[j], done, came, slices = lax.optimization_barrier((got_q[j], done, came, slices))
             got.append(lax.all_to_all(done, "ctx", split_axis=0, concat_axis=0, tiled=True))
         done = attend(cls_j.reshape(1), kept_count, got_q[j], keys, values, block)
     if traded:
-        done, came = lax.optimization_barrier((done, came))
+        came = came + [trade(slices[3])]
+        done, aside = lax.optimization_barrier((done, aside))
     got.append(lax.all_to_all(done, "ctx", split_axis=0, concat_axis=0, tiled=True))
     if traded:
-        theirs = [lax.ppermute(one, "tp", both) for one in got]
+        theirs = [trade(one) for one in got]
+        came = came + aside
         came = came + [chip_swap(part, 1) for part in came]
         own = project(tp_me * columns, got, out_weight, columns, classes)
-        per = depth // HD
-        order = [jnp.where(side == 0, p, 3 - p) for p in range(3)] + [jnp.where(side == 0, 3, 0)]
-        first_heads = jnp.stack(
-            [(c * 4 + p) * per for c in (core, 1 - core) for p in order]
-        ).astype(jnp.int32)
-        return join(first_heads, theirs, came, own)
+        ups = [sum(sizes[:p]) for p in range(5)]
+        order = [
+            jnp.where(side == 0, up, 8 - up - size) for up, size in zip(ups, sizes)
+        ] + [jnp.where(side == 0, 7 - n, n) for n in range(2)]
+        first_heads = jnp.stack([c * 8 + at for c in (core, 1 - core) for at in order])
+        return join(first_heads.astype(jnp.int32), theirs, came, own)
     full = project(jnp.int32(0) * tp_me, got, out_weight, columns * tp_size, classes)
     split = jnp.transpose(full.reshape(full.shape[0], tp_size, columns), (1, 0, 2))
     swapped = lax.all_to_all(split, "tp", split_axis=0, concat_axis=0, tiled=True)

time: 269 us -> 288 us (1.071)
  waiting for transfers between devices: 102 us -> 119 us
  starting transfers between devices: 42.3 us -> 46.2 us
  Pallas kernels: 111 us -> 108 us
    ppermute x5 -> x8, waiting for transfers between devices: 0.01 us -> 38.3 us  [chip_swap(): return lax.ppermute(part, 'ctx', [(d, d ^ bit) for d in range(ctx_size)])]
    ppermute x5 -> x6, waiting for transfers between devices: 36.2 us -> 23.2 us  [trade(): return lax.ppermute(part, 'tp', both)]
    ppermute x6, waiting for transfers between devices: 30.8 us -> 40.8 us  [swap(): return parts + [lax.ppermute(part, 'ctx', pairs) for part in parts]]
    all_to_all x2, waiting for transfers between devices: 16.3 us -> 6.64 us  [local(): lax.all_to_all(done, 'ctx', split_axis=0, concat_axis=0, tiled=True)]
    all_to_all x2, waiting for transfers between devices: 18.3 us -> 9.76 us  [send_across(): lax.all_to_all(packed, 'ctx', split_axis=0, concat_axis=0, tiled=True, ax...]
    pallas_call x2, Pallas kernels: 54.8 us -> 50.9 us  [attend(): pl.pallas_call(functools.partial(attend_kernel, ctx_size, block), in_spec...]
    dynamic_slice x1 -> x2, local copies, waits for them, and re-layouts: 5.71 us -> 7.5 us  [weight_rows(): lax.dynamic_slice(out_weight, (first * HD, (1 - tp_me) * columns), (sizes...]
    ppermute x5 -> x6, starting transfers between devices: 6.59 us -> 7.29 us  [trade(): return lax.ppermute(part, 'tp', both)]
  transfers between devices with their start and end apart: 22 -> 26, of which waited for: 8 -> 16; matrix products, arithmetic and copies ran while one was open for 2% -> 3% of each run, Pallas kernels for 34% -> 30%
where the time goes in v6:
time: 288 us; the launch traced here: 287 us
  waiting for transfers between devices  119 us (41%)
  Pallas kernels  108 us (38%)
  starting transfers between devices  46.2 us (16%)
  local copies, waits for them, and re-layouts  10.9 us (4%)
    pallas_call x2, Pallas kernels, attend(): pl.pallas_call(functools.partial(attend_kernel, ctx_size, block), in_spec...  50.9 us
    ppermute x6, waiting for transfers between devices, swap(): return parts + [lax.ppermute(part, 'ctx', pairs) for part in parts]  40.8 us
    ppermute x8, waiting for transfers between devices, chip_swap(): return lax.ppermute(part, 'ctx', [(d, d ^ bit) for d in range(ctx_size)])  38.3 us
    ppermute x6, waiting for transfers between devices, trade(): return lax.ppermute(part, 'tp', both)  23.2 us
    pallas_call x1, Pallas kernels, join(): pl.pallas_call(functools.partial(join_kernel, len(got), len(weights)), gr...  16.6 us
    pallas_call x3, Pallas kernels, pack(): pl.pallas_call(functools.partial(pack_kernel, turned, classes, cap, width...  15.4 us
    pallas_call x1, Pallas kernels, project(): pl.pallas_call(functools.partial(project_kernel, classes, len(got)), grid...  13.8 us
    all_to_all x2, starting transfers between devices, send_query(): lax.all_to_all(packed.reshape(ctx_size, cap, HD), 'ctx', split_axis=0, co...  10.5 us
  transfers between devices with their start and end apart: 26, of which 16 were waited for; matrix products, arithmetic and copies ran while one was open for 3% of the time, Pallas kernels for 30%

profile of v6, /device:TPU:0, one launch (start us, length us, event | category | flops | bytes accessed | tf_op | source)
XLA Modules:
  0.0 286.8 jit_solution(4099248632988671910)
XLA Ops:
  4.1 3.5 %shard_map.67 = bf16[4,1,784,128]{3,2,1,0:T(8,128)(2,1)} custom-call(s32[1,768]{1,0:T(1,128)} %get-tuple-element.43.slot_ref, f32[768,128]{1,0:T(8,128)} %get-tuple-element.80.cos_ref, f32[768,128]{1,0:T(8,128)} %get-tuple-element.79.sin_ref, bf16[768,512]{1,0:T(8,128)(2,1)} %row_ref.5), custom_call_target="tpu_custom_call" | custom-call | flops 616562688 | bytes 1572864 | tf_op jit(solution)/shard_map/pallas_call | solution.py:124
  7.5 6.3 %all-to-all-start = ((bf16[4,784,128]{2,1,0:T(8,128)(2,1)}), bf16[4,784,128]{2,1,0:T(8,128)(2,1)S(1)}, u32[]{:S(2)}, u32[]{:S(2)}) async-start(bf16[4,784,128]{2,1,0:T(8,128)(2,1)} %bitcast.19), calls=%async_computation | async-start | bytes 1605632 | tf_op jit(solution)/shard_map/all_to_all | solution.py:469
  19.8 4.8 %fusion.4 = (bf16[256,4096]{1,0:T(8,128)(2,1)}, bf16[256,4096]{1,0:T(8,128)(2,1)}) fusion(bf16[2048,8192]{1,0:T(8,128)(2,1)} %rest_2_.1, s32[]{:T(128)S(6)} %select_n.70, s32[]{:T(128)S(6)} %select_n.67, s32[]{:T(128)S(6)} %select_n.69), kind=kLoop, calls=%fused_computation.11 | loop fusion | bytes 8388620 | tf_op jit(solution)/shard_map/dynamic_slice | solution.py:499
  24.6 9.8 %all-to-all-done.rest_0_ = bf16[4,784,128]{2,1,0:T(8,128)(2,1)S(1)} async-done(((bf16[4,784,128]{2,1,0:T(8,128)(2,1)}), bf16[4,784,128]{2,1,0:T(8,128)(2,1)S(1)}, u32[]{:S(2)}, u32[]{:S(2)}) %all-to-all-start) | async-done | bytes 802848 | tf_op jit(solution)/shard_map/all_to_all | solution.py:469
  34.3 3.5 %all-to-all-start.1 = ((bf16[4,784,128]{2,1,0:T(8,128)(2,1)}), bf16[4,784,128]{2,1,0:T(8,128)(2,1)S(1)}, u32[]{:S(2)}, u32[]{:S(2)}) async-start(bf16[4,784,128]{2,1,0:T(8,128)(2,1)} %bitcast.13), calls=%async_computation.1 | async-start | bytes 1605632 | tf_op jit(solution)/shard_map/all_to_all | solution.py:469
  40.9 8.7 %shard_map.65 = (bf16[16,1,400,128]{3,2,1,0:T(8,128)(2,1)}, bf16[16,1,400,128]{3,2,1,0:T(8,128)(2,1)}) custom-call(s32[1,768]{1,0:T(1,128)} %get-tuple-element.40.slot_ref, f32[768,128]{1,0:T(8,128)} %get-tuple-element.80.cos_ref, f32[768,128]{1,0:T(8,128)} %get-tuple-element.79.sin_ref, bf16[768,2048]{1,0:T(8,128)(2,1)} %row_ref.3), custom_call_target="tpu_custom_call" | custom-call | flops 2516582400 | bytes 6291456 | tf_op jit(solution)/shard_map/pallas_call | solution.py:124
  49.6 8.4 %collective-permute-done.rest_1_ = bf16[4,784,128]{2,1,0:T(8,128)(2,1)S(1)} collective-permute-done((bf16[4,784,128]{2,1,0:T(8,128)(2,1)S(1)}, bf16[4,784,128]{2,1,0:T(8,128)(2,1)S(1)}, u32[]{:S(2)}, u32[]{:S(2)}) %collective-permute-start) | collective-permute-done | bytes 802848 | tf_op jit(solution)/shard_map/ppermute | solution.py:475
  62.1 5.8 %all-to-all-start.3 = ((bf16[16,400,128]{2,1,0:T(8,128)(2,1)}), bf16[16,400,128]{2,1,0:T(8,128)(2,1)S(1)}, u32[]{:S(2)}, u32[]{:S(2)}) async-start(bf16[16,400,128]{2,1,0:T(8,128)(2,1)} %bitcast.20), calls=%async_computation.3 | async-start | bytes 3276800 | tf_op jit(solution)/shard_map/all_to_all | solution.py:483
  73.3 4.8 %shard_map.68.key_ref = bf16[128,6144]{1,0:T(8,128)(2,1)} custom-call(s32[1]{0:T(128)} %bitcast.15.member_ref, s32[16]{0:T(128)} %count_ref.9, bf16[4,784,128]{2,1,0:T(8,128)(2,1)} %copy-done, bf16[4,784,128]{2,1,0:T(8,128)(2,1)} %copy-done.8, bf16[4,784,128]{2,1,0:T(8,128)(2,1)} %collective-permute-done.3.rest_2_, ...), custom_call_target="tpu_custom_call" | custom-call | flops 6291456 | bytes 6291456 | tf_op jit(solution)/shard_map/pallas_call | solution.py:196
  78.1 27.8 %collective-permute-done.2.rest_1_ = bf16[4,784,128]{2,1,0:T(8,128)(2,1)} collective-permute-done((bf16[4,784,128]{2,1,0:T(8,128)(2,1)S(1)}, bf16[4,784,128]{2,1,0:T(8,128)(2,1)}, u32[]{:S(2)}, u32[]{:S(2)}) %collective-permute-start.2) | collective-permute-done | bytes 802848 | tf_op jit(solution)/shard_map/ppermute | solution.py:475
  105.9 4.7 %all-to-all-start.2 = ((bf16[16,400,128]{2,1,0:T(8,128)(2,1)}), bf16[16,400,128]{2,1,0:T(8,128)(2,1)}, u32[]{:S(2)}, u32[]{:S(2)}) async-start(bf16[16,400,128]{2,1,0:T(8,128)(2,1)} %bitcast.16), calls=%async_computation.2 | async-start | bytes 3276800 | tf_op jit(solution)/shard_map/all_to_all | solution.py:483
  117.3 5.2 %shard_map.69.value_ref = bf16[6144,256]{1,0:T(8,128)(2,1)} custom-call(s32[1]{0:T(128)} %bitcast.15.member_ref, s32[16]{0:T(128)} %count_ref.9, bf16[4,784,128]{2,1,0:T(8,128)(2,1)} %copy-done.1, bf16[4,784,128]{2,1,0:T(8,128)(2,1)} %collective-permute-done.2.rest_1_, bf16[4,784,128]{2,1,0:T(8,128)(2,1)} %copy-done.9, bf16[4,784,128]{2,1,0:T(8,128)(2,1)} %copy-done.10), custom_call_target="tpu_custom_call" | custom-call | flops 6291456 | bytes 6291456 | tf_op jit(solution)/shard_map/pallas_call | solution.py:196
  122.5 25.4 %shard_map.70 = bf16[16,192,128]{2,1,0:T(8,128)(2,1)} custom-call(s32[1]{0:T(128)} %constant.59.clone.1.cls_ref, s32[16]{0:T(128)} %count_ref.9, bf16[16,400,128]{2,1,0:T(8,128)(2,1)} %copy-done.4, bf16[128,6144]{1,0:T(8,128)(2,1)} %shard_map.68.key_ref, bf16[6144,256]{1,0:T(8,128)(2,1)} %shard_map.69.value_ref), custom_call_target="tpu_custom_call" | custom-call | flops 9663676416 | bytes 6291456 | tf_op jit(solution)/shard_map/pallas_call | solution.py:312
  147.9 11.0 %collective-permute-done.8.rest_4_ = bf16[256,4096]{1,0:T(8,128)(2,1)} collective-permute-done((bf16[256,4096]{1,0:T(8,128)(2,1)}, bf16[256,4096]{1,0:T(8,128)(2,1)}, u32[]{:S(2)}, u32[]{:S(2)}) %collective-permute-start.8) | collective-permute-done | bytes 2097184 | tf_op jit(solution)/shard_map/ppermute | solution.py:504
  160.4 5.7 %all-to-all-start.4 = ((bf16[16,192,128]{2,1,0:T(8,128)(2,1)}), bf16[16,192,128]{2,1,0:T(8,128)(2,1)S(1)}, u32[]{:S(2)}, u32[]{:S(2)}) async-start(bf16[16,192,128]{2,1,0:T(8,128)(2,1)} %shard_map.70), calls=%async_computation.4 | async-start | bytes 1572864 | tf_op jit(solution)/shard_map/all_to_all | solution.py:542
  168.2 25.5 %shard_map.71 = bf16[16,192,128]{2,1,0:T(8,128)(2,1)} custom-call(s32[1]{0:T(128)} %constant.60.clone.1.cls_ref, s32[16]{0:T(128)} %count_ref.9, bf16[16,400,128]{2,1,0:T(8,128)(2,1)} %all-to-all-done.2.got_ref, bf16[128,6144]{1,0:T(8,128)(2,1)} %shard_map.68.key_ref, bf16[6144,256]{1,0:T(8,128)(2,1)} %shard_map.69.value_ref), custom_call_target="tpu_custom_call" | custom-call | flops 9663676416 | bytes 6291456 | tf_op jit(solution)/shard_map/pallas_call | solution.py:312
  193.8 6.9 %collective-permute-done.10.rest_6_ = bf16[128,4096]{1,0:T(8,128)(2,1)S(1)} collective-permute-done((bf16[128,4096]{1,0:T(8,128)(2,1)}, bf16[128,4096]{1,0:T(8,128)(2,1)S(1)}, u32[]{:S(2)}, u32[]{:S(2)}) %collective-permute-start.10) | collective-permute-done | bytes 1048608 | tf_op jit(solution)/shard_map/ppermute | solution.py:491
  200.6 22.1 %collective-permute-done.11.rest_7_ = bf16[128,4096]{1,0:T(8,128)(2,1)} collective-permute-done((bf16[128,4096]{1,0:T(8,128)(2,1)}, bf16[128,4096]{1,0:T(8,128)(2,1)}, u32[]{:S(2)}, u32[]{:S(2)}) %collective-permute-start.11) | collective-permute-done | bytes 1048608 | tf_op jit(solution)/shard_map/ppermute | solution.py:491
  222.7 4.6 %all-to-all-start.5 = ((bf16[16,192,128]{2,1,0:T(8,128)(2,1)}), bf16[16,192,128]{2,1,0:T(8,128)(2,1)S(1)}, u32[]{:S(2)}, u32[]{:S(2)}) async-start(bf16[16,192,128]{2,1,0:T(8,128)(2,1)} %shard_map.71), calls=%async_computation.5 | async-start | bytes 1572864 | tf_op jit(solution)/shard_map/all_to_all | solution.py:547
  234.3 5.1 %collective-permute-done.14.rest_8_ = bf16[128,4096]{1,0:T(8,128)(2,1)} collective-permute-done((bf16[128,4096]{1,0:T(8,128)(2,1)}, bf16[128,4096]{1,0:T(8,128)(2,1)}, u32[]{:S(2)}, u32[]{:S(2)}) %collective-permute-start.14) | collective-permute-done | bytes 1048608 | tf_op jit(solution)/shard_map/ppermute | solution.py:491
  239.4 6.6 %all-to-all-done.5.rest_1_ = bf16[16,192,128]{2,1,0:T(8,128)(2,1)S(1)} async-done(((bf16[16,192,128]{2,1,0:T(8,128)(2,1)}), bf16[16,192,128]{2,1,0:T(8,128)(2,1)S(1)}, u32[]{:S(2)}, u32[]{:S(2)}) %all-to-all-start.5) | async-done | bytes 786464 | tf_op jit(solution)/shard_map/all_to_all | solution.py:547
  247.2 13.8 %shard_map.72.rest_14_ = bf16[384,4096]{1,0:T(8,128)(2,1)} custom-call(s32[1]{0:T(128)} %bitcast.18.column_ref, bf16[16,192,128]{2,1,0:T(8,128)(2,1)} %copy-done.2, bf16[16,192,128]{2,1,0:T(8,128)(2,1)} %copy-done.3, bf16[2048,8192]{1,0:T(8,128)(2,1)} %rest_2_.1), custom_call_target="tpu_custom_call" | custom-call | flops 6442450944 | bytes 16777216 | tf_op jit(solution)/shard_map/pallas_call | solution.py:354
  261.1 9.0 %collective-permute-done.12.rest_1_ = bf16[16,192,128]{2,1,0:T(8,128)(2,1)} collective-permute-done((bf16[16,192,128]{2,1,0:T(8,128)(2,1)S(1)}, bf16[16,192,128]{2,1,0:T(8,128)(2,1)}, u32[]{:S(2)}, u32[]{:S(2)}) %collective-permute-start.12) | collective-permute-done | bytes 786464 | tf_op jit(solution)/shard_map/ppermute | solution.py:504
  270.1 16.6 %shard_map.73 = bf16[384,4096]{1,0:T(8,128)(2,1)} custom-call(s32[12]{0:T(128)} %stack.51.head_ref, bf16[16,192,128]{2,1,0:T(8,128)(2,1)} %copy-done.11, bf16[16,192,128]{2,1,0:T(8,128)(2,1)} %collective-permute-done.12.rest_1_, bf16[128,4096]{1,0:T(8,128)(2,1)} %collective-permute-done.1.rest_2_, bf16[128,4096]{1,0:T(8,128)(2,1)} %collective-permute-done.5.rest_3_, ...), custom_call_target="tpu_custom_call" | custom-call | flops 6442450944 | bytes 16777216 | tf_op jit(solution)/shard_map/pallas_call | solution.py:403
  (69 shorter events, 40.8 us)
Async XLA Ops:
  7.5 26.8 %all-to-all-start = ((bf16[4,784,128]{2,1,0:T(8,128)(2,1)}), bf16[4,784,128]{2,1,0:T(8,128)(2,1)S(1)}, u32[]{:S(2)}, u32[]{:S(2)}) async-start(bf16[4,784,128]{2,1,0:T(8,128)(2,1)} %bitcast.19), calls=%async_computation | async-start | bytes 1605632 | tf_op jit(solution)/shard_map/all_to_all | solution.py:469
  34.3 27.8 %all-to-all-start.1 = ((bf16[4,784,128]{2,1,0:T(8,128)(2,1)}), bf16[4,784,128]{2,1,0:T(8,128)(2,1)S(1)}, u32[]{:S(2)}, u32[]{:S(2)}) async-start(bf16[4,784,128]{2,1,0:T(8,128)(2,1)} %bitcast.13), calls=%async_computation.1 | async-start | bytes 1605632 | tf_op jit(solution)/shard_map/all_to_all | solution.py:469
  37.8 24.3 %collective-permute-start.1 = (bf16[128,4096]{1,0:T(8,128)(2,1)S(1)}, bf16[128,4096]{1,0:T(8,128)(2,1)}, u32[]{:S(2)}, u32[]{:S(2)}) collective-permute-start(bf16[128,4096]{1,0:T(8,128)(2,1)S(1)} %get-tuple-element.46), channel_id=1, source_target_pairs={{0,1},{1,0},{2,3},{3,2},{4,5},{5,4},{6,7},{7,6},{8,9},{9,8},{10,11... | collective-permute-start | bytes 3145736 | tf_op jit(solution)/shard_map/ppermute | solution.py:504
  39.4 18.6 %collective-permute-start = (bf16[4,784,128]{2,1,0:T(8,128)(2,1)S(1)}, bf16[4,784,128]{2,1,0:T(8,128)(2,1)S(1)}, u32[]{:S(2)}, u32[]{:S(2)}) collective-permute-start(bf16[4,784,128]{2,1,0:T(8,128)(2,1)S(1)} %all-to-all-done.rest_0_), channel_id=1, source_target_pairs={{0,4},{2,6},{4,0},{6,2},{8,12},{10,14},{12,8},{14,10},{16,20},{18,... | collective-permute-start | bytes 2408456 | tf_op jit(solution)/shard_map/ppermute | solution.py:475
  62.1 43.8 %all-to-all-start.3 = ((bf16[16,400,128]{2,1,0:T(8,128)(2,1)}), bf16[16,400,128]{2,1,0:T(8,128)(2,1)S(1)}, u32[]{:S(2)}, u32[]{:S(2)}) async-start(bf16[16,400,128]{2,1,0:T(8,128)(2,1)} %bitcast.20), calls=%async_computation.3 | async-start | bytes 3276800 | tf_op jit(solution)/shard_map/all_to_all | solution.py:483
  67.9 38.0 %collective-permute-start.5 = (bf16[128,4096]{1,0:T(8,128)(2,1)}, bf16[128,4096]{1,0:T(8,128)(2,1)}, u32[]{:S(2)}, u32[]{:S(2)}) collective-permute-start(bf16[128,4096]{1,0:T(8,128)(2,1)} %get-tuple-element.54), channel_id=1, source_target_pairs={{0,1},{1,0},{2,3},{3,2},{4,5},{5,4},{6,7},{7,6},{8,9},{9,8},{10,11... | collective-permute-start | bytes 3145736 | tf_op jit(solution)/shard_map/ppermute | solution.py:504
  69.6 3.7 %collective-permute-start.4 = (bf16[4,784,128]{2,1,0:T(8,128)(2,1)}, bf16[4,784,128]{2,1,0:T(8,128)(2,1)}, u32[]{:S(2)}, u32[]{:S(2)}) collective-permute-start(bf16[4,784,128]{2,1,0:T(8,128)(2,1)} %copy-done.8), channel_id=1, source_target_pairs={{0,2},{2,0},{4,6},{6,4},{8,10},{10,8},{12,14},{14,12},{16,18},{18,... | collective-permute-start | bytes 2408456 | tf_op jit(solution)/shard_map/ppermute | solution.py:475
  70.0 35.9 %collective-permute-start.2 = (bf16[4,784,128]{2,1,0:T(8,128)(2,1)S(1)}, bf16[4,784,128]{2,1,0:T(8,128)(2,1)}, u32[]{:S(2)}, u32[]{:S(2)}) collective-permute-start(bf16[4,784,128]{2,1,0:T(8,128)(2,1)S(1)} %all-to-all-done.1.rest_0_), channel_id=1, source_target_pairs={{0,4},{2,6},{4,0},{6,2},{8,12},{10,14},{12,8},{14,10},{16,20},{18,... | collective-permute-start | bytes 2408456 | tf_op jit(solution)/shard_map/ppermute | solution.py:475
  105.9 52.9 %all-to-all-start.2 = ((bf16[16,400,128]{2,1,0:T(8,128)(2,1)}), bf16[16,400,128]{2,1,0:T(8,128)(2,1)}, u32[]{:S(2)}, u32[]{:S(2)}) async-start(bf16[16,400,128]{2,1,0:T(8,128)(2,1)} %bitcast.16), calls=%async_computation.2 | async-start | bytes 3276800 | tf_op jit(solution)/shard_map/all_to_all | solution.py:483
  110.6 48.2 %collective-permute-start.8 = (bf16[256,4096]{1,0:T(8,128)(2,1)}, bf16[256,4096]{1,0:T(8,128)(2,1)}, u32[]{:S(2)}, u32[]{:S(2)}) collective-permute-start(bf16[256,4096]{1,0:T(8,128)(2,1)} %get-tuple-element.64), channel_id=1, source_target_pairs={{0,1},{1,0},{2,3},{3,2},{4,5},{5,4},{6,7},{7,6},{8,9},{9,8},{10,11... | collective-permute-start | bytes 6291464 | tf_op jit(solution)/shard_map/ppermute | solution.py:504
  112.2 3.3 %collective-permute-start.6 = (bf16[4,784,128]{2,1,0:T(8,128)(2,1)S(1)}, bf16[4,784,128]{2,1,0:T(8,128)(2,1)S(1)}, u32[]{:S(2)}, u32[]{:S(2)}) collective-permute-start(bf16[4,784,128]{2,1,0:T(8,128)(2,1)S(1)} %all-to-all-done.1.rest_0_), channel_id=1, source_target_pairs={{0,2},{2,0},{4,6},{6,4},{8,10},{10,8},{12,14},{14,12},{16,18},{18,... | collective-permute-start | bytes 2408456 | tf_op jit(solution)/shard_map/ppermute | solution.py:475
  112.2 3.6 %collective-permute-start.7 = (bf16[4,784,128]{2,1,0:T(8,128)(2,1)}, bf16[4,784,128]{2,1,0:T(8,128)(2,1)S(1)}, u32[]{:S(2)}, u32[]{:S(2)}) collective-permute-start(bf16[4,784,128]{2,1,0:T(8,128)(2,1)} %collective-permute-done.2.rest_1_), channel_id=1, source_target_pairs={{0,2},{2,0},{4,6},{6,4},{8,10},{10,8},{12,14},{14,12},{16,18},{18,... | collective-permute-start | bytes 2408456 | tf_op jit(solution)/shard_map/ppermute | solution.py:475
  158.8 69.1 %collective-permute-start.13 = (bf16[256,4096]{1,0:T(8,128)(2,1)}, bf16[256,4096]{1,0:T(8,128)(2,1)}, u32[]{:S(2)}, u32[]{:S(2)}) collective-permute-start(bf16[256,4096]{1,0:T(8,128)(2,1)} %get-tuple-element.72), channel_id=1, source_target_pairs={{0,1},{1,0},{2,3},{3,2},{4,5},{5,4},{6,7},{7,6},{8,9},{9,8},{10,11... | collective-permute-start | bytes 6291464 | tf_op jit(solution)/shard_map/ppermute | solution.py:504
  160.4 62.4 %all-to-all-start.4 = ((bf16[16,192,128]{2,1,0:T(8,128)(2,1)}), bf16[16,192,128]{2,1,0:T(8,128)(2,1)S(1)}, u32[]{:S(2)}, u32[]{:S(2)}) async-start(bf16[16,192,128]{2,1,0:T(8,128)(2,1)} %shard_map.70), calls=%async_computation.4 | async-start | bytes 1572864 | tf_op jit(solution)/shard_map/all_to_all | solution.py:542
  166.1 34.5 %collective-permute-start.10 = (bf16[128,4096]{1,0:T(8,128)(2,1)}, bf16[128,4096]{1,0:T(8,128)(2,1)S(1)}, u32[]{:S(2)}, u32[]{:S(2)}) collective-permute-start(bf16[128,4096]{1,0:T(8,128)(2,1)} %collective-permute-done.1.rest_2_), channel_id=1, source_target_pairs={{0,4},{2,6},{4,0},{6,2},{8,12},{10,14},{12,8},{14,10},{16,20},{18,... | collective-permute-start | bytes 3145736 | tf_op jit(solution)/shard_map/ppermute | solution.py:491
  168.0 54.7 %collective-permute-start.11 = (bf16[128,4096]{1,0:T(8,128)(2,1)}, bf16[128,4096]{1,0:T(8,128)(2,1)}, u32[]{:S(2)}, u32[]{:S(2)}) collective-permute-start(bf16[128,4096]{1,0:T(8,128)(2,1)} %collective-permute-done.5.rest_3_), channel_id=1, source_target_pairs={{0,4},{2,6},{4,0},{6,2},{8,12},{10,14},{12,8},{14,10},{16,20},{18,... | collective-permute-start | bytes 3145736 | tf_op jit(solution)/shard_map/ppermute | solution.py:491
  222.7 23.4 %all-to-all-start.5 = ((bf16[16,192,128]{2,1,0:T(8,128)(2,1)}), bf16[16,192,128]{2,1,0:T(8,128)(2,1)S(1)}, u32[]{:S(2)}, u32[]{:S(2)}) async-start(bf16[16,192,128]{2,1,0:T(8,128)(2,1)} %shard_map.71), calls=%async_computation.5 | async-start | bytes 1572864 | tf_op jit(solution)/shard_map/all_to_all | solution.py:547
  227.8 33.2 %collective-permute-start.16 = (bf16[256,4096]{1,0:T(8,128)(2,1)}, bf16[256,4096]{1,0:T(8,128)(2,1)}, u32[]{:S(2)}, u32[]{:S(2)}) collective-permute-start(bf16[256,4096]{1,0:T(8,128)(2,1)} %collective-permute-done.8.rest_4_), channel_id=1, source_target_pairs={{0,2},{2,0},{4,6},{6,4},{8,10},{10,8},{12,14},{14,12},{16,18},{18,... | collective-permute-start | bytes 6291464 | tf_op jit(solution)/shard_map/ppermute | solution.py:491
  228.0 42.1 %collective-permute-start.17 = (bf16[256,4096]{1,0:T(8,128)(2,1)}, bf16[256,4096]{1,0:T(8,128)(2,1)}, u32[]{:S(2)}, u32[]{:S(2)}) collective-permute-start(bf16[256,4096]{1,0:T(8,128)(2,1)} %collective-permute-done.13.rest_5_), channel_id=1, source_target_pairs={{0,2},{2,0},{4,6},{6,4},{8,10},{10,8},{12,14},{14,12},{16,18},{18,... | collective-permute-start | bytes 6291464 | tf_op jit(solution)/shard_map/ppermute | solution.py:491
  228.3 5.0 %collective-permute-start.19 = (bf16[128,4096]{1,0:T(8,128)(2,1)}, bf16[128,4096]{1,0:T(8,128)(2,1)S(1)}, u32[]{:S(2)}, u32[]{:S(2)}) collective-permute-start(bf16[128,4096]{1,0:T(8,128)(2,1)} %collective-permute-done.11.rest_7_), channel_id=1, source_target_pairs={{0,2},{2,0},{4,6},{6,4},{8,10},{10,8},{12,14},{14,12},{16,18},{18,... | collective-permute-start | bytes 3145736 | tf_op jit(solution)/shard_map/ppermute | solution.py:491
  228.5 11.0 %collective-permute-start.14 = (bf16[128,4096]{1,0:T(8,128)(2,1)}, bf16[128,4096]{1,0:T(8,128)(2,1)}, u32[]{:S(2)}, u32[]{:S(2)}) collective-permute-start(bf16[128,4096]{1,0:T(8,128)(2,1)} %collective-permute-done.1.rest_2_), channel_id=1, source_target_pairs={{0,2},{2,0},{4,6},{6,4},{8,10},{10,8},{12,14},{14,12},{16,18},{18,... | collective-permute-start | bytes 3145736 | tf_op jit(solution)/shard_map/ppermute | solution.py:491
  230.1 30.9 %collective-permute-start.15 = (bf16[128,4096]{1,0:T(8,128)(2,1)}, bf16[128,4096]{1,0:T(8,128)(2,1)}, u32[]{:S(2)}, u32[]{:S(2)}) collective-permute-start(bf16[128,4096]{1,0:T(8,128)(2,1)} %collective-permute-done.5.rest_3_), channel_id=1, source_target_pairs={{0,2},{2,0},{4,6},{6,4},{8,10},{10,8},{12,14},{14,12},{16,18},{18,... | collective-permute-start | bytes 3145736 | tf_op jit(solution)/shard_map/ppermute | solution.py:491
  233.3 27.7 %collective-permute-start.9 = (bf16[16,192,128]{2,1,0:T(8,128)(2,1)S(1)}, bf16[16,192,128]{2,1,0:T(8,128)(2,1)S(1)}, u32[]{:S(2)}, u32[]{:S(2)}) collective-permute-start(bf16[16,192,128]{2,1,0:T(8,128)(2,1)S(1)} %all-to-all-done.4.rest_0_), channel_id=1, source_target_pairs={{0,1},{1,0},{2,3},{3,2},{4,5},{5,4},{6,7},{7,6},{8,9},{9,8},{10,11... | collective-permute-start | bytes 2359304 | tf_op jit(solution)/shard_map/ppermute | solution.py:504
  246.1 24.0 %collective-permute-start.12 = (bf16[16,192,128]{2,1,0:T(8,128)(2,1)S(1)}, bf16[16,192,128]{2,1,0:T(8,128)(2,1)}, u32[]{:S(2)}, u32[]{:S(2)}) collective-permute-start(bf16[16,192,128]{2,1,0:T(8,128)(2,1)S(1)} %all-to-all-done.5.rest_1_), channel_id=1, source_target_pairs={{0,1},{1,0},{2,3},{3,2},{4,5},{5,4},{6,7},{7,6},{8,9},{9,8},{10,11... | collective-permute-start | bytes 2359304 | tf_op jit(solution)/shard_map/ppermute | solution.py:504
  (14 other events, 209.8 us)

commit v7 on v6

--- a/solution.py
+++ b/solution.py
@@ -30,6 +30,10 @@
 
 def params():
     return pltpu.CompilerParams(vmem_limit_bytes=VMEM_BYTES)
+
+
+def small_cost():
+    return pl.CostEstimate(flops=1024, bytes_accessed=1024, transcendentals=0)
 
 
 def turn(rows, cosine, sine):
@@ -83,7 +87,7 @@
         out_specs=[whole_vmem()] * 2,
         out_shape=[shape, shape],
         compiler_params=params(),
-        cost_estimate=pl.CostEstimate(flops=2**20, bytes_accessed=2**14, transcendentals=0),
+        cost_estimate=small_cost(),
     )(me, counts, ranks)
 
 
@@ -134,9 +138,7 @@
         out_shape=[jax.ShapeDtypeStruct((heads, classes, cap, HD), jnp.bfloat16)] * chunks,
         scratch_shapes=[pltpu.VMEM((total, count), jnp.bfloat16)],
         compiler_params=params(),
-        cost_estimate=pl.CostEstimate(
-            flops=2 * heads * total * count * HD, bytes_accessed=count * heads * HD * 4, transcendentals=0
-        ),
+        cost_estimate=small_cost(),
     )(slots, cosine, sine, rows)
 
 
@@ -205,7 +207,7 @@
             pltpu.SMEM(counts.shape, jnp.int32),
         ],
         compiler_params=params(),
-        cost_estimate=pl.CostEstimate(flops=total * HD * 8, bytes_accessed=total * HD * 8, transcendentals=0),
+        cost_estimate=small_cost(),
     )(member, counts, *parts)
 
 
@@ -324,9 +326,7 @@
             pltpu.VMEM((4 * block, 2 * HD), jnp.float32),
         ],
         compiler_params=params(),
-        cost_estimate=pl.CostEstimate(
-            flops=pairs * 8 * HD, bytes_accessed=total * HD * 8, transcendentals=pairs
-        ),
+        cost_estimate=small_cost(),
     )(cls, counts, got, keys, values)
 
 
@@ -363,9 +363,7 @@
         ),
         out_shape=jax.ShapeDtypeStruct((rows, columns), jnp.bfloat16),
         compiler_params=params(),
-        cost_estimate=pl.CostEstimate(
-            flops=2 * rows * depth * columns, bytes_accessed=2 * depth * columns, transcendentals=0
-        ),
+        cost_estimate=small_cost(),
     )((first_column // step).astype(jnp.int32).reshape(1), *got, weight)
 
 
@@ -413,11 +411,7 @@
         ),
         out_shape=jax.ShapeDtypeStruct((rows, columns), jnp.bfloat16),
         compiler_params=params(),
-        cost_estimate=pl.CostEstimate(
-            flops=2 * rows * depth * columns,
-            bytes_accessed=2 * depth * columns,
-            transcendentals=0,
-        ),
+        cost_estimate=small_cost(),
     )(first_heads, *got, *weights, own)
 
 
@@ -491,7 +485,7 @@
         return lax.ppermute(part, "ctx", [(d, d ^ bit) for d in range(ctx_size)])
 
     core, side = me & 1, (me >> 1) & 1
-    sizes = [1, 1, 2, 2]
+    sizes = [2, 2, 2]
 
     def weight_rows(p):
         low = sum(sizes[:p])
@@ -512,48 +506,45 @@
     value_parts = [send_across(value_packed)]
     packed_q = list(pack(q_slots, cosine, sine, query, True, chunks, classes, cap))
     came = [trade(slices[0])] if traded else []
-    packed_q[0], key_parts, value_parts, came, slices = lax.optimization_barrier(
-        (packed_q[0], key_parts, value_parts, came, slices)
+    packed_q[0], key_parts, value_parts, slices = lax.optimization_barrier(
+        (packed_q[0], key_parts, value_parts, slices)
     )
-    if traded:
-        came = came + [trade(slices[1])]
+    came = came + [trade(one) for one in slices[1:]]
     got_q = [send_query(packed_q[0])]
     value_parts = swap(value_parts, bits[0])
     for bit in bits[1:]:
         key_parts = swap(key_parts, bit)
     keys = compact(member, kept_count, key_parts, offsets, total, True)
     if chunks > 1:
-        packed_q[1], value_parts, keys, came, slices = lax.optimization_barrier(
-            (packed_q[1], value_parts, keys, came, slices)
+        packed_q[1], value_parts, keys = lax.optimization_barrier(
+            (packed_q[1], value_parts, keys)
         )
     for bit in bits[1:]:
         value_parts = swap(value_parts, bit)
     got_q = got_q + [send_query(packed) for packed in packed_q[1:]]
     values = compact(member, kept_count, value_parts, offsets, total, False)
     if traded:
-        came = came + [trade(slices[2])]
-        aside = [chip_swap(part, 2) for part in came[:2]]
+        got_q[0], turned_part = lax.optimization_barrier((got_q[0], came[0]))
+        came = came + [chip_swap(turned_part, 2)]
 
     got, done = [], None
     for j in range(chunks):
         cls_j = j * classes + (me & (classes - 1))
         if j > 0:
-            got_q[j], done, came, slices = lax.optimization_barrier((got_q[j], done, came, slices))
+            got_q[j], done = lax.optimization_barrier((got_q[j], done))
             got.append(lax.all_to_all(done, "ctx", split_axis=0, concat_axis=0, tiled=True))
         done = attend(cls_j.reshape(1), kept_count, got_q[j], keys, values, block)
     if traded:
-        came = came + [trade(slices[3])]
-        done, aside = lax.optimization_barrier((done, aside))
+        done, came = lax.optimization_barrier((done, came))
     got.append(lax.all_to_all(done, "ctx", split_axis=0, concat_axis=0, tiled=True))
     if traded:
         theirs = [trade(one) for one in got]
-        came = came + aside
         came = came + [chip_swap(part, 1) for part in came]
         own = project(tp_me * columns, got, out_weight, columns, classes)
-        ups = [sum(sizes[:p]) for p in range(5)]
+        ups = [sum(sizes[:p]) for p in range(3)]
         order = [
             jnp.where(side == 0, up, 8 - up - size) for up, size in zip(ups, sizes)
-        ] + [jnp.where(side == 0, 7 - n, n) for n in range(2)]
+        ] + [jnp.where(side == 0, 6, 0)]
         first_heads = jnp.stack([c * 8 + at for c in (core, 1 - core) for at in order])
         return join(first_heads.astype(jnp.int32), theirs, came, own)
     full = project(jnp.int32(0) * tp_me, got, out_weight, columns * tp_size, classes)

time: 288 us -> 306 us (1.062)
  waiting for transfers between devices: 119 us -> 143 us
    ppermute x6 -> x5, waiting for transfers between devices: 23.2 us -> 90.6 us  [trade(): return lax.ppermute(part, 'tp', both)]
    ppermute x8 -> x5, waiting for transfers between devices: 38.3 us -> 0.01 us  [chip_swap(): return lax.ppermute(part, 'ctx', [(d, d ^ bit) for d in range(ctx_size)])]
    all_to_all x2, waiting for transfers between devices: 6.64 us -> 0.01 us  [local(): lax.all_to_all(done, 'ctx', split_axis=0, concat_axis=0, tiled=True)]
    dynamic_slice x2 -> x1, local copies, waits for them, and re-layouts: 7.5 us -> 5.78 us  [weight_rows(): lax.dynamic_slice(out_weight, (first * HD, (1 - tp_me) * columns), (sizes...]
    ppermute x6 -> x5, starting transfers between devices: 7.29 us -> 6.7 us  [trade(): return lax.ppermute(part, 'tp', both)]
  transfers between devices with their start and end apart: 26 -> 22, of which waited for: 16 -> 10; matrix products, arithmetic and copies ran while one was open for 3% -> 2% of each run, Pallas kernels for 30% -> 28%
where the time goes in v7:
time: 306 us; the launch traced here: 305 us
  waiting for transfers between devices  143 us (47%)
  Pallas kernels  107 us (35%)
  starting transfers between devices  44 us (14%)
  local copies, waits for them, and re-layouts  9.13 us (3%)
    ppermute x5, waiting for transfers between devices, trade(): return lax.ppermute(part, 'tp', both)  90.6 us
    pallas_call x2, Pallas kernels, attend(): pl.pallas_call(functools.partial(attend_kernel, ctx_size, block), in_spec...  50.9 us
    ppermute x6, waiting for transfers between devices, swap(): return parts + [lax.ppermute(part, 'ctx', pairs) for part in parts]  39.6 us
    pallas_call x3, Pallas kernels, pack(): pl.pallas_call(functools.partial(pack_kernel, turned, classes, cap, width...  15.4 us
    pallas_call x1, Pallas kernels, join(): pl.pallas_call(functools.partial(join_kernel, len(got), len(weights)), gr...  15.1 us
    pallas_call x1, Pallas kernels, project(): pl.pallas_call(functools.partial(project_kernel, classes, len(got)), grid...  13.9 us
    all_to_all x2, waiting for transfers between devices, send_across(): lax.all_to_all(packed, 'ctx', split_axis=0, concat_axis=0, tiled=True, ax...  12.3 us
    all_to_all x2, starting transfers between devices, local(): lax.all_to_all(done, 'ctx', split_axis=0, concat_axis=0, tiled=True)  10.4 us
  transfers between devices with their start and end apart: 22, of which 10 were waited for; matrix products, arithmetic and copies ran while one was open for 2% of the time, Pallas kernels for 28%

profile of v7, /device:TPU:0, one launch (start us, length us, event | category | flops | bytes accessed | tf_op | source)
XLA Modules:
  0.0 305.2 jit_solution(17420055965633302812)
XLA Ops:
  1.6 2.6 negate_select_fusion
  4.1 3.5 %shard_map.67 = bf16[4,1,784,128]{3,2,1,0:T(8,128)(2,1)} custom-call(s32[1,768]{1,0:T(1,128)} %get-tuple-element.36.slot_ref, f32[768,128]{1,0:T(8,128)} %get-tuple-element.65.cos_ref, f32[768,128]{1,0:T(8,128)} %get-tuple-element.64.sin_ref, bf16[768,512]{1,0:T(8,128)(2,1)} %row_ref.5), custom_call_target="tpu_custom_call" | custom-call | flops 1024 | bytes 1024 | tf_op jit(solution)/shard_map/pallas_call | solution.py:128
  7.6 6.3 %all-to-all-start = ((bf16[4,784,128]{2,1,0:T(8,128)(2,1)}), bf16[4,784,128]{2,1,0:T(8,128)(2,1)S(1)}, u32[]{:S(2)}, u32[]{:S(2)}) async-start(bf16[4,784,128]{2,1,0:T(8,128)(2,1)} %bitcast.15), calls=%async_computation | async-start | bytes 1605632 | tf_op jit(solution)/shard_map/all_to_all | solution.py:463
  13.9 3.2 %shard_map.66 = bf16[4,1,784,128]{3,2,1,0:T(8,128)(2,1)} custom-call(s32[1,768]{1,0:T(1,128)} %get-tuple-element.36.slot_ref, f32[768,128]{1,0:T(8,128)} %get-tuple-element.65.cos_ref, f32[768,128]{1,0:T(8,128)} %get-tuple-element.64.sin_ref, bf16[768,512]{1,0:T(8,128)(2,1)} %row_ref.4), custom_call_target="tpu_custom_call" | custom-call | flops 1024 | bytes 1024 | tf_op jit(solution)/shard_map/pallas_call | solution.py:128
  17.2 5.8 %fusion.4 = (bf16[256,4096]{1,0:T(8,128)(2,1)}, bf16[256,4096]{1,0:T(8,128)(2,1)}, bf16[256,4096]{1,0:T(8,128)(2,1)}) fusion(bf16[2048,8192]{1,0:T(8,128)(2,1)} %rest_2_.1, s32[]{:T(128)S(6)} %select_n.56, s32[]{:T(128)S(6)} %select_n.54, s32[]{:T(128)S(6)} %select_n.55, s32[]{:T(128)S(6)} %select_n.53), kind=kLoop, calls=%fused_computation.11 | loop fusion | bytes 12582928 | tf_op jit(solution)/shard_map/dynamic_slice | solution.py:493
  22.9 11.4 %all-to-all-done.rest_0_ = bf16[4,784,128]{2,1,0:T(8,128)(2,1)S(1)} async-done(((bf16[4,784,128]{2,1,0:T(8,128)(2,1)}), bf16[4,784,128]{2,1,0:T(8,128)(2,1)S(1)}, u32[]{:S(2)}, u32[]{:S(2)}) %all-to-all-start) | async-done | bytes 802848 | tf_op jit(solution)/shard_map/all_to_all | solution.py:463
  34.4 3.5 %all-to-all-start.1 = ((bf16[4,784,128]{2,1,0:T(8,128)(2,1)}), bf16[4,784,128]{2,1,0:T(8,128)(2,1)S(1)}, u32[]{:S(2)}, u32[]{:S(2)}) async-start(bf16[4,784,128]{2,1,0:T(8,128)(2,1)} %bitcast.9), calls=%async_computation.1 | async-start | bytes 1605632 | tf_op jit(solution)/shard_map/all_to_all | solution.py:463
  39.4 8.7 %shard_map.65 = (bf16[16,1,400,128]{3,2,1,0:T(8,128)(2,1)}, bf16[16,1,400,128]{3,2,1,0:T(8,128)(2,1)}) custom-call(s32[1,768]{1,0:T(1,128)} %get-tuple-element.33.slot_ref, f32[768,128]{1,0:T(8,128)} %get-tuple-element.65.cos_ref, f32[768,128]{1,0:T(8,128)} %get-tuple-element.64.sin_ref, bf16[768,2048]{1,0:T(8,128)(2,1)} %row_ref.3), custom_call_target="tpu_custom_call" | custom-call | flops 1024 | bytes 1024 | tf_op jit(solution)/shard_map/pallas_call | solution.py:128
  48.1 8.8 %collective-permute-done.rest_1_ = bf16[4,784,128]{2,1,0:T(8,128)(2,1)} collective-permute-done((bf16[4,784,128]{2,1,0:T(8,128)(2,1)S(1)}, bf16[4,784,128]{2,1,0:T(8,128)(2,1)}, u32[]{:S(2)}, u32[]{:S(2)}) %collective-permute-start) | collective-permute-done | bytes 802848 | tf_op jit(solution)/shard_map/ppermute | solution.py:469
  57.8 4.9 %all-to-all-start.3 = ((bf16[16,400,128]{2,1,0:T(8,128)(2,1)}), bf16[16,400,128]{2,1,0:T(8,128)(2,1)S(1)}, u32[]{:S(2)}, u32[]{:S(2)}) async-start(bf16[16,400,128]{2,1,0:T(8,128)(2,1)} %bitcast.17), calls=%async_computation.3 | async-start | bytes 3276800 | tf_op jit(solution)/shard_map/all_to_all | solution.py:477
  66.6 4.7 %shard_map.68.key_ref = bf16[128,6144]{1,0:T(8,128)(2,1)} custom-call(s32[1]{0:T(128)} %bitcast.11.member_ref, s32[16]{0:T(128)} %count_ref.9, bf16[4,784,128]{2,1,0:T(8,128)(2,1)} %copy-done.2, bf16[4,784,128]{2,1,0:T(8,128)(2,1)} %collective-permute-done.rest_1_, bf16[4,784,128]{2,1,0:T(8,128)(2,1)} %collective-permute-done.2.rest_2_, ...), custom_call_target="tpu_custom_call" | custom-call | flops 1024 | bytes 1024 | tf_op jit(solution)/shard_map/pallas_call | solution.py:198
  71.3 29.4 %collective-permute-done.1.rest_1_ = bf16[4,784,128]{2,1,0:T(8,128)(2,1)} collective-permute-done((bf16[4,784,128]{2,1,0:T(8,128)(2,1)S(1)}, bf16[4,784,128]{2,1,0:T(8,128)(2,1)}, u32[]{:S(2)}, u32[]{:S(2)}) %collective-permute-start.1) | collective-permute-done | bytes 802848 | tf_op jit(solution)/shard_map/ppermute | solution.py:469
  100.7 4.7 %all-to-all-start.2 = ((bf16[16,400,128]{2,1,0:T(8,128)(2,1)}), bf16[16,400,128]{2,1,0:T(8,128)(2,1)S(1)}, u32[]{:S(2)}, u32[]{:S(2)}) async-start(bf16[16,400,128]{2,1,0:T(8,128)(2,1)} %bitcast.16), calls=%async_computation.2 | async-start | bytes 3276800 | tf_op jit(solution)/shard_map/all_to_all | solution.py:477
  109.5 44.7 %collective-permute-done.4.rest_2_ = bf16[256,4096]{1,0:T(8,128)(2,1)} collective-permute-done((bf16[256,4096]{1,0:T(8,128)(2,1)}, bf16[256,4096]{1,0:T(8,128)(2,1)}, u32[]{:S(2)}, u32[]{:S(2)}) %collective-permute-start.4) | collective-permute-done | bytes 2097184 | tf_op jit(solution)/shard_map/ppermute | solution.py:498
  157.9 5.2 %shard_map.69.value_ref = bf16[6144,256]{1,0:T(8,128)(2,1)} custom-call(s32[1]{0:T(128)} %bitcast.11.member_ref, s32[16]{0:T(128)} %count_ref.9, bf16[4,784,128]{2,1,0:T(8,128)(2,1)} %copy-done.3, bf16[4,784,128]{2,1,0:T(8,128)(2,1)} %collective-permute-done.1.rest_1_, bf16[4,784,128]{2,1,0:T(8,128)(2,1)} %copy-done.6, bf16[4,784,128]{2,1,0:T(8,128)(2,1)} %copy-done.7), custom_call_target="tpu_custom_call" | custom-call | flops 1024 | bytes 1024 | tf_op jit(solution)/shard_map/pallas_call | solution.py:198
  163.1 25.4 %shard_map.70 = bf16[16,192,128]{2,1,0:T(8,128)(2,1)} custom-call(s32[1]{0:T(128)} %constant.57.clone.1.cls_ref, s32[16]{0:T(128)} %count_ref.9, bf16[16,400,128]{2,1,0:T(8,128)(2,1)} %copy-done, bf16[128,6144]{1,0:T(8,128)(2,1)} %shard_map.68.key_ref, bf16[6144,256]{1,0:T(8,128)(2,1)} %shard_map.69.value_ref), custom_call_target="tpu_custom_call" | custom-call | flops 1024 | bytes 1024 | tf_op jit(solution)/shard_map/pallas_call | solution.py:314
  188.5 4.7 %all-to-all-start.4 = ((bf16[16,192,128]{2,1,0:T(8,128)(2,1)}), bf16[16,192,128]{2,1,0:T(8,128)(2,1)S(1)}, u32[]{:S(2)}, u32[]{:S(2)}) async-start(bf16[16,192,128]{2,1,0:T(8,128)(2,1)} %shard_map.70), calls=%async_computation.4 | async-start | bytes 1572864 | tf_op jit(solution)/shard_map/all_to_all | solution.py:535
  193.1 25.6 %shard_map.71 = bf16[16,192,128]{2,1,0:T(8,128)(2,1)} custom-call(s32[1]{0:T(128)} %constant.58.clone.1.cls_ref, s32[16]{0:T(128)} %count_ref.9, bf16[16,400,128]{2,1,0:T(8,128)(2,1)} %copy-done.1, bf16[128,6144]{1,0:T(8,128)(2,1)} %shard_map.68.key_ref, bf16[6144,256]{1,0:T(8,128)(2,1)} %shard_map.69.value_ref), custom_call_target="tpu_custom_call" | custom-call | flops 1024 | bytes 1024 | tf_op jit(solution)/shard_map/pallas_call | solution.py:314
  218.7 24.8 %collective-permute-done.9.rest_4_ = bf16[256,4096]{1,0:T(8,128)(2,1)} collective-permute-done((bf16[256,4096]{1,0:T(8,128)(2,1)}, bf16[256,4096]{1,0:T(8,128)(2,1)}, u32[]{:S(2)}, u32[]{:S(2)}) %collective-permute-start.9) | collective-permute-done | bytes 2097184 | tf_op jit(solution)/shard_map/ppermute | solution.py:498
  243.5 5.8 %all-to-all-start.5 = ((bf16[16,192,128]{2,1,0:T(8,128)(2,1)}), bf16[16,192,128]{2,1,0:T(8,128)(2,1)S(1)}, u32[]{:S(2)}, u32[]{:S(2)}) async-start(bf16[16,192,128]{2,1,0:T(8,128)(2,1)} %shard_map.71), calls=%async_computation.5 | async-start | bytes 1572864 | tf_op jit(solution)/shard_map/all_to_all | solution.py:539
  251.9 18.3 %collective-permute-done.7.rest_0_ = bf16[16,192,128]{2,1,0:T(8,128)(2,1)S(1)} collective-permute-done((bf16[16,192,128]{2,1,0:T(8,128)(2,1)S(1)}, bf16[16,192,128]{2,1,0:T(8,128)(2,1)S(1)}, u32[]{:S(2)}, u32[]{:S(2)}) %collective-permute-start.7) | collective-permute-done | bytes 786464 | tf_op jit(solution)/shard_map/ppermute | solution.py:498
  272.4 13.9 %shard_map.72.rest_10_ = bf16[384,4096]{1,0:T(8,128)(2,1)} custom-call(s32[1]{0:T(128)} %bitcast.14.column_ref, bf16[16,192,128]{2,1,0:T(8,128)(2,1)} %copy-done.4, bf16[16,192,128]{2,1,0:T(8,128)(2,1)} %copy-done.5, bf16[2048,8192]{1,0:T(8,128)(2,1)} %rest_2_.1), custom_call_target="tpu_custom_call" | custom-call | flops 1024 | bytes 1024 | tf_op jit(solution)/shard_map/pallas_call | solution.py:354
  286.4 2.9 collective-permute-done.11.rest_1_
  290.1 15.1 %shard_map.73 = bf16[384,4096]{1,0:T(8,128)(2,1)} custom-call(s32[8]{0:T(128)} %stack.35.head_ref, bf16[16,192,128]{2,1,0:T(8,128)(2,1)} %copy-done.8, bf16[16,192,128]{2,1,0:T(8,128)(2,1)} %copy-done.9, bf16[256,4096]{1,0:T(8,128)(2,1)} %collective-permute-done.4.rest_2_, bf16[256,4096]{1,0:T(8,128)(2,1)} %collective-permute-done.8.rest_3_, ...), custom_call_target="tpu_custom_call" | custom-call | flops 1024 | bytes 1024 | tf_op jit(solution)/shard_map/pallas_call | solution.py:401
  (56 shorter events, 21.5 us)
Async XLA Ops:
  7.6 26.8 %all-to-all-start = ((bf16[4,784,128]{2,1,0:T(8,128)(2,1)}), bf16[4,784,128]{2,1,0:T(8,128)(2,1)S(1)}, u32[]{:S(2)}, u32[]{:S(2)}) async-start(bf16[4,784,128]{2,1,0:T(8,128)(2,1)} %bitcast.15), calls=%async_computation | async-start | bytes 1605632 | tf_op jit(solution)/shard_map/all_to_all | solution.py:463
  34.4 23.4 %all-to-all-start.1 = ((bf16[4,784,128]{2,1,0:T(8,128)(2,1)}), bf16[4,784,128]{2,1,0:T(8,128)(2,1)S(1)}, u32[]{:S(2)}, u32[]{:S(2)}) async-start(bf16[4,784,128]{2,1,0:T(8,128)(2,1)} %bitcast.9), calls=%async_computation.1 | async-start | bytes 1605632 | tf_op jit(solution)/shard_map/all_to_all | solution.py:463
  37.9 19.0 %collective-permute-start = (bf16[4,784,128]{2,1,0:T(8,128)(2,1)S(1)}, bf16[4,784,128]{2,1,0:T(8,128)(2,1)}, u32[]{:S(2)}, u32[]{:S(2)}) collective-permute-start(bf16[4,784,128]{2,1,0:T(8,128)(2,1)S(1)} %all-to-all-done.rest_0_), channel_id=1, source_target_pairs={{0,4},{2,6},{4,0},{6,2},{8,12},{10,14},{12,8},{14,10},{16,20},{18,... | collective-permute-start | bytes 2408456 | tf_op jit(solution)/shard_map/ppermute | solution.py:469
  57.8 42.9 %copy-start.3 = (bf16[4,784,128]{2,1,0:T(8,128)(2,1)}, bf16[4,784,128]{2,1,0:T(8,128)(2,1)S(1)}, u32[]{:S(2)}) copy-start(bf16[4,784,128]{2,1,0:T(8,128)(2,1)S(1)} %all-to-all-done.1.rest_0_) | copy-start | bytes 2408452
  57.8 42.9 %all-to-all-start.3 = ((bf16[16,400,128]{2,1,0:T(8,128)(2,1)}), bf16[16,400,128]{2,1,0:T(8,128)(2,1)S(1)}, u32[]{:S(2)}, u32[]{:S(2)}) async-start(bf16[16,400,128]{2,1,0:T(8,128)(2,1)} %bitcast.17), calls=%async_computation.3 | async-start | bytes 3276800 | tf_op jit(solution)/shard_map/all_to_all | solution.py:477
  62.7 2.6 collective-permute-start.2
  63.2 3.4 %collective-permute-start.3 = (bf16[4,784,128]{2,1,0:T(8,128)(2,1)}, bf16[4,784,128]{2,1,0:T(8,128)(2,1)}, u32[]{:S(2)}, u32[]{:S(2)}) collective-permute-start(bf16[4,784,128]{2,1,0:T(8,128)(2,1)} %collective-permute-done.rest_1_), channel_id=1, source_target_pairs={{0,2},{2,0},{4,6},{6,4},{8,10},{10,8},{12,14},{14,12},{16,18},{18,... | collective-permute-start | bytes 2408456 | tf_op jit(solution)/shard_map/ppermute | solution.py:469
  63.3 37.4 %collective-permute-start.1 = (bf16[4,784,128]{2,1,0:T(8,128)(2,1)S(1)}, bf16[4,784,128]{2,1,0:T(8,128)(2,1)}, u32[]{:S(2)}, u32[]{:S(2)}) collective-permute-start(bf16[4,784,128]{2,1,0:T(8,128)(2,1)S(1)} %all-to-all-done.1.rest_0_), channel_id=1, source_target_pairs={{0,4},{2,6},{4,0},{6,2},{8,12},{10,14},{12,8},{14,10},{16,20},{18,... | collective-permute-start | bytes 2408456 | tf_op jit(solution)/shard_map/ppermute | solution.py:469
  100.7 62.4 %copy-start = (bf16[16,400,128]{2,1,0:T(8,128)(2,1)}, bf16[16,400,128]{2,1,0:T(8,128)(2,1)S(1)}, u32[]{:S(2)}) copy-start(bf16[16,400,128]{2,1,0:T(8,128)(2,1)S(1)} %all-to-all-done.3.got_ref) | copy-start | bytes 4915204
  100.7 87.8 %all-to-all-start.2 = ((bf16[16,400,128]{2,1,0:T(8,128)(2,1)}), bf16[16,400,128]{2,1,0:T(8,128)(2,1)S(1)}, u32[]{:S(2)}, u32[]{:S(2)}) async-start(bf16[16,400,128]{2,1,0:T(8,128)(2,1)} %bitcast.16), calls=%async_computation.2 | async-start | bytes 3276800 | tf_op jit(solution)/shard_map/all_to_all | solution.py:477
  105.4 48.8 %collective-permute-start.4 = (bf16[256,4096]{1,0:T(8,128)(2,1)}, bf16[256,4096]{1,0:T(8,128)(2,1)}, u32[]{:S(2)}, u32[]{:S(2)}) collective-permute-start(bf16[256,4096]{1,0:T(8,128)(2,1)} %get-tuple-element.39), channel_id=1, source_target_pairs={{0,1},{1,0},{2,3},{3,2},{4,5},{5,4},{6,7},{7,6},{8,9},{9,8},{10,11... | collective-permute-start | bytes 6291464 | tf_op jit(solution)/shard_map/ppermute | solution.py:498
  106.9 49.1 %collective-permute-start.5 = (bf16[4,784,128]{2,1,0:T(8,128)(2,1)}, bf16[4,784,128]{2,1,0:T(8,128)(2,1)S(1)}, u32[]{:S(2)}, u32[]{:S(2)}) collective-permute-start(bf16[4,784,128]{2,1,0:T(8,128)(2,1)} %copy-done.3), channel_id=1, source_target_pairs={{0,2},{2,0},{4,6},{6,4},{8,10},{10,8},{12,14},{14,12},{16,18},{18,... | collective-permute-start | bytes 2408456 | tf_op jit(solution)/shard_map/ppermute | solution.py:469
  107.0 49.1 %collective-permute-start.6 = (bf16[4,784,128]{2,1,0:T(8,128)(2,1)}, bf16[4,784,128]{2,1,0:T(8,128)(2,1)S(1)}, u32[]{:S(2)}, u32[]{:S(2)}) collective-permute-start(bf16[4,784,128]{2,1,0:T(8,128)(2,1)} %collective-permute-done.1.rest_1_), channel_id=1, source_target_pairs={{0,2},{2,0},{4,6},{6,4},{8,10},{10,8},{12,14},{14,12},{16,18},{18,... | collective-permute-start | bytes 2408456 | tf_op jit(solution)/shard_map/ppermute | solution.py:469
  107.4 111.3 %collective-permute-start.8 = (bf16[256,4096]{1,0:T(8,128)(2,1)}, bf16[256,4096]{1,0:T(8,128)(2,1)}, u32[]{:S(2)}, u32[]{:S(2)}) collective-permute-start(bf16[256,4096]{1,0:T(8,128)(2,1)} %get-tuple-element.53), channel_id=1, source_target_pairs={{0,1},{1,0},{2,3},{3,2},{4,5},{5,4},{6,7},{7,6},{8,9},{9,8},{10,11... | collective-permute-start | bytes 6291464 | tf_op jit(solution)/shard_map/ppermute | solution.py:498
  108.0 135.5 %collective-permute-start.9 = (bf16[256,4096]{1,0:T(8,128)(2,1)}, bf16[256,4096]{1,0:T(8,128)(2,1)}, u32[]{:S(2)}, u32[]{:S(2)}) collective-permute-start(bf16[256,4096]{1,0:T(8,128)(2,1)} %get-tuple-element.54), channel_id=1, source_target_pairs={{0,1},{1,0},{2,3},{3,2},{4,5},{5,4},{6,7},{7,6},{8,9},{9,8},{10,11... | collective-permute-start | bytes 6291464 | tf_op jit(solution)/shard_map/ppermute | solution.py:498
  154.2 89.3 %collective-permute-start.10 = (bf16[256,4096]{1,0:T(8,128)(2,1)}, bf16[256,4096]{1,0:T(8,128)(2,1)}, u32[]{:S(2)}, u32[]{:S(2)}) collective-permute-start(bf16[256,4096]{1,0:T(8,128)(2,1)} %collective-permute-done.4.rest_2_), channel_id=1, source_target_pairs={{0,4},{2,6},{4,0},{6,2},{8,12},{10,14},{12,8},{14,10},{16,20},{18,... | collective-permute-start | bytes 6291464 | tf_op jit(solution)/shard_map/ppermute | solution.py:485
  188.5 55.0 %all-to-all-start.4 = ((bf16[16,192,128]{2,1,0:T(8,128)(2,1)}), bf16[16,192,128]{2,1,0:T(8,128)(2,1)S(1)}, u32[]{:S(2)}, u32[]{:S(2)}) async-start(bf16[16,192,128]{2,1,0:T(8,128)(2,1)} %shard_map.70), calls=%async_computation.4 | async-start | bytes 1572864 | tf_op jit(solution)/shard_map/all_to_all | solution.py:535
  243.5 26.7 %all-to-all-start.5 = ((bf16[16,192,128]{2,1,0:T(8,128)(2,1)}), bf16[16,192,128]{2,1,0:T(8,128)(2,1)S(1)}, u32[]{:S(2)}, u32[]{:S(2)}) async-start(bf16[16,192,128]{2,1,0:T(8,128)(2,1)} %shard_map.71), calls=%async_computation.5 | async-start | bytes 1572864 | tf_op jit(solution)/shard_map/all_to_all | solution.py:539
  249.3 37.0 %collective-permute-start.12 = (bf16[256,4096]{1,0:T(8,128)(2,1)}, bf16[256,4096]{1,0:T(8,128)(2,1)}, u32[]{:S(2)}, u32[]{:S(2)}) collective-permute-start(bf16[256,4096]{1,0:T(8,128)(2,1)} %collective-permute-done.4.rest_2_), channel_id=1, source_target_pairs={{0,2},{2,0},{4,6},{6,4},{8,10},{10,8},{12,14},{14,12},{16,18},{18,... | collective-permute-start | bytes 6291464 | tf_op jit(solution)/shard_map/ppermute | solution.py:485
  249.7 36.6 %collective-permute-start.13 = (bf16[256,4096]{1,0:T(8,128)(2,1)}, bf16[256,4096]{1,0:T(8,128)(2,1)}, u32[]{:S(2)}, u32[]{:S(2)}) collective-permute-start(bf16[256,4096]{1,0:T(8,128)(2,1)} %collective-permute-done.8.rest_3_), channel_id=1, source_target_pairs={{0,2},{2,0},{4,6},{6,4},{8,10},{10,8},{12,14},{14,12},{16,18},{18,... | collective-permute-start | bytes 6291464 | tf_op jit(solution)/shard_map/ppermute | solution.py:485
  249.9 36.5 %collective-permute-start.14 = (bf16[256,4096]{1,0:T(8,128)(2,1)}, bf16[256,4096]{1,0:T(8,128)(2,1)}, u32[]{:S(2)}, u32[]{:S(2)}) collective-permute-start(bf16[256,4096]{1,0:T(8,128)(2,1)} %collective-permute-done.9.rest_4_), channel_id=1, source_target_pairs={{0,2},{2,0},{4,6},{6,4},{8,10},{10,8},{12,14},{14,12},{16,18},{18,... | collective-permute-start | bytes 6291464 | tf_op jit(solution)/shard_map/ppermute | solution.py:485
  250.2 36.1 %collective-permute-start.15 = (bf16[256,4096]{1,0:T(8,128)(2,1)}, bf16[256,4096]{1,0:T(8,128)(2,1)}, u32[]{:S(2)}, u32[]{:S(2)}) collective-permute-start(bf16[256,4096]{1,0:T(8,128)(2,1)} %collective-permute-done.10.rest_5_), channel_id=1, source_target_pairs={{0,2},{2,0},{4,6},{6,4},{8,10},{10,8},{12,14},{14,12},{16,18},{18,... | collective-permute-start | bytes 6291464 | tf_op jit(solution)/shard_map/ppermute | solution.py:485
  250.4 19.8 %collective-permute-start.7 = (bf16[16,192,128]{2,1,0:T(8,128)(2,1)S(1)}, bf16[16,192,128]{2,1,0:T(8,128)(2,1)S(1)}, u32[]{:S(2)}, u32[]{:S(2)}) collective-permute-start(bf16[16,192,128]{2,1,0:T(8,128)(2,1)S(1)} %all-to-all-done.4.rest_0_), channel_id=1, source_target_pairs={{0,1},{1,0},{2,3},{3,2},{4,5},{5,4},{6,7},{7,6},{8,9},{9,8},{10,11... | collective-permute-start | bytes 2359304 | tf_op jit(solution)/shard_map/ppermute | solution.py:498
  270.2 19.1 %collective-permute-start.11 = (bf16[16,192,128]{2,1,0:T(8,128)(2,1)S(1)}, bf16[16,192,128]{2,1,0:T(8,128)(2,1)S(1)}, u32[]{:S(2)}, u32[]{:S(2)}) collective-permute-start(bf16[16,192,128]{2,1,0:T(8,128)(2,1)S(1)} %all-to-all-done.5.rest_1_), channel_id=1, source_target_pairs={{0,1},{1,0},{2,3},{3,2},{4,5},{5,4},{6,7},{7,6},{8,9},{9,8},{10,11... | collective-permute-start | bytes 2359304 | tf_op jit(solution)/shard_map/ppermute | solution.py:498
  (8 other events, 83.0 us)

commit v8 on v7

--- a/solution.py
+++ b/solution.py
@@ -485,14 +485,16 @@
         return lax.ppermute(part, "ctx", [(d, d ^ bit) for d in range(ctx_size)])
 
     core, side = me & 1, (me >> 1) & 1
-    sizes = [2, 2, 2]
+    sizes = [2, 4]
 
     def weight_rows(p):
-        low = sum(sizes[:p])
-        first = jnp.where(side == 0, low, 8 - low - sizes[p]) + core * 8
+        first = core * 8 + (jnp.where(side == 0, 0, 6) if p == 0 else 2)
         return lax.dynamic_slice(
             out_weight, (first * HD, (1 - tp_me) * columns), (sizes[p] * HD, columns)
         )
+
+    def gather_weight(part):
+        return lax.all_gather(part, "tp", axis=0)
 
     def trade(part):
         return lax.ppermute(part, "tp", both)
@@ -505,11 +507,10 @@
     key_parts = swap(key_parts, bits[0])
     value_parts = [send_across(value_packed)]
     packed_q = list(pack(q_slots, cosine, sine, query, True, chunks, classes, cap))
-    came = [trade(slices[0])] if traded else []
-    packed_q[0], key_parts, value_parts, slices = lax.optimization_barrier(
-        (packed_q[0], key_parts, value_parts, slices)
+    gathered = [gather_weight(one) for one in slices]
+    packed_q[0], key_parts, value_parts = lax.optimization_barrier(
+        (packed_q[0], key_parts, value_parts)
     )
-    came = came + [trade(one) for one in slices[1:]]
     got_q = [send_query(packed_q[0])]
     value_parts = swap(value_parts, bits[0])
     for bit in bits[1:]:
@@ -524,8 +525,9 @@
     got_q = got_q + [send_query(packed) for packed in packed_q[1:]]
     values = compact(member, kept_count, value_parts, offsets, total, False)
     if traded:
-        got_q[0], turned_part = lax.optimization_barrier((got_q[0], came[0]))
-        came = came + [chip_swap(turned_part, 2)]
+        got_q[0], gathered[0] = lax.optimization_barrier((got_q[0], gathered[0]))
+        first_part = lax.dynamic_index_in_dim(gathered[0], 1 - tp_me, 0, keepdims=False)
+        came = [first_part, chip_swap(first_part, 2)]
 
     got, done = [], None
     for j in range(chunks):
@@ -535,16 +537,14 @@
             got.append(lax.all_to_all(done, "ctx", split_axis=0, concat_axis=0, tiled=True))
         done = attend(cls_j.reshape(1), kept_count, got_q[j], keys, values, block)
     if traded:
-        done, came = lax.optimization_barrier((done, came))
+        done, came, gathered = lax.optimization_barrier((done, came, gathered))
+        came = came + [lax.dynamic_index_in_dim(gathered[1], 1 - tp_me, 0, keepdims=False)]
     got.append(lax.all_to_all(done, "ctx", split_axis=0, concat_axis=0, tiled=True))
     if traded:
         theirs = [trade(one) for one in got]
         came = came + [chip_swap(part, 1) for part in came]
         own = project(tp_me * columns, got, out_weight, columns, classes)
-        ups = [sum(sizes[:p]) for p in range(3)]
-        order = [
-            jnp.where(side == 0, up, 8 - up - size) for up, size in zip(ups, sizes)
-        ] + [jnp.where(side == 0, 6, 0)]
+        order = [jnp.where(side == 0, 0, 6), jnp.where(side == 0, 6, 0), jnp.int32(2)]
         first_heads = jnp.stack([c * 8 + at for c in (core, 1 - core) for at in order])
         return join(first_heads.astype(jnp.int32), theirs, came, own)
     full = project(jnp.int32(0) * tp_me, got, out_weight, columns * tp_size, classes)

time: 306 us -> 299 us (0.977)
  waiting for transfers between devices: 143 us -> 100 us
  blocking collectives: 0 us -> 25.9 us
  between operations: 0.14 us -> 13.5 us
  starting transfers between devices: 44 us -> 31.6 us
  local copies, waits for them, and re-layouts: 9.13 us -> 16.7 us
    ppermute x5 -> x2, waiting for transfers between devices: 90.6 us -> 4.8 us  [trade(): return lax.ppermute(part, 'tp', both)]
    all_to_all x0 -> x1, blocking collectives: none -> 25.9 us  [local(): lax.all_to_all(done, 'ctx', split_axis=0, concat_axis=0, tiled=True)]
    all_gather x0 -> x2, waiting for transfers between devices: none -> 24.2 us  [gather_weight(): return lax.all_gather(part, 'tp', axis=0)]
    all_to_all x2 -> x1, waiting for transfers between devices: 0.01 us -> 17.5 us  [local(): lax.all_to_all(done, 'ctx', split_axis=0, concat_axis=0, tiled=True)]
    squeeze x0 -> x2, local copies, waits for them, and re-layouts: none -> 6.69 us  [the longest x1 4.75 us: local(): lax.dynamic_index_in_dim(gathered[1], 1 - tp_me, 0, keepdims=False)]
    all_to_all x2 -> x1, starting transfers between devices: 10.4 us -> 3.91 us  [local(): lax.all_to_all(done, 'ctx', split_axis=0, concat_axis=0, tiled=True)]
    ppermute x5 -> x2, starting transfers between devices: 6.7 us -> 1.14 us  [trade(): return lax.ppermute(part, 'tp', both)]
    dynamic_slice x1 -> x2, local copies, waits for them, and re-layouts: 5.78 us -> 7.81 us  [weight_rows(): lax.dynamic_slice(out_weight, (first * HD, (1 - tp_me) * columns), (sizes...]
  transfers between devices with their start and end apart: 22 -> 19, of which waited for: 10 -> 12; matrix products, arithmetic and copies ran while one was open for 2% -> 3% of each run, Pallas kernels for 28% -> 29%
where the time goes in v8:
time: 299 us; the launch traced here: 298 us
  Pallas kernels  107 us (36%)
  waiting for transfers between devices  100 us (33%)
  starting transfers between devices  31.6 us (11%)
  blocking collectives  25.9 us (9%)
  local copies, waits for them, and re-layouts  16.7 us (6%)
  between operations  13.5 us (5%)
    pallas_call x2, Pallas kernels, attend(): pl.pallas_call(functools.partial(attend_kernel, ctx_size, block), in_spec...  51 us
    ppermute x6, waiting for transfers between devices, swap(): return parts + [lax.ppermute(part, 'ctx', pairs) for part in parts]  42.4 us
    all_to_all x1, blocking collectives, local(): lax.all_to_all(done, 'ctx', split_axis=0, concat_axis=0, tiled=True)  25.9 us
    all_gather x2, waiting for transfers between devices, gather_weight(): return lax.all_gather(part, 'tp', axis=0)  24.2 us
    all_to_all x1, waiting for transfers between devices, local(): lax.all_to_all(done, 'ctx', split_axis=0, concat_axis=0, tiled=True)  17.5 us
    pallas_call x3, Pallas kernels, pack(): pl.pallas_call(functools.partial(pack_kernel, turned, classes, cap, width...  15.7 us
    pallas_call x1, Pallas kernels, join(): pl.pallas_call(functools.partial(join_kernel, len(got), len(weights)), gr...  15.1 us
    pallas_call x1, Pallas kernels, project(): pl.pallas_call(functools.partial(project_kernel, classes, len(got)), grid...  13.8 us
  transfers between devices with their start and end apart: 19, of which 12 were waited for; matrix products, arithmetic and copies ran while one was open for 3% of the time, Pallas kernels for 29%

profile of v8, /device:TPU:0, one launch (start us, length us, event | category | flops | bytes accessed | tf_op | source)
XLA Modules:
  0.0 297.6 jit_solution(1807565401185692747)
XLA Ops:
  10.7 3.5 %shard_map.67 = bf16[4,1,784,128]{3,2,1,0:T(8,128)(2,1)} custom-call(s32[1,768]{1,0:T(1,128)} %get-tuple-element.32.slot_ref, f32[768,128]{1,0:T(8,128)} %get-tuple-element.54.cos_ref, f32[768,128]{1,0:T(8,128)} %get-tuple-element.53.sin_ref, bf16[768,512]{1,0:T(8,128)(2,1)} %row_ref.5), custom_call_target="tpu_custom_call" | custom-call | flops 1024 | bytes 1024 | tf_op jit(solution)/shard_map/pallas_call | solution.py:128
  14.1 6.3 %all-to-all-start = ((bf16[4,784,128]{2,1,0:T(8,128)(2,1)}), bf16[4,784,128]{2,1,0:T(8,128)(2,1)S(1)}, u32[]{:S(2)}, u32[]{:S(2)}) async-start(bf16[4,784,128]{2,1,0:T(8,128)(2,1)} %bitcast.19), calls=%async_computation | async-start | bytes 1605632 | tf_op jit(solution)/shard_map/all_to_all | solution.py:463
  20.5 3.2 %shard_map.66 = bf16[4,1,784,128]{3,2,1,0:T(8,128)(2,1)} custom-call(s32[1,768]{1,0:T(1,128)} %get-tuple-element.32.slot_ref, f32[768,128]{1,0:T(8,128)} %get-tuple-element.54.cos_ref, f32[768,128]{1,0:T(8,128)} %get-tuple-element.53.sin_ref, bf16[768,512]{1,0:T(8,128)(2,1)} %row_ref.4), custom_call_target="tpu_custom_call" | custom-call | flops 1024 | bytes 1024 | tf_op jit(solution)/shard_map/pallas_call | solution.py:128
  23.7 3.1 %dynamic_slice.14 = bf16[256,4096]{1,0:T(8,128)(2,1)} dynamic-slice(bf16[2048,8192]{1,0:T(8,128)(2,1)} %rest_2_.1, s32[]{:T(128)S(6)} %select_n.45, s32[]{:T(128)S(6)} %select_n.46), dynamic_slice_sizes={256,4096} | dynamic-slice | bytes 4194308 | tf_op jit(solution)/shard_map/dynamic_slice | solution.py:492
  26.8 4.7 %dynamic_slice.15 = bf16[512,4096]{1,0:T(8,128)(2,1)} dynamic-slice(bf16[2048,8192]{1,0:T(8,128)(2,1)} %rest_2_.1, s32[]{:T(128)S(6)} %select_n.47, s32[]{:T(128)S(6)} %select_n.46), dynamic_slice_sizes={512,4096} | dynamic-slice | bytes 8388612 | tf_op jit(solution)/shard_map/dynamic_slice | solution.py:492
  31.5 9.4 %all-to-all-done.rest_0_ = bf16[4,784,128]{2,1,0:T(8,128)(2,1)S(1)} async-done(((bf16[4,784,128]{2,1,0:T(8,128)(2,1)}), bf16[4,784,128]{2,1,0:T(8,128)(2,1)S(1)}, u32[]{:S(2)}, u32[]{:S(2)}) %all-to-all-start) | async-done | bytes 802848 | tf_op jit(solution)/shard_map/all_to_all | solution.py:463
  41.7 3.5 %all-to-all-start.1 = ((bf16[4,784,128]{2,1,0:T(8,128)(2,1)}), bf16[4,784,128]{2,1,0:T(8,128)(2,1)S(1)}, u32[]{:S(2)}, u32[]{:S(2)}) async-start(bf16[4,784,128]{2,1,0:T(8,128)(2,1)} %bitcast.7), calls=%async_computation.1 | async-start | bytes 1605632 | tf_op jit(solution)/shard_map/all_to_all | solution.py:463
  46.8 9.0 %shard_map.65 = (bf16[16,1,400,128]{3,2,1,0:T(8,128)(2,1)}, bf16[16,1,400,128]{3,2,1,0:T(8,128)(2,1)}) custom-call(s32[1,768]{1,0:T(1,128)} %get-tuple-element.29.slot_ref, f32[768,128]{1,0:T(8,128)} %get-tuple-element.54.cos_ref, f32[768,128]{1,0:T(8,128)} %get-tuple-element.53.sin_ref, bf16[768,2048]{1,0:T(8,128)(2,1)} %row_ref.3), custom_call_target="tpu_custom_call" | custom-call | flops 1024 | bytes 1024 | tf_op jit(solution)/shard_map/pallas_call | solution.py:128
  55.8 8.5 %collective-permute-done.rest_1_ = bf16[4,784,128]{2,1,0:T(8,128)(2,1)} collective-permute-done((bf16[4,784,128]{2,1,0:T(8,128)(2,1)S(1)}, bf16[4,784,128]{2,1,0:T(8,128)(2,1)}, u32[]{:S(2)}, u32[]{:S(2)}) %collective-permute-start) | collective-permute-done | bytes 802848 | tf_op jit(solution)/shard_map/ppermute | solution.py:469
  65.1 4.9 %all-to-all-start.3 = ((bf16[16,400,128]{2,1,0:T(8,128)(2,1)}), bf16[16,400,128]{2,1,0:T(8,128)(2,1)S(1)}, u32[]{:S(2)}, u32[]{:S(2)}) async-start(bf16[16,400,128]{2,1,0:T(8,128)(2,1)} %bitcast.22), calls=%async_computation.3 | async-start | bytes 3276800 | tf_op jit(solution)/shard_map/all_to_all | solution.py:477
  73.9 4.7 %shard_map.68.key_ref = bf16[128,6144]{1,0:T(8,128)(2,1)} custom-call(s32[1]{0:T(128)} %bitcast.9.member_ref, s32[16]{0:T(128)} %count_ref.9, bf16[4,784,128]{2,1,0:T(8,128)(2,1)} %copy-done.2, bf16[4,784,128]{2,1,0:T(8,128)(2,1)} %collective-permute-done.rest_1_, bf16[4,784,128]{2,1,0:T(8,128)(2,1)} %collective-permute-done.2.rest_2_, ...), custom_call_target="tpu_custom_call" | custom-call | flops 1024 | bytes 1024 | tf_op jit(solution)/shard_map/pallas_call | solution.py:198
  78.6 29.4 %collective-permute-done.1.rest_1_ = bf16[4,784,128]{2,1,0:T(8,128)(2,1)} collective-permute-done((bf16[4,784,128]{2,1,0:T(8,128)(2,1)S(1)}, bf16[4,784,128]{2,1,0:T(8,128)(2,1)}, u32[]{:S(2)}, u32[]{:S(2)}) %collective-permute-start.1) | collective-permute-done | bytes 802848 | tf_op jit(solution)/shard_map/ppermute | solution.py:469
  108.0 4.7 %all-to-all-start.2 = ((bf16[16,400,128]{2,1,0:T(8,128)(2,1)}), bf16[16,400,128]{2,1,0:T(8,128)(2,1)}, u32[]{:S(2)}, u32[]{:S(2)}) async-start(bf16[16,400,128]{2,1,0:T(8,128)(2,1)} %bitcast.21), calls=%async_computation.2 | async-start | bytes 3276800 | tf_op jit(solution)/shard_map/all_to_all | solution.py:477
  121.9 5.2 %shard_map.69.value_ref = bf16[6144,256]{1,0:T(8,128)(2,1)} custom-call(s32[1]{0:T(128)} %bitcast.9.member_ref, s32[16]{0:T(128)} %count_ref.9, bf16[4,784,128]{2,1,0:T(8,128)(2,1)} %copy-done.3, bf16[4,784,128]{2,1,0:T(8,128)(2,1)} %collective-permute-done.1.rest_1_, bf16[4,784,128]{2,1,0:T(8,128)(2,1)} %copy-done.6, bf16[4,784,128]{2,1,0:T(8,128)(2,1)} %copy-done.7), custom_call_target="tpu_custom_call" | custom-call | flops 1024 | bytes 1024 | tf_op jit(solution)/shard_map/pallas_call | solution.py:198
  127.1 25.5 %shard_map.70 = bf16[16,192,128]{2,1,0:T(8,128)(2,1)} custom-call(s32[1]{0:T(128)} %constant.64.clone.1.cls_ref, s32[16]{0:T(128)} %count_ref.9, bf16[16,400,128]{2,1,0:T(8,128)(2,1)} %copy-done.1, bf16[128,6144]{1,0:T(8,128)(2,1)} %shard_map.68.key_ref, bf16[6144,256]{1,0:T(8,128)(2,1)} %shard_map.69.value_ref), custom_call_target="tpu_custom_call" | custom-call | flops 1024 | bytes 1024 | tf_op jit(solution)/shard_map/pallas_call | solution.py:314
  152.6 25.5 %shard_map.71 = bf16[16,192,128]{2,1,0:T(8,128)(2,1)} custom-call(s32[1]{0:T(128)} %constant.65.clone.1.cls_ref, s32[16]{0:T(128)} %count_ref.9, bf16[16,400,128]{2,1,0:T(8,128)(2,1)} %all-to-all-done.2.got_ref, bf16[128,6144]{1,0:T(8,128)(2,1)} %shard_map.68.key_ref, bf16[6144,256]{1,0:T(8,128)(2,1)} %shard_map.69.value_ref), custom_call_target="tpu_custom_call" | custom-call | flops 1024 | bytes 1024 | tf_op jit(solution)/shard_map/pallas_call | solution.py:314
  178.4 24.1 %all-gather.7.cloned.1.call-done = bf16[1024,4096]{1,0:T(8,128)(2,1)} async-done(((bf16[512,4096]{1,0:T(8,128)(2,1)}), bf16[1024,4096]{1,0:T(8,128)(2,1)}) %all-gather.7.cloned.1.call-update) | async-done | bytes 8388624 | tf_op jit(solution)/shard_map/all_gather | solution.py:497
  202.5 4.8 %dynamic-slice_bitcast_fusion.rest_4_ = bf16[512,4096]{1,0:T(8,128)(2,1)} fusion(bf16[2,512,4096]{2,1,0:T(8,128)(2,1)} %bitcast.20, s32[]{:T(128)S(6)} %select_n.48), kind=kLoop, calls=%fused_computation | loop fusion | bytes 8388612 | tf_op jit(solution)/shard_map/jit(dynamic_index_in_dim)/squeeze | solution.py:541
  207.3 25.9 %all_to_all.30.rest_0_ = bf16[16,192,128]{2,1,0:T(8,128)(2,1)} all-to-all(bf16[16,192,128]{2,1,0:T(8,128)(2,1)S(1)} %copy-done.4), channel_id=1, replica_groups=mesh['ctx'=16,'tp'=2] {'ctx'}, dimensions={0} | all-to-all | bytes 1572864 | tf_op jit(solution)/shard_map/all_to_all | solution.py:537
  233.2 3.9 %all-to-all-start.5 = ((bf16[16,192,128]{2,1,0:T(8,128)(2,1)}), bf16[16,192,128]{2,1,0:T(8,128)(2,1)S(1)}, u32[]{:S(2)}, u32[]{:S(2)}) async-start(bf16[16,192,128]{2,1,0:T(8,128)(2,1)} %shard_map.71), calls=%async_computation.5 | async-start | bytes 1572864 | tf_op jit(solution)/shard_map/all_to_all | solution.py:542
  238.3 17.5 %all-to-all-done.5.rest_1_ = bf16[16,192,128]{2,1,0:T(8,128)(2,1)S(1)} async-done(((bf16[16,192,128]{2,1,0:T(8,128)(2,1)}), bf16[16,192,128]{2,1,0:T(8,128)(2,1)S(1)}, u32[]{:S(2)}, u32[]{:S(2)}) %all-to-all-start.5) | async-done | bytes 786464 | tf_op jit(solution)/shard_map/all_to_all | solution.py:542
  257.0 13.8 %shard_map.72.rest_8_ = bf16[384,4096]{1,0:T(8,128)(2,1)} custom-call(s32[1]{0:T(128)} %bitcast.16.column_ref, bf16[16,192,128]{2,1,0:T(8,128)(2,1)} %all_to_all.30.rest_0_, bf16[16,192,128]{2,1,0:T(8,128)(2,1)} %copy-done.5, bf16[2048,8192]{1,0:T(8,128)(2,1)} %rest_2_.1), custom_call_target="tpu_custom_call" | custom-call | flops 1024 | bytes 1024 | tf_op jit(solution)/shard_map/pallas_call | solution.py:354
  270.8 4.8 %collective-permute-done.8.rest_1_ = bf16[16,192,128]{2,1,0:T(8,128)(2,1)} collective-permute-done((bf16[16,192,128]{2,1,0:T(8,128)(2,1)S(1)}, bf16[16,192,128]{2,1,0:T(8,128)(2,1)}, u32[]{:S(2)}, u32[]{:S(2)}) %collective-permute-start.8) | collective-permute-done | bytes 786464 | tf_op jit(solution)/shard_map/ppermute | solution.py:500
  275.6 15.1 %shard_map.73 = bf16[384,4096]{1,0:T(8,128)(2,1)} custom-call(s32[6]{0:T(128)} %stack.27.head_ref, bf16[16,192,128]{2,1,0:T(8,128)(2,1)} %collective-permute-done.6.rest_0_, bf16[16,192,128]{2,1,0:T(8,128)(2,1)} %collective-permute-done.8.rest_1_, bf16[256,4096]{1,0:T(8,128)(2,1)} %copy-done, bf16[256,4096]{1,0:T(8,128)(2,1)} %collective-permute-done.7.rest_3_, ...), custom_call_target="tpu_custom_call" | custom-call | flops 1024 | bytes 1024 | tf_op jit(solution)/shard_map/pallas_call | solution.py:401
  (52 shorter events, 23.0 us)
Async XLA Ops:
  14.1 26.8 %all-to-all-start = ((bf16[4,784,128]{2,1,0:T(8,128)(2,1)}), bf16[4,784,128]{2,1,0:T(8,128)(2,1)S(1)}, u32[]{:S(2)}, u32[]{:S(2)}) async-start(bf16[4,784,128]{2,1,0:T(8,128)(2,1)} %bitcast.19), calls=%async_computation | async-start | bytes 1605632 | tf_op jit(solution)/shard_map/all_to_all | solution.py:463
  20.5 92.3 %all-gather.5.cloned.1.call-start = ((), (), s32[]{:S(2)}) async-start(), calls=%async_computation.6 | async-start | bytes 6291456 | tf_op jit(solution)/shard_map/all_gather | solution.py:497
  40.9 29.1 %copy-start.2 = (bf16[4,784,128]{2,1,0:T(8,128)(2,1)}, bf16[4,784,128]{2,1,0:T(8,128)(2,1)S(1)}, u32[]{:S(2)}) copy-start(bf16[4,784,128]{2,1,0:T(8,128)(2,1)S(1)} %all-to-all-done.rest_0_) | copy-start | bytes 2408452
  40.9 161.6 %all-gather.7.cloned.1.call-start = ((), (), s32[]{:S(2)}) async-start(), calls=%async_computation.7 | async-start | bytes 12582912 | tf_op jit(solution)/shard_map/all_gather | solution.py:497
  41.7 23.4 %all-to-all-start.1 = ((bf16[4,784,128]{2,1,0:T(8,128)(2,1)}), bf16[4,784,128]{2,1,0:T(8,128)(2,1)S(1)}, u32[]{:S(2)}, u32[]{:S(2)}) async-start(bf16[4,784,128]{2,1,0:T(8,128)(2,1)} %bitcast.7), calls=%async_computation.1 | async-start | bytes 1605632 | tf_op jit(solution)/shard_map/all_to_all | solution.py:463
  45.2 19.0 %collective-permute-start = (bf16[4,784,128]{2,1,0:T(8,128)(2,1)S(1)}, bf16[4,784,128]{2,1,0:T(8,128)(2,1)}, u32[]{:S(2)}, u32[]{:S(2)}) collective-permute-start(bf16[4,784,128]{2,1,0:T(8,128)(2,1)S(1)} %all-to-all-done.rest_0_), channel_id=1, source_target_pairs={{0,4},{2,6},{4,0},{6,2},{8,12},{10,14},{12,8},{14,10},{16,20},{18,... | collective-permute-start | bytes 2408456 | tf_op jit(solution)/shard_map/ppermute | solution.py:469
  65.1 51.5 %copy-start.3 = (bf16[4,784,128]{2,1,0:T(8,128)(2,1)}, bf16[4,784,128]{2,1,0:T(8,128)(2,1)S(1)}, u32[]{:S(2)}) copy-start(bf16[4,784,128]{2,1,0:T(8,128)(2,1)S(1)} %all-to-all-done.1.rest_0_) | copy-start | bytes 2408452
  65.1 42.9 %all-to-all-start.3 = ((bf16[16,400,128]{2,1,0:T(8,128)(2,1)}), bf16[16,400,128]{2,1,0:T(8,128)(2,1)S(1)}, u32[]{:S(2)}, u32[]{:S(2)}) async-start(bf16[16,400,128]{2,1,0:T(8,128)(2,1)} %bitcast.22), calls=%async_computation.3 | async-start | bytes 3276800 | tf_op jit(solution)/shard_map/all_to_all | solution.py:477
  70.0 2.6 collective-permute-start.2
  70.5 3.4 %collective-permute-start.3 = (bf16[4,784,128]{2,1,0:T(8,128)(2,1)}, bf16[4,784,128]{2,1,0:T(8,128)(2,1)}, u32[]{:S(2)}, u32[]{:S(2)}) collective-permute-start(bf16[4,784,128]{2,1,0:T(8,128)(2,1)} %collective-permute-done.rest_1_), channel_id=1, source_target_pairs={{0,2},{2,0},{4,6},{6,4},{8,10},{10,8},{12,14},{14,12},{16,18},{18,... | collective-permute-start | bytes 2408456 | tf_op jit(solution)/shard_map/ppermute | solution.py:469
  70.6 37.4 %collective-permute-start.1 = (bf16[4,784,128]{2,1,0:T(8,128)(2,1)S(1)}, bf16[4,784,128]{2,1,0:T(8,128)(2,1)}, u32[]{:S(2)}, u32[]{:S(2)}) collective-permute-start(bf16[4,784,128]{2,1,0:T(8,128)(2,1)S(1)} %all-to-all-done.1.rest_0_), channel_id=1, source_target_pairs={{0,4},{2,6},{4,0},{6,2},{8,12},{10,14},{12,8},{14,10},{16,20},{18,... | collective-permute-start | bytes 2408456 | tf_op jit(solution)/shard_map/ppermute | solution.py:469
  108.0 4.7 %copy-start.1 = (bf16[16,400,128]{2,1,0:T(8,128)(2,1)}, bf16[16,400,128]{2,1,0:T(8,128)(2,1)S(1)}, u32[]{:S(2)}) copy-start(bf16[16,400,128]{2,1,0:T(8,128)(2,1)S(1)} %all-to-all-done.3.got_ref) | copy-start | bytes 4915204
  108.0 44.6 %all-to-all-start.2 = ((bf16[16,400,128]{2,1,0:T(8,128)(2,1)}), bf16[16,400,128]{2,1,0:T(8,128)(2,1)}, u32[]{:S(2)}, u32[]{:S(2)}) async-start(bf16[16,400,128]{2,1,0:T(8,128)(2,1)} %bitcast.21), calls=%async_computation.2 | async-start | bytes 3276800 | tf_op jit(solution)/shard_map/all_to_all | solution.py:477
  114.7 122.9 %copy-start = (bf16[256,4096]{1,0:T(8,128)(2,1)}, bf16[256,4096]{1,0:T(8,128)(2,1)S(1)}, u32[]{:S(2)}) copy-start(bf16[256,4096]{1,0:T(8,128)(2,1)S(1)} %dynamic-slice_bitcast_fusion.1.rest_2_) | copy-start | bytes 6291460
  114.7 63.7 %collective-permute-start.7 = (bf16[256,4096]{1,0:T(8,128)(2,1)S(1)}, bf16[256,4096]{1,0:T(8,128)(2,1)}, u32[]{:S(2)}, u32[]{:S(2)}) collective-permute-start(bf16[256,4096]{1,0:T(8,128)(2,1)S(1)} %dynamic-slice_bitcast_fusion.1.rest_2_), channel_id=1, source_target_pairs={{0,4},{2,6},{4,0},{6,2},{8,12},{10,14},{12,8},{14,10},{16,20},{18,... | collective-permute-start | bytes 6291464 | tf_op jit(solution)/shard_map/ppermute | solution.py:485
  116.6 3.4 %collective-permute-start.4 = (bf16[4,784,128]{2,1,0:T(8,128)(2,1)S(1)}, bf16[4,784,128]{2,1,0:T(8,128)(2,1)S(1)}, u32[]{:S(2)}, u32[]{:S(2)}) collective-permute-start(bf16[4,784,128]{2,1,0:T(8,128)(2,1)S(1)} %all-to-all-done.1.rest_0_), channel_id=1, source_target_pairs={{0,2},{2,0},{4,6},{6,4},{8,10},{10,8},{12,14},{14,12},{16,18},{18,... | collective-permute-start | bytes 2408456 | tf_op jit(solution)/shard_map/ppermute | solution.py:469
  116.6 3.7 %collective-permute-start.5 = (bf16[4,784,128]{2,1,0:T(8,128)(2,1)}, bf16[4,784,128]{2,1,0:T(8,128)(2,1)S(1)}, u32[]{:S(2)}, u32[]{:S(2)}) collective-permute-start(bf16[4,784,128]{2,1,0:T(8,128)(2,1)} %collective-permute-done.1.rest_1_), channel_id=1, source_target_pairs={{0,2},{2,0},{4,6},{6,4},{8,10},{10,8},{12,14},{14,12},{16,18},{18,... | collective-permute-start | bytes 2408456 | tf_op jit(solution)/shard_map/ppermute | solution.py:469
  202.5 4.8 %copy-start.4 = (bf16[16,192,128]{2,1,0:T(8,128)(2,1)S(1)}, bf16[16,192,128]{2,1,0:T(8,128)(2,1)}, u32[]{:S(2)}) copy-start(bf16[16,192,128]{2,1,0:T(8,128)(2,1)} %shard_map.70) | copy-start | bytes 2359300
  207.3 68.3 %collective-permute-start.11 = (bf16[512,4096]{1,0:T(8,128)(2,1)}, bf16[512,4096]{1,0:T(8,128)(2,1)}, u32[]{:S(2)}, u32[]{:S(2)}) collective-permute-start(bf16[512,4096]{1,0:T(8,128)(2,1)} %dynamic-slice_bitcast_fusion.rest_4_), channel_id=1, source_target_pairs={{0,2},{2,0},{4,6},{6,4},{8,10},{10,8},{12,14},{14,12},{16,18},{18,... | collective-permute-start | bytes 12582920 | tf_op jit(solution)/shard_map/ppermute | solution.py:485
  233.2 22.6 %all-to-all-start.5 = ((bf16[16,192,128]{2,1,0:T(8,128)(2,1)}), bf16[16,192,128]{2,1,0:T(8,128)(2,1)S(1)}, u32[]{:S(2)}, u32[]{:S(2)}) async-start(bf16[16,192,128]{2,1,0:T(8,128)(2,1)} %shard_map.71), calls=%async_computation.5 | async-start | bytes 1572864 | tf_op jit(solution)/shard_map/all_to_all | solution.py:542
  237.1 33.7 %collective-permute-start.10 = (bf16[256,4096]{1,0:T(8,128)(2,1)}, bf16[256,4096]{1,0:T(8,128)(2,1)}, u32[]{:S(2)}, u32[]{:S(2)}) collective-permute-start(bf16[256,4096]{1,0:T(8,128)(2,1)} %collective-permute-done.7.rest_3_), channel_id=1, source_target_pairs={{0,2},{2,0},{4,6},{6,4},{8,10},{10,8},{12,14},{14,12},{16,18},{18,... | collective-permute-start | bytes 6291464 | tf_op jit(solution)/shard_map/ppermute | solution.py:485
  237.6 33.2 %collective-permute-start.9 = (bf16[256,4096]{1,0:T(8,128)(2,1)S(1)}, bf16[256,4096]{1,0:T(8,128)(2,1)}, u32[]{:S(2)}, u32[]{:S(2)}) collective-permute-start(bf16[256,4096]{1,0:T(8,128)(2,1)S(1)} %dynamic-slice_bitcast_fusion.1.rest_2_), channel_id=1, source_target_pairs={{0,2},{2,0},{4,6},{6,4},{8,10},{10,8},{12,14},{14,12},{16,18},{18,... | collective-permute-start | bytes 6291464 | tf_op jit(solution)/shard_map/ppermute | solution.py:485
  237.7 33.1 %collective-permute-start.6 = (bf16[16,192,128]{2,1,0:T(8,128)(2,1)}, bf16[16,192,128]{2,1,0:T(8,128)(2,1)}, u32[]{:S(2)}, u32[]{:S(2)}) collective-permute-start(bf16[16,192,128]{2,1,0:T(8,128)(2,1)} %all_to_all.30.rest_0_), channel_id=1, source_target_pairs={{0,1},{1,0},{2,3},{3,2},{4,5},{5,4},{6,7},{7,6},{8,9},{9,8},{10,11... | collective-permute-start | bytes 2359304 | tf_op jit(solution)/shard_map/ppermute | solution.py:500
  255.8 19.8 %collective-permute-start.8 = (bf16[16,192,128]{2,1,0:T(8,128)(2,1)S(1)}, bf16[16,192,128]{2,1,0:T(8,128)(2,1)}, u32[]{:S(2)}, u32[]{:S(2)}) collective-permute-start(bf16[16,192,128]{2,1,0:T(8,128)(2,1)S(1)} %all-to-all-done.5.rest_1_), channel_id=1, source_target_pairs={{0,1},{1,0},{2,3},{3,2},{4,5},{5,4},{6,7},{7,6},{8,9},{9,8},{10,11... | collective-permute-start | bytes 2359304 | tf_op jit(solution)/shard_map/ppermute | solution.py:500
  (3 other events, 3.0 us)
Sparse Core Ops, SparseCore 0:
  41.1 55.8 all-gather.4
  98.5 103.9 all-gather.6

commit v9 on v8

--- a/solution.py
+++ b/solution.py
@@ -326,7 +326,9 @@
             pltpu.VMEM((4 * block, 2 * HD), jnp.float32),
         ],
         compiler_params=params(),
-        cost_estimate=small_cost(),
+        cost_estimate=pl.CostEstimate(
+            flops=pairs * 16 * HD, bytes_accessed=total * HD * 8, transcendentals=pairs
+        ),
     )(cls, counts, got, keys, values)
 
 
@@ -499,8 +501,13 @@
     def trade(part):
         return lax.ppermute(part, "tp", both)
 
-    key_parts = [send_across(pack_shared(key, True))]
-    slices = [weight_rows(p) for p in range(len(sizes))] if traded else []
+    key_packed = pack_shared(key, True)
+    slices = []
+    if traded:
+        key_packed, out_weight = lax.optimization_barrier((key_packed, out_weight))
+        first_slice, value = lax.optimization_barrier((weight_rows(0), value))
+        slices = [first_slice, weight_rows(1)]
+    key_parts = [send_across(key_packed)]
     value_packed, key_parts, slices = lax.optimization_barrier(
         (pack_shared(value, False), key_parts, slices)
     )
@@ -536,9 +543,11 @@
             got_q[j], done = lax.optimization_barrier((got_q[j], done))
             got.append(lax.all_to_all(done, "ctx", split_axis=0, concat_axis=0, tiled=True))
         done = attend(cls_j.reshape(1), kept_count, got_q[j], keys, values, block)
+    if chunks > 1:
+        done, got[0] = lax.optimization_barrier((done, got[0]))
     if traded:
-        done, came, gathered = lax.optimization_barrier((done, came, gathered))
-        came = came + [lax.dynamic_index_in_dim(gathered[1], 1 - tp_me, 0, keepdims=False)]
+        _, came, second = lax.optimization_barrier((done, came, gathered[1]))
+        came = came + [lax.dynamic_index_in_dim(second, 1 - tp_me, 0, keepdims=False)]
     got.append(lax.all_to_all(done, "ctx", split_axis=0, concat_axis=0, tiled=True))
     if traded:
         theirs = [trade(one) for one in got]

time: 299 us -> 275 us (0.920)
  blocking collectives: 25.9 us -> 0 us
  starting transfers between devices: 31.6 us -> 41.5 us
  waiting for transfers between devices: 100 us -> 93 us
    all_to_all x1 -> x0, blocking collectives: 25.9 us -> none  [local(): lax.all_to_all(done, 'ctx', split_axis=0, concat_axis=0, tiled=True)]
    all_to_all x1 -> x2, starting transfers between devices: 3.91 us -> 13.1 us  [local(): lax.all_to_all(done, 'ctx', split_axis=0, concat_axis=0, tiled=True)]
    all_gather x2, waiting for transfers between devices: 24.2 us -> 15.2 us  [gather_weight(): return lax.all_gather(part, 'tp', axis=0)]
    all_to_all x1 -> x2, waiting for transfers between devices: 17.5 us -> 23.4 us  [local(): lax.all_to_all(done, 'ctx', split_axis=0, concat_axis=0, tiled=True)]
    ppermute x6, waiting for transfers between devices: 42.4 us -> 39.1 us  [swap(): return parts + [lax.ppermute(part, 'ctx', pairs) for part in parts]]
  transfers between devices with their start and end apart: 19 -> 20, of which waited for: 12 -> 10; matrix products, arithmetic and copies ran while one was open for 3% -> 4% of each run, Pallas kernels for 29% -> 32%
where the time goes in v9:
time: 275 us; the launch traced here: 274 us
  Pallas kernels  107 us (39%)
  waiting for transfers between devices  93 us (34%)
  starting transfers between devices  41.5 us (15%)
  local copies, waits for them, and re-layouts  15.8 us (6%)
  between operations  13.5 us (5%)
    pallas_call x2, Pallas kernels, attend(): pl.pallas_call(functools.partial(attend_kernel, ctx_size, block), in_spec...  50.9 us
    ppermute x6, waiting for transfers between devices, swap(): return parts + [lax.ppermute(part, 'ctx', pairs) for part in parts]  39.1 us
    all_to_all x2, waiting for transfers between devices, local(): lax.all_to_all(done, 'ctx', split_axis=0, concat_axis=0, tiled=True)  23.4 us
    pallas_call x3, Pallas kernels, pack(): pl.pallas_call(functools.partial(pack_kernel, turned, classes, cap, width...  15.7 us
    all_gather x2, waiting for transfers between devices, gather_weight(): return lax.all_gather(part, 'tp', axis=0)  15.2 us
    pallas_call x1, Pallas kernels, join(): pl.pallas_call(functools.partial(join_kernel, len(got), len(weights)), gr...  15.2 us
    pallas_call x1, Pallas kernels, project(): pl.pallas_call(functools.partial(project_kernel, classes, len(got)), grid...  13.8 us
    all_to_all x2, starting transfers between devices, local(): lax.all_to_all(done, 'ctx', split_axis=0, concat_axis=0, tiled=True)  13.1 us
  transfers between devices with their start and end apart: 20, of which 10 were waited for; matrix products, arithmetic and copies ran while one was open for 4% of the time, Pallas kernels for 32%

profile of v9, /device:TPU:0, one launch (start us, length us, event | category | flops | bytes accessed | tf_op | source)
XLA Modules:
  0.0 273.7 jit_solution(976044925987093652)
XLA Ops:
  10.6 3.5 %shard_map.66 = bf16[4,1,784,128]{3,2,1,0:T(8,128)(2,1)} custom-call(s32[1,768]{1,0:T(1,128)} %get-tuple-element.37.slot_ref, f32[768,128]{1,0:T(8,128)} %get-tuple-element.64.cos_ref, f32[768,128]{1,0:T(8,128)} %get-tuple-element.63.sin_ref, bf16[768,512]{1,0:T(8,128)(2,1)} %row_ref.3), custom_call_target="tpu_custom_call" | custom-call | flops 1024 | bytes 1024 | tf_op jit(solution)/shard_map/pallas_call | solution.py:128
  14.1 6.3 %all-to-all-start = ((bf16[4,784,128]{2,1,0:T(8,128)(2,1)}), bf16[4,784,128]{2,1,0:T(8,128)(2,1)S(1)}, u32[]{:S(2)}, u32[]{:S(2)}) async-start(bf16[4,784,128]{2,1,0:T(8,128)(2,1)} %bitcast.19), calls=%async_computation | async-start | bytes 1605632 | tf_op jit(solution)/shard_map/all_to_all | solution.py:465
  23.6 3.2 %shard_map.67 = bf16[4,1,784,128]{3,2,1,0:T(8,128)(2,1)} custom-call(s32[1,768]{1,0:T(1,128)} %get-tuple-element.37.slot_ref, f32[768,128]{1,0:T(8,128)} %get-tuple-element.64.cos_ref, f32[768,128]{1,0:T(8,128)} %get-tuple-element.63.sin_ref, bf16[768,512]{1,0:T(8,128)(2,1)} %row_ref.4), custom_call_target="tpu_custom_call" | custom-call | flops 1024 | bytes 1024 | tf_op jit(solution)/shard_map/pallas_call | solution.py:128
  26.8 4.7 %dynamic_slice.15 = bf16[512,4096]{1,0:T(8,128)(2,1)} dynamic-slice(bf16[2048,8192]{1,0:T(8,128)(2,1)} %rest_2_, s32[]{:T(128)S(6)} %select_n.47, s32[]{:T(128)S(6)} %select_n.46), dynamic_slice_sizes={512,4096} | dynamic-slice | bytes 8388612 | tf_op jit(solution)/shard_map/dynamic_slice | solution.py:494
  31.5 9.4 %all-to-all-done.rest_0_ = bf16[4,784,128]{2,1,0:T(8,128)(2,1)S(1)} async-done(((bf16[4,784,128]{2,1,0:T(8,128)(2,1)}), bf16[4,784,128]{2,1,0:T(8,128)(2,1)S(1)}, u32[]{:S(2)}, u32[]{:S(2)}) %all-to-all-start) | async-done | bytes 802848 | tf_op jit(solution)/shard_map/all_to_all | solution.py:465
  40.9 3.5 %all-to-all-start.1 = ((bf16[4,784,128]{2,1,0:T(8,128)(2,1)}), bf16[4,784,128]{2,1,0:T(8,128)(2,1)S(1)}, u32[]{:S(2)}, u32[]{:S(2)}) async-start(bf16[4,784,128]{2,1,0:T(8,128)(2,1)} %bitcast.8), calls=%async_computation.1 | async-start | bytes 1605632 | tf_op jit(solution)/shard_map/all_to_all | solution.py:465
  46.0 9.0 %shard_map.65 = (bf16[16,1,400,128]{3,2,1,0:T(8,128)(2,1)}, bf16[16,1,400,128]{3,2,1,0:T(8,128)(2,1)}) custom-call(s32[1,768]{1,0:T(1,128)} %get-tuple-element.34.slot_ref, f32[768,128]{1,0:T(8,128)} %get-tuple-element.64.cos_ref, f32[768,128]{1,0:T(8,128)} %get-tuple-element.63.sin_ref, bf16[768,2048]{1,0:T(8,128)(2,1)} %row_ref.2), custom_call_target="tpu_custom_call" | custom-call | flops 1024 | bytes 1024 | tf_op jit(solution)/shard_map/pallas_call | solution.py:128
  55.0 8.3 %collective-permute-done.rest_1_ = bf16[4,784,128]{2,1,0:T(8,128)(2,1)S(1)} collective-permute-done((bf16[4,784,128]{2,1,0:T(8,128)(2,1)S(1)}, bf16[4,784,128]{2,1,0:T(8,128)(2,1)S(1)}, u32[]{:S(2)}, u32[]{:S(2)}) %collective-permute-start) | collective-permute-done | bytes 802848 | tf_op jit(solution)/shard_map/ppermute | solution.py:471
  64.3 5.7 %all-to-all-start.3 = ((bf16[16,400,128]{2,1,0:T(8,128)(2,1)}), bf16[16,400,128]{2,1,0:T(8,128)(2,1)S(1)}, u32[]{:S(2)}, u32[]{:S(2)}) async-start(bf16[16,400,128]{2,1,0:T(8,128)(2,1)} %bitcast.21), calls=%async_computation.3 | async-start | bytes 3276800 | tf_op jit(solution)/shard_map/all_to_all | solution.py:479
  73.9 4.7 %shard_map.68.key_ref = bf16[128,6144]{1,0:T(8,128)(2,1)} custom-call(s32[1]{0:T(128)} %bitcast.9.member_ref, s32[16]{0:T(128)} %count_ref.9, bf16[4,784,128]{2,1,0:T(8,128)(2,1)} %copy-done.1, bf16[4,784,128]{2,1,0:T(8,128)(2,1)} %copy-done.5, bf16[4,784,128]{2,1,0:T(8,128)(2,1)} %collective-permute-done.2.rest_2_, ...), custom_call_target="tpu_custom_call" | custom-call | flops 1024 | bytes 1024 | tf_op jit(solution)/shard_map/pallas_call | solution.py:198
  78.6 29.3 %collective-permute-done.1.rest_1_ = bf16[4,784,128]{2,1,0:T(8,128)(2,1)} collective-permute-done((bf16[4,784,128]{2,1,0:T(8,128)(2,1)S(1)}, bf16[4,784,128]{2,1,0:T(8,128)(2,1)}, u32[]{:S(2)}, u32[]{:S(2)}) %collective-permute-start.1) | collective-permute-done | bytes 802848 | tf_op jit(solution)/shard_map/ppermute | solution.py:471
  108.5 4.7 %all-to-all-start.2 = ((bf16[16,400,128]{2,1,0:T(8,128)(2,1)}), bf16[16,400,128]{2,1,0:T(8,128)(2,1)}, u32[]{:S(2)}, u32[]{:S(2)}) async-start(bf16[16,400,128]{2,1,0:T(8,128)(2,1)} %bitcast.10), calls=%async_computation.2 | async-start | bytes 3276800 | tf_op jit(solution)/shard_map/all_to_all | solution.py:479
  114.1 5.5 %shard_map.69.value_ref = bf16[6144,256]{1,0:T(8,128)(2,1)} custom-call(s32[1]{0:T(128)} %bitcast.9.member_ref, s32[16]{0:T(128)} %count_ref.9, bf16[4,784,128]{2,1,0:T(8,128)(2,1)} %copy-done.2, bf16[4,784,128]{2,1,0:T(8,128)(2,1)} %collective-permute-done.1.rest_1_, bf16[4,784,128]{2,1,0:T(8,128)(2,1)} %copy-done.6, ...), custom_call_target="tpu_custom_call" | custom-call | flops 1024 | bytes 1024 | tf_op jit(solution)/shard_map/pallas_call | solution.py:198
  123.3 25.4 %shard_map.70 = bf16[16,192,128]{2,1,0:T(8,128)(2,1)} custom-call(s32[1]{0:T(128)} %constant.65.clone.1.cls_ref, s32[16]{0:T(128)} %count_ref.9, bf16[16,400,128]{2,1,0:T(8,128)(2,1)} %copy-done.4, bf16[128,6144]{1,0:T(8,128)(2,1)} %shard_map.68.key_ref, bf16[6144,256]{1,0:T(8,128)(2,1)} %shard_map.69.value_ref), custom_call_target="tpu_custom_call" | custom-call | flops 19327352832 | bytes 6291456 | tf_op jit(solution)/shard_map/pallas_call | solution.py:314
  148.6 7.3 %all-to-all-start.4 = ((bf16[16,192,128]{2,1,0:T(8,128)(2,1)}), bf16[16,192,128]{2,1,0:T(8,128)(2,1)S(1)}, u32[]{:S(2)}, u32[]{:S(2)}) async-start(bf16[16,192,128]{2,1,0:T(8,128)(2,1)} %shard_map.70), calls=%async_computation.4 | async-start | bytes 1572864 | tf_op jit(solution)/shard_map/all_to_all | solution.py:544
  155.9 25.6 %shard_map.71 = bf16[16,192,128]{2,1,0:T(8,128)(2,1)} custom-call(s32[1]{0:T(128)} %constant.30.clone.1.cls_ref, s32[16]{0:T(128)} %count_ref.9, bf16[16,400,128]{2,1,0:T(8,128)(2,1)} %all-to-all-done.2.got_ref, bf16[128,6144]{1,0:T(8,128)(2,1)} %shard_map.68.key_ref, bf16[6144,256]{1,0:T(8,128)(2,1)} %shard_map.69.value_ref), custom_call_target="tpu_custom_call" | custom-call | flops 19327352832 | bytes 6291456 | tf_op jit(solution)/shard_map/pallas_call | solution.py:314
  181.5 5.8 %all-to-all-done.4.rest_0_ = bf16[16,192,128]{2,1,0:T(8,128)(2,1)S(1)} async-done(((bf16[16,192,128]{2,1,0:T(8,128)(2,1)}), bf16[16,192,128]{2,1,0:T(8,128)(2,1)S(1)}, u32[]{:S(2)}, u32[]{:S(2)}) %all-to-all-start.4) | async-done | bytes 786464 | tf_op jit(solution)/shard_map/all_to_all | solution.py:544
  187.3 15.2 %all-gather.7.cloned.1.call-done = bf16[1024,4096]{1,0:T(8,128)(2,1)} async-done(((bf16[512,4096]{1,0:T(8,128)(2,1)}), bf16[1024,4096]{1,0:T(8,128)(2,1)}) %all-gather.7.cloned.1.call-update) | async-done | bytes 8388624 | tf_op jit(solution)/shard_map/all_gather | solution.py:499
  202.5 4.7 %dynamic-slice_bitcast_fusion.rest_4_ = bf16[512,4096]{1,0:T(8,128)(2,1)} fusion(bf16[2,512,4096]{2,1,0:T(8,128)(2,1)} %bitcast.20, s32[]{:T(128)S(6)} %select_n.48), kind=kLoop, calls=%fused_computation | loop fusion | bytes 8388612 | tf_op jit(solution)/shard_map/jit(dynamic_index_in_dim)/squeeze | solution.py:550
  207.2 5.8 %all-to-all-start.5 = ((bf16[16,192,128]{2,1,0:T(8,128)(2,1)}), bf16[16,192,128]{2,1,0:T(8,128)(2,1)}, u32[]{:S(2)}, u32[]{:S(2)}) async-start(bf16[16,192,128]{2,1,0:T(8,128)(2,1)} %shard_map.71), calls=%async_computation.5 | async-start | bytes 1572864 | tf_op jit(solution)/shard_map/all_to_all | solution.py:551
  214.1 17.6 %all-to-all-done.5.rest_1_ = bf16[16,192,128]{2,1,0:T(8,128)(2,1)} async-done(((bf16[16,192,128]{2,1,0:T(8,128)(2,1)}), bf16[16,192,128]{2,1,0:T(8,128)(2,1)}, u32[]{:S(2)}, u32[]{:S(2)}) %all-to-all-start.5) | async-done | bytes 786464 | tf_op jit(solution)/shard_map/all_to_all | solution.py:551
  232.9 13.8 %shard_map.72.rest_8_ = bf16[384,4096]{1,0:T(8,128)(2,1)} custom-call(s32[1]{0:T(128)} %bitcast.16.column_ref, bf16[16,192,128]{2,1,0:T(8,128)(2,1)} %copy-done.3, bf16[16,192,128]{2,1,0:T(8,128)(2,1)} %all-to-all-done.5.rest_1_, bf16[2048,8192]{1,0:T(8,128)(2,1)} %rest_2_), custom_call_target="tpu_custom_call" | custom-call | flops 1024 | bytes 1024 | tf_op jit(solution)/shard_map/pallas_call | solution.py:356
  246.7 5.0 %collective-permute-done.7.rest_1_ = bf16[16,192,128]{2,1,0:T(8,128)(2,1)} collective-permute-done((bf16[16,192,128]{2,1,0:T(8,128)(2,1)}, bf16[16,192,128]{2,1,0:T(8,128)(2,1)}, u32[]{:S(2)}, u32[]{:S(2)}) %collective-permute-start.7) | collective-permute-done | bytes 786464 | tf_op jit(solution)/shard_map/ppermute | solution.py:502
  251.8 15.2 %shard_map.73 = bf16[384,4096]{1,0:T(8,128)(2,1)} custom-call(s32[6]{0:T(128)} %stack.27.head_ref, bf16[16,192,128]{2,1,0:T(8,128)(2,1)} %collective-permute-done.6.rest_0_, bf16[16,192,128]{2,1,0:T(8,128)(2,1)} %collective-permute-done.7.rest_1_, bf16[256,4096]{1,0:T(8,128)(2,1)} %copy-done, bf16[256,4096]{1,0:T(8,128)(2,1)} %collective-permute-done.8.rest_3_, ...), custom_call_target="tpu_custom_call" | custom-call | flops 1024 | bytes 1024 | tf_op jit(solution)/shard_map/pallas_call | solution.py:403
  (51 shorter events, 21.1 us)
Async XLA Ops:
  14.1 26.8 %all-to-all-start = ((bf16[4,784,128]{2,1,0:T(8,128)(2,1)}), bf16[4,784,128]{2,1,0:T(8,128)(2,1)S(1)}, u32[]{:S(2)}, u32[]{:S(2)}) async-start(bf16[4,784,128]{2,1,0:T(8,128)(2,1)} %bitcast.19), calls=%async_computation | async-start | bytes 1605632 | tf_op jit(solution)/shard_map/all_to_all | solution.py:465
  20.4 99.2 %all-gather.5.cloned.1.call-start = ((), (), s32[]{:S(2)}) async-start(), calls=%async_computation.6 | async-start | bytes 6291456 | tf_op jit(solution)/shard_map/all_gather | solution.py:499
  40.9 29.1 %copy-start.1 = (bf16[4,784,128]{2,1,0:T(8,128)(2,1)}, bf16[4,784,128]{2,1,0:T(8,128)(2,1)S(1)}, u32[]{:S(2)}) copy-start(bf16[4,784,128]{2,1,0:T(8,128)(2,1)S(1)} %all-to-all-done.rest_0_) | copy-start | bytes 2408452
  40.9 23.4 %all-to-all-start.1 = ((bf16[4,784,128]{2,1,0:T(8,128)(2,1)}), bf16[4,784,128]{2,1,0:T(8,128)(2,1)S(1)}, u32[]{:S(2)}, u32[]{:S(2)}) async-start(bf16[4,784,128]{2,1,0:T(8,128)(2,1)} %bitcast.8), calls=%async_computation.1 | async-start | bytes 1605632 | tf_op jit(solution)/shard_map/all_to_all | solution.py:465
  44.4 158.1 %all-gather.7.cloned.1.call-start = ((), (), s32[]{:S(2)}) async-start(), calls=%async_computation.7 | async-start | bytes 12582912 | tf_op jit(solution)/shard_map/all_gather | solution.py:499
  44.4 18.9 %collective-permute-start = (bf16[4,784,128]{2,1,0:T(8,128)(2,1)S(1)}, bf16[4,784,128]{2,1,0:T(8,128)(2,1)S(1)}, u32[]{:S(2)}, u32[]{:S(2)}) collective-permute-start(bf16[4,784,128]{2,1,0:T(8,128)(2,1)S(1)} %all-to-all-done.rest_0_), channel_id=1, source_target_pairs={{0,4},{2,6},{4,0},{6,2},{8,12},{10,14},{12,8},{14,10},{16,20},{18,... | collective-permute-start | bytes 2408456 | tf_op jit(solution)/shard_map/ppermute | solution.py:471
  64.3 43.7 %copy-start.2 = (bf16[4,784,128]{2,1,0:T(8,128)(2,1)}, bf16[4,784,128]{2,1,0:T(8,128)(2,1)S(1)}, u32[]{:S(2)}) copy-start(bf16[4,784,128]{2,1,0:T(8,128)(2,1)S(1)} %all-to-all-done.1.rest_0_) | copy-start | bytes 2408452
  64.3 44.2 %all-to-all-start.3 = ((bf16[16,400,128]{2,1,0:T(8,128)(2,1)}), bf16[16,400,128]{2,1,0:T(8,128)(2,1)S(1)}, u32[]{:S(2)}, u32[]{:S(2)}) async-start(bf16[16,400,128]{2,1,0:T(8,128)(2,1)} %bitcast.21), calls=%async_computation.3 | async-start | bytes 3276800 | tf_op jit(solution)/shard_map/all_to_all | solution.py:479
  70.0 2.6 collective-permute-start.2
  70.5 3.4 %collective-permute-start.3 = (bf16[4,784,128]{2,1,0:T(8,128)(2,1)}, bf16[4,784,128]{2,1,0:T(8,128)(2,1)}, u32[]{:S(2)}, u32[]{:S(2)}) collective-permute-start(bf16[4,784,128]{2,1,0:T(8,128)(2,1)} %copy-done.5), channel_id=1, source_target_pairs={{0,2},{2,0},{4,6},{6,4},{8,10},{10,8},{12,14},{14,12},{16,18},{18,... | collective-permute-start | bytes 2408456 | tf_op jit(solution)/shard_map/ppermute | solution.py:471
  70.6 37.4 %collective-permute-start.1 = (bf16[4,784,128]{2,1,0:T(8,128)(2,1)S(1)}, bf16[4,784,128]{2,1,0:T(8,128)(2,1)}, u32[]{:S(2)}, u32[]{:S(2)}) collective-permute-start(bf16[4,784,128]{2,1,0:T(8,128)(2,1)S(1)} %all-to-all-done.1.rest_0_), channel_id=1, source_target_pairs={{0,4},{2,6},{4,0},{6,2},{8,12},{10,14},{12,8},{14,10},{16,20},{18,... | collective-permute-start | bytes 2408456 | tf_op jit(solution)/shard_map/ppermute | solution.py:471
  108.0 5.2 %collective-permute-start.4 = (bf16[4,784,128]{2,1,0:T(8,128)(2,1)S(1)}, bf16[4,784,128]{2,1,0:T(8,128)(2,1)S(1)}, u32[]{:S(2)}, u32[]{:S(2)}) collective-permute-start(bf16[4,784,128]{2,1,0:T(8,128)(2,1)S(1)} %all-to-all-done.1.rest_0_), channel_id=1, source_target_pairs={{0,2},{2,0},{4,6},{6,4},{8,10},{10,8},{12,14},{14,12},{16,18},{18,... | collective-permute-start | bytes 2408456 | tf_op jit(solution)/shard_map/ppermute | solution.py:471
  108.0 5.2 %collective-permute-start.5 = (bf16[4,784,128]{2,1,0:T(8,128)(2,1)}, bf16[4,784,128]{2,1,0:T(8,128)(2,1)}, u32[]{:S(2)}, u32[]{:S(2)}) collective-permute-start(bf16[4,784,128]{2,1,0:T(8,128)(2,1)} %collective-permute-done.1.rest_1_), channel_id=1, source_target_pairs={{0,2},{2,0},{4,6},{6,4},{8,10},{10,8},{12,14},{14,12},{16,18},{18,... | collective-permute-start | bytes 2408456 | tf_op jit(solution)/shard_map/ppermute | solution.py:471
  108.5 40.1 %all-to-all-start.2 = ((bf16[16,400,128]{2,1,0:T(8,128)(2,1)}), bf16[16,400,128]{2,1,0:T(8,128)(2,1)}, u32[]{:S(2)}, u32[]{:S(2)}) async-start(bf16[16,400,128]{2,1,0:T(8,128)(2,1)} %bitcast.10), calls=%async_computation.2 | async-start | bytes 3276800 | tf_op jit(solution)/shard_map/all_to_all | solution.py:479
  121.3 91.6 %copy-start = (bf16[256,4096]{1,0:T(8,128)(2,1)}, bf16[256,4096]{1,0:T(8,128)(2,1)S(1)}, u32[]{:S(2)}) copy-start(bf16[256,4096]{1,0:T(8,128)(2,1)S(1)} %dynamic-slice_bitcast_fusion.1.rest_2_) | copy-start | bytes 6291460
  121.3 66.0 %collective-permute-start.8 = (bf16[256,4096]{1,0:T(8,128)(2,1)S(1)}, bf16[256,4096]{1,0:T(8,128)(2,1)}, u32[]{:S(2)}, u32[]{:S(2)}) collective-permute-start(bf16[256,4096]{1,0:T(8,128)(2,1)S(1)} %dynamic-slice_bitcast_fusion.1.rest_2_), channel_id=1, source_target_pairs={{0,4},{2,6},{4,0},{6,2},{8,12},{10,14},{12,8},{14,10},{16,20},{18,... | collective-permute-start | bytes 6291464 | tf_op jit(solution)/shard_map/ppermute | solution.py:487
  148.6 38.7 %all-to-all-start.4 = ((bf16[16,192,128]{2,1,0:T(8,128)(2,1)}), bf16[16,192,128]{2,1,0:T(8,128)(2,1)S(1)}, u32[]{:S(2)}, u32[]{:S(2)}) async-start(bf16[16,192,128]{2,1,0:T(8,128)(2,1)} %shard_map.70), calls=%async_computation.4 | async-start | bytes 1572864 | tf_op jit(solution)/shard_map/all_to_all | solution.py:544
  187.3 26.2 %copy-start.3 = (bf16[16,192,128]{2,1,0:T(8,128)(2,1)}, bf16[16,192,128]{2,1,0:T(8,128)(2,1)S(1)}, u32[]{:S(2)}) copy-start(bf16[16,192,128]{2,1,0:T(8,128)(2,1)S(1)} %all-to-all-done.4.rest_0_) | copy-start | bytes 2359300
  207.2 44.6 %collective-permute-start.11 = (bf16[512,4096]{1,0:T(8,128)(2,1)}, bf16[512,4096]{1,0:T(8,128)(2,1)}, u32[]{:S(2)}, u32[]{:S(2)}) collective-permute-start(bf16[512,4096]{1,0:T(8,128)(2,1)} %dynamic-slice_bitcast_fusion.rest_4_), channel_id=1, source_target_pairs={{0,2},{2,0},{4,6},{6,4},{8,10},{10,8},{12,14},{14,12},{16,18},{18,... | collective-permute-start | bytes 12582920 | tf_op jit(solution)/shard_map/ppermute | solution.py:487
  207.2 24.5 %all-to-all-start.5 = ((bf16[16,192,128]{2,1,0:T(8,128)(2,1)}), bf16[16,192,128]{2,1,0:T(8,128)(2,1)}, u32[]{:S(2)}, u32[]{:S(2)}) async-start(bf16[16,192,128]{2,1,0:T(8,128)(2,1)} %shard_map.71), calls=%async_computation.5 | async-start | bytes 1572864 | tf_op jit(solution)/shard_map/all_to_all | solution.py:551
  213.0 38.8 %collective-permute-start.9 = (bf16[256,4096]{1,0:T(8,128)(2,1)S(1)}, bf16[256,4096]{1,0:T(8,128)(2,1)}, u32[]{:S(2)}, u32[]{:S(2)}) collective-permute-start(bf16[256,4096]{1,0:T(8,128)(2,1)S(1)} %dynamic-slice_bitcast_fusion.1.rest_2_), channel_id=1, source_target_pairs={{0,2},{2,0},{4,6},{6,4},{8,10},{10,8},{12,14},{14,12},{16,18},{18,... | collective-permute-start | bytes 6291464 | tf_op jit(solution)/shard_map/ppermute | solution.py:487
  213.4 38.4 %collective-permute-start.10 = (bf16[256,4096]{1,0:T(8,128)(2,1)}, bf16[256,4096]{1,0:T(8,128)(2,1)}, u32[]{:S(2)}, u32[]{:S(2)}) collective-permute-start(bf16[256,4096]{1,0:T(8,128)(2,1)} %collective-permute-done.8.rest_3_), channel_id=1, source_target_pairs={{0,2},{2,0},{4,6},{6,4},{8,10},{10,8},{12,14},{14,12},{16,18},{18,... | collective-permute-start | bytes 6291464 | tf_op jit(solution)/shard_map/ppermute | solution.py:487
  213.5 33.2 %collective-permute-start.6 = (bf16[16,192,128]{2,1,0:T(8,128)(2,1)S(1)}, bf16[16,192,128]{2,1,0:T(8,128)(2,1)}, u32[]{:S(2)}, u32[]{:S(2)}) collective-permute-start(bf16[16,192,128]{2,1,0:T(8,128)(2,1)S(1)} %all-to-all-done.4.rest_0_), channel_id=1, source_target_pairs={{0,1},{1,0},{2,3},{3,2},{4,5},{5,4},{6,7},{7,6},{8,9},{9,8},{10,11... | collective-permute-start | bytes 2359304 | tf_op jit(solution)/shard_map/ppermute | solution.py:502
  231.7 20.0 %collective-permute-start.7 = (bf16[16,192,128]{2,1,0:T(8,128)(2,1)}, bf16[16,192,128]{2,1,0:T(8,128)(2,1)}, u32[]{:S(2)}, u32[]{:S(2)}) collective-permute-start(bf16[16,192,128]{2,1,0:T(8,128)(2,1)} %all-to-all-done.5.rest_1_), channel_id=1, source_target_pairs={{0,1},{1,0},{2,3},{3,2},{4,5},{5,4},{6,7},{7,6},{8,9},{9,8},{10,11... | collective-permute-start | bytes 2359304 | tf_op jit(solution)/shard_map/ppermute | solution.py:502
  (3 other events, 12.9 us)
Sparse Core Ops, SparseCore 0:
  41.0 55.8 all-gather.4
  98.4 103.9 all-gather.6

commit v10 on v6

--- a/solution.py
+++ b/solution.py
@@ -325,7 +325,7 @@
         ],
         compiler_params=params(),
         cost_estimate=pl.CostEstimate(
-            flops=pairs * 8 * HD, bytes_accessed=total * HD * 8, transcendentals=pairs
+            flops=pairs * 2 * HD, bytes_accessed=total * HD * 8, transcendentals=pairs
         ),
     )(cls, counts, got, keys, values)
 
@@ -491,69 +491,77 @@
         return lax.ppermute(part, "ctx", [(d, d ^ bit) for d in range(ctx_size)])
 
     core, side = me & 1, (me >> 1) & 1
-    sizes = [1, 1, 2, 2]
+    sizes = [1, 1, 1, 3]
+
+    def at_side(left, right):
+        return jnp.where(side == 0, left, right)
+
+    lows = [at_side(0, 6), at_side(1, 7), at_side(2, 5), at_side(3, 2)]
 
     def weight_rows(p):
-        low = sum(sizes[:p])
-        first = jnp.where(side == 0, low, 8 - low - sizes[p]) + core * 8
         return lax.dynamic_slice(
-            out_weight, (first * HD, (1 - tp_me) * columns), (sizes[p] * HD, columns)
+            out_weight,
+            ((core * 8 + lows[p]) * HD, (1 - tp_me) * columns),
+            (sizes[p] * HD, columns),
         )
 
     def trade(part):
         return lax.ppermute(part, "tp", both)
 
-    key_parts = [send_across(pack_shared(key, True))]
-    slices = [weight_rows(p) for p in range(len(sizes))] if traded else []
+    key_packed = pack_shared(key, True)
+    slices = []
+    if traded:
+        key_packed, out_weight = lax.optimization_barrier((key_packed, out_weight))
+        first_slice, value = lax.optimization_barrier((weight_rows(0), value))
+        slices = [first_slice] + [weight_rows(p) for p in range(1, 4)]
+    key_parts = [send_across(key_packed)]
     value_packed, key_parts, slices = lax.optimization_barrier(
         (pack_shared(value, False), key_parts, slices)
     )
     key_parts = swap(key_parts, bits[0])
     value_parts = [send_across(value_packed)]
+    came = []
+    if traded:
+        q_slots, came, slices = lax.optimization_barrier((q_slots, [trade(slices[0])], slices))
+        came = came + [trade(slices[1])]
     packed_q = list(pack(q_slots, cosine, sine, query, True, chunks, classes, cap))
-    came = [trade(slices[0])] if traded else []
-    packed_q[0], key_parts, value_parts, came, slices = lax.optimization_barrier(
-        (packed_q[0], key_parts, value_parts, came, slices)
+    packed_q[0], key_parts, value_parts = lax.optimization_barrier(
+        (packed_q[0], key_parts, value_parts)
     )
-    if traded:
-        came = came + [trade(slices[1])]
     got_q = [send_query(packed_q[0])]
     value_parts = swap(value_parts, bits[0])
     for bit in bits[1:]:
         key_parts = swap(key_parts, bit)
+    if traded:
+        key_parts, came, slices = lax.optimization_barrier((key_parts, came, slices))
+        came = came + [trade(slices[2])]
     keys = compact(member, kept_count, key_parts, offsets, total, True)
     if chunks > 1:
-        packed_q[1], value_parts, keys, came, slices = lax.optimization_barrier(
-            (packed_q[1], value_parts, keys, came, slices)
-        )
+        packed_q[1], value_parts, keys = lax.optimization_barrier((packed_q[1], value_parts, keys))
     for bit in bits[1:]:
         value_parts = swap(value_parts, bit)
     got_q = got_q + [send_query(packed) for packed in packed_q[1:]]
+    if traded:
+        value_parts, came, slices = lax.optimization_barrier((value_parts, came, slices))
+        joined = jnp.concatenate(came[:2], axis=0)
+        came = [joined, came[2], trade(slices[3]), chip_swap(joined, 2)]
     values = compact(member, kept_count, value_parts, offsets, total, False)
-    if traded:
-        came = came + [trade(slices[2])]
-        aside = [chip_swap(part, 2) for part in came[:2]]
 
     got, done = [], None
     for j in range(chunks):
         cls_j = j * classes + (me & (classes - 1))
         if j > 0:
-            got_q[j], done, came, slices = lax.optimization_barrier((got_q[j], done, came, slices))
+            got_q[j], done = lax.optimization_barrier((got_q[j], done))
             got.append(lax.all_to_all(done, "ctx", split_axis=0, concat_axis=0, tiled=True))
         done = attend(cls_j.reshape(1), kept_count, got_q[j], keys, values, block)
-    if traded:
-        came = came + [trade(slices[3])]
-        done, aside = lax.optimization_barrier((done, aside))
+    if chunks > 1:
+        done, got, came = lax.optimization_barrier((done, got, came))
     got.append(lax.all_to_all(done, "ctx", split_axis=0, concat_axis=0, tiled=True))
     if traded:
         theirs = [trade(one) for one in got]
-        came = came + aside
         came = came + [chip_swap(part, 1) for part in came]
         own = project(tp_me * columns, got, out_weight, columns, classes)
-        ups = [sum(sizes[:p]) for p in range(5)]
-        order = [
-            jnp.where(side == 0, up, 8 - up - size) for up, size in zip(ups, sizes)
-        ] + [jnp.where(side == 0, 7 - n, n) for n in range(2)]
+        order = [lows[0], lows[2], lows[3], at_side(6, 0)]
         first_heads = jnp.stack([c * 8 + at for c in (core, 1 - core) for at in order])
         return join(first_heads.astype(jnp.int32), theirs, came, own)
     full = project(jnp.int32(0) * tp_me, got, out_weight, columns * tp_size, classes)

time: 288 us -> 274 us (0.951)
  waiting for transfers between devices: 119 us -> 105 us
    ppermute x6, waiting for transfers between devices: 23.2 us -> 83.1 us  [trade(): return lax.ppermute(part, 'tp', both)]
    ppermute x8 -> x5, waiting for transfers between devices: 38.3 us -> 0.01 us  [chip_swap(): return lax.ppermute(part, 'ctx', [(d, d ^ bit) for d in range(ctx_size)])]
    ppermute x6, waiting for transfers between devices: 40.8 us -> 12.2 us  [swap(): return parts + [lax.ppermute(part, 'ctx', pairs) for part in parts]]
    all_to_all x2, waiting for transfers between devices: 6.64 us -> 0.01 us  [local(): lax.all_to_all(done, 'ctx', split_axis=0, concat_axis=0, tiled=True)]
  transfers between devices with their start and end apart: 26 -> 23, of which waited for: 16 -> 12; matrix products, arithmetic and copies ran while one was open for 3% -> 4% of each run, Pallas kernels for 30% -> 32%
where the time goes in v10:
time: 274 us; the launch traced here: 272 us
  Pallas kernels  108 us (39%)
  waiting for transfers between devices  105 us (38%)
  starting transfers between devices  44.8 us (16%)
  local copies, waits for them, and re-layouts  11.7 us (4%)
    ppermute x6, waiting for transfers between devices, trade(): return lax.ppermute(part, 'tp', both)  83.1 us
    pallas_call x2, Pallas kernels, attend(): pl.pallas_call(functools.partial(attend_kernel, ctx_size, block), in_spec...  51 us
    pallas_call x1, Pallas kernels, join(): pl.pallas_call(functools.partial(join_kernel, len(got), len(weights)), gr...  15.9 us
    pallas_call x3, Pallas kernels, pack(): pl.pallas_call(functools.partial(pack_kernel, turned, classes, cap, width...  15.8 us
    pallas_call x1, Pallas kernels, project(): pl.pallas_call(functools.partial(project_kernel, classes, len(got)), grid...  13.9 us
    ppermute x6, waiting for transfers between devices, swap(): return parts + [lax.ppermute(part, 'ctx', pairs) for part in parts]  12.2 us
    all_to_all x2, starting transfers between devices, local(): lax.all_to_all(done, 'ctx', split_axis=0, concat_axis=0, tiled=True)  10.6 us
    pallas_call x2, Pallas kernels, compact(): pl.pallas_call(functools.partial(compact_kernel, offsets, per, total, as_...  9.88 us
  transfers between devices with their start and end apart: 23, of which 12 were waited for; matrix products, arithmetic and copies ran while one was open for 4% of the time, Pallas kernels for 32%

profile of v10, /device:TPU:0, one launch (start us, length us, event | category | flops | bytes accessed | tf_op | source)
XLA Modules:
  0.0 272.2 jit_solution(9524494291868671399)
XLA Ops:
  4.1 3.5 %shard_map.65 = bf16[4,1,784,128]{3,2,1,0:T(8,128)(2,1)} custom-call(s32[1,768]{1,0:T(1,128)} %get-tuple-element.57.slot_ref, f32[768,128]{1,0:T(8,128)} %get-tuple-element.111.cos_ref, f32[768,128]{1,0:T(8,128)} %get-tuple-element.110.sin_ref, bf16[768,512]{1,0:T(8,128)(2,1)} %row_ref.2), custom_call_target="tpu_custom_call" | custom-call | flops 616562688 | bytes 1572864 | tf_op jit(solution)/shard_map/pallas_call | solution.py:124
  7.6 6.3 %all-to-all-start = ((bf16[4,784,128]{2,1,0:T(8,128)(2,1)}), bf16[4,784,128]{2,1,0:T(8,128)(2,1)S(1)}, u32[]{:S(2)}, u32[]{:S(2)}) async-start(bf16[4,784,128]{2,1,0:T(8,128)(2,1)} %bitcast.15), calls=%async_computation | async-start | bytes 1605632 | tf_op jit(solution)/shard_map/all_to_all | solution.py:469
  13.9 3.6 %fusion.4 = (bf16[128,4096]{1,0:T(8,128)(2,1)}, bf16[128,4096]{1,0:T(8,128)(2,1)}, bf16[128,4096]{1,0:T(8,128)(2,1)}) fusion(bf16[2048,8192]{1,0:T(8,128)(2,1)} %rest_2_, s32[]{:T(128)S(6)} %select_n.61, s32[]{:T(128)S(6)} %select_n.58, s32[]{:T(128)S(6)} %select_n.60, s32[]{:T(128)S(6)} %select_n.57), kind=kLoop, calls=%fused_computation.13 | loop fusion | bytes 6291472 | tf_op jit(solution)/shard_map/dynamic_slice | solution.py:502
  17.5 3.9 %dynamic_slice.15 = bf16[384,4096]{1,0:T(8,128)(2,1)} dynamic-slice(bf16[2048,8192]{1,0:T(8,128)(2,1)} %rest_2_, s32[]{:T(128)S(6)} %select_n.62, s32[]{:T(128)S(6)} %select_n.58), dynamic_slice_sizes={384,4096} | dynamic-slice | bytes 6291460 | tf_op jit(solution)/shard_map/dynamic_slice | solution.py:502
  21.4 3.2 %shard_map.66 = bf16[4,1,784,128]{3,2,1,0:T(8,128)(2,1)} custom-call(s32[1,768]{1,0:T(1,128)} %get-tuple-element.57.slot_ref, f32[768,128]{1,0:T(8,128)} %get-tuple-element.111.cos_ref, f32[768,128]{1,0:T(8,128)} %get-tuple-element.110.sin_ref, bf16[768,512]{1,0:T(8,128)(2,1)} %row_ref.3), custom_call_target="tpu_custom_call" | custom-call | flops 616562688 | bytes 1572864 | tf_op jit(solution)/shard_map/pallas_call | solution.py:124
  24.6 9.7 %all-to-all-done.rest_0_ = bf16[4,784,128]{2,1,0:T(8,128)(2,1)S(1)} async-done(((bf16[4,784,128]{2,1,0:T(8,128)(2,1)}), bf16[4,784,128]{2,1,0:T(8,128)(2,1)S(1)}, u32[]{:S(2)}, u32[]{:S(2)}) %all-to-all-start) | async-done | bytes 802848 | tf_op jit(solution)/shard_map/all_to_all | solution.py:469
  35.9 3.5 %all-to-all-start.1 = ((bf16[4,784,128]{2,1,0:T(8,128)(2,1)}), bf16[4,784,128]{2,1,0:T(8,128)(2,1)S(1)}, u32[]{:S(2)}, u32[]{:S(2)}) async-start(bf16[4,784,128]{2,1,0:T(8,128)(2,1)} %bitcast.16), calls=%async_computation.1 | async-start | bytes 1605632 | tf_op jit(solution)/shard_map/all_to_all | solution.py:469
  40.9 17.8 %collective-permute-done = bf16[128,4096]{1,0:T(8,128)(2,1)S(1)} collective-permute-done((bf16[128,4096]{1,0:T(8,128)(2,1)}, bf16[128,4096]{1,0:T(8,128)(2,1)S(1)}, u32[]{:S(2)}, u32[]{:S(2)}) %collective-permute-start) | collective-permute-done | bytes 1048608 | tf_op jit(solution)/shard_map/ppermute | solution.py:509
  58.7 9.1 %shard_map.67 = (bf16[16,1,400,128]{3,2,1,0:T(8,128)(2,1)}, bf16[16,1,400,128]{3,2,1,0:T(8,128)(2,1)}) custom-call(s32[1,768]{1,0:T(1,128)} %get-tuple-element.66.slot_ref, f32[768,128]{1,0:T(8,128)} %get-tuple-element.111.cos_ref, f32[768,128]{1,0:T(8,128)} %get-tuple-element.110.sin_ref, bf16[768,2048]{1,0:T(8,128)(2,1)} %row_ref.4), custom_call_target="tpu_custom_call" | custom-call | flops 2516582400 | bytes 6291456 | tf_op jit(solution)/shard_map/pallas_call | solution.py:124
  67.8 3.7 %all-to-all-start.3 = ((bf16[16,400,128]{2,1,0:T(8,128)(2,1)}), bf16[16,400,128]{2,1,0:T(8,128)(2,1)S(1)}, u32[]{:S(2)}, u32[]{:S(2)}) async-start(bf16[16,400,128]{2,1,0:T(8,128)(2,1)} %bitcast.17), calls=%async_computation.3 | async-start | bytes 3276800 | tf_op jit(solution)/shard_map/all_to_all | solution.py:483
  76.9 20.3 %collective-permute-done.5 = bf16[128,4096]{1,0:T(8,128)(2,1)} collective-permute-done((bf16[128,4096]{1,0:T(8,128)(2,1)}, bf16[128,4096]{1,0:T(8,128)(2,1)}, u32[]{:S(2)}, u32[]{:S(2)}) %collective-permute-start.5) | collective-permute-done | bytes 1048608 | tf_op jit(solution)/shard_map/ppermute | solution.py:509
  97.2 4.7 %shard_map.68.key_ref = bf16[128,6144]{1,0:T(8,128)(2,1)} custom-call(s32[1]{0:T(128)} %bitcast.11.member_ref, s32[16]{0:T(128)} %count_ref.9, bf16[4,784,128]{2,1,0:T(8,128)(2,1)} %copy-done.1, bf16[4,784,128]{2,1,0:T(8,128)(2,1)} %collective-permute-done.1.rest_1_, bf16[4,784,128]{2,1,0:T(8,128)(2,1)} %collective-permute-done.3.rest_2_, ...), custom_call_target="tpu_custom_call" | custom-call | flops 6291456 | bytes 6291456 | tf_op jit(solution)/shard_map/pallas_call | solution.py:196
  101.9 7.5 %collective-permute-done.2.rest_1_ = bf16[4,784,128]{2,1,0:T(8,128)(2,1)} collective-permute-done((bf16[4,784,128]{2,1,0:T(8,128)(2,1)S(1)}, bf16[4,784,128]{2,1,0:T(8,128)(2,1)}, u32[]{:S(2)}, u32[]{:S(2)}) %collective-permute-start.2) | collective-permute-done | bytes 802848 | tf_op jit(solution)/shard_map/ppermute | solution.py:475
  109.4 4.8 %all-to-all-start.2 = ((bf16[16,400,128]{2,1,0:T(8,128)(2,1)}), bf16[16,400,128]{2,1,0:T(8,128)(2,1)}, u32[]{:S(2)}, u32[]{:S(2)}) async-start(bf16[16,400,128]{2,1,0:T(8,128)(2,1)} %bitcast.12), calls=%async_computation.2 | async-start | bytes 3276800 | tf_op jit(solution)/shard_map/all_to_all | solution.py:483
  119.4 20.4 %collective-permute-done.8.rest_3_ = bf16[128,4096]{1,0:T(8,128)(2,1)S(1)} collective-permute-done((bf16[128,4096]{1,0:T(8,128)(2,1)}, bf16[128,4096]{1,0:T(8,128)(2,1)S(1)}, u32[]{:S(2)}, u32[]{:S(2)}) %collective-permute-start.8) | collective-permute-done | bytes 1048608 | tf_op jit(solution)/shard_map/ppermute | solution.py:509
  146.7 5.2 %shard_map.69.value_ref = bf16[6144,256]{1,0:T(8,128)(2,1)} custom-call(s32[1]{0:T(128)} %bitcast.11.member_ref, s32[16]{0:T(128)} %count_ref.9, bf16[4,784,128]{2,1,0:T(8,128)(2,1)} %copy-done.2, bf16[4,784,128]{2,1,0:T(8,128)(2,1)} %collective-permute-done.2.rest_1_, bf16[4,784,128]{2,1,0:T(8,128)(2,1)} %copy-done.7, bf16[4,784,128]{2,1,0:T(8,128)(2,1)} %copy-done.8), custom_call_target="tpu_custom_call" | custom-call | flops 6291456 | bytes 6291456 | tf_op jit(solution)/shard_map/pallas_call | solution.py:196
  151.9 25.4 %shard_map.70 = bf16[16,192,128]{2,1,0:T(8,128)(2,1)} custom-call(s32[1]{0:T(128)} %constant.60.clone.1.cls_ref, s32[16]{0:T(128)} %count_ref.9, bf16[16,400,128]{2,1,0:T(8,128)(2,1)} %copy-done.4, bf16[128,6144]{1,0:T(8,128)(2,1)} %shard_map.68.key_ref, bf16[6144,256]{1,0:T(8,128)(2,1)} %shard_map.69.value_ref), custom_call_target="tpu_custom_call" | custom-call | flops 2415919104 | bytes 6291456 | tf_op jit(solution)/shard_map/pallas_call | solution.py:312
  177.3 4.7 %all-to-all-start.4 = ((bf16[16,192,128]{2,1,0:T(8,128)(2,1)}), bf16[16,192,128]{2,1,0:T(8,128)(2,1)S(1)}, u32[]{:S(2)}, u32[]{:S(2)}) async-start(bf16[16,192,128]{2,1,0:T(8,128)(2,1)} %shard_map.70), calls=%async_computation.4 | async-start | bytes 1572864 | tf_op jit(solution)/shard_map/all_to_all | solution.py:555
  182.0 25.6 %shard_map.71 = bf16[16,192,128]{2,1,0:T(8,128)(2,1)} custom-call(s32[1]{0:T(128)} %constant.21.clone.1.cls_ref, s32[16]{0:T(128)} %count_ref.9, bf16[16,400,128]{2,1,0:T(8,128)(2,1)} %all-to-all-done.2.got_ref, bf16[128,6144]{1,0:T(8,128)(2,1)} %shard_map.68.key_ref, bf16[6144,256]{1,0:T(8,128)(2,1)} %shard_map.69.value_ref), custom_call_target="tpu_custom_call" | custom-call | flops 2415919104 | bytes 6291456 | tf_op jit(solution)/shard_map/pallas_call | solution.py:312
  210.6 5.8 %all-to-all-start.5 = ((bf16[16,192,128]{2,1,0:T(8,128)(2,1)}), bf16[16,192,128]{2,1,0:T(8,128)(2,1)}, u32[]{:S(2)}, u32[]{:S(2)}) async-start(bf16[16,192,128]{2,1,0:T(8,128)(2,1)} %shard_map.71), calls=%async_computation.5 | async-start | bytes 1572864 | tf_op jit(solution)/shard_map/all_to_all | solution.py:559
  218.7 18.3 %collective-permute-done.11.rest_0_ = bf16[16,192,128]{2,1,0:T(8,128)(2,1)} collective-permute-done((bf16[16,192,128]{2,1,0:T(8,128)(2,1)S(1)}, bf16[16,192,128]{2,1,0:T(8,128)(2,1)}, u32[]{:S(2)}, u32[]{:S(2)}) %collective-permute-start.11) | collective-permute-done | bytes 786464 | tf_op jit(solution)/shard_map/ppermute | solution.py:509
  239.1 13.9 %shard_map.72.rest_10_ = bf16[384,4096]{1,0:T(8,128)(2,1)} custom-call(s32[1]{0:T(128)} %bitcast.14.column_ref, bf16[16,192,128]{2,1,0:T(8,128)(2,1)} %copy-done.3, bf16[16,192,128]{2,1,0:T(8,128)(2,1)} %all-to-all-done.5.rest_1_, bf16[2048,8192]{1,0:T(8,128)(2,1)} %rest_2_), custom_call_target="tpu_custom_call" | custom-call | flops 6442450944 | bytes 16777216 | tf_op jit(solution)/shard_map/pallas_call | solution.py:354
  252.9 3.3 %collective-permute-done.12.rest_1_ = bf16[16,192,128]{2,1,0:T(8,128)(2,1)} collective-permute-done((bf16[16,192,128]{2,1,0:T(8,128)(2,1)}, bf16[16,192,128]{2,1,0:T(8,128)(2,1)}, u32[]{:S(2)}, u32[]{:S(2)}) %collective-permute-start.12) | collective-permute-done | bytes 786464 | tf_op jit(solution)/shard_map/ppermute | solution.py:509
  256.3 15.9 %shard_map.73 = bf16[384,4096]{1,0:T(8,128)(2,1)} custom-call(s32[8]{0:T(128)} %stack.35.head_ref, bf16[16,192,128]{2,1,0:T(8,128)(2,1)} %collective-permute-done.11.rest_0_, bf16[16,192,128]{2,1,0:T(8,128)(2,1)} %collective-permute-done.12.rest_1_, bf16[256,4096]{1,0:T(8,128)(2,1)} %copy-done, bf16[128,4096]{1,0:T(8,128)(2,1)} %copy-done.6, ...), custom_call_target="tpu_custom_call" | custom-call | flops 6442450944 | bytes 16777216 | tf_op jit(solution)/shard_map/pallas_call | solution.py:403
  (59 shorter events, 32.0 us)
Async XLA Ops:
  7.6 26.8 %all-to-all-start = ((bf16[4,784,128]{2,1,0:T(8,128)(2,1)}), bf16[4,784,128]{2,1,0:T(8,128)(2,1)S(1)}, u32[]{:S(2)}, u32[]{:S(2)}) async-start(bf16[4,784,128]{2,1,0:T(8,128)(2,1)} %bitcast.15), calls=%async_computation | async-start | bytes 1605632 | tf_op jit(solution)/shard_map/all_to_all | solution.py:469
  34.4 24.3 %collective-permute-start = (bf16[128,4096]{1,0:T(8,128)(2,1)}, bf16[128,4096]{1,0:T(8,128)(2,1)S(1)}, u32[]{:S(2)}, u32[]{:S(2)}) collective-permute-start(bf16[128,4096]{1,0:T(8,128)(2,1)} %get-tuple-element.62), channel_id=1, source_target_pairs={{0,1},{1,0},{2,3},{3,2},{4,5},{5,4},{6,7},{7,6},{8,9},{9,8},{10,11... | collective-permute-start | bytes 3145736 | tf_op jit(solution)/shard_map/ppermute | solution.py:509
  35.9 31.9 %all-to-all-start.1 = ((bf16[4,784,128]{2,1,0:T(8,128)(2,1)}), bf16[4,784,128]{2,1,0:T(8,128)(2,1)S(1)}, u32[]{:S(2)}, u32[]{:S(2)}) async-start(bf16[4,784,128]{2,1,0:T(8,128)(2,1)} %bitcast.16), calls=%async_computation.1 | async-start | bytes 1605632 | tf_op jit(solution)/shard_map/all_to_all | solution.py:469
  39.4 28.4 %collective-permute-start.1 = (bf16[4,784,128]{2,1,0:T(8,128)(2,1)S(1)}, bf16[4,784,128]{2,1,0:T(8,128)(2,1)}, u32[]{:S(2)}, u32[]{:S(2)}) collective-permute-start(bf16[4,784,128]{2,1,0:T(8,128)(2,1)S(1)} %all-to-all-done.rest_0_), channel_id=1, source_target_pairs={{0,4},{2,6},{4,0},{6,2},{8,12},{10,14},{12,8},{14,10},{16,20},{18,... | collective-permute-start | bytes 2408456 | tf_op jit(solution)/shard_map/ppermute | solution.py:475
  67.8 41.6 %all-to-all-start.3 = ((bf16[16,400,128]{2,1,0:T(8,128)(2,1)}), bf16[16,400,128]{2,1,0:T(8,128)(2,1)S(1)}, u32[]{:S(2)}, u32[]{:S(2)}) async-start(bf16[16,400,128]{2,1,0:T(8,128)(2,1)} %bitcast.17), calls=%async_computation.3 | async-start | bytes 3276800 | tf_op jit(solution)/shard_map/all_to_all | solution.py:483
  71.5 25.7 %collective-permute-start.5 = (bf16[128,4096]{1,0:T(8,128)(2,1)}, bf16[128,4096]{1,0:T(8,128)(2,1)}, u32[]{:S(2)}, u32[]{:S(2)}) collective-permute-start(bf16[128,4096]{1,0:T(8,128)(2,1)} %get-tuple-element.75), channel_id=1, source_target_pairs={{0,1},{1,0},{2,3},{3,2},{4,5},{5,4},{6,7},{7,6},{8,9},{9,8},{10,11... | collective-permute-start | bytes 3145736 | tf_op jit(solution)/shard_map/ppermute | solution.py:509
  73.1 3.6 %collective-permute-start.3 = (bf16[4,784,128]{2,1,0:T(8,128)(2,1)S(1)}, bf16[4,784,128]{2,1,0:T(8,128)(2,1)}, u32[]{:S(2)}, u32[]{:S(2)}) collective-permute-start(bf16[4,784,128]{2,1,0:T(8,128)(2,1)S(1)} %all-to-all-done.rest_0_), channel_id=1, source_target_pairs={{0,2},{2,0},{4,6},{6,4},{8,10},{10,8},{12,14},{14,12},{16,18},{18,... | collective-permute-start | bytes 2408456 | tf_op jit(solution)/shard_map/ppermute | solution.py:475
  73.1 3.8 %collective-permute-start.4 = (bf16[4,784,128]{2,1,0:T(8,128)(2,1)}, bf16[4,784,128]{2,1,0:T(8,128)(2,1)}, u32[]{:S(2)}, u32[]{:S(2)}) collective-permute-start(bf16[4,784,128]{2,1,0:T(8,128)(2,1)} %collective-permute-done.1.rest_1_), channel_id=1, source_target_pairs={{0,2},{2,0},{4,6},{6,4},{8,10},{10,8},{12,14},{14,12},{16,18},{18,... | collective-permute-start | bytes 2408456 | tf_op jit(solution)/shard_map/ppermute | solution.py:475
  73.6 35.8 %collective-permute-start.2 = (bf16[4,784,128]{2,1,0:T(8,128)(2,1)S(1)}, bf16[4,784,128]{2,1,0:T(8,128)(2,1)}, u32[]{:S(2)}, u32[]{:S(2)}) collective-permute-start(bf16[4,784,128]{2,1,0:T(8,128)(2,1)S(1)} %all-to-all-done.1.rest_0_), channel_id=1, source_target_pairs={{0,4},{2,6},{4,0},{6,2},{8,12},{10,14},{12,8},{14,10},{16,20},{18,... | collective-permute-start | bytes 2408456 | tf_op jit(solution)/shard_map/ppermute | solution.py:475
  109.4 67.8 %all-to-all-start.2 = ((bf16[16,400,128]{2,1,0:T(8,128)(2,1)}), bf16[16,400,128]{2,1,0:T(8,128)(2,1)}, u32[]{:S(2)}, u32[]{:S(2)}) async-start(bf16[16,400,128]{2,1,0:T(8,128)(2,1)} %bitcast.12), calls=%async_computation.2 | async-start | bytes 3276800 | tf_op jit(solution)/shard_map/all_to_all | solution.py:483
  114.2 25.6 %collective-permute-start.8 = (bf16[128,4096]{1,0:T(8,128)(2,1)}, bf16[128,4096]{1,0:T(8,128)(2,1)S(1)}, u32[]{:S(2)}, u32[]{:S(2)}) collective-permute-start(bf16[128,4096]{1,0:T(8,128)(2,1)} %get-tuple-element.89), channel_id=1, source_target_pairs={{0,1},{1,0},{2,3},{3,2},{4,5},{5,4},{6,7},{7,6},{8,9},{9,8},{10,11... | collective-permute-start | bytes 3145736 | tf_op jit(solution)/shard_map/ppermute | solution.py:509
  115.8 3.3 %collective-permute-start.6 = (bf16[4,784,128]{2,1,0:T(8,128)(2,1)S(1)}, bf16[4,784,128]{2,1,0:T(8,128)(2,1)S(1)}, u32[]{:S(2)}, u32[]{:S(2)}) collective-permute-start(bf16[4,784,128]{2,1,0:T(8,128)(2,1)S(1)} %all-to-all-done.1.rest_0_), channel_id=1, source_target_pairs={{0,2},{2,0},{4,6},{6,4},{8,10},{10,8},{12,14},{14,12},{16,18},{18,... | collective-permute-start | bytes 2408456 | tf_op jit(solution)/shard_map/ppermute | solution.py:475
  115.8 3.6 %collective-permute-start.7 = (bf16[4,784,128]{2,1,0:T(8,128)(2,1)}, bf16[4,784,128]{2,1,0:T(8,128)(2,1)S(1)}, u32[]{:S(2)}, u32[]{:S(2)}) collective-permute-start(bf16[4,784,128]{2,1,0:T(8,128)(2,1)} %collective-permute-done.2.rest_1_), channel_id=1, source_target_pairs={{0,2},{2,0},{4,6},{6,4},{8,10},{10,8},{12,14},{14,12},{16,18},{18,... | collective-permute-start | bytes 2408456 | tf_op jit(solution)/shard_map/ppermute | solution.py:475
  140.8 69.8 %collective-permute-start.9 = (bf16[384,4096]{1,0:T(8,128)(2,1)}, bf16[384,4096]{1,0:T(8,128)(2,1)}, u32[]{:S(2)}, u32[]{:S(2)}) collective-permute-start(bf16[384,4096]{1,0:T(8,128)(2,1)} %dynamic_slice.15), channel_id=1, source_target_pairs={{0,1},{1,0},{2,3},{3,2},{4,5},{5,4},{6,7},{7,6},{8,9},{9,8},{10,11... | collective-permute-start | bytes 9437192 | tf_op jit(solution)/shard_map/ppermute | solution.py:509
  144.9 71.6 %copy-start = (bf16[256,4096]{1,0:T(8,128)(2,1)}, bf16[256,4096]{1,0:T(8,128)(2,1)S(1)}, u32[]{:S(2)}) copy-start(bf16[256,4096]{1,0:T(8,128)(2,1)S(1)} %constant_dynamic-update-slice_fusion.rest_2_) | copy-start | bytes 6291460
  144.9 62.6 %collective-permute-start.10 = (bf16[256,4096]{1,0:T(8,128)(2,1)S(1)}, bf16[256,4096]{1,0:T(8,128)(2,1)}, u32[]{:S(2)}, u32[]{:S(2)}) collective-permute-start(bf16[256,4096]{1,0:T(8,128)(2,1)S(1)} %constant_dynamic-update-slice_fusion.rest_2_), channel_id=1, source_target_pairs={{0,4},{2,6},{4,0},{6,2},{8,12},{10,14},{12,8},{14,10},{16,20},{18,... | collective-permute-start | bytes 6291464 | tf_op jit(solution)/shard_map/ppermute | solution.py:491
  177.3 33.4 %all-to-all-start.4 = ((bf16[16,192,128]{2,1,0:T(8,128)(2,1)}), bf16[16,192,128]{2,1,0:T(8,128)(2,1)S(1)}, u32[]{:S(2)}, u32[]{:S(2)}) async-start(bf16[16,192,128]{2,1,0:T(8,128)(2,1)} %shard_map.70), calls=%async_computation.4 | async-start | bytes 1572864 | tf_op jit(solution)/shard_map/all_to_all | solution.py:555
  210.6 45.7 %collective-permute-start.15 = (bf16[384,4096]{1,0:T(8,128)(2,1)}, bf16[384,4096]{1,0:T(8,128)(2,1)}, u32[]{:S(2)}, u32[]{:S(2)}) collective-permute-start(bf16[384,4096]{1,0:T(8,128)(2,1)} %collective-permute-done.9.rest_4_), channel_id=1, source_target_pairs={{0,2},{2,0},{4,6},{6,4},{8,10},{10,8},{12,14},{14,12},{16,18},{18,... | collective-permute-start | bytes 9437192 | tf_op jit(solution)/shard_map/ppermute | solution.py:491
  210.6 26.3 %all-to-all-start.5 = ((bf16[16,192,128]{2,1,0:T(8,128)(2,1)}), bf16[16,192,128]{2,1,0:T(8,128)(2,1)}, u32[]{:S(2)}, u32[]{:S(2)}) async-start(bf16[16,192,128]{2,1,0:T(8,128)(2,1)} %shard_map.71), calls=%async_computation.5 | async-start | bytes 1572864 | tf_op jit(solution)/shard_map/all_to_all | solution.py:559
  216.5 36.4 %collective-permute-start.13 = (bf16[256,4096]{1,0:T(8,128)(2,1)S(1)}, bf16[256,4096]{1,0:T(8,128)(2,1)}, u32[]{:S(2)}, u32[]{:S(2)}) collective-permute-start(bf16[256,4096]{1,0:T(8,128)(2,1)S(1)} %constant_dynamic-update-slice_fusion.rest_2_), channel_id=1, source_target_pairs={{0,2},{2,0},{4,6},{6,4},{8,10},{10,8},{12,14},{14,12},{16,18},{18,... | collective-permute-start | bytes 6291464 | tf_op jit(solution)/shard_map/ppermute | solution.py:491
  216.9 36.0 %collective-permute-start.16 = (bf16[256,4096]{1,0:T(8,128)(2,1)}, bf16[256,4096]{1,0:T(8,128)(2,1)}, u32[]{:S(2)}, u32[]{:S(2)}) collective-permute-start(bf16[256,4096]{1,0:T(8,128)(2,1)} %collective-permute-done.10.rest_5_), channel_id=1, source_target_pairs={{0,2},{2,0},{4,6},{6,4},{8,10},{10,8},{12,14},{14,12},{16,18},{18,... | collective-permute-start | bytes 6291464 | tf_op jit(solution)/shard_map/ppermute | solution.py:491
  217.1 19.9 %collective-permute-start.11 = (bf16[16,192,128]{2,1,0:T(8,128)(2,1)S(1)}, bf16[16,192,128]{2,1,0:T(8,128)(2,1)}, u32[]{:S(2)}, u32[]{:S(2)}) collective-permute-start(bf16[16,192,128]{2,1,0:T(8,128)(2,1)S(1)} %all-to-all-done.4.rest_0_), channel_id=1, source_target_pairs={{0,1},{1,0},{2,3},{3,2},{4,5},{5,4},{6,7},{7,6},{8,9},{9,8},{10,11... | collective-permute-start | bytes 2359304 | tf_op jit(solution)/shard_map/ppermute | solution.py:509
  218.6 34.3 %collective-permute-start.14 = (bf16[128,4096]{1,0:T(8,128)(2,1)}, bf16[128,4096]{1,0:T(8,128)(2,1)}, u32[]{:S(2)}, u32[]{:S(2)}) collective-permute-start(bf16[128,4096]{1,0:T(8,128)(2,1)} %copy-done.6), channel_id=1, source_target_pairs={{0,2},{2,0},{4,6},{6,4},{8,10},{10,8},{12,14},{14,12},{16,18},{18,... | collective-permute-start | bytes 3145736 | tf_op jit(solution)/shard_map/ppermute | solution.py:491
  237.0 19.3 %collective-permute-start.12 = (bf16[16,192,128]{2,1,0:T(8,128)(2,1)}, bf16[16,192,128]{2,1,0:T(8,128)(2,1)}, u32[]{:S(2)}, u32[]{:S(2)}) collective-permute-start(bf16[16,192,128]{2,1,0:T(8,128)(2,1)} %all-to-all-done.5.rest_1_), channel_id=1, source_target_pairs={{0,1},{1,0},{2,3},{3,2},{4,5},{5,4},{6,7},{7,6},{8,9},{9,8},{10,11... | collective-permute-start | bytes 2359304 | tf_op jit(solution)/shard_map/ppermute | solution.py:509
  (8 other events, 210.5 us)

commit v11 on v10

--- a/solution.py
+++ b/solution.py
@@ -325,7 +325,7 @@
         ],
         compiler_params=params(),
         cost_estimate=pl.CostEstimate(
-            flops=pairs * 2 * HD, bytes_accessed=total * HD * 8, transcendentals=pairs
+            flops=pairs * 8 * HD, bytes_accessed=total * HD * 8, transcendentals=pairs
         ),
     )(cls, counts, got, keys, values)
 
@@ -491,12 +491,12 @@
         return lax.ppermute(part, "ctx", [(d, d ^ bit) for d in range(ctx_size)])
 
     core, side = me & 1, (me >> 1) & 1
-    sizes = [1, 1, 1, 3]
+    sizes = [2, 2, 2]
 
     def at_side(left, right):
         return jnp.where(side == 0, left, right)
 
-    lows = [at_side(0, 6), at_side(1, 7), at_side(2, 5), at_side(3, 2)]
+    lows = [at_side(0, 6), at_side(2, 4), at_side(4, 2)]
 
     def weight_rows(p):
         return lax.dynamic_slice(
@@ -513,28 +513,23 @@
     if traded:
         key_packed, out_weight = lax.optimization_barrier((key_packed, out_weight))
         first_slice, value = lax.optimization_barrier((weight_rows(0), value))
-        slices = [first_slice] + [weight_rows(p) for p in range(1, 4)]
+        slices = [first_slice] + [weight_rows(p) for p in range(1, 3)]
     key_parts = [send_across(key_packed)]
     value_packed, key_parts, slices = lax.optimization_barrier(
         (pack_shared(value, False), key_parts, slices)
     )
     key_parts = swap(key_parts, bits[0])
     value_parts = [send_across(value_packed)]
-    came = []
-    if traded:
-        q_slots, came, slices = lax.optimization_barrier((q_slots, [trade(slices[0])], slices))
-        came = came + [trade(slices[1])]
+    came = [trade(slices[0])] if traded else []
     packed_q = list(pack(q_slots, cosine, sine, query, True, chunks, classes, cap))
-    packed_q[0], key_parts, value_parts = lax.optimization_barrier(
-        (packed_q[0], key_parts, value_parts)
+    packed_q[0], key_parts, value_parts, came, slices = lax.optimization_barrier(
+        (packed_q[0], key_parts, value_parts, came, slices)
     )
+    came = came + [trade(one) for one in slices[1:2]]
     got_q = [send_query(packed_q[0])]
     value_parts = swap(value_parts, bits[0])
     for bit in bits[1:]:
         key_parts = swap(key_parts, bit)
-    if traded:
-        key_parts, came, slices = lax.optimization_barrier((key_parts, came, slices))
-        came = came + [trade(slices[2])]
     keys = compact(member, kept_count, key_parts, offsets, total, True)
     if chunks > 1:
         packed_q[1], value_parts, keys = lax.optimization_barrier((packed_q[1], value_parts, keys))
@@ -543,8 +538,8 @@
     got_q = got_q + [send_query(packed) for packed in packed_q[1:]]
     if traded:
         value_parts, came, slices = lax.optimization_barrier((value_parts, came, slices))
-        joined = jnp.concatenate(came[:2], axis=0)
-        came = [joined, came[2], trade(slices[3]), chip_swap(joined, 2)]
+        crossed = [chip_swap(part, 1) for part in came]
+        came = came + [trade(slices[2]), chip_swap(came[0], 2)]
     values = compact(member, kept_count, value_parts, offsets, total, False)
 
     got, done = [], None
@@ -559,9 +554,9 @@
     got.append(lax.all_to_all(done, "ctx", split_axis=0, concat_axis=0, tiled=True))
     if traded:
         theirs = [trade(one) for one in got]
-        came = came + [chip_swap(part, 1) for part in came]
+        came = came + crossed + [chip_swap(part, 1) for part in came[2:]]
         own = project(tp_me * columns, got, out_weight, columns, classes)
-        order = [lows[0], lows[2], lows[3], at_side(6, 0)]
+        order = lows + [at_side(6, 0)]
         first_heads = jnp.stack([c * 8 + at for c in (core, 1 - core) for at in order])
         return join(first_heads.astype(jnp.int32), theirs, came, own)
     full = project(jnp.int32(0) * tp_me, got, out_weight, columns * tp_size, classes)

time: 274 us -> 303 us (1.11)
  waiting for transfers between devices: 105 us -> 142 us
    ppermute x6, waiting for transfers between devices: 12.2 us -> 42.4 us  [swap(): return parts + [lax.ppermute(part, 'ctx', pairs) for part in parts]]
    all_to_all x2, waiting for transfers between devices: 0.01 us -> 17.3 us  [local(): lax.all_to_all(done, 'ctx', split_axis=0, concat_axis=0, tiled=True)]
    ppermute x6 -> x5, waiting for transfers between devices: 83.1 us -> 69.8 us  [trade(): return lax.ppermute(part, 'tp', both)]
    ppermute x6 -> x5, starting transfers between devices: 9.25 us -> 5.63 us  [trade(): return lax.ppermute(part, 'tp', both)]
    dynamic_slice x2 -> x1, local copies, waits for them, and re-layouts: 7.5 us -> 5.78 us  [weight_rows(): lax.dynamic_slice(out_weight, ((core * 8 + lows[p]) * HD, (1 - tp_me) * c...]
  transfers between devices with their start and end apart: 23 -> 22, of which waited for: 12 -> 12; matrix products, arithmetic and copies ran while one was open for 4% -> 2% of each run, Pallas kernels for 32% -> 29%
where the time goes in v11:
time: 303 us; the launch traced here: 302 us
  waiting for transfers between devices  142 us (47%)
  Pallas kernels  107 us (35%)
  starting transfers between devices  41.8 us (14%)
  local copies, waits for them, and re-layouts  8.7 us (3%)
    ppermute x5, waiting for transfers between devices, trade(): return lax.ppermute(part, 'tp', both)  69.8 us
    pallas_call x2, Pallas kernels, attend(): pl.pallas_call(functools.partial(attend_kernel, ctx_size, block), in_spec...  50.9 us
    ppermute x6, waiting for transfers between devices, swap(): return parts + [lax.ppermute(part, 'ctx', pairs) for part in parts]  42.4 us
    all_to_all x2, waiting for transfers between devices, local(): lax.all_to_all(done, 'ctx', split_axis=0, concat_axis=0, tiled=True)  17.3 us
    pallas_call x3, Pallas kernels, pack(): pl.pallas_call(functools.partial(pack_kernel, turned, classes, cap, width...  15.4 us
    pallas_call x1, Pallas kernels, join(): pl.pallas_call(functools.partial(join_kernel, len(got), len(weights)), gr...  15.1 us
    pallas_call x1, Pallas kernels, project(): pl.pallas_call(functools.partial(project_kernel, classes, len(got)), grid...  13.9 us
    all_to_all x2, waiting for transfers between devices, send_across(): lax.all_to_all(packed, 'ctx', split_axis=0, concat_axis=0, tiled=True, ax...  12.4 us
  transfers between devices with their start and end apart: 22, of which 12 were waited for; matrix products, arithmetic and copies ran while one was open for 2% of the time, Pallas kernels for 29%

profile of v11, /device:TPU:0, one launch (start us, length us, event | category | flops | bytes accessed | tf_op | source)
XLA Modules:
  0.0 301.8 jit_solution(7863702759624948806)
XLA Ops:
  4.1 3.5 %shard_map.66 = bf16[4,1,784,128]{3,2,1,0:T(8,128)(2,1)} custom-call(s32[1,768]{1,0:T(1,128)} %get-tuple-element.47.slot_ref, f32[768,128]{1,0:T(8,128)} %get-tuple-element.87.cos_ref, f32[768,128]{1,0:T(8,128)} %get-tuple-element.86.sin_ref, bf16[768,512]{1,0:T(8,128)(2,1)} %row_ref.3), custom_call_target="tpu_custom_call" | custom-call | flops 616562688 | bytes 1572864 | tf_op jit(solution)/shard_map/pallas_call | solution.py:124
  7.6 6.3 %all-to-all-start = ((bf16[4,784,128]{2,1,0:T(8,128)(2,1)}), bf16[4,784,128]{2,1,0:T(8,128)(2,1)S(1)}, u32[]{:S(2)}, u32[]{:S(2)}) async-start(bf16[4,784,128]{2,1,0:T(8,128)(2,1)} %bitcast.15), calls=%async_computation | async-start | bytes 1605632 | tf_op jit(solution)/shard_map/all_to_all | solution.py:469
  13.9 5.8 %fusion.4 = (bf16[256,4096]{1,0:T(8,128)(2,1)}, bf16[256,4096]{1,0:T(8,128)(2,1)}, bf16[256,4096]{1,0:T(8,128)(2,1)}) fusion(bf16[2048,8192]{1,0:T(8,128)(2,1)} %rest_2_, s32[]{:T(128)S(6)} %select_n.53, s32[]{:T(128)S(6)} %select_n.51, s32[]{:T(128)S(6)} %select_n.52, s32[]{:T(128)S(6)} %select_n.50), kind=kLoop, calls=%fused_computation.11 | loop fusion | bytes 12582928 | tf_op jit(solution)/shard_map/dynamic_slice | solution.py:502
  19.7 3.2 %shard_map.67 = bf16[4,1,784,128]{3,2,1,0:T(8,128)(2,1)} custom-call(s32[1,768]{1,0:T(1,128)} %get-tuple-element.47.slot_ref, f32[768,128]{1,0:T(8,128)} %get-tuple-element.87.cos_ref, f32[768,128]{1,0:T(8,128)} %get-tuple-element.86.sin_ref, bf16[768,512]{1,0:T(8,128)(2,1)} %row_ref.4), custom_call_target="tpu_custom_call" | custom-call | flops 616562688 | bytes 1572864 | tf_op jit(solution)/shard_map/pallas_call | solution.py:124
  22.8 11.5 %all-to-all-done.rest_0_ = bf16[4,784,128]{2,1,0:T(8,128)(2,1)S(1)} async-done(((bf16[4,784,128]{2,1,0:T(8,128)(2,1)}), bf16[4,784,128]{2,1,0:T(8,128)(2,1)S(1)}, u32[]{:S(2)}, u32[]{:S(2)}) %all-to-all-start) | async-done | bytes 802848 | tf_op jit(solution)/shard_map/all_to_all | solution.py:469
  35.9 3.5 %all-to-all-start.1 = ((bf16[4,784,128]{2,1,0:T(8,128)(2,1)}), bf16[4,784,128]{2,1,0:T(8,128)(2,1)S(1)}, u32[]{:S(2)}, u32[]{:S(2)}) async-start(bf16[4,784,128]{2,1,0:T(8,128)(2,1)} %bitcast.16), calls=%async_computation.1 | async-start | bytes 1605632 | tf_op jit(solution)/shard_map/all_to_all | solution.py:469
  40.9 8.7 %shard_map.65 = (bf16[16,1,400,128]{3,2,1,0:T(8,128)(2,1)}, bf16[16,1,400,128]{3,2,1,0:T(8,128)(2,1)}) custom-call(s32[1,768]{1,0:T(1,128)} %get-tuple-element.44.slot_ref, f32[768,128]{1,0:T(8,128)} %get-tuple-element.87.cos_ref, f32[768,128]{1,0:T(8,128)} %get-tuple-element.86.sin_ref, bf16[768,2048]{1,0:T(8,128)(2,1)} %row_ref.2), custom_call_target="tpu_custom_call" | custom-call | flops 2516582400 | bytes 6291456 | tf_op jit(solution)/shard_map/pallas_call | solution.py:124
  49.6 8.5 %collective-permute-done.rest_1_ = bf16[4,784,128]{2,1,0:T(8,128)(2,1)} collective-permute-done((bf16[4,784,128]{2,1,0:T(8,128)(2,1)S(1)}, bf16[4,784,128]{2,1,0:T(8,128)(2,1)}, u32[]{:S(2)}, u32[]{:S(2)}) %collective-permute-start) | collective-permute-done | bytes 802848 | tf_op jit(solution)/shard_map/ppermute | solution.py:475
  59.0 22.2 %collective-permute-done.1.rest_2_ = bf16[256,4096]{1,0:T(8,128)(2,1)} collective-permute-done((bf16[256,4096]{1,0:T(8,128)(2,1)}, bf16[256,4096]{1,0:T(8,128)(2,1)}, u32[]{:S(2)}, u32[]{:S(2)}) %collective-permute-start.1) | collective-permute-done | bytes 2097184 | tf_op jit(solution)/shard_map/ppermute | solution.py:509
  81.2 3.7 %all-to-all-start.3 = ((bf16[16,400,128]{2,1,0:T(8,128)(2,1)}), bf16[16,400,128]{2,1,0:T(8,128)(2,1)S(1)}, u32[]{:S(2)}, u32[]{:S(2)}) async-start(bf16[16,400,128]{2,1,0:T(8,128)(2,1)} %bitcast.17), calls=%async_computation.3 | async-start | bytes 3276800 | tf_op jit(solution)/shard_map/all_to_all | solution.py:483
  88.8 4.7 %shard_map.68.key_ref = bf16[128,6144]{1,0:T(8,128)(2,1)} custom-call(s32[1]{0:T(128)} %bitcast.11.member_ref, s32[16]{0:T(128)} %count_ref.9, bf16[4,784,128]{2,1,0:T(8,128)(2,1)} %copy-done, bf16[4,784,128]{2,1,0:T(8,128)(2,1)} %collective-permute-done.rest_1_, bf16[4,784,128]{2,1,0:T(8,128)(2,1)} %collective-permute-done.3.rest_2_, ...), custom_call_target="tpu_custom_call" | custom-call | flops 6291456 | bytes 6291456 | tf_op jit(solution)/shard_map/pallas_call | solution.py:196
  93.5 29.3 %collective-permute-done.2.rest_1_ = bf16[4,784,128]{2,1,0:T(8,128)(2,1)} collective-permute-done((bf16[4,784,128]{2,1,0:T(8,128)(2,1)S(1)}, bf16[4,784,128]{2,1,0:T(8,128)(2,1)}, u32[]{:S(2)}, u32[]{:S(2)}) %collective-permute-start.2) | collective-permute-done | bytes 802848 | tf_op jit(solution)/shard_map/ppermute | solution.py:475
  122.9 4.8 %all-to-all-start.2 = ((bf16[16,400,128]{2,1,0:T(8,128)(2,1)}), bf16[16,400,128]{2,1,0:T(8,128)(2,1)}, u32[]{:S(2)}, u32[]{:S(2)}) async-start(bf16[16,400,128]{2,1,0:T(8,128)(2,1)} %bitcast.12), calls=%async_computation.2 | async-start | bytes 3276800 | tf_op jit(solution)/shard_map/all_to_all | solution.py:483
  129.7 2.7 collective-permute-done.5.rest_2_
  132.9 43.0 %collective-permute-done.7.rest_3_ = bf16[256,4096]{1,0:T(8,128)(2,1)} collective-permute-done((bf16[256,4096]{1,0:T(8,128)(2,1)}, bf16[256,4096]{1,0:T(8,128)(2,1)}, u32[]{:S(2)}, u32[]{:S(2)}) %collective-permute-start.7) | collective-permute-done | bytes 2097184 | tf_op jit(solution)/shard_map/ppermute | solution.py:509
  179.0 5.2 %shard_map.69.value_ref = bf16[6144,256]{1,0:T(8,128)(2,1)} custom-call(s32[1]{0:T(128)} %bitcast.11.member_ref, s32[16]{0:T(128)} %count_ref.9, bf16[4,784,128]{2,1,0:T(8,128)(2,1)} %copy-done.1, bf16[4,784,128]{2,1,0:T(8,128)(2,1)} %collective-permute-done.2.rest_1_, bf16[4,784,128]{2,1,0:T(8,128)(2,1)} %copy-done.6, bf16[4,784,128]{2,1,0:T(8,128)(2,1)} %copy-done.7), custom_call_target="tpu_custom_call" | custom-call | flops 6291456 | bytes 6291456 | tf_op jit(solution)/shard_map/pallas_call | solution.py:196
  184.3 25.4 %shard_map.70 = bf16[16,192,128]{2,1,0:T(8,128)(2,1)} custom-call(s32[1]{0:T(128)} %constant.58.clone.1.cls_ref, s32[16]{0:T(128)} %count_ref.9, bf16[16,400,128]{2,1,0:T(8,128)(2,1)} %copy-done.5, bf16[128,6144]{1,0:T(8,128)(2,1)} %shard_map.68.key_ref, bf16[6144,256]{1,0:T(8,128)(2,1)} %shard_map.69.value_ref), custom_call_target="tpu_custom_call" | custom-call | flops 9663676416 | bytes 6291456 | tf_op jit(solution)/shard_map/pallas_call | solution.py:312
  209.6 4.6 %all-to-all-start.4 = ((bf16[16,192,128]{2,1,0:T(8,128)(2,1)}), bf16[16,192,128]{2,1,0:T(8,128)(2,1)S(1)}, u32[]{:S(2)}, u32[]{:S(2)}) async-start(bf16[16,192,128]{2,1,0:T(8,128)(2,1)} %shard_map.70), calls=%async_computation.4 | async-start | bytes 1572864 | tf_op jit(solution)/shard_map/all_to_all | solution.py:550
  214.7 25.5 %shard_map.71 = bf16[16,192,128]{2,1,0:T(8,128)(2,1)} custom-call(s32[1]{0:T(128)} %constant.20.clone.1.cls_ref, s32[16]{0:T(128)} %count_ref.9, bf16[16,400,128]{2,1,0:T(8,128)(2,1)} %all-to-all-done.2.got_ref, bf16[128,6144]{1,0:T(8,128)(2,1)} %shard_map.68.key_ref, bf16[6144,256]{1,0:T(8,128)(2,1)} %shard_map.69.value_ref), custom_call_target="tpu_custom_call" | custom-call | flops 9663676416 | bytes 6291456 | tf_op jit(solution)/shard_map/pallas_call | solution.py:312
  241.6 5.7 %all-to-all-start.5 = ((bf16[16,192,128]{2,1,0:T(8,128)(2,1)}), bf16[16,192,128]{2,1,0:T(8,128)(2,1)S(1)}, u32[]{:S(2)}, u32[]{:S(2)}) async-start(bf16[16,192,128]{2,1,0:T(8,128)(2,1)} %shard_map.71), calls=%async_computation.5 | async-start | bytes 1572864 | tf_op jit(solution)/shard_map/all_to_all | solution.py:554
  248.8 17.3 %all-to-all-done.5.rest_1_ = bf16[16,192,128]{2,1,0:T(8,128)(2,1)S(1)} async-done(((bf16[16,192,128]{2,1,0:T(8,128)(2,1)}), bf16[16,192,128]{2,1,0:T(8,128)(2,1)S(1)}, u32[]{:S(2)}, u32[]{:S(2)}) %all-to-all-start.5) | async-done | bytes 786464 | tf_op jit(solution)/shard_map/all_to_all | solution.py:554
  267.3 13.9 %shard_map.72.rest_10_ = bf16[384,4096]{1,0:T(8,128)(2,1)} custom-call(s32[1]{0:T(128)} %bitcast.14.column_ref, bf16[16,192,128]{2,1,0:T(8,128)(2,1)} %copy-done.2, bf16[16,192,128]{2,1,0:T(8,128)(2,1)} %copy-done.3, bf16[2048,8192]{1,0:T(8,128)(2,1)} %rest_2_), custom_call_target="tpu_custom_call" | custom-call | flops 6442450944 | bytes 16777216 | tf_op jit(solution)/shard_map/pallas_call | solution.py:354
  281.2 4.6 %collective-permute-done.11.rest_1_ = bf16[16,192,128]{2,1,0:T(8,128)(2,1)S(1)} collective-permute-done((bf16[16,192,128]{2,1,0:T(8,128)(2,1)S(1)}, bf16[16,192,128]{2,1,0:T(8,128)(2,1)S(1)}, u32[]{:S(2)}, u32[]{:S(2)}) %collective-permute-start.11) | collective-permute-done | bytes 786464 | tf_op jit(solution)/shard_map/ppermute | solution.py:509
  286.7 15.1 %shard_map.73 = bf16[384,4096]{1,0:T(8,128)(2,1)} custom-call(s32[8]{0:T(128)} %stack.35.head_ref, bf16[16,192,128]{2,1,0:T(8,128)(2,1)} %copy-done.8, bf16[16,192,128]{2,1,0:T(8,128)(2,1)} %copy-done.9, bf16[256,4096]{1,0:T(8,128)(2,1)} %collective-permute-done.1.rest_2_, bf16[256,4096]{1,0:T(8,128)(2,1)} %collective-permute-done.7.rest_3_, ...), custom_call_target="tpu_custom_call" | custom-call | flops 6442450944 | bytes 16777216 | tf_op jit(solution)/shard_map/pallas_call | solution.py:403
  (56 shorter events, 22.9 us)
Async XLA Ops:
  7.6 26.8 %all-to-all-start = ((bf16[4,784,128]{2,1,0:T(8,128)(2,1)}), bf16[4,784,128]{2,1,0:T(8,128)(2,1)S(1)}, u32[]{:S(2)}, u32[]{:S(2)}) async-start(bf16[4,784,128]{2,1,0:T(8,128)(2,1)} %bitcast.15), calls=%async_computation | async-start | bytes 1605632 | tf_op jit(solution)/shard_map/all_to_all | solution.py:469
  34.3 50.6 %copy-start = (bf16[4,784,128]{2,1,0:T(8,128)(2,1)}, bf16[4,784,128]{2,1,0:T(8,128)(2,1)S(1)}, u32[]{:S(2)}) copy-start(bf16[4,784,128]{2,1,0:T(8,128)(2,1)S(1)} %all-to-all-done.rest_0_) | copy-start | bytes 2408452
  34.3 46.9 %collective-permute-start.1 = (bf16[256,4096]{1,0:T(8,128)(2,1)}, bf16[256,4096]{1,0:T(8,128)(2,1)}, u32[]{:S(2)}, u32[]{:S(2)}) collective-permute-start(bf16[256,4096]{1,0:T(8,128)(2,1)} %get-tuple-element.54), channel_id=1, source_target_pairs={{0,1},{1,0},{2,3},{3,2},{4,5},{5,4},{6,7},{7,6},{8,9},{9,8},{10,11... | collective-permute-start | bytes 6291464 | tf_op jit(solution)/shard_map/ppermute | solution.py:509
  35.9 23.2 %all-to-all-start.1 = ((bf16[4,784,128]{2,1,0:T(8,128)(2,1)}), bf16[4,784,128]{2,1,0:T(8,128)(2,1)S(1)}, u32[]{:S(2)}, u32[]{:S(2)}) async-start(bf16[4,784,128]{2,1,0:T(8,128)(2,1)} %bitcast.16), calls=%async_computation.1 | async-start | bytes 1605632 | tf_op jit(solution)/shard_map/all_to_all | solution.py:469
  39.4 18.8 %collective-permute-start = (bf16[4,784,128]{2,1,0:T(8,128)(2,1)S(1)}, bf16[4,784,128]{2,1,0:T(8,128)(2,1)}, u32[]{:S(2)}, u32[]{:S(2)}) collective-permute-start(bf16[4,784,128]{2,1,0:T(8,128)(2,1)S(1)} %all-to-all-done.rest_0_), channel_id=1, source_target_pairs={{0,4},{2,6},{4,0},{6,2},{8,12},{10,14},{12,8},{14,10},{16,20},{18,... | collective-permute-start | bytes 2408456 | tf_op jit(solution)/shard_map/ppermute | solution.py:475
  59.0 70.2 %copy-start.1 = (bf16[4,784,128]{2,1,0:T(8,128)(2,1)}, bf16[4,784,128]{2,1,0:T(8,128)(2,1)S(1)}, u32[]{:S(2)}) copy-start(bf16[4,784,128]{2,1,0:T(8,128)(2,1)S(1)} %all-to-all-done.1.rest_0_) | copy-start | bytes 2408452
  81.2 41.6 %all-to-all-start.3 = ((bf16[16,400,128]{2,1,0:T(8,128)(2,1)}), bf16[16,400,128]{2,1,0:T(8,128)(2,1)S(1)}, u32[]{:S(2)}, u32[]{:S(2)}) async-start(bf16[16,400,128]{2,1,0:T(8,128)(2,1)} %bitcast.17), calls=%async_computation.3 | async-start | bytes 3276800 | tf_op jit(solution)/shard_map/all_to_all | solution.py:483
  85.0 2.5 collective-permute-start.3
  85.3 3.5 %collective-permute-start.4 = (bf16[4,784,128]{2,1,0:T(8,128)(2,1)}, bf16[4,784,128]{2,1,0:T(8,128)(2,1)}, u32[]{:S(2)}, u32[]{:S(2)}) collective-permute-start(bf16[4,784,128]{2,1,0:T(8,128)(2,1)} %collective-permute-done.rest_1_), channel_id=1, source_target_pairs={{0,2},{2,0},{4,6},{6,4},{8,10},{10,8},{12,14},{14,12},{16,18},{18,... | collective-permute-start | bytes 2408456 | tf_op jit(solution)/shard_map/ppermute | solution.py:475
  85.6 37.3 %collective-permute-start.2 = (bf16[4,784,128]{2,1,0:T(8,128)(2,1)S(1)}, bf16[4,784,128]{2,1,0:T(8,128)(2,1)}, u32[]{:S(2)}, u32[]{:S(2)}) collective-permute-start(bf16[4,784,128]{2,1,0:T(8,128)(2,1)S(1)} %all-to-all-done.1.rest_0_), channel_id=1, source_target_pairs={{0,4},{2,6},{4,0},{6,2},{8,12},{10,14},{12,8},{14,10},{16,20},{18,... | collective-permute-start | bytes 2408456 | tf_op jit(solution)/shard_map/ppermute | solution.py:475
  122.9 86.8 %all-to-all-start.2 = ((bf16[16,400,128]{2,1,0:T(8,128)(2,1)}), bf16[16,400,128]{2,1,0:T(8,128)(2,1)}, u32[]{:S(2)}, u32[]{:S(2)}) async-start(bf16[16,400,128]{2,1,0:T(8,128)(2,1)} %bitcast.12), calls=%async_computation.2 | async-start | bytes 3276800 | tf_op jit(solution)/shard_map/all_to_all | solution.py:483
  127.6 48.2 %collective-permute-start.7 = (bf16[256,4096]{1,0:T(8,128)(2,1)}, bf16[256,4096]{1,0:T(8,128)(2,1)}, u32[]{:S(2)}, u32[]{:S(2)}) collective-permute-start(bf16[256,4096]{1,0:T(8,128)(2,1)} %get-tuple-element.66), channel_id=1, source_target_pairs={{0,1},{1,0},{2,3},{3,2},{4,5},{5,4},{6,7},{7,6},{8,9},{9,8},{10,11... | collective-permute-start | bytes 6291464 | tf_op jit(solution)/shard_map/ppermute | solution.py:509
  129.2 3.3 %collective-permute-start.5 = (bf16[4,784,128]{2,1,0:T(8,128)(2,1)S(1)}, bf16[4,784,128]{2,1,0:T(8,128)(2,1)S(1)}, u32[]{:S(2)}, u32[]{:S(2)}) collective-permute-start(bf16[4,784,128]{2,1,0:T(8,128)(2,1)S(1)} %all-to-all-done.1.rest_0_), channel_id=1, source_target_pairs={{0,2},{2,0},{4,6},{6,4},{8,10},{10,8},{12,14},{14,12},{16,18},{18,... | collective-permute-start | bytes 2408456 | tf_op jit(solution)/shard_map/ppermute | solution.py:475
  129.2 3.6 %collective-permute-start.6 = (bf16[4,784,128]{2,1,0:T(8,128)(2,1)}, bf16[4,784,128]{2,1,0:T(8,128)(2,1)S(1)}, u32[]{:S(2)}, u32[]{:S(2)}) collective-permute-start(bf16[4,784,128]{2,1,0:T(8,128)(2,1)} %collective-permute-done.2.rest_1_), channel_id=1, source_target_pairs={{0,2},{2,0},{4,6},{6,4},{8,10},{10,8},{12,14},{14,12},{16,18},{18,... | collective-permute-start | bytes 2408456 | tf_op jit(solution)/shard_map/ppermute | solution.py:475
  175.8 64.4 %collective-permute-start.8 = (bf16[256,4096]{1,0:T(8,128)(2,1)}, bf16[256,4096]{1,0:T(8,128)(2,1)S(1)}, u32[]{:S(2)}, u32[]{:S(2)}) collective-permute-start(bf16[256,4096]{1,0:T(8,128)(2,1)} %get-tuple-element.76), channel_id=1, source_target_pairs={{0,1},{1,0},{2,3},{3,2},{4,5},{5,4},{6,7},{7,6},{8,9},{9,8},{10,11... | collective-permute-start | bytes 6291464 | tf_op jit(solution)/shard_map/ppermute | solution.py:509
  177.4 62.9 %collective-permute-start.9 = (bf16[256,4096]{1,0:T(8,128)(2,1)}, bf16[256,4096]{1,0:T(8,128)(2,1)}, u32[]{:S(2)}, u32[]{:S(2)}) collective-permute-start(bf16[256,4096]{1,0:T(8,128)(2,1)} %collective-permute-done.1.rest_2_), channel_id=1, source_target_pairs={{0,4},{2,6},{4,0},{6,2},{8,12},{10,14},{12,8},{14,10},{16,20},{18,... | collective-permute-start | bytes 6291464 | tf_op jit(solution)/shard_map/ppermute | solution.py:491
  209.6 30.6 %all-to-all-start.4 = ((bf16[16,192,128]{2,1,0:T(8,128)(2,1)}), bf16[16,192,128]{2,1,0:T(8,128)(2,1)S(1)}, u32[]{:S(2)}, u32[]{:S(2)}) async-start(bf16[16,192,128]{2,1,0:T(8,128)(2,1)} %shard_map.70), calls=%async_computation.4 | async-start | bytes 1572864 | tf_op jit(solution)/shard_map/all_to_all | solution.py:550
  214.3 34.5 %collective-permute-start.13 = (bf16[256,4096]{1,0:T(8,128)(2,1)}, bf16[256,4096]{1,0:T(8,128)(2,1)}, u32[]{:S(2)}, u32[]{:S(2)}) collective-permute-start(bf16[256,4096]{1,0:T(8,128)(2,1)} %collective-permute-done.7.rest_3_), channel_id=1, source_target_pairs={{0,2},{2,0},{4,6},{6,4},{8,10},{10,8},{12,14},{14,12},{16,18},{18,... | collective-permute-start | bytes 6291464 | tf_op jit(solution)/shard_map/ppermute | solution.py:491
  241.6 24.5 %all-to-all-start.5 = ((bf16[16,192,128]{2,1,0:T(8,128)(2,1)}), bf16[16,192,128]{2,1,0:T(8,128)(2,1)S(1)}, u32[]{:S(2)}, u32[]{:S(2)}) async-start(bf16[16,192,128]{2,1,0:T(8,128)(2,1)} %shard_map.71), calls=%async_computation.5 | async-start | bytes 1572864 | tf_op jit(solution)/shard_map/all_to_all | solution.py:554
  247.4 33.8 %collective-permute-start.12 = (bf16[256,4096]{1,0:T(8,128)(2,1)}, bf16[256,4096]{1,0:T(8,128)(2,1)}, u32[]{:S(2)}, u32[]{:S(2)}) collective-permute-start(bf16[256,4096]{1,0:T(8,128)(2,1)} %collective-permute-done.1.rest_2_), channel_id=1, source_target_pairs={{0,2},{2,0},{4,6},{6,4},{8,10},{10,8},{12,14},{14,12},{16,18},{18,... | collective-permute-start | bytes 6291464 | tf_op jit(solution)/shard_map/ppermute | solution.py:491
  247.8 33.4 %collective-permute-start.14 = (bf16[256,4096]{1,0:T(8,128)(2,1)}, bf16[256,4096]{1,0:T(8,128)(2,1)}, u32[]{:S(2)}, u32[]{:S(2)}) collective-permute-start(bf16[256,4096]{1,0:T(8,128)(2,1)} %copy-done.4), channel_id=1, source_target_pairs={{0,2},{2,0},{4,6},{6,4},{8,10},{10,8},{12,14},{14,12},{16,18},{18,... | collective-permute-start | bytes 6291464 | tf_op jit(solution)/shard_map/ppermute | solution.py:491
  248.0 33.2 %collective-permute-start.15 = (bf16[256,4096]{1,0:T(8,128)(2,1)}, bf16[256,4096]{1,0:T(8,128)(2,1)}, u32[]{:S(2)}, u32[]{:S(2)}) collective-permute-start(bf16[256,4096]{1,0:T(8,128)(2,1)} %collective-permute-done.9.rest_5_), channel_id=1, source_target_pairs={{0,2},{2,0},{4,6},{6,4},{8,10},{10,8},{12,14},{14,12},{16,18},{18,... | collective-permute-start | bytes 6291464 | tf_op jit(solution)/shard_map/ppermute | solution.py:491
  248.3 32.9 %collective-permute-start.10 = (bf16[16,192,128]{2,1,0:T(8,128)(2,1)S(1)}, bf16[16,192,128]{2,1,0:T(8,128)(2,1)S(1)}, u32[]{:S(2)}, u32[]{:S(2)}) collective-permute-start(bf16[16,192,128]{2,1,0:T(8,128)(2,1)S(1)} %all-to-all-done.4.rest_0_), channel_id=1, source_target_pairs={{0,1},{1,0},{2,3},{3,2},{4,5},{5,4},{6,7},{7,6},{8,9},{9,8},{10,11... | collective-permute-start | bytes 2359304 | tf_op jit(solution)/shard_map/ppermute | solution.py:509
  266.1 19.7 %collective-permute-start.11 = (bf16[16,192,128]{2,1,0:T(8,128)(2,1)S(1)}, bf16[16,192,128]{2,1,0:T(8,128)(2,1)S(1)}, u32[]{:S(2)}, u32[]{:S(2)}) collective-permute-start(bf16[16,192,128]{2,1,0:T(8,128)(2,1)S(1)} %all-to-all-done.5.rest_1_), channel_id=1, source_target_pairs={{0,1},{1,0},{2,3},{3,2},{4,5},{5,4},{6,7},{7,6},{8,9},{9,8},{10,11... | collective-permute-start | bytes 2359304 | tf_op jit(solution)/shard_map/ppermute | solution.py:509
  (8 other events, 137.8 us)

commit v12 on v11

--- a/solution.py
+++ b/solution.py
@@ -11,8 +11,8 @@
 HD = 128
 TOK_DEV = 384
 TILE = 16
-PAD = 128
-CHUNKS = 2
+PAD = 288
+CHUNKS = 3
 
 rope_base = 1000000.0
 masked_score = -1e30
@@ -369,58 +369,6 @@
     )((first_column // step).astype(jnp.int32).reshape(1), *got, weight)
 
 
-def join_kernel(chunks, parts, head_ref, *rest):
-    got_refs, weight_refs = rest[:chunks], rest[chunks : chunks + parts]
-    own_ref, out_ref, rows_ref = rest[chunks + parts :]
-    block = got_refs[0].shape[1]
-    firsts = [sum(ref.shape[0] for ref in weight_refs[:p]) for p in range(parts)]
-
-    @pl.when(pl.program_id(0) == 0)
-    def _():
-        for j, got_ref in enumerate(got_refs):
-            for p in range(parts):
-                for n in range(weight_refs[p].shape[0] // HD):
-                    at = firsts[p] + n * HD
-                    rows_ref[j * block : (j + 1) * block, at : at + HD] = got_ref[head_ref[p] + n]
-
-    total = jnp.zeros(out_ref.shape, jnp.float32)
-    for first, weight_ref in zip(firsts, weight_refs):
-        total = total + jnp.dot(
-            rows_ref[:, first : first + weight_ref.shape[0]],
-            weight_ref[...],
-            preferred_element_type=jnp.float32,
-        )
-    theirs = total.astype(jnp.bfloat16).astype(jnp.float32)
-    out_ref[...] = (own_ref[...].astype(jnp.float32) + theirs).astype(jnp.bfloat16)
-
-
-def join(first_heads, got, weights, own):
-    ctx_size, block, _ = got[0].shape
-    rows, columns = own.shape
-    depth = sum(weight.shape[0] for weight in weights)
-    step = min(512, columns)
-    tile = pl.BlockSpec((rows, step), lambda i, first: (0, i))
-    return pl.pallas_call(
-        functools.partial(join_kernel, len(got), len(weights)),
-        grid_spec=pltpu.PrefetchScalarGridSpec(
-            num_scalar_prefetch=1,
-            grid=(columns // step,),
-            in_specs=[pl.BlockSpec((ctx_size, block, HD), lambda i, first: (0, 0, 0))] * len(got)
-            + [pl.BlockSpec((weight.shape[0], step), lambda i, first: (0, i)) for weight in weights]
-            + [tile],
-            out_specs=tile,
-            scratch_shapes=[pltpu.VMEM((rows, depth), jnp.bfloat16)],
-        ),
-        out_shape=jax.ShapeDtypeStruct((rows, columns), jnp.bfloat16),
-        compiler_params=params(),
-        cost_estimate=pl.CostEstimate(
-            flops=2 * rows * depth * columns,
-            bytes_accessed=2 * depth * columns,
-            transcendentals=0,
-        ),
-    )(first_heads, *got, *weights, own)
-
-
 def tables(query_rows):
     half_dim = HD // 2
     positions = lax.axis_index("ctx") * query_rows + jnp.arange(query_rows, dtype=jnp.int32)
@@ -484,48 +432,15 @@
             packed.reshape(ctx_size, cap, HD), "ctx", split_axis=0, concat_axis=0, tiled=True
         )
 
-    traded = tp_size == 2 and classes == 1 and heads == 16 and chunks == 2
     both = [(0, 1), (1, 0)]
-
-    def chip_swap(part, bit):
-        return lax.ppermute(part, "ctx", [(d, d ^ bit) for d in range(ctx_size)])
-
-    core, side = me & 1, (me >> 1) & 1
-    sizes = [2, 2, 2]
-
-    def at_side(left, right):
-        return jnp.where(side == 0, left, right)
-
-    lows = [at_side(0, 6), at_side(2, 4), at_side(4, 2)]
-
-    def weight_rows(p):
-        return lax.dynamic_slice(
-            out_weight,
-            ((core * 8 + lows[p]) * HD, (1 - tp_me) * columns),
-            (sizes[p] * HD, columns),
-        )
-
-    def trade(part):
-        return lax.ppermute(part, "tp", both)
-
-    key_packed = pack_shared(key, True)
-    slices = []
-    if traded:
-        key_packed, out_weight = lax.optimization_barrier((key_packed, out_weight))
-        first_slice, value = lax.optimization_barrier((weight_rows(0), value))
-        slices = [first_slice] + [weight_rows(p) for p in range(1, 3)]
-    key_parts = [send_across(key_packed)]
-    value_packed, key_parts, slices = lax.optimization_barrier(
-        (pack_shared(value, False), key_parts, slices)
-    )
+    key_parts = [send_across(pack_shared(key, True))]
+    value_packed, key_parts = lax.optimization_barrier((pack_shared(value, False), key_parts))
     key_parts = swap(key_parts, bits[0])
     value_parts = [send_across(value_packed)]
-    came = [trade(slices[0])] if traded else []
     packed_q = list(pack(q_slots, cosine, sine, query, True, chunks, classes, cap))
-    packed_q[0], key_parts, value_parts, came, slices = lax.optimization_barrier(
-        (packed_q[0], key_parts, value_parts, came, slices)
+    packed_q[0], key_parts, value_parts = lax.optimization_barrier(
+        (packed_q[0], key_parts, value_parts)
     )
-    came = came + [trade(one) for one in slices[1:2]]
     got_q = [send_query(packed_q[0])]
     value_parts = swap(value_parts, bits[0])
     for bit in bits[1:]:
@@ -535,11 +450,8 @@
         packed_q[1], value_parts, keys = lax.optimization_barrier((packed_q[1], value_parts, keys))
     for bit in bits[1:]:
         value_parts = swap(value_parts, bit)
-    got_q = got_q + [send_query(packed) for packed in packed_q[1:]]
-    if traded:
-        value_parts, came, slices = lax.optimization_barrier((value_parts, came, slices))
-        crossed = [chip_swap(part, 1) for part in came]
-        came = came + [trade(slices[2]), chip_swap(came[0], 2)]
+    if chunks > 1:
+        got_q.append(send_query(packed_q[1]))
     values = compact(member, kept_count, value_parts, offsets, total, False)
 
     got, done = [], None
@@ -549,16 +461,44 @@
             got_q[j], done = lax.optimization_barrier((got_q[j], done))
             got.append(lax.all_to_all(done, "ctx", split_axis=0, concat_axis=0, tiled=True))
         done = attend(cls_j.reshape(1), kept_count, got_q[j], keys, values, block)
-    if chunks > 1:
-        done, got, came = lax.optimization_barrier((done, got, came))
+        if j > 1:
+            done, got[j - 2] = lax.optimization_barrier((done, got[j - 2]))
+        if j + 2 < chunks:
+            packed_q[j + 2], done = lax.optimization_barrier((packed_q[j + 2], done))
+            got_q.append(send_query(packed_q[j + 2]))
     got.append(lax.all_to_all(done, "ctx", split_axis=0, concat_axis=0, tiled=True))
-    if traded:
-        theirs = [trade(one) for one in got]
-        came = came + crossed + [chip_swap(part, 1) for part in came[2:]]
-        own = project(tp_me * columns, got, out_weight, columns, classes)
-        order = lows + [at_side(6, 0)]
-        first_heads = jnp.stack([c * 8 + at for c in (core, 1 - core) for at in order])
-        return join(first_heads.astype(jnp.int32), theirs, came, own)
+    if tp_size == 2:
+        half = columns // 2
+        came = [
+            [
+                lax.ppermute(
+                    project((1 - tp_me) * columns + n * half, [one], out_weight, half, classes),
+                    "tp",
+                    both,
+                )
+                for n in range(2)
+            ]
+            for one in got
+        ]
+        own = project(tp_me * columns, got, out_weight, columns, classes).astype(jnp.float32)
+        rows = own.shape[0] // chunks
+        return jnp.concatenate(
+            [
+                jnp.concatenate(
+                    [
+                        (own[j * rows : (j + 1) * rows, n * half : (n + 1) * half]
+                            + part.astype(jnp.float32)
+                        ).astype(
+                            jnp.bfloat16
+                        )
+                        for n, part in enumerate(parts)
+                    ],
+                    axis=1,
+                )
+                for j, parts in enumerate(came)
+            ],
+            axis=0,
+        )
     full = project(jnp.int32(0) * tp_me, got, out_weight, columns * tp_size, classes)
     split = jnp.transpose(full.reshape(full.shape[0], tp_size, columns), (1, 0, 2))
     swapped = lax.all_to_all(split, "tp", split_axis=0, concat_axis=0, tiled=True)

time: 303 us -> 329 us (1.086)
  waiting for transfers between devices: 142 us -> 97.1 us
  Pallas kernels: 107 us -> 135 us
  other arithmetic: 2.53 us -> 25.4 us
  blocking collectives: 0 us -> 20.6 us
  local copies, waits for them, and re-layouts: 8.7 us -> 1.77 us
  starting transfers between devices: 41.8 us -> 47.2 us
    ppermute x10 -> x6, waiting for transfers between devices: 69.8 us -> 17.9 us  [local(): lax.ppermute(project((1 - tp_me) * columns + n * half, [one], out_weight,...]
    pallas_call x1 -> x7, Pallas kernels: 13.9 us -> 49 us  [project(): pl.pallas_call(functools.partial(project_kernel, classes, len(got)), grid...]
    all_to_all x2 -> x3, waiting for transfers between devices: 0.01 us -> 24 us  [send_query(): lax.all_to_all(packed.reshape(ctx_size, cap, HD), 'ctx', split_axis=0, co...]
    all_to_all x0 -> x1, blocking collectives: none -> 20.6 us  [local(): lax.all_to_all(done, 'ctx', split_axis=0, concat_axis=0, tiled=True)]
    concatenate x0 -> x1, other arithmetic: none -> 19 us  [local(): jnp.concatenate([jnp.concatenate([(own[j * rows:(j + 1) * rows, n * half:...]
    all_to_all x2, waiting for transfers between devices: 17.3 us -> 0.01 us  [local(): lax.all_to_all(done, 'ctx', split_axis=0, concat_axis=0, tiled=True)]
    pallas_call x1 -> x0, Pallas kernels: 15.1 us -> none  [join(): pl.pallas_call(functools.partial(join_kernel, len(got), len(weights)), gr...]
    pallas_call x2 -> x3, Pallas kernels: 50.9 us -> 58.9 us  [attend(): pl.pallas_call(functools.partial(attend_kernel, ctx_size, block), in_spec...]
  transfers between devices with their start and end apart: 22 -> 19, of which waited for: 12 -> 10; matrix products, arithmetic and copies ran while one was open for 2% -> 1% of each run, Pallas kernels for 29% -> 40%
where the time goes in v12:
time: 329 us; the launch traced here: 327 us
  Pallas kernels  135 us (41%)
  waiting for transfers between devices  97.1 us (30%)
  starting transfers between devices  47.2 us (14%)
  other arithmetic  25.4 us (8%)
  blocking collectives  20.6 us (6%)
    pallas_call x3, Pallas kernels, attend(): pl.pallas_call(functools.partial(attend_kernel, ctx_size, block), in_spec...  58.9 us
    pallas_call x7, Pallas kernels, project(): pl.pallas_call(functools.partial(project_kernel, classes, len(got)), grid...  49 us
    ppermute x6, waiting for transfers between devices, swap(): return parts + [lax.ppermute(part, 'ctx', pairs) for part in parts]  36.9 us
    all_to_all x3, waiting for transfers between devices, send_query(): lax.all_to_all(packed.reshape(ctx_size, cap, HD), 'ctx', split_axis=0, co...  24 us
    all_to_all x1, blocking collectives, local(): lax.all_to_all(done, 'ctx', split_axis=0, concat_axis=0, tiled=True)  20.6 us
    concatenate x1, other arithmetic, local(): jnp.concatenate([jnp.concatenate([(own[j * rows:(j + 1) * rows, n * half:...  19 us
    all_to_all x2, waiting for transfers between devices, send_across(): lax.all_to_all(packed, 'ctx', split_axis=0, concat_axis=0, tiled=True, ax...  18.3 us
    ppermute x6, waiting for transfers between devices, local(): lax.ppermute(project((1 - tp_me) * columns + n * half, [one], out_weight,...  17.9 us
  transfers between devices with their start and end apart: 19, of which 10 were waited for; matrix products, arithmetic and copies ran while one was open for 1% of the time, Pallas kernels for 40%

profile of v12, /device:TPU:0, one launch (start us, length us, event | category | flops | bytes accessed | tf_op | source)
XLA Modules:
  0.0 327.1 jit_solution(8645428673813731512)
XLA Ops:
  7.6 6.3 %all-to-all-start = ((bf16[4,784,128]{2,1,0:T(8,128)(2,1)}), bf16[4,784,128]{2,1,0:T(8,128)(2,1)S(1)}, u32[]{:S(2)}, u32[]{:S(2)}) async-start(bf16[4,784,128]{2,1,0:T(8,128)(2,1)} %bitcast.11), calls=%async_computation | async-start | bytes 1605632 | tf_op jit(solution)/shard_map/all_to_all | solution.py:417
  17.1 17.3 %all-to-all-done.rest_0_ = bf16[4,784,128]{2,1,0:T(8,128)(2,1)S(1)} async-done(((bf16[4,784,128]{2,1,0:T(8,128)(2,1)}), bf16[4,784,128]{2,1,0:T(8,128)(2,1)S(1)}, u32[]{:S(2)}, u32[]{:S(2)}) %all-to-all-start) | async-done | bytes 802848 | tf_op jit(solution)/shard_map/all_to_all | solution.py:417
  39.4 8.8 %shard_map.65 = (bf16[16,1,272,128]{3,2,1,0:T(8,128)(2,1)}, bf16[16,1,272,128]{3,2,1,0:T(8,128)(2,1)}, bf16[16,1,272,128]{3,2,1,0:T(8,128)(2,1)}) custom-call(s32[1,768]{1,0:T(1,128)} %get-tuple-element.28.slot_ref, f32[768,128]{1,0:T(8,128)} %get-tuple-element.58.cos_ref, f32[768,128]{1,0:T(8,128)} %get-tuple-element.57.sin_ref, bf16[768,2048]{1,0:T(8,128)(2,1)} %row_ref.3), custom_call_target="tpu_custom_call" | custom-call | flops 2566914048 | bytes 6291456 | tf_op jit(solution)/shard_map/pallas_call | solution.py:124
  48.2 8.6 %collective-permute-done.rest_1_ = bf16[4,784,128]{2,1,0:T(8,128)(2,1)S(1)} collective-permute-done((bf16[4,784,128]{2,1,0:T(8,128)(2,1)S(1)}, bf16[4,784,128]{2,1,0:T(8,128)(2,1)S(1)}, u32[]{:S(2)}, u32[]{:S(2)}) %collective-permute-start) | collective-permute-done | bytes 802848 | tf_op jit(solution)/shard_map/ppermute | solution.py:423
  57.8 4.8 %all-to-all-start.2 = ((bf16[16,272,128]{2,1,0:T(8,128)(2,1)}), bf16[16,272,128]{2,1,0:T(8,128)(2,1)S(1)}, u32[]{:S(2)}, u32[]{:S(2)}) async-start(bf16[16,272,128]{2,1,0:T(8,128)(2,1)} %bitcast.12), calls=%async_computation.2 | async-start | bytes 2228224 | tf_op jit(solution)/shard_map/all_to_all | solution.py:431
  71.0 23.9 %collective-permute-done.1.rest_1_ = bf16[4,784,128]{2,1,0:T(8,128)(2,1)} collective-permute-done((bf16[4,784,128]{2,1,0:T(8,128)(2,1)S(1)}, bf16[4,784,128]{2,1,0:T(8,128)(2,1)}, u32[]{:S(2)}, u32[]{:S(2)}) %collective-permute-start.1) | collective-permute-done | bytes 802848 | tf_op jit(solution)/shard_map/ppermute | solution.py:423
  104.3 5.2 %shard_map.69.value_ref = bf16[6144,256]{1,0:T(8,128)(2,1)} custom-call(s32[1]{0:T(128)} %bitcast.5.member_ref, s32[16]{0:T(128)} %count_ref.11, bf16[4,784,128]{2,1,0:T(8,128)(2,1)} %copy-done.2, bf16[4,784,128]{2,1,0:T(8,128)(2,1)} %collective-permute-done.1.rest_1_, bf16[4,784,128]{2,1,0:T(8,128)(2,1)} %copy-done.7, bf16[4,784,128]{2,1,0:T(8,128)(2,1)} %copy-done.8), custom_call_target="tpu_custom_call" | custom-call | flops 6291456 | bytes 6291456 | tf_op jit(solution)/shard_map/pallas_call | solution.py:196
  109.5 19.6 %shard_map.70 = bf16[16,128,128]{2,1,0:T(8,128)(2,1)} custom-call(s32[1]{0:T(128)} %constant.69.clone.1.cls_ref, s32[16]{0:T(128)} %count_ref.11, bf16[16,272,128]{2,1,0:T(8,128)(2,1)} %copy-done.4, bf16[128,6144]{1,0:T(8,128)(2,1)} %shard_map.68.key_ref, bf16[6144,256]{1,0:T(8,128)(2,1)} %shard_map.69.value_ref), custom_call_target="tpu_custom_call" | custom-call | flops 6442450944 | bytes 6291456 | tf_op jit(solution)/shard_map/pallas_call | solution.py:312
  129.1 6.0 %all-to-all-start.3 = ((bf16[16,272,128]{2,1,0:T(8,128)(2,1)}), bf16[16,272,128]{2,1,0:T(8,128)(2,1)S(1)}, u32[]{:S(2)}, u32[]{:S(2)}) async-start(bf16[16,272,128]{2,1,0:T(8,128)(2,1)} %bitcast.6), calls=%async_computation.3 | async-start | bytes 2228224 | tf_op jit(solution)/shard_map/all_to_all | solution.py:431
  135.1 24.0 %all-to-all-done.3.got_ref = bf16[16,272,128]{2,1,0:T(8,128)(2,1)S(1)} async-done(((bf16[16,272,128]{2,1,0:T(8,128)(2,1)}), bf16[16,272,128]{2,1,0:T(8,128)(2,1)S(1)}, u32[]{:S(2)}, u32[]{:S(2)}) %all-to-all-start.3) | async-done | bytes 1114144 | tf_op jit(solution)/shard_map/all_to_all | solution.py:431
  159.1 7.2 %all-to-all-start.5 = ((bf16[16,128,128]{2,1,0:T(8,128)(2,1)}), bf16[16,128,128]{2,1,0:T(8,128)(2,1)S(1)}, u32[]{:S(2)}, u32[]{:S(2)}) async-start(bf16[16,128,128]{2,1,0:T(8,128)(2,1)} %shard_map.70), calls=%async_computation.5 | async-start | bytes 1048576 | tf_op jit(solution)/shard_map/all_to_all | solution.py:462
  166.3 19.8 %shard_map.71 = bf16[16,128,128]{2,1,0:T(8,128)(2,1)} custom-call(s32[1]{0:T(128)} %constant.71.clone.1.cls_ref, s32[16]{0:T(128)} %count_ref.11, bf16[16,272,128]{2,1,0:T(8,128)(2,1)} %all-to-all-done.4.got_ref, bf16[128,6144]{1,0:T(8,128)(2,1)} %shard_map.68.key_ref, bf16[6144,256]{1,0:T(8,128)(2,1)} %shard_map.69.value_ref), custom_call_target="tpu_custom_call" | custom-call | flops 6442450944 | bytes 6291456 | tf_op jit(solution)/shard_map/pallas_call | solution.py:312
  186.1 19.6 %shard_map.72 = bf16[16,128,128]{2,1,0:T(8,128)(2,1)} custom-call(s32[1]{0:T(128)} %constant.62.clone.1.cls_ref, s32[16]{0:T(128)} %count_ref.11, bf16[16,272,128]{2,1,0:T(8,128)(2,1)} %copy-done.5, bf16[128,6144]{1,0:T(8,128)(2,1)} %shard_map.68.key_ref, bf16[6144,256]{1,0:T(8,128)(2,1)} %shard_map.69.value_ref), custom_call_target="tpu_custom_call" | custom-call | flops 6442450944 | bytes 6291456 | tf_op jit(solution)/shard_map/pallas_call | solution.py:312
  205.6 20.6 %all_to_all.40.rest_2_.rest_0_ = bf16[16,128,128]{2,1,0:T(8,128)(2,1)} all-to-all(bf16[16,128,128]{2,1,0:T(8,128)(2,1)} %shard_map.72), channel_id=1, replica_groups=mesh['ctx'=16,'tp'=2] {'ctx'}, dimensions={0} | all-to-all | bytes 1048576 | tf_op jit(solution)/shard_map/all_to_all | solution.py:469
  230.3 5.9 %shard_map.74 = bf16[128,2048]{1,0:T(8,128)(2,1)} custom-call(s32[1]{0:T(128)} %bitcast.8.column_ref, bf16[16,128,128]{2,1,0:T(8,128)(2,1)} %copy-done, bf16[2048,8192]{1,0:T(8,128)(2,1)} %rest_1_.11), custom_call_target="tpu_custom_call" | custom-call | flops 1073741824 | bytes 8388608 | tf_op jit(solution)/shard_map/pallas_call | solution.py:354
  237.8 5.9 %shard_map.75 = bf16[128,2048]{1,0:T(8,128)(2,1)} custom-call(s32[1]{0:T(128)} %bitcast.9.column_ref, bf16[16,128,128]{2,1,0:T(8,128)(2,1)} %copy-done, bf16[2048,8192]{1,0:T(8,128)(2,1)} %rest_1_.11), custom_call_target="tpu_custom_call" | custom-call | flops 1073741824 | bytes 8388608 | tf_op jit(solution)/shard_map/pallas_call | solution.py:354
  244.1 5.9 %shard_map.78 = bf16[128,2048]{1,0:T(8,128)(2,1)} custom-call(s32[1]{0:T(128)} %bitcast.8.column_ref, bf16[16,128,128]{2,1,0:T(8,128)(2,1)} %all_to_all.40.rest_2_.rest_0_, bf16[2048,8192]{1,0:T(8,128)(2,1)} %rest_1_.11), custom_call_target="tpu_custom_call" | custom-call | flops 1073741824 | bytes 8388608 | tf_op jit(solution)/shard_map/pallas_call | solution.py:354
  251.5 5.9 %shard_map.79 = bf16[128,2048]{1,0:T(8,128)(2,1)} custom-call(s32[1]{0:T(128)} %bitcast.9.column_ref, bf16[16,128,128]{2,1,0:T(8,128)(2,1)} %all_to_all.40.rest_2_.rest_0_, bf16[2048,8192]{1,0:T(8,128)(2,1)} %rest_1_.11), custom_call_target="tpu_custom_call" | custom-call | flops 1073741824 | bytes 8388608 | tf_op jit(solution)/shard_map/pallas_call | solution.py:354
  258.7 5.9 %shard_map.76 = bf16[128,2048]{1,0:T(8,128)(2,1)} custom-call(s32[1]{0:T(128)} %bitcast.8.column_ref, bf16[16,128,128]{2,1,0:T(8,128)(2,1)} %copy-done.1, bf16[2048,8192]{1,0:T(8,128)(2,1)} %rest_1_.11), custom_call_target="tpu_custom_call" | custom-call | flops 1073741824 | bytes 8388608 | tf_op jit(solution)/shard_map/pallas_call | solution.py:354
  266.1 5.9 %shard_map.77 = bf16[128,2048]{1,0:T(8,128)(2,1)} custom-call(s32[1]{0:T(128)} %bitcast.9.column_ref, bf16[16,128,128]{2,1,0:T(8,128)(2,1)} %copy-done.1, bf16[2048,8192]{1,0:T(8,128)(2,1)} %rest_1_.11), custom_call_target="tpu_custom_call" | custom-call | flops 1073741824 | bytes 8388608 | tf_op jit(solution)/shard_map/pallas_call | solution.py:354
  272.5 13.8 %shard_map.73 = bf16[384,4096]{1,0:T(8,128)(2,1)} custom-call(s32[1]{0:T(128)} %bitcast.column_ref, bf16[16,128,128]{2,1,0:T(8,128)(2,1)} %copy-done, bf16[16,128,128]{2,1,0:T(8,128)(2,1)} %copy-done.1, bf16[16,128,128]{2,1,0:T(8,128)(2,1)} %all_to_all.40.rest_2_.rest_0_, bf16[2048,8192]{1,0:T(8,128)(2,1)} %rest_1_.11), custom_call_target="tpu_custom_call" | custom-call | flops 6442450944 | bytes 16777216 | tf_op jit(solution)/shard_map/pallas_call | solution.py:354
  288.9 7.2 %collective-permute-done.8 = bf16[128,2048]{1,0:T(8,128)(2,1)S(1)} collective-permute-done((bf16[128,2048]{1,0:T(8,128)(2,1)}, bf16[128,2048]{1,0:T(8,128)(2,1)S(1)}, u32[]{:S(2)}, u32[]{:S(2)}) %collective-permute-start.8) | collective-permute-done | bytes 524320 | tf_op jit(solution)/shard_map/ppermute | solution.py:474
  296.1 10.7 %collective-permute-done.9 = bf16[128,2048]{1,0:T(8,128)(2,1)S(1)} collective-permute-done((bf16[128,2048]{1,0:T(8,128)(2,1)}, bf16[128,2048]{1,0:T(8,128)(2,1)S(1)}, u32[]{:S(2)}, u32[]{:S(2)}) %collective-permute-start.9) | collective-permute-done | bytes 524320 | tf_op jit(solution)/shard_map/ppermute | solution.py:474
  308.1 19.0 %maximum_maximum_fusion = bf16[384,4096]{1,0:T(8,128)(2,1)} fusion(bf16[128,2048]{1,0:T(8,128)(2,1)S(1)} %get-tuple-element.52, bf16[128,2048]{1,0:T(8,128)(2,1)S(1)} %get-tuple-element.53, bf16[128,2048]{1,0:T(8,128)(2,1)S(1)} %get-tuple-element.54, bf16[128,2048]{1,0:T(8,128)(2,1)S(1)} %get-tuple-element.55, bf16[128,2048]{1,0:T(8,128)(2,1)S(1)} %get-tuple-element.56, ...), kind=kLoop, calls=%fused_computation | loop fusion | flops 18874368 | bytes 6291456 | tf_op jit(solution)/shard_map/concatenate | solution.py:485
  (56 shorter events, 49.5 us)
Async XLA Ops:
  7.6 26.8 %all-to-all-start = ((bf16[4,784,128]{2,1,0:T(8,128)(2,1)}), bf16[4,784,128]{2,1,0:T(8,128)(2,1)S(1)}, u32[]{:S(2)}, u32[]{:S(2)}) async-start(bf16[4,784,128]{2,1,0:T(8,128)(2,1)} %bitcast.11), calls=%async_computation | async-start | bytes 1605632 | tf_op jit(solution)/shard_map/all_to_all | solution.py:417
  34.3 28.2 %copy-start.3 = (bf16[4,784,128]{2,1,0:T(8,128)(2,1)}, bf16[4,784,128]{2,1,0:T(8,128)(2,1)S(1)}, u32[]{:S(2)}) copy-start(bf16[4,784,128]{2,1,0:T(8,128)(2,1)S(1)} %all-to-all-done.rest_0_) | copy-start | bytes 2408452
  34.3 23.4 %all-to-all-start.1 = ((bf16[4,784,128]{2,1,0:T(8,128)(2,1)}), bf16[4,784,128]{2,1,0:T(8,128)(2,1)S(1)}, u32[]{:S(2)}, u32[]{:S(2)}) async-start(bf16[4,784,128]{2,1,0:T(8,128)(2,1)} %bitcast.10), calls=%async_computation.1 | async-start | bytes 1605632 | tf_op jit(solution)/shard_map/all_to_all | solution.py:417
  37.8 18.9 %collective-permute-start = (bf16[4,784,128]{2,1,0:T(8,128)(2,1)S(1)}, bf16[4,784,128]{2,1,0:T(8,128)(2,1)S(1)}, u32[]{:S(2)}, u32[]{:S(2)}) collective-permute-start(bf16[4,784,128]{2,1,0:T(8,128)(2,1)S(1)} %all-to-all-done.rest_0_), channel_id=1, source_target_pairs={{0,4},{2,6},{4,0},{6,2},{8,12},{10,14},{12,8},{14,10},{16,20},{18,... | collective-permute-start | bytes 2408456 | tf_op jit(solution)/shard_map/ppermute | solution.py:423
  57.8 41.9 %copy-start.2 = (bf16[4,784,128]{2,1,0:T(8,128)(2,1)}, bf16[4,784,128]{2,1,0:T(8,128)(2,1)S(1)}, u32[]{:S(2)}) copy-start(bf16[4,784,128]{2,1,0:T(8,128)(2,1)S(1)} %all-to-all-done.1.rest_0_) | copy-start | bytes 2408452
  57.8 37.1 %all-to-all-start.2 = ((bf16[16,272,128]{2,1,0:T(8,128)(2,1)}), bf16[16,272,128]{2,1,0:T(8,128)(2,1)S(1)}, u32[]{:S(2)}, u32[]{:S(2)}) async-start(bf16[16,272,128]{2,1,0:T(8,128)(2,1)} %bitcast.12), calls=%async_computation.2 | async-start | bytes 2228224 | tf_op jit(solution)/shard_map/all_to_all | solution.py:431
  62.6 2.5 collective-permute-start.2
  63.0 3.2 collective-permute-start.3
  63.1 31.8 %collective-permute-start.1 = (bf16[4,784,128]{2,1,0:T(8,128)(2,1)S(1)}, bf16[4,784,128]{2,1,0:T(8,128)(2,1)}, u32[]{:S(2)}, u32[]{:S(2)}) collective-permute-start(bf16[4,784,128]{2,1,0:T(8,128)(2,1)S(1)} %all-to-all-done.1.rest_0_), channel_id=1, source_target_pairs={{0,4},{2,6},{4,0},{6,2},{8,12},{10,14},{12,8},{14,10},{16,20},{18,... | collective-permute-start | bytes 2408456 | tf_op jit(solution)/shard_map/ppermute | solution.py:423
  94.9 14.6 %copy-start.4 = (bf16[16,272,128]{2,1,0:T(8,128)(2,1)}, bf16[16,272,128]{2,1,0:T(8,128)(2,1)S(1)}, u32[]{:S(2)}) copy-start(bf16[16,272,128]{2,1,0:T(8,128)(2,1)S(1)} %all-to-all-done.2.got_ref) | copy-start | bytes 3342340
  94.9 34.2 %all-to-all-start.4 = ((bf16[16,272,128]{2,1,0:T(8,128)(2,1)}), bf16[16,272,128]{2,1,0:T(8,128)(2,1)}, u32[]{:S(2)}, u32[]{:S(2)}) async-start(bf16[16,272,128]{2,1,0:T(8,128)(2,1)} %bitcast.7), calls=%async_computation.4 | async-start | bytes 2228224 | tf_op jit(solution)/shard_map/all_to_all | solution.py:431
  99.6 2.4 collective-permute-start.4
  100.1 3.3 %collective-permute-start.5 = (bf16[4,784,128]{2,1,0:T(8,128)(2,1)}, bf16[4,784,128]{2,1,0:T(8,128)(2,1)S(1)}, u32[]{:S(2)}, u32[]{:S(2)}) collective-permute-start(bf16[4,784,128]{2,1,0:T(8,128)(2,1)} %collective-permute-done.1.rest_1_), channel_id=1, source_target_pairs={{0,2},{2,0},{4,6},{6,4},{8,10},{10,8},{12,14},{14,12},{16,18},{18,... | collective-permute-start | bytes 2408456 | tf_op jit(solution)/shard_map/ppermute | solution.py:423
  129.1 30.0 %all-to-all-start.3 = ((bf16[16,272,128]{2,1,0:T(8,128)(2,1)}), bf16[16,272,128]{2,1,0:T(8,128)(2,1)S(1)}, u32[]{:S(2)}, u32[]{:S(2)}) async-start(bf16[16,272,128]{2,1,0:T(8,128)(2,1)} %bitcast.6), calls=%async_computation.3 | async-start | bytes 2228224 | tf_op jit(solution)/shard_map/all_to_all | solution.py:431
  159.1 27.0 %copy-start.5 = (bf16[16,272,128]{2,1,0:T(8,128)(2,1)}, bf16[16,272,128]{2,1,0:T(8,128)(2,1)S(1)}, u32[]{:S(2)}) copy-start(bf16[16,272,128]{2,1,0:T(8,128)(2,1)S(1)} %all-to-all-done.3.got_ref) | copy-start | bytes 3342340
  159.1 46.5 %all-to-all-start.5 = ((bf16[16,128,128]{2,1,0:T(8,128)(2,1)}), bf16[16,128,128]{2,1,0:T(8,128)(2,1)S(1)}, u32[]{:S(2)}, u32[]{:S(2)}) async-start(bf16[16,128,128]{2,1,0:T(8,128)(2,1)} %shard_map.70), calls=%async_computation.5 | async-start | bytes 1048576 | tf_op jit(solution)/shard_map/all_to_all | solution.py:462
  205.6 24.7 %copy-start = (bf16[16,128,128]{2,1,0:T(8,128)(2,1)}, bf16[16,128,128]{2,1,0:T(8,128)(2,1)S(1)}, u32[]{:S(2)}) copy-start(bf16[16,128,128]{2,1,0:T(8,128)(2,1)S(1)} %all-to-all-done.5.rest_0_) | copy-start | bytes 1572868
  226.2 31.7 %all-to-all-start.6 = ((bf16[16,128,128]{2,1,0:T(8,128)(2,1)}), bf16[16,128,128]{2,1,0:T(8,128)(2,1)S(1)}, u32[]{:S(2)}, u32[]{:S(2)}) async-start(bf16[16,128,128]{2,1,0:T(8,128)(2,1)} %shard_map.71), calls=%async_computation.6 | async-start | bytes 1048576 | tf_op jit(solution)/shard_map/all_to_all | solution.py:462
  236.2 35.8 %collective-permute-start.6 = (bf16[128,2048]{1,0:T(8,128)(2,1)}, bf16[128,2048]{1,0:T(8,128)(2,1)S(1)}, u32[]{:S(2)}, u32[]{:S(2)}) collective-permute-start(bf16[128,2048]{1,0:T(8,128)(2,1)} %shard_map.74), channel_id=1, source_target_pairs={{0,1},{1,0},{2,3},{3,2},{4,5},{5,4},{6,7},{7,6},{8,9},{9,8},{10,11... | collective-permute-start | bytes 1572872 | tf_op jit(solution)/shard_map/ppermute | solution.py:474
  243.6 45.3 %collective-permute-start.7 = (bf16[128,2048]{1,0:T(8,128)(2,1)}, bf16[128,2048]{1,0:T(8,128)(2,1)S(1)}, u32[]{:S(2)}, u32[]{:S(2)}) collective-permute-start(bf16[128,2048]{1,0:T(8,128)(2,1)} %shard_map.75), channel_id=1, source_target_pairs={{0,1},{1,0},{2,3},{3,2},{4,5},{5,4},{6,7},{7,6},{8,9},{9,8},{10,11... | collective-permute-start | bytes 1572872 | tf_op jit(solution)/shard_map/ppermute | solution.py:474
  250.0 38.9 %collective-permute-start.10 = (bf16[128,2048]{1,0:T(8,128)(2,1)}, bf16[128,2048]{1,0:T(8,128)(2,1)S(1)}, u32[]{:S(2)}, u32[]{:S(2)}) collective-permute-start(bf16[128,2048]{1,0:T(8,128)(2,1)} %shard_map.78), channel_id=1, source_target_pairs={{0,1},{1,0},{2,3},{3,2},{4,5},{5,4},{6,7},{7,6},{8,9},{9,8},{10,11... | collective-permute-start | bytes 1572872 | tf_op jit(solution)/shard_map/ppermute | solution.py:474
  257.4 31.5 %collective-permute-start.11 = (bf16[128,2048]{1,0:T(8,128)(2,1)}, bf16[128,2048]{1,0:T(8,128)(2,1)S(1)}, u32[]{:S(2)}, u32[]{:S(2)}) collective-permute-start(bf16[128,2048]{1,0:T(8,128)(2,1)} %shard_map.79), channel_id=1, source_target_pairs={{0,1},{1,0},{2,3},{3,2},{4,5},{5,4},{6,7},{7,6},{8,9},{9,8},{10,11... | collective-permute-start | bytes 1572872 | tf_op jit(solution)/shard_map/ppermute | solution.py:474
  264.6 31.5 %collective-permute-start.8 = (bf16[128,2048]{1,0:T(8,128)(2,1)}, bf16[128,2048]{1,0:T(8,128)(2,1)S(1)}, u32[]{:S(2)}, u32[]{:S(2)}) collective-permute-start(bf16[128,2048]{1,0:T(8,128)(2,1)} %shard_map.76), channel_id=1, source_target_pairs={{0,1},{1,0},{2,3},{3,2},{4,5},{5,4},{6,7},{7,6},{8,9},{9,8},{10,11... | collective-permute-start | bytes 1572872 | tf_op jit(solution)/shard_map/ppermute | solution.py:474
  272.0 34.8 %collective-permute-start.9 = (bf16[128,2048]{1,0:T(8,128)(2,1)}, bf16[128,2048]{1,0:T(8,128)(2,1)S(1)}, u32[]{:S(2)}, u32[]{:S(2)}) collective-permute-start(bf16[128,2048]{1,0:T(8,128)(2,1)} %shard_map.77), channel_id=1, source_target_pairs={{0,1},{1,0},{2,3},{3,2},{4,5},{5,4},{6,7},{7,6},{8,9},{9,8},{10,11... | collective-permute-start | bytes 1572872 | tf_op jit(solution)/shard_map/ppermute | solution.py:474
  (4 other events, 12.6 us)

commit v13 on v12

--- a/solution.py
+++ b/solution.py
@@ -12,7 +12,7 @@
 TOK_DEV = 384
 TILE = 16
 PAD = 288
-CHUNKS = 3
+CHUNKS = 2
 
 rope_base = 1000000.0
 masked_score = -1e30

time: 329 us -> 277 us (0.84)
  blocking collectives: 20.6 us -> 0 us
  Pallas kernels: 135 us -> 118 us
  other arithmetic: 25.4 us -> 20.7 us
  waiting for transfers between devices: 97.1 us -> 92.4 us
  starting transfers between devices: 47.2 us -> 43 us
    all_to_all x3 -> x2, waiting for transfers between devices: 24 us -> 0.01 us  [send_query(): lax.all_to_all(packed.reshape(ctx_size, cap, HD), 'ctx', split_axis=0, co...]
    all_to_all x1 -> x0, blocking collectives: 20.6 us -> none  [local(): lax.all_to_all(done, 'ctx', split_axis=0, concat_axis=0, tiled=True)]
    all_to_all x2, waiting for transfers between devices: 0.01 us -> 10.7 us  [local(): lax.all_to_all(done, 'ctx', split_axis=0, concat_axis=0, tiled=True)]
    pallas_call x7 -> x5, Pallas kernels: 49 us -> 39.4 us  [project(): pl.pallas_call(functools.partial(project_kernel, classes, len(got)), grid...]
    pallas_call x3 -> x2, Pallas kernels: 58.9 us -> 51.4 us  [attend(): pl.pallas_call(functools.partial(attend_kernel, ctx_size, block), in_spec...]
    ppermute x6, waiting for transfers between devices: 36.9 us -> 42.6 us  [swap(): return parts + [lax.ppermute(part, 'ctx', pairs) for part in parts]]
    all_to_all x3 -> x2, starting transfers between devices: 15.4 us -> 10.3 us  [send_query(): lax.all_to_all(packed.reshape(ctx_size, cap, HD), 'ctx', split_axis=0, co...]
    concatenate x1, other arithmetic: 19 us -> 14.2 us  [local(): jnp.concatenate([jnp.concatenate([(own[j * rows:(j + 1) * rows, n * half:...]
  transfers between devices with their start and end apart: 19 -> 16, of which waited for: 10 -> 11; matrix products, arithmetic and copies ran while one was open for 1% -> 1% of each run, Pallas kernels for 40% -> 41%
where the time goes in v13:
time: 277 us; the launch traced here: 276 us
  Pallas kernels  118 us (43%)
  waiting for transfers between devices  92.4 us (33%)
  starting transfers between devices  43 us (16%)
  other arithmetic  20.7 us (7%)
    pallas_call x2, Pallas kernels, attend(): pl.pallas_call(functools.partial(attend_kernel, ctx_size, block), in_spec...  51.4 us
    ppermute x6, waiting for transfers between devices, swap(): return parts + [lax.ppermute(part, 'ctx', pairs) for part in parts]  42.6 us
    pallas_call x5, Pallas kernels, project(): pl.pallas_call(functools.partial(project_kernel, classes, len(got)), grid...  39.4 us
    ppermute x4, waiting for transfers between devices, local(): lax.ppermute(project((1 - tp_me) * columns + n * half, [one], out_weight,...  20.8 us
    all_to_all x2, waiting for transfers between devices, send_across(): lax.all_to_all(packed, 'ctx', split_axis=0, concat_axis=0, tiled=True, ax...  18.3 us
    pallas_call x3, Pallas kernels, pack(): pl.pallas_call(functools.partial(pack_kernel, turned, classes, cap, width...  15.4 us
    concatenate x1, other arithmetic, local(): jnp.concatenate([jnp.concatenate([(own[j * rows:(j + 1) * rows, n * half:...  14.2 us
    all_to_all x2, starting transfers between devices, local(): lax.all_to_all(done, 'ctx', split_axis=0, concat_axis=0, tiled=True)  13.1 us
  transfers between devices with their start and end apart: 16, of which 11 were waited for; matrix products, arithmetic and copies ran while one was open for 1% of the time, Pallas kernels for 41%

profile of v13, /device:TPU:0, one launch (start us, length us, event | category | flops | bytes accessed | tf_op | source)
XLA Modules:
  0.0 275.6 jit_solution(4231296715383774288)
XLA Ops:
  4.1 3.5 %shard_map.67 = bf16[4,1,784,128]{3,2,1,0:T(8,128)(2,1)} custom-call(s32[1,768]{1,0:T(1,128)} %get-tuple-element.24.slot_ref, f32[768,128]{1,0:T(8,128)} %get-tuple-element.42.cos_ref, f32[768,128]{1,0:T(8,128)} %get-tuple-element.41.sin_ref, bf16[768,512]{1,0:T(8,128)(2,1)} %row_ref.5), custom_call_target="tpu_custom_call" | custom-call | flops 616562688 | bytes 1572864 | tf_op jit(solution)/shard_map/pallas_call | solution.py:124
  7.6 6.3 %all-to-all-start = ((bf16[4,784,128]{2,1,0:T(8,128)(2,1)}), bf16[4,784,128]{2,1,0:T(8,128)(2,1)S(1)}, u32[]{:S(2)}, u32[]{:S(2)}) async-start(bf16[4,784,128]{2,1,0:T(8,128)(2,1)} %bitcast.10), calls=%async_computation | async-start | bytes 1605632 | tf_op jit(solution)/shard_map/all_to_all | solution.py:417
  17.1 17.3 %all-to-all-done.rest_0_ = bf16[4,784,128]{2,1,0:T(8,128)(2,1)S(1)} async-done(((bf16[4,784,128]{2,1,0:T(8,128)(2,1)}), bf16[4,784,128]{2,1,0:T(8,128)(2,1)S(1)}, u32[]{:S(2)}, u32[]{:S(2)}) %all-to-all-start) | async-done | bytes 802848 | tf_op jit(solution)/shard_map/all_to_all | solution.py:417
  34.4 3.5 %all-to-all-start.1 = ((bf16[4,784,128]{2,1,0:T(8,128)(2,1)}), bf16[4,784,128]{2,1,0:T(8,128)(2,1)S(1)}, u32[]{:S(2)}, u32[]{:S(2)}) async-start(bf16[4,784,128]{2,1,0:T(8,128)(2,1)} %bitcast.9), calls=%async_computation.1 | async-start | bytes 1605632 | tf_op jit(solution)/shard_map/all_to_all | solution.py:417
  39.4 8.7 %shard_map.65 = (bf16[16,1,400,128]{3,2,1,0:T(8,128)(2,1)}, bf16[16,1,400,128]{3,2,1,0:T(8,128)(2,1)}) custom-call(s32[1,768]{1,0:T(1,128)} %get-tuple-element.21.slot_ref, f32[768,128]{1,0:T(8,128)} %get-tuple-element.42.cos_ref, f32[768,128]{1,0:T(8,128)} %get-tuple-element.41.sin_ref, bf16[768,2048]{1,0:T(8,128)(2,1)} %row_ref.3), custom_call_target="tpu_custom_call" | custom-call | flops 2516582400 | bytes 6291456 | tf_op jit(solution)/shard_map/pallas_call | solution.py:124
  48.1 8.7 %collective-permute-done.rest_1_ = bf16[4,784,128]{2,1,0:T(8,128)(2,1)S(1)} collective-permute-done((bf16[4,784,128]{2,1,0:T(8,128)(2,1)S(1)}, bf16[4,784,128]{2,1,0:T(8,128)(2,1)S(1)}, u32[]{:S(2)}, u32[]{:S(2)}) %collective-permute-start) | collective-permute-done | bytes 802848 | tf_op jit(solution)/shard_map/ppermute | solution.py:423
  57.8 5.6 %all-to-all-start.3 = ((bf16[16,400,128]{2,1,0:T(8,128)(2,1)}), bf16[16,400,128]{2,1,0:T(8,128)(2,1)S(1)}, u32[]{:S(2)}, u32[]{:S(2)}) async-start(bf16[16,400,128]{2,1,0:T(8,128)(2,1)} %bitcast.11), calls=%async_computation.3 | async-start | bytes 3276800 | tf_op jit(solution)/shard_map/all_to_all | solution.py:431
  67.3 4.7 %shard_map.68.key_ref = bf16[128,6144]{1,0:T(8,128)(2,1)} custom-call(s32[1]{0:T(128)} %bitcast.4.member_ref, s32[16]{0:T(128)} %count_ref.9, bf16[4,784,128]{2,1,0:T(8,128)(2,1)} %copy-done.3, bf16[4,784,128]{2,1,0:T(8,128)(2,1)} %copy-done.5, bf16[4,784,128]{2,1,0:T(8,128)(2,1)} %collective-permute-done.2.rest_2_, ...), custom_call_target="tpu_custom_call" | custom-call | flops 6291456 | bytes 6291456 | tf_op jit(solution)/shard_map/pallas_call | solution.py:196
  72.1 29.4 %collective-permute-done.1.rest_1_ = bf16[4,784,128]{2,1,0:T(8,128)(2,1)} collective-permute-done((bf16[4,784,128]{2,1,0:T(8,128)(2,1)S(1)}, bf16[4,784,128]{2,1,0:T(8,128)(2,1)}, u32[]{:S(2)}, u32[]{:S(2)}) %collective-permute-start.1) | collective-permute-done | bytes 802848 | tf_op jit(solution)/shard_map/ppermute | solution.py:423
  101.4 4.7 %all-to-all-start.2 = ((bf16[16,400,128]{2,1,0:T(8,128)(2,1)}), bf16[16,400,128]{2,1,0:T(8,128)(2,1)}, u32[]{:S(2)}, u32[]{:S(2)}) async-start(bf16[16,400,128]{2,1,0:T(8,128)(2,1)} %bitcast.5), calls=%async_computation.2 | async-start | bytes 3276800 | tf_op jit(solution)/shard_map/all_to_all | solution.py:431
  110.8 5.2 %shard_map.69.value_ref = bf16[6144,256]{1,0:T(8,128)(2,1)} custom-call(s32[1]{0:T(128)} %bitcast.4.member_ref, s32[16]{0:T(128)} %count_ref.9, bf16[4,784,128]{2,1,0:T(8,128)(2,1)} %copy-done.2, bf16[4,784,128]{2,1,0:T(8,128)(2,1)} %collective-permute-done.1.rest_1_, bf16[4,784,128]{2,1,0:T(8,128)(2,1)} %copy-done.6, bf16[4,784,128]{2,1,0:T(8,128)(2,1)} %copy-done.7), custom_call_target="tpu_custom_call" | custom-call | flops 6291456 | bytes 6291456 | tf_op jit(solution)/shard_map/pallas_call | solution.py:196
  116.0 25.6 %shard_map.70 = bf16[16,192,128]{2,1,0:T(8,128)(2,1)} custom-call(s32[1]{0:T(128)} %constant.64.clone.1.cls_ref, s32[16]{0:T(128)} %count_ref.9, bf16[16,400,128]{2,1,0:T(8,128)(2,1)} %copy-done.4, bf16[128,6144]{1,0:T(8,128)(2,1)} %shard_map.68.key_ref, bf16[6144,256]{1,0:T(8,128)(2,1)} %shard_map.69.value_ref), custom_call_target="tpu_custom_call" | custom-call | flops 9663676416 | bytes 6291456 | tf_op jit(solution)/shard_map/pallas_call | solution.py:312
  141.6 7.1 %all-to-all-start.4 = ((bf16[16,192,128]{2,1,0:T(8,128)(2,1)}), bf16[16,192,128]{2,1,0:T(8,128)(2,1)S(1)}, u32[]{:S(2)}, u32[]{:S(2)}) async-start(bf16[16,192,128]{2,1,0:T(8,128)(2,1)} %shard_map.70), calls=%async_computation.4 | async-start | bytes 1572864 | tf_op jit(solution)/shard_map/all_to_all | solution.py:462
  148.7 25.8 %shard_map.71 = bf16[16,192,128]{2,1,0:T(8,128)(2,1)} custom-call(s32[1]{0:T(128)} %constant.65.clone.1.cls_ref, s32[16]{0:T(128)} %count_ref.9, bf16[16,400,128]{2,1,0:T(8,128)(2,1)} %all-to-all-done.2.got_ref, bf16[128,6144]{1,0:T(8,128)(2,1)} %shard_map.68.key_ref, bf16[6144,256]{1,0:T(8,128)(2,1)} %shard_map.69.value_ref), custom_call_target="tpu_custom_call" | custom-call | flops 9663676416 | bytes 6291456 | tf_op jit(solution)/shard_map/pallas_call | solution.py:312
  174.5 6.0 %all-to-all-start.5 = ((bf16[16,192,128]{2,1,0:T(8,128)(2,1)}), bf16[16,192,128]{2,1,0:T(8,128)(2,1)S(1)}, u32[]{:S(2)}, u32[]{:S(2)}) async-start(bf16[16,192,128]{2,1,0:T(8,128)(2,1)} %shard_map.71), calls=%async_computation.5 | async-start | bytes 1572864 | tf_op jit(solution)/shard_map/all_to_all | solution.py:469
  180.6 6.4 %shard_map.73 = bf16[192,2048]{1,0:T(8,128)(2,1)} custom-call(s32[1]{0:T(128)} %bitcast.7.column_ref, bf16[16,192,128]{2,1,0:T(8,128)(2,1)} %copy-done, bf16[2048,8192]{1,0:T(8,128)(2,1)} %rest_1_.7), custom_call_target="tpu_custom_call" | custom-call | flops 1610612736 | bytes 8388608 | tf_op jit(solution)/shard_map/pallas_call | solution.py:354
  188.5 10.7 %all-to-all-done.5.rest_1_.rest_0_ = bf16[16,192,128]{2,1,0:T(8,128)(2,1)S(1)} async-done(((bf16[16,192,128]{2,1,0:T(8,128)(2,1)}), bf16[16,192,128]{2,1,0:T(8,128)(2,1)S(1)}, u32[]{:S(2)}, u32[]{:S(2)}) %all-to-all-start.5) | async-done | bytes 786464 | tf_op jit(solution)/shard_map/all_to_all | solution.py:469
  200.1 6.4 %shard_map.75 = bf16[192,2048]{1,0:T(8,128)(2,1)} custom-call(s32[1]{0:T(128)} %bitcast.7.column_ref, bf16[16,192,128]{2,1,0:T(8,128)(2,1)} %copy-done.1, bf16[2048,8192]{1,0:T(8,128)(2,1)} %rest_1_.7), custom_call_target="tpu_custom_call" | custom-call | flops 1610612736 | bytes 8388608 | tf_op jit(solution)/shard_map/pallas_call | solution.py:354
  208.1 6.4 %shard_map.74 = bf16[192,2048]{1,0:T(8,128)(2,1)} custom-call(s32[1]{0:T(128)} %bitcast.8.column_ref, bf16[16,192,128]{2,1,0:T(8,128)(2,1)} %copy-done, bf16[2048,8192]{1,0:T(8,128)(2,1)} %rest_1_.7), custom_call_target="tpu_custom_call" | custom-call | flops 1610612736 | bytes 8388608 | tf_op jit(solution)/shard_map/pallas_call | solution.py:354
  215.0 6.4 %shard_map.76 = bf16[192,2048]{1,0:T(8,128)(2,1)} custom-call(s32[1]{0:T(128)} %bitcast.8.column_ref, bf16[16,192,128]{2,1,0:T(8,128)(2,1)} %copy-done.1, bf16[2048,8192]{1,0:T(8,128)(2,1)} %rest_1_.7), custom_call_target="tpu_custom_call" | custom-call | flops 1610612736 | bytes 8388608 | tf_op jit(solution)/shard_map/pallas_call | solution.py:354
  222.8 13.8 %shard_map.72 = bf16[384,4096]{1,0:T(8,128)(2,1)} custom-call(s32[1]{0:T(128)} %bitcast.column_ref, bf16[16,192,128]{2,1,0:T(8,128)(2,1)} %copy-done, bf16[16,192,128]{2,1,0:T(8,128)(2,1)} %copy-done.1, bf16[2048,8192]{1,0:T(8,128)(2,1)} %rest_1_.7), custom_call_target="tpu_custom_call" | custom-call | flops 6442450944 | bytes 16777216 | tf_op jit(solution)/shard_map/pallas_call | solution.py:354
  239.3 4.7 %collective-permute-done.7 = bf16[192,2048]{1,0:T(8,128)(2,1)S(1)} collective-permute-done((bf16[192,2048]{1,0:T(8,128)(2,1)}, bf16[192,2048]{1,0:T(8,128)(2,1)S(1)}, u32[]{:S(2)}, u32[]{:S(2)}) %collective-permute-start.7) | collective-permute-done | bytes 786464 | tf_op jit(solution)/shard_map/ppermute | solution.py:474
  244.0 16.2 %collective-permute-done.9 = bf16[192,2048]{1,0:T(8,128)(2,1)S(1)} collective-permute-done((bf16[192,2048]{1,0:T(8,128)(2,1)}, bf16[192,2048]{1,0:T(8,128)(2,1)S(1)}, u32[]{:S(2)}, u32[]{:S(2)}) %collective-permute-start.9) | collective-permute-done | bytes 786464 | tf_op jit(solution)/shard_map/ppermute | solution.py:474
  261.4 14.2 %maximum_maximum_fusion = bf16[384,4096]{1,0:T(8,128)(2,1)} fusion(bf16[192,2048]{1,0:T(8,128)(2,1)S(1)} %get-tuple-element.38, bf16[192,2048]{1,0:T(8,128)(2,1)S(1)} %get-tuple-element.39, bf16[192,2048]{1,0:T(8,128)(2,1)S(1)} %get-tuple-element.40, bf16[192,2048]{1,0:T(8,128)(2,1)S(1)} %get-tuple-element.37), kind=kLoop, calls=%fused_computation | loop fusion | flops 12582912 | bytes 6291456 | tf_op jit(solution)/shard_map/concatenate | solution.py:485
  (44 shorter events, 28.3 us)
Async XLA Ops:
  7.6 26.8 %all-to-all-start = ((bf16[4,784,128]{2,1,0:T(8,128)(2,1)}), bf16[4,784,128]{2,1,0:T(8,128)(2,1)S(1)}, u32[]{:S(2)}, u32[]{:S(2)}) async-start(bf16[4,784,128]{2,1,0:T(8,128)(2,1)} %bitcast.10), calls=%async_computation | async-start | bytes 1605632 | tf_op jit(solution)/shard_map/all_to_all | solution.py:417
  34.4 29.1 %copy-start.3 = (bf16[4,784,128]{2,1,0:T(8,128)(2,1)}, bf16[4,784,128]{2,1,0:T(8,128)(2,1)S(1)}, u32[]{:S(2)}) copy-start(bf16[4,784,128]{2,1,0:T(8,128)(2,1)S(1)} %all-to-all-done.rest_0_) | copy-start | bytes 2408452
  34.4 23.4 %all-to-all-start.1 = ((bf16[4,784,128]{2,1,0:T(8,128)(2,1)}), bf16[4,784,128]{2,1,0:T(8,128)(2,1)S(1)}, u32[]{:S(2)}, u32[]{:S(2)}) async-start(bf16[4,784,128]{2,1,0:T(8,128)(2,1)} %bitcast.9), calls=%async_computation.1 | async-start | bytes 1605632 | tf_op jit(solution)/shard_map/all_to_all | solution.py:417
  37.9 18.9 %collective-permute-start = (bf16[4,784,128]{2,1,0:T(8,128)(2,1)S(1)}, bf16[4,784,128]{2,1,0:T(8,128)(2,1)S(1)}, u32[]{:S(2)}, u32[]{:S(2)}) collective-permute-start(bf16[4,784,128]{2,1,0:T(8,128)(2,1)S(1)} %all-to-all-done.rest_0_), channel_id=1, source_target_pairs={{0,4},{2,6},{4,0},{6,2},{8,12},{10,14},{12,8},{14,10},{16,20},{18,... | collective-permute-start | bytes 2408456 | tf_op jit(solution)/shard_map/ppermute | solution.py:423
  56.8 1.0 copy-start.5
  57.8 48.3 %copy-start.2 = (bf16[4,784,128]{2,1,0:T(8,128)(2,1)}, bf16[4,784,128]{2,1,0:T(8,128)(2,1)S(1)}, u32[]{:S(2)}) copy-start(bf16[4,784,128]{2,1,0:T(8,128)(2,1)S(1)} %all-to-all-done.1.rest_0_) | copy-start | bytes 2408452
  57.8 43.6 %all-to-all-start.3 = ((bf16[16,400,128]{2,1,0:T(8,128)(2,1)}), bf16[16,400,128]{2,1,0:T(8,128)(2,1)S(1)}, u32[]{:S(2)}, u32[]{:S(2)}) async-start(bf16[16,400,128]{2,1,0:T(8,128)(2,1)} %bitcast.11), calls=%async_computation.3 | async-start | bytes 3276800 | tf_op jit(solution)/shard_map/all_to_all | solution.py:431
  63.4 2.6 collective-permute-start.2
  63.9 3.4 %collective-permute-start.3 = (bf16[4,784,128]{2,1,0:T(8,128)(2,1)}, bf16[4,784,128]{2,1,0:T(8,128)(2,1)}, u32[]{:S(2)}, u32[]{:S(2)}) collective-permute-start(bf16[4,784,128]{2,1,0:T(8,128)(2,1)} %copy-done.5), channel_id=1, source_target_pairs={{0,2},{2,0},{4,6},{6,4},{8,10},{10,8},{12,14},{14,12},{16,18},{18,... | collective-permute-start | bytes 2408456 | tf_op jit(solution)/shard_map/ppermute | solution.py:423
  64.0 37.4 %collective-permute-start.1 = (bf16[4,784,128]{2,1,0:T(8,128)(2,1)S(1)}, bf16[4,784,128]{2,1,0:T(8,128)(2,1)}, u32[]{:S(2)}, u32[]{:S(2)}) collective-permute-start(bf16[4,784,128]{2,1,0:T(8,128)(2,1)S(1)} %all-to-all-done.1.rest_0_), channel_id=1, source_target_pairs={{0,4},{2,6},{4,0},{6,2},{8,12},{10,14},{12,8},{14,10},{16,20},{18,... | collective-permute-start | bytes 2408456 | tf_op jit(solution)/shard_map/ppermute | solution.py:423
  101.4 14.6 %copy-start.4 = (bf16[16,400,128]{2,1,0:T(8,128)(2,1)}, bf16[16,400,128]{2,1,0:T(8,128)(2,1)S(1)}, u32[]{:S(2)}) copy-start(bf16[16,400,128]{2,1,0:T(8,128)(2,1)S(1)} %all-to-all-done.3.got_ref) | copy-start | bytes 4915204
  101.4 40.2 %all-to-all-start.2 = ((bf16[16,400,128]{2,1,0:T(8,128)(2,1)}), bf16[16,400,128]{2,1,0:T(8,128)(2,1)}, u32[]{:S(2)}, u32[]{:S(2)}) async-start(bf16[16,400,128]{2,1,0:T(8,128)(2,1)} %bitcast.5), calls=%async_computation.2 | async-start | bytes 3276800 | tf_op jit(solution)/shard_map/all_to_all | solution.py:431
  106.1 2.4 collective-permute-start.4
  106.6 3.3 %collective-permute-start.5 = (bf16[4,784,128]{2,1,0:T(8,128)(2,1)}, bf16[4,784,128]{2,1,0:T(8,128)(2,1)S(1)}, u32[]{:S(2)}, u32[]{:S(2)}) collective-permute-start(bf16[4,784,128]{2,1,0:T(8,128)(2,1)} %collective-permute-done.1.rest_1_), channel_id=1, source_target_pairs={{0,2},{2,0},{4,6},{6,4},{8,10},{10,8},{12,14},{14,12},{16,18},{18,... | collective-permute-start | bytes 2408456 | tf_op jit(solution)/shard_map/ppermute | solution.py:423
  108.5 1.4 copy-start.6
  109.9 0.9 copy-start.7
  141.6 32.9 %all-to-all-start.4 = ((bf16[16,192,128]{2,1,0:T(8,128)(2,1)}), bf16[16,192,128]{2,1,0:T(8,128)(2,1)S(1)}, u32[]{:S(2)}, u32[]{:S(2)}) async-start(bf16[16,192,128]{2,1,0:T(8,128)(2,1)} %shard_map.70), calls=%async_computation.4 | async-start | bytes 1572864 | tf_op jit(solution)/shard_map/all_to_all | solution.py:462
  174.5 6.0 %copy-start = (bf16[16,192,128]{2,1,0:T(8,128)(2,1)}, bf16[16,192,128]{2,1,0:T(8,128)(2,1)S(1)}, u32[]{:S(2)}) copy-start(bf16[16,192,128]{2,1,0:T(8,128)(2,1)S(1)} %all-to-all-done.4.rest_0_) | copy-start | bytes 2359300
  174.5 24.7 %all-to-all-start.5 = ((bf16[16,192,128]{2,1,0:T(8,128)(2,1)}), bf16[16,192,128]{2,1,0:T(8,128)(2,1)S(1)}, u32[]{:S(2)}, u32[]{:S(2)}) async-start(bf16[16,192,128]{2,1,0:T(8,128)(2,1)} %shard_map.71), calls=%async_computation.5 | async-start | bytes 1572864 | tf_op jit(solution)/shard_map/all_to_all | solution.py:469
  187.0 52.3 %collective-permute-start.6 = (bf16[192,2048]{1,0:T(8,128)(2,1)}, bf16[192,2048]{1,0:T(8,128)(2,1)S(1)}, u32[]{:S(2)}, u32[]{:S(2)}) collective-permute-start(bf16[192,2048]{1,0:T(8,128)(2,1)} %shard_map.73), channel_id=1, source_target_pairs={{0,1},{1,0},{2,3},{3,2},{4,5},{5,4},{6,7},{7,6},{8,9},{9,8},{10,11... | collective-permute-start | bytes 2359304 | tf_op jit(solution)/shard_map/ppermute | solution.py:474
  199.3 0.9 copy-start.1
  206.5 32.8 %collective-permute-start.8 = (bf16[192,2048]{1,0:T(8,128)(2,1)}, bf16[192,2048]{1,0:T(8,128)(2,1)S(1)}, u32[]{:S(2)}, u32[]{:S(2)}) collective-permute-start(bf16[192,2048]{1,0:T(8,128)(2,1)} %shard_map.75), channel_id=1, source_target_pairs={{0,1},{1,0},{2,3},{3,2},{4,5},{5,4},{6,7},{7,6},{8,9},{9,8},{10,11... | collective-permute-start | bytes 2359304 | tf_op jit(solution)/shard_map/ppermute | solution.py:474
  214.5 29.5 %collective-permute-start.7 = (bf16[192,2048]{1,0:T(8,128)(2,1)}, bf16[192,2048]{1,0:T(8,128)(2,1)S(1)}, u32[]{:S(2)}, u32[]{:S(2)}) collective-permute-start(bf16[192,2048]{1,0:T(8,128)(2,1)} %shard_map.74), channel_id=1, source_target_pairs={{0,1},{1,0},{2,3},{3,2},{4,5},{5,4},{6,7},{7,6},{8,9},{9,8},{10,11... | collective-permute-start | bytes 2359304 | tf_op jit(solution)/shard_map/ppermute | solution.py:474
  221.3 38.8 %collective-permute-start.9 = (bf16[192,2048]{1,0:T(8,128)(2,1)}, bf16[192,2048]{1,0:T(8,128)(2,1)S(1)}, u32[]{:S(2)}, u32[]{:S(2)}) collective-permute-start(bf16[192,2048]{1,0:T(8,128)(2,1)} %shard_map.76), channel_id=1, source_target_pairs={{0,1},{1,0},{2,3},{3,2},{4,5},{5,4},{6,7},{7,6},{8,9},{9,8},{10,11... | collective-permute-start | bytes 2359304 | tf_op jit(solution)/shard_map/ppermute | solution.py:474

commit v14 on v13

--- a/solution.py
+++ b/solution.py
@@ -369,6 +369,31 @@
     )((first_column // step).astype(jnp.int32).reshape(1), *got, weight)
 
 
+def add_piece_kernel(sum_ref, part_ref, out_ref):
+    out_ref[...] = (
+        sum_ref[...].astype(jnp.float32) + part_ref[...].astype(jnp.float32)
+    ).astype(jnp.bfloat16)
+
+
+def add_piece(total_sum, part, j, n):
+    rows, width = part.shape
+    step = min(1024, width)
+    steps = width // step
+    here = pl.BlockSpec((rows, step), lambda i: (j, n * steps + i))
+    return pl.pallas_call(
+        add_piece_kernel,
+        grid=(steps,),
+        in_specs=[here, pl.BlockSpec((rows, step), lambda i: (0, i))],
+        out_specs=here,
+        out_shape=jax.ShapeDtypeStruct(total_sum.shape, total_sum.dtype),
+        input_output_aliases={0: 0},
+        compiler_params=params(),
+        cost_estimate=pl.CostEstimate(
+            flops=rows * width, bytes_accessed=6 * rows * width, transcendentals=0
+        ),
+    )(total_sum, part)
+
+
 def tables(query_rows):
     half_dim = HD // 2
     positions = lax.axis_index("ctx") * query_rows + jnp.arange(query_rows, dtype=jnp.int32)
@@ -466,39 +491,31 @@
         if j + 2 < chunks:
             packed_q[j + 2], done = lax.optimization_barrier((packed_q[j + 2], done))
             got_q.append(send_query(packed_q[j + 2]))
-    got.append(lax.all_to_all(done, "ctx", split_axis=0, concat_axis=0, tiled=True))
-    if tp_size == 2:
-        half = columns // 2
-        came = [
-            [
-                lax.ppermute(
-                    project((1 - tp_me) * columns + n * half, [one], out_weight, half, classes),
-                    "tp",
-                    both,
-                )
-                for n in range(2)
-            ]
-            for one in got
+    half = columns // 2
+
+    def for_peer(one):
+        return [
+            project((1 - tp_me) * columns + n * half, [one], out_weight, half, classes)
+            for n in range(2)
         ]
-        own = project(tp_me * columns, got, out_weight, columns, classes).astype(jnp.float32)
-        rows = own.shape[0] // chunks
-        return jnp.concatenate(
-            [
-                jnp.concatenate(
-                    [
-                        (own[j * rows : (j + 1) * rows, n * half : (n + 1) * half]
-                            + part.astype(jnp.float32)
-                        ).astype(
-                            jnp.bfloat16
-                        )
-                        for n, part in enumerate(parts)
-                    ],
-                    axis=1,
-                )
-                for j, parts in enumerate(came)
-            ],
-            axis=0,
-        )
+
+    def trade(parts):
+        return [lax.ppermute(part, "tp", [(0, 1), (1, 0)]) for part in parts]
+
+    paired = tp_size == 2 and chunks == 2
+    if paired:
+        first = for_peer(got[0])
+        done, first[0] = lax.optimization_barrier((done, first[0]))
+    last = lax.all_to_all(done, "ctx", split_axis=0, concat_axis=0, tiled=True)
+    if paired:
+        last, first[1] = lax.optimization_barrier((last, first[1]))
+        came = [trade(first), trade(for_peer(last))]
+        total_sum = project(tp_me * columns, got + [last], out_weight, columns, classes)
+        for j, parts in enumerate(came):
+            for n, part in enumerate(parts):
+                total_sum = add_piece(total_sum, part, j, n)
+        return total_sum
+    got.append(last)
     full = project(jnp.int32(0) * tp_me, got, out_weight, columns * tp_size, classes)
     split = jnp.transpose(full.reshape(full.shape[0], tp_size, columns), (1, 0, 2))
     swapped = lax.all_to_all(split, "tp", split_axis=0, concat_axis=0, tiled=True)

time: 277 us -> 265 us (0.957)
  other arithmetic: 20.7 us -> 2.56 us
  Pallas kernels: 118 us -> 126 us
  waiting for transfers between devices: 92.4 us -> 85.9 us
  local copies, waits for them, and re-layouts: 1.81 us -> 6.6 us
    concatenate x1 -> x0, other arithmetic: 14.2 us -> none  [local(): jnp.concatenate([jnp.concatenate([(own[j * rows:(j + 1) * rows, n * half:...]
    all_to_all x0 -> x1, waiting for transfers between devices: none -> 10.7 us  [local(): last = lax.all_to_all(done, 'ctx', split_axis=0, concat_axis=0, tiled=True)]
    all_to_all x2 -> x1, waiting for transfers between devices: 10.7 us -> 0.01 us  [local(): lax.all_to_all(done, 'ctx', split_axis=0, concat_axis=0, tiled=True)]
    pallas_call x0 -> x4, Pallas kernels: none -> 8.77 us  [add_piece(): pl.pallas_call(add_piece_kernel, grid=(steps,), in_specs=[here, pl.BlockS...]
    ppermute x4, waiting for transfers between devices: 20.8 us -> 14.2 us  [trade(): return [lax.ppermute(part, 'tp', [(0, 1), (1, 0)]) for part in parts]]
    all_to_all x2 -> x1, starting transfers between devices: 13.1 us -> 6.85 us  [local(): lax.all_to_all(done, 'ctx', split_axis=0, concat_axis=0, tiled=True)]
    all_to_all x0 -> x1, starting transfers between devices: none -> 5.99 us  [local(): last = lax.all_to_all(done, 'ctx', split_axis=0, concat_axis=0, tiled=True)]
    unnamed x16 -> x24, local copies, waits for them, and re-layouts: 1.81 us -> 6.6 us
  transfers between devices with their start and end apart: 16 -> 16, of which waited for: 11 -> 11; matrix products, arithmetic and copies ran while one was open for 1% -> 0% of each run, Pallas kernels for 41% -> 43%
where the time goes in v14:
time: 265 us; the launch traced here: 264 us
  Pallas kernels  126 us (48%)
  waiting for transfers between devices  85.9 us (32%)
  starting transfers between devices  41.9 us (16%)
  local copies, waits for them, and re-layouts  6.6 us (2%)
    pallas_call x2, Pallas kernels, attend(): pl.pallas_call(functools.partial(attend_kernel, ctx_size, block), in_spec...  51.5 us
    ppermute x6, waiting for transfers between devices, swap(): return parts + [lax.ppermute(part, 'ctx', pairs) for part in parts]  42.8 us
    pallas_call x5, Pallas kernels, project(): pl.pallas_call(functools.partial(project_kernel, classes, len(got)), grid...  39.4 us
    all_to_all x2, waiting for transfers between devices, send_across(): lax.all_to_all(packed, 'ctx', split_axis=0, concat_axis=0, tiled=True, ax...  18.1 us
    pallas_call x3, Pallas kernels, pack(): pl.pallas_call(functools.partial(pack_kernel, turned, classes, cap, width...  15.4 us
    ppermute x4, waiting for transfers between devices, trade(): return [lax.ppermute(part, 'tp', [(0, 1), (1, 0)]) for part in parts]  14.2 us
    all_to_all x1, waiting for transfers between devices, local(): last = lax.all_to_all(done, 'ctx', split_axis=0, concat_axis=0, tiled=True)  10.7 us
    pallas_call x2, Pallas kernels, compact(): pl.pallas_call(functools.partial(compact_kernel, offsets, per, total, as_...  9.89 us
  transfers between devices with their start and end apart: 16, of which 11 were waited for; matrix products, arithmetic and copies ran while one was open for 0% of the time, Pallas kernels for 43%

profile of v14, /device:TPU:0, one launch (start us, length us, event | category | flops | bytes accessed | tf_op | source)
XLA Modules:
  0.0 263.5 jit_solution(10758549499913867357)
XLA Ops:
  0.0 2.5 negate_select_fusion
  4.1 3.5 %shard_map.67 = bf16[4,1,784,128]{3,2,1,0:T(8,128)(2,1)} custom-call(s32[1,768]{1,0:T(1,128)} %get-tuple-element.28.slot_ref, f32[768,128]{1,0:T(8,128)} %get-tuple-element.46.cos_ref, f32[768,128]{1,0:T(8,128)} %get-tuple-element.45.sin_ref, bf16[768,512]{1,0:T(8,128)(2,1)} %row_ref.5), custom_call_target="tpu_custom_call" | custom-call | flops 616562688 | bytes 1572864 | tf_op jit(solution)/shard_map/pallas_call | solution.py:124
  7.6 6.3 %all-to-all-start = ((bf16[4,784,128]{2,1,0:T(8,128)(2,1)}), bf16[4,784,128]{2,1,0:T(8,128)(2,1)S(1)}, u32[]{:S(2)}, u32[]{:S(2)}) async-start(bf16[4,784,128]{2,1,0:T(8,128)(2,1)} %bitcast.10), calls=%async_computation | async-start | bytes 1605632 | tf_op jit(solution)/shard_map/all_to_all | solution.py:442
  13.9 3.2 %shard_map.66 = bf16[4,1,784,128]{3,2,1,0:T(8,128)(2,1)} custom-call(s32[1,768]{1,0:T(1,128)} %get-tuple-element.28.slot_ref, f32[768,128]{1,0:T(8,128)} %get-tuple-element.46.cos_ref, f32[768,128]{1,0:T(8,128)} %get-tuple-element.45.sin_ref, bf16[768,512]{1,0:T(8,128)(2,1)} %row_ref.4), custom_call_target="tpu_custom_call" | custom-call | flops 616562688 | bytes 1572864 | tf_op jit(solution)/shard_map/pallas_call | solution.py:124
  17.1 17.2 %all-to-all-done.rest_0_ = bf16[4,784,128]{2,1,0:T(8,128)(2,1)S(1)} async-done(((bf16[4,784,128]{2,1,0:T(8,128)(2,1)}), bf16[4,784,128]{2,1,0:T(8,128)(2,1)S(1)}, u32[]{:S(2)}, u32[]{:S(2)}) %all-to-all-start) | async-done | bytes 802848 | tf_op jit(solution)/shard_map/all_to_all | solution.py:442
  34.4 3.5 %all-to-all-start.1 = ((bf16[4,784,128]{2,1,0:T(8,128)(2,1)}), bf16[4,784,128]{2,1,0:T(8,128)(2,1)S(1)}, u32[]{:S(2)}, u32[]{:S(2)}) async-start(bf16[4,784,128]{2,1,0:T(8,128)(2,1)} %bitcast.9), calls=%async_computation.1 | async-start | bytes 1605632 | tf_op jit(solution)/shard_map/all_to_all | solution.py:442
  39.4 8.7 %shard_map.65 = (bf16[16,1,400,128]{3,2,1,0:T(8,128)(2,1)}, bf16[16,1,400,128]{3,2,1,0:T(8,128)(2,1)}) custom-call(s32[1,768]{1,0:T(1,128)} %get-tuple-element.25.slot_ref, f32[768,128]{1,0:T(8,128)} %get-tuple-element.46.cos_ref, f32[768,128]{1,0:T(8,128)} %get-tuple-element.45.sin_ref, bf16[768,2048]{1,0:T(8,128)(2,1)} %row_ref.3), custom_call_target="tpu_custom_call" | custom-call | flops 2516582400 | bytes 6291456 | tf_op jit(solution)/shard_map/pallas_call | solution.py:124
  48.1 8.8 %collective-permute-done.rest_1_ = bf16[4,784,128]{2,1,0:T(8,128)(2,1)} collective-permute-done((bf16[4,784,128]{2,1,0:T(8,128)(2,1)S(1)}, bf16[4,784,128]{2,1,0:T(8,128)(2,1)}, u32[]{:S(2)}, u32[]{:S(2)}) %collective-permute-start) | collective-permute-done | bytes 802848 | tf_op jit(solution)/shard_map/ppermute | solution.py:448
  57.8 4.9 %all-to-all-start.3 = ((bf16[16,400,128]{2,1,0:T(8,128)(2,1)}), bf16[16,400,128]{2,1,0:T(8,128)(2,1)S(1)}, u32[]{:S(2)}, u32[]{:S(2)}) async-start(bf16[16,400,128]{2,1,0:T(8,128)(2,1)} %bitcast.11), calls=%async_computation.3 | async-start | bytes 3276800 | tf_op jit(solution)/shard_map/all_to_all | solution.py:456
  66.6 4.7 %shard_map.68.key_ref = bf16[128,6144]{1,0:T(8,128)(2,1)} custom-call(s32[1]{0:T(128)} %bitcast.4.member_ref, s32[16]{0:T(128)} %count_ref.9, bf16[4,784,128]{2,1,0:T(8,128)(2,1)} %copy-done.3, bf16[4,784,128]{2,1,0:T(8,128)(2,1)} %collective-permute-done.rest_1_, bf16[4,784,128]{2,1,0:T(8,128)(2,1)} %collective-permute-done.2.rest_2_, ...), custom_call_target="tpu_custom_call" | custom-call | flops 6291456 | bytes 6291456 | tf_op jit(solution)/shard_map/pallas_call | solution.py:196
  71.3 29.4 %collective-permute-done.1.rest_1_ = bf16[4,784,128]{2,1,0:T(8,128)(2,1)} collective-permute-done((bf16[4,784,128]{2,1,0:T(8,128)(2,1)S(1)}, bf16[4,784,128]{2,1,0:T(8,128)(2,1)}, u32[]{:S(2)}, u32[]{:S(2)}) %collective-permute-start.1) | collective-permute-done | bytes 802848 | tf_op jit(solution)/shard_map/ppermute | solution.py:448
  101.8 4.6 %all-to-all-start.2 = ((bf16[16,400,128]{2,1,0:T(8,128)(2,1)}), bf16[16,400,128]{2,1,0:T(8,128)(2,1)S(1)}, u32[]{:S(2)}, u32[]{:S(2)}) async-start(bf16[16,400,128]{2,1,0:T(8,128)(2,1)} %bitcast.5), calls=%async_computation.2 | async-start | bytes 3276800 | tf_op jit(solution)/shard_map/all_to_all | solution.py:456
  111.2 5.2 %shard_map.69.value_ref = bf16[6144,256]{1,0:T(8,128)(2,1)} custom-call(s32[1]{0:T(128)} %bitcast.4.member_ref, s32[16]{0:T(128)} %count_ref.9, bf16[4,784,128]{2,1,0:T(8,128)(2,1)} %copy-done.2, bf16[4,784,128]{2,1,0:T(8,128)(2,1)} %collective-permute-done.1.rest_1_, bf16[4,784,128]{2,1,0:T(8,128)(2,1)} %copy-done.6, bf16[4,784,128]{2,1,0:T(8,128)(2,1)} %copy-done.7), custom_call_target="tpu_custom_call" | custom-call | flops 6291456 | bytes 6291456 | tf_op jit(solution)/shard_map/pallas_call | solution.py:196
  116.4 25.7 %shard_map.70 = bf16[16,192,128]{2,1,0:T(8,128)(2,1)} custom-call(s32[1]{0:T(128)} %constant.64.clone.1.cls_ref, s32[16]{0:T(128)} %count_ref.9, bf16[16,400,128]{2,1,0:T(8,128)(2,1)} %copy-done.5, bf16[128,6144]{1,0:T(8,128)(2,1)} %shard_map.68.key_ref, bf16[6144,256]{1,0:T(8,128)(2,1)} %shard_map.69.value_ref), custom_call_target="tpu_custom_call" | custom-call | flops 9663676416 | bytes 6291456 | tf_op jit(solution)/shard_map/pallas_call | solution.py:312
  142.1 6.9 %all-to-all-start.4 = ((bf16[16,192,128]{2,1,0:T(8,128)(2,1)}), bf16[16,192,128]{2,1,0:T(8,128)(2,1)S(1)}, u32[]{:S(2)}, u32[]{:S(2)}) async-start(bf16[16,192,128]{2,1,0:T(8,128)(2,1)} %shard_map.70), calls=%async_computation.4 | async-start | bytes 1572864 | tf_op jit(solution)/shard_map/all_to_all | solution.py:487
  149.0 25.8 %shard_map.71 = bf16[16,192,128]{2,1,0:T(8,128)(2,1)} custom-call(s32[1]{0:T(128)} %constant.65.clone.1.cls_ref, s32[16]{0:T(128)} %count_ref.9, bf16[16,400,128]{2,1,0:T(8,128)(2,1)} %copy-done.4, bf16[128,6144]{1,0:T(8,128)(2,1)} %shard_map.68.key_ref, bf16[6144,256]{1,0:T(8,128)(2,1)} %shard_map.69.value_ref), custom_call_target="tpu_custom_call" | custom-call | flops 9663676416 | bytes 6291456 | tf_op jit(solution)/shard_map/pallas_call | solution.py:312
  175.7 6.4 %shard_map.72 = bf16[192,2048]{1,0:T(8,128)(2,1)} custom-call(s32[1]{0:T(128)} %bitcast.7.column_ref, bf16[16,192,128]{2,1,0:T(8,128)(2,1)} %copy-done, bf16[2048,8192]{1,0:T(8,128)(2,1)} %rest_1_.7), custom_call_target="tpu_custom_call" | custom-call | flops 1610612736 | bytes 8388608 | tf_op jit(solution)/shard_map/pallas_call | solution.py:354
  182.1 6.0 %all-to-all-start.5 = ((bf16[16,192,128]{2,1,0:T(8,128)(2,1)}), bf16[16,192,128]{2,1,0:T(8,128)(2,1)S(1)}, u32[]{:S(2)}, u32[]{:S(2)}) async-start(bf16[16,192,128]{2,1,0:T(8,128)(2,1)} %shard_map.71), calls=%async_computation.5 | async-start | bytes 1572864 | tf_op jit(solution)/shard_map/all_to_all | solution.py:509
  189.7 6.4 %shard_map.73 = bf16[192,2048]{1,0:T(8,128)(2,1)} custom-call(s32[1]{0:T(128)} %bitcast.8.column_ref, bf16[16,192,128]{2,1,0:T(8,128)(2,1)} %copy-done, bf16[2048,8192]{1,0:T(8,128)(2,1)} %rest_1_.7), custom_call_target="tpu_custom_call" | custom-call | flops 1610612736 | bytes 8388608 | tf_op jit(solution)/shard_map/pallas_call | solution.py:354
  196.1 10.7 %all-to-all-done.5.rest_1_.rest_0_ = bf16[16,192,128]{2,1,0:T(8,128)(2,1)S(1)} async-done(((bf16[16,192,128]{2,1,0:T(8,128)(2,1)}), bf16[16,192,128]{2,1,0:T(8,128)(2,1)S(1)}, u32[]{:S(2)}, u32[]{:S(2)}) %all-to-all-start.5) | async-done | bytes 786464 | tf_op jit(solution)/shard_map/all_to_all | solution.py:509
  208.4 6.4 %shard_map.77 = bf16[192,2048]{1,0:T(8,128)(2,1)} custom-call(s32[1]{0:T(128)} %bitcast.7.column_ref, bf16[16,192,128]{2,1,0:T(8,128)(2,1)} %copy-done.1, bf16[2048,8192]{1,0:T(8,128)(2,1)} %rest_1_.7), custom_call_target="tpu_custom_call" | custom-call | flops 1610612736 | bytes 8388608 | tf_op jit(solution)/shard_map/pallas_call | solution.py:354
  215.6 6.4 %shard_map.79 = bf16[192,2048]{1,0:T(8,128)(2,1)} custom-call(s32[1]{0:T(128)} %bitcast.8.column_ref, bf16[16,192,128]{2,1,0:T(8,128)(2,1)} %copy-done.1, bf16[2048,8192]{1,0:T(8,128)(2,1)} %rest_1_.7), custom_call_target="tpu_custom_call" | custom-call | flops 1610612736 | bytes 8388608 | tf_op jit(solution)/shard_map/pallas_call | solution.py:354
  223.2 13.8 %shard_map.74.sum_ref = bf16[384,4096]{1,0:T(8,128)(2,1)} custom-call(s32[1]{0:T(128)} %bitcast.column_ref, bf16[16,192,128]{2,1,0:T(8,128)(2,1)} %copy-done, bf16[16,192,128]{2,1,0:T(8,128)(2,1)} %copy-done.1, bf16[2048,8192]{1,0:T(8,128)(2,1)} %rest_1_.7), custom_call_target="tpu_custom_call" | custom-call | flops 6442450944 | bytes 16777216 | tf_op jit(solution)/shard_map/pallas_call | solution.py:354
  247.4 13.1 %collective-permute-done.9.part_ref = bf16[192,2048]{1,0:T(8,128)(2,1)S(1)} collective-permute-done((bf16[192,2048]{1,0:T(8,128)(2,1)}, bf16[192,2048]{1,0:T(8,128)(2,1)S(1)}, u32[]{:S(2)}, u32[]{:S(2)}) %collective-permute-start.9) | collective-permute-done | bytes 786464 | tf_op jit(solution)/shard_map/ppermute | solution.py:503
  (53 shorter events, 33.3 us)
Async XLA Ops:
  7.6 26.8 %all-to-all-start = ((bf16[4,784,128]{2,1,0:T(8,128)(2,1)}), bf16[4,784,128]{2,1,0:T(8,128)(2,1)S(1)}, u32[]{:S(2)}, u32[]{:S(2)}) async-start(bf16[4,784,128]{2,1,0:T(8,128)(2,1)} %bitcast.10), calls=%async_computation | async-start | bytes 1605632 | tf_op jit(solution)/shard_map/all_to_all | solution.py:442
  34.4 28.3 %copy-start.3 = (bf16[4,784,128]{2,1,0:T(8,128)(2,1)}, bf16[4,784,128]{2,1,0:T(8,128)(2,1)S(1)}, u32[]{:S(2)}) copy-start(bf16[4,784,128]{2,1,0:T(8,128)(2,1)S(1)} %all-to-all-done.rest_0_) | copy-start | bytes 2408452
  34.4 23.4 %all-to-all-start.1 = ((bf16[4,784,128]{2,1,0:T(8,128)(2,1)}), bf16[4,784,128]{2,1,0:T(8,128)(2,1)S(1)}, u32[]{:S(2)}, u32[]{:S(2)}) async-start(bf16[4,784,128]{2,1,0:T(8,128)(2,1)} %bitcast.9), calls=%async_computation.1 | async-start | bytes 1605632 | tf_op jit(solution)/shard_map/all_to_all | solution.py:442
  37.9 19.0 %collective-permute-start = (bf16[4,784,128]{2,1,0:T(8,128)(2,1)S(1)}, bf16[4,784,128]{2,1,0:T(8,128)(2,1)}, u32[]{:S(2)}, u32[]{:S(2)}) collective-permute-start(bf16[4,784,128]{2,1,0:T(8,128)(2,1)S(1)} %all-to-all-done.rest_0_), channel_id=1, source_target_pairs={{0,4},{2,6},{4,0},{6,2},{8,12},{10,14},{12,8},{14,10},{16,20},{18,... | collective-permute-start | bytes 2408456 | tf_op jit(solution)/shard_map/ppermute | solution.py:448
  57.8 48.7 %copy-start.2 = (bf16[4,784,128]{2,1,0:T(8,128)(2,1)}, bf16[4,784,128]{2,1,0:T(8,128)(2,1)S(1)}, u32[]{:S(2)}) copy-start(bf16[4,784,128]{2,1,0:T(8,128)(2,1)S(1)} %all-to-all-done.1.rest_0_) | copy-start | bytes 2408452
  57.8 42.9 %all-to-all-start.3 = ((bf16[16,400,128]{2,1,0:T(8,128)(2,1)}), bf16[16,400,128]{2,1,0:T(8,128)(2,1)S(1)}, u32[]{:S(2)}, u32[]{:S(2)}) async-start(bf16[16,400,128]{2,1,0:T(8,128)(2,1)} %bitcast.11), calls=%async_computation.3 | async-start | bytes 3276800 | tf_op jit(solution)/shard_map/all_to_all | solution.py:456
  62.7 2.6 collective-permute-start.2
  63.1 3.4 %collective-permute-start.3 = (bf16[4,784,128]{2,1,0:T(8,128)(2,1)}, bf16[4,784,128]{2,1,0:T(8,128)(2,1)}, u32[]{:S(2)}, u32[]{:S(2)}) collective-permute-start(bf16[4,784,128]{2,1,0:T(8,128)(2,1)} %collective-permute-done.rest_1_), channel_id=1, source_target_pairs={{0,2},{2,0},{4,6},{6,4},{8,10},{10,8},{12,14},{14,12},{16,18},{18,... | collective-permute-start | bytes 2408456 | tf_op jit(solution)/shard_map/ppermute | solution.py:448
  63.2 37.4 %collective-permute-start.1 = (bf16[4,784,128]{2,1,0:T(8,128)(2,1)S(1)}, bf16[4,784,128]{2,1,0:T(8,128)(2,1)}, u32[]{:S(2)}, u32[]{:S(2)}) collective-permute-start(bf16[4,784,128]{2,1,0:T(8,128)(2,1)S(1)} %all-to-all-done.1.rest_0_), channel_id=1, source_target_pairs={{0,4},{2,6},{4,0},{6,2},{8,12},{10,14},{12,8},{14,10},{16,20},{18,... | collective-permute-start | bytes 2408456 | tf_op jit(solution)/shard_map/ppermute | solution.py:448
  100.7 1.2 copy-start.5
  101.8 40.3 %all-to-all-start.2 = ((bf16[16,400,128]{2,1,0:T(8,128)(2,1)}), bf16[16,400,128]{2,1,0:T(8,128)(2,1)S(1)}, u32[]{:S(2)}, u32[]{:S(2)}) async-start(bf16[16,400,128]{2,1,0:T(8,128)(2,1)} %bitcast.5), calls=%async_computation.2 | async-start | bytes 3276800 | tf_op jit(solution)/shard_map/all_to_all | solution.py:456
  106.5 2.5 collective-permute-start.4
  107.0 3.3 %collective-permute-start.5 = (bf16[4,784,128]{2,1,0:T(8,128)(2,1)}, bf16[4,784,128]{2,1,0:T(8,128)(2,1)S(1)}, u32[]{:S(2)}, u32[]{:S(2)}) collective-permute-start(bf16[4,784,128]{2,1,0:T(8,128)(2,1)} %collective-permute-done.1.rest_1_), channel_id=1, source_target_pairs={{0,2},{2,0},{4,6},{6,4},{8,10},{10,8},{12,14},{14,12},{16,18},{18,... | collective-permute-start | bytes 2408456 | tf_op jit(solution)/shard_map/ppermute | solution.py:448
  109.0 1.3 copy-start.6
  110.3 1.0 copy-start.7
  142.1 6.9 %copy-start.4 = (bf16[16,400,128]{2,1,0:T(8,128)(2,1)}, bf16[16,400,128]{2,1,0:T(8,128)(2,1)S(1)}, u32[]{:S(2)}) copy-start(bf16[16,400,128]{2,1,0:T(8,128)(2,1)S(1)} %all-to-all-done.2.got_ref) | copy-start | bytes 4915204
  142.1 32.7 %all-to-all-start.4 = ((bf16[16,192,128]{2,1,0:T(8,128)(2,1)}), bf16[16,192,128]{2,1,0:T(8,128)(2,1)S(1)}, u32[]{:S(2)}, u32[]{:S(2)}) async-start(bf16[16,192,128]{2,1,0:T(8,128)(2,1)} %shard_map.70), calls=%async_computation.4 | async-start | bytes 1572864 | tf_op jit(solution)/shard_map/all_to_all | solution.py:487
  182.1 24.7 %all-to-all-start.5 = ((bf16[16,192,128]{2,1,0:T(8,128)(2,1)}), bf16[16,192,128]{2,1,0:T(8,128)(2,1)S(1)}, u32[]{:S(2)}, u32[]{:S(2)}) async-start(bf16[16,192,128]{2,1,0:T(8,128)(2,1)} %shard_map.71), calls=%async_computation.5 | async-start | bytes 1572864 | tf_op jit(solution)/shard_map/all_to_all | solution.py:509
  188.1 48.8 %collective-permute-start.6 = (bf16[192,2048]{1,0:T(8,128)(2,1)}, bf16[192,2048]{1,0:T(8,128)(2,1)S(1)}, u32[]{:S(2)}, u32[]{:S(2)}) collective-permute-start(bf16[192,2048]{1,0:T(8,128)(2,1)} %shard_map.72), channel_id=1, source_target_pairs={{0,1},{1,0},{2,3},{3,2},{4,5},{5,4},{6,7},{7,6},{8,9},{9,8},{10,11... | collective-permute-start | bytes 2359304 | tf_op jit(solution)/shard_map/ppermute | solution.py:503
  206.8 1.5 copy-start.1
  206.8 33.2 %collective-permute-start.7 = (bf16[192,2048]{1,0:T(8,128)(2,1)}, bf16[192,2048]{1,0:T(8,128)(2,1)S(1)}, u32[]{:S(2)}, u32[]{:S(2)}) collective-permute-start(bf16[192,2048]{1,0:T(8,128)(2,1)} %shard_map.73), channel_id=1, source_target_pairs={{0,1},{1,0},{2,3},{3,2},{4,5},{5,4},{6,7},{7,6},{8,9},{9,8},{10,11... | collective-permute-start | bytes 2359304 | tf_op jit(solution)/shard_map/ppermute | solution.py:503
  214.8 29.5 %collective-permute-start.8 = (bf16[192,2048]{1,0:T(8,128)(2,1)}, bf16[192,2048]{1,0:T(8,128)(2,1)S(1)}, u32[]{:S(2)}, u32[]{:S(2)}) collective-permute-start(bf16[192,2048]{1,0:T(8,128)(2,1)} %shard_map.77), channel_id=1, source_target_pairs={{0,1},{1,0},{2,3},{3,2},{4,5},{5,4},{6,7},{7,6},{8,9},{9,8},{10,11... | collective-permute-start | bytes 2359304 | tf_op jit(solution)/shard_map/ppermute | solution.py:503
  222.0 38.4 %collective-permute-start.9 = (bf16[192,2048]{1,0:T(8,128)(2,1)}, bf16[192,2048]{1,0:T(8,128)(2,1)S(1)}, u32[]{:S(2)}, u32[]{:S(2)}) collective-permute-start(bf16[192,2048]{1,0:T(8,128)(2,1)} %shard_map.79), channel_id=1, source_target_pairs={{0,1},{1,0},{2,3},{3,2},{4,5},{5,4},{6,7},{7,6},{8,9},{9,8},{10,11... | collective-permute-start | bytes 2359304 | tf_op jit(solution)/shard_map/ppermute | solution.py:503
  240.0 0.9 copy-start.11
  (4 other events, 3.5 us)

commit v15 on v14

--- a/solution.py
+++ b/solution.py
@@ -234,38 +234,52 @@
         )
         start = end
 
+    upper = 2 * block
+    keep_all, lower = slice(0, pair), slice(upper, pair)
+
     def row_top(found):
-        return jnp.broadcast_to(jnp.max(found, axis=1, keepdims=True), (pair, HD))
+        return jnp.broadcast_to(jnp.max(found, axis=1, keepdims=True), (found.shape[0], HD))
+
+    def allowed(first_row, count, first_key):
+        ids = lax.broadcasted_iota(jnp.int32, (count, HD), 0) + first_row
+        row = ids + cls * block - first_key
+        for n in range(1, 4):
+            row = row + jnp.where(ids >= n * block, TOK_DEV - block, 0)
+        col = lax.broadcasted_iota(jnp.int32, (count, span), 1)
+        return col <= jnp.concatenate([row] * (span // HD), axis=1)
+
+    def put(scores, top, part, found):
+        scores[part, :] = found
+        top[part, :] = row_top(found)
+
+    def dot_keys(i, k, first_row, count):
+        at = jnp.minimum(i, supers - 1) * pair + first_row
+        rows = query_all[pl.ds(pl.multiple_of(at, TILE), count), :]
+        keys = key_ref[:, pl.ds(pl.multiple_of(k * span, HD), span)]
+        return jnp.dot(rows, keys, preferred_element_type=jnp.float32)
 
     def score(scores, top, i, k):
-        rows = query_all[pl.ds(pl.multiple_of(jnp.minimum(i, supers - 1) * pair, TILE), pair), :]
-        keys = key_ref[:, pl.ds(pl.multiple_of(k * span, HD), span)]
-        found = jnp.dot(rows, keys, preferred_element_type=jnp.float32)
-        scores[...] = found
-        top[...] = row_top(found)
-
-    def mask(scores, top, first):
-        row_ids = lax.broadcasted_iota(jnp.int32, (pair, HD), 0)
-        row = row_ids + cls * block - first
-        for n in range(1, 4):
-            row = row + jnp.where(row_ids >= n * block, TOK_DEV - block, 0)
-        col = lax.broadcasted_iota(jnp.int32, (pair, span), 1)
-        found = jnp.where(
-            col <= jnp.concatenate([row] * (span // HD), axis=1), scores[...], masked_score
-        )
-        scores[...] = found
-        top[...] = row_top(found)
-
-    def absorb(scores, top, k):
-        before = run_max[...]
-        after = jnp.maximum(before, top[...])
+        put(scores, top, keep_all, dot_keys(i, k, 0, pair))
+
+    def score_lower(scores, top, i, k):
+        found = dot_keys(i, k, upper, pair - upper)
+        found = jnp.where(allowed(upper, pair - upper, span), found, masked_score)
+        put(scores, top, lower, found)
+
+    def mask_upper(scores, top):
+        found = jnp.where(allowed(0, upper, 0), scores[:upper, :], masked_score)
+        put(scores, top, slice(0, upper), found)
+
+    def absorb(scores, top, k, part):
+        before = run_max[part, :]
+        after = jnp.maximum(before, top[part, :])
         rescale = jnp.exp2((before - after) * exp2_scale)
-        run_max[...] = after
+        run_max[part, :] = after
         weights = jnp.exp2(
-            (scores[...] - jnp.concatenate([after] * (span // HD), axis=1)) * exp2_scale
+            (scores[part, :] - jnp.concatenate([after] * (span // HD), axis=1)) * exp2_scale
         )
         values = value_ref[pl.ds(pl.multiple_of(k * span, TILE), span), :]
-        run_acc[...] = run_acc[...] * jnp.concatenate([rescale, rescale], axis=1) + jnp.dot(
+        run_acc[part, :] = run_acc[part, :] * jnp.concatenate([rescale, rescale], axis=1) + jnp.dot(
             weights.astype(jnp.bfloat16), values, preferred_element_type=jnp.float32
         )
 
@@ -273,34 +287,38 @@
         run_max[...] = jnp.full_like(run_max, masked_score)
         run_acc[...] = jnp.zeros_like(run_acc)
 
-    def one_step(now, later, i, k):
-        last = k == 2 * i + 1
-        next_i = jnp.where(last, i + 1, i)
-        next_k = jnp.where(last, 0, k + 1)
-        score(*later, next_i, next_k)
-        absorb(*now, k)
+    buffers_a, buffers_b = (scores_a, top_a), (scores_b, top_b)
+    clear()
+    score(*buffers_a, 0, 0)
+    mask_upper(*buffers_a)
+
+    def two_steps(t, at):
+        i, k = at
+        last = k == 2 * i
 
         @pl.when(last)
         def _():
+            score_lower(*buffers_b, i, k + 1)
+            absorb(*buffers_a, k, keep_all)
+            score(*buffers_a, i + 1, 0)
+            absorb(*buffers_b, k + 1, lower)
             result = (run_acc[:, :HD] / run_acc[:, HD:]).astype(jnp.bfloat16)
             for n in range(4):
                 out_ref[4 * i + n] = result[n * block : (n + 1) * block]
             clear()
 
-        @pl.when(next_k >= 2 * next_i)
+        @pl.when(jnp.logical_not(last))
         def _():
-            mask(*later, (next_k - 2 * next_i) * span)
-
-        return next_i, next_k
-
-    buffers_a, buffers_b = (scores_a, top_a), (scores_b, top_b)
-    clear()
-    score(*buffers_a, 0, 0)
-    mask(*buffers_a, 0)
-
-    def two_steps(t, at):
-        at = one_step(buffers_a, buffers_b, *at)
-        return one_step(buffers_b, buffers_a, *at)
+            score(*buffers_b, i, k + 1)
+            absorb(*buffers_a, k, keep_all)
+            score(*buffers_a, i, k + 2)
+            absorb(*buffers_b, k + 1, keep_all)
+
+            @pl.when(k + 2 == 2 * i)
+            def _():
+                mask_upper(*buffers_a)
+
+        return jnp.where(last, i + 1, i), jnp.where(last, 0, k + 2)
 
     lax.fori_loop(0, steps // 2, two_steps, (jnp.int32(0), jnp.int32(0)))
 

time: 265 us -> 260 us (0.981)
  Pallas kernels: 126 us -> 117 us
    pallas_call x2, Pallas kernels: 51.5 us -> 42.1 us  [attend(): pl.pallas_call(functools.partial(attend_kernel, ctx_size, block), in_spec...]
  transfers between devices with their start and end apart: 16 -> 16, of which waited for: 11 -> 12; matrix products, arithmetic and copies ran while one was open for 0% -> 0% of each run, Pallas kernels for 43% -> 40%
where the time goes in v15:
time: 260 us; the launch traced here: 259 us
  Pallas kernels  117 us (45%)
  waiting for transfers between devices  88.1 us (34%)
  starting transfers between devices  44.5 us (17%)
  local copies, waits for them, and re-layouts  6.6 us (3%)
    ppermute x6, waiting for transfers between devices, swap(): return parts + [lax.ppermute(part, 'ctx', pairs) for part in parts]  42.8 us
    pallas_call x2, Pallas kernels, attend(): pl.pallas_call(functools.partial(attend_kernel, ctx_size, block), in_spec...  42.1 us
    pallas_call x5, Pallas kernels, project(): pl.pallas_call(functools.partial(project_kernel, classes, len(got)), grid...  39.4 us
    all_to_all x2, waiting for transfers between devices, send_across(): lax.all_to_all(packed, 'ctx', split_axis=0, concat_axis=0, tiled=True, ax...  18.1 us
    pallas_call x3, Pallas kernels, pack(): pl.pallas_call(functools.partial(pack_kernel, turned, classes, cap, width...  15.4 us
    ppermute x4, waiting for transfers between devices, trade(): return [lax.ppermute(part, 'tp', [(0, 1), (1, 0)]) for part in parts]  14.2 us
    all_to_all x1, waiting for transfers between devices, local(): last = lax.all_to_all(done, 'ctx', split_axis=0, concat_axis=0, tiled=True)  10.7 us
    pallas_call x2, Pallas kernels, compact(): pl.pallas_call(functools.partial(compact_kernel, offsets, per, total, as_...  9.87 us
  transfers between devices with their start and end apart: 16, of which 12 were waited for; matrix products, arithmetic and copies ran while one was open for 0% of the time, Pallas kernels for 40%

profile of v15, /device:TPU:0, one launch (start us, length us, event | category | flops | bytes accessed | tf_op | source)
XLA Modules:
  0.0 258.8 jit_solution(821804092858006397)
XLA Ops:
  0.0 2.5 negate_select_fusion
  4.1 3.5 %shard_map.67 = bf16[4,1,784,128]{3,2,1,0:T(8,128)(2,1)} custom-call(s32[1,768]{1,0:T(1,128)} %get-tuple-element.28.slot_ref, f32[768,128]{1,0:T(8,128)} %get-tuple-element.46.cos_ref, f32[768,128]{1,0:T(8,128)} %get-tuple-element.45.sin_ref, bf16[768,512]{1,0:T(8,128)(2,1)} %row_ref.5), custom_call_target="tpu_custom_call" | custom-call | flops 616562688 | bytes 1572864 | tf_op jit(solution)/shard_map/pallas_call | solution.py:124
  7.6 6.3 %all-to-all-start = ((bf16[4,784,128]{2,1,0:T(8,128)(2,1)}), bf16[4,784,128]{2,1,0:T(8,128)(2,1)S(1)}, u32[]{:S(2)}, u32[]{:S(2)}) async-start(bf16[4,784,128]{2,1,0:T(8,128)(2,1)} %bitcast.10), calls=%async_computation | async-start | bytes 1605632 | tf_op jit(solution)/shard_map/all_to_all | solution.py:460
  13.9 3.2 %shard_map.66 = bf16[4,1,784,128]{3,2,1,0:T(8,128)(2,1)} custom-call(s32[1,768]{1,0:T(1,128)} %get-tuple-element.28.slot_ref, f32[768,128]{1,0:T(8,128)} %get-tuple-element.46.cos_ref, f32[768,128]{1,0:T(8,128)} %get-tuple-element.45.sin_ref, bf16[768,512]{1,0:T(8,128)(2,1)} %row_ref.4), custom_call_target="tpu_custom_call" | custom-call | flops 616562688 | bytes 1572864 | tf_op jit(solution)/shard_map/pallas_call | solution.py:124
  17.1 17.2 %all-to-all-done.rest_0_ = bf16[4,784,128]{2,1,0:T(8,128)(2,1)S(1)} async-done(((bf16[4,784,128]{2,1,0:T(8,128)(2,1)}), bf16[4,784,128]{2,1,0:T(8,128)(2,1)S(1)}, u32[]{:S(2)}, u32[]{:S(2)}) %all-to-all-start) | async-done | bytes 802848 | tf_op jit(solution)/shard_map/all_to_all | solution.py:460
  34.4 3.5 %all-to-all-start.1 = ((bf16[4,784,128]{2,1,0:T(8,128)(2,1)}), bf16[4,784,128]{2,1,0:T(8,128)(2,1)S(1)}, u32[]{:S(2)}, u32[]{:S(2)}) async-start(bf16[4,784,128]{2,1,0:T(8,128)(2,1)} %bitcast.9), calls=%async_computation.1 | async-start | bytes 1605632 | tf_op jit(solution)/shard_map/all_to_all | solution.py:460
  39.4 8.7 %shard_map.65 = (bf16[16,1,400,128]{3,2,1,0:T(8,128)(2,1)}, bf16[16,1,400,128]{3,2,1,0:T(8,128)(2,1)}) custom-call(s32[1,768]{1,0:T(1,128)} %get-tuple-element.25.slot_ref, f32[768,128]{1,0:T(8,128)} %get-tuple-element.46.cos_ref, f32[768,128]{1,0:T(8,128)} %get-tuple-element.45.sin_ref, bf16[768,2048]{1,0:T(8,128)(2,1)} %row_ref.3), custom_call_target="tpu_custom_call" | custom-call | flops 2516582400 | bytes 6291456 | tf_op jit(solution)/shard_map/pallas_call | solution.py:124
  48.1 8.8 %collective-permute-done.rest_1_ = bf16[4,784,128]{2,1,0:T(8,128)(2,1)} collective-permute-done((bf16[4,784,128]{2,1,0:T(8,128)(2,1)S(1)}, bf16[4,784,128]{2,1,0:T(8,128)(2,1)}, u32[]{:S(2)}, u32[]{:S(2)}) %collective-permute-start) | collective-permute-done | bytes 802848 | tf_op jit(solution)/shard_map/ppermute | solution.py:466
  57.8 4.9 %all-to-all-start.3 = ((bf16[16,400,128]{2,1,0:T(8,128)(2,1)}), bf16[16,400,128]{2,1,0:T(8,128)(2,1)S(1)}, u32[]{:S(2)}, u32[]{:S(2)}) async-start(bf16[16,400,128]{2,1,0:T(8,128)(2,1)} %bitcast.11), calls=%async_computation.3 | async-start | bytes 3276800 | tf_op jit(solution)/shard_map/all_to_all | solution.py:474
  66.6 4.7 %shard_map.68.key_ref = bf16[128,6144]{1,0:T(8,128)(2,1)} custom-call(s32[1]{0:T(128)} %bitcast.4.member_ref, s32[16]{0:T(128)} %count_ref.9, bf16[4,784,128]{2,1,0:T(8,128)(2,1)} %copy-done.3, bf16[4,784,128]{2,1,0:T(8,128)(2,1)} %collective-permute-done.rest_1_, bf16[4,784,128]{2,1,0:T(8,128)(2,1)} %collective-permute-done.2.rest_2_, ...), custom_call_target="tpu_custom_call" | custom-call | flops 6291456 | bytes 6291456 | tf_op jit(solution)/shard_map/pallas_call | solution.py:196
  71.2 29.4 %collective-permute-done.1.rest_1_ = bf16[4,784,128]{2,1,0:T(8,128)(2,1)} collective-permute-done((bf16[4,784,128]{2,1,0:T(8,128)(2,1)S(1)}, bf16[4,784,128]{2,1,0:T(8,128)(2,1)}, u32[]{:S(2)}, u32[]{:S(2)}) %collective-permute-start.1) | collective-permute-done | bytes 802848 | tf_op jit(solution)/shard_map/ppermute | solution.py:466
  101.8 4.6 %all-to-all-start.2 = ((bf16[16,400,128]{2,1,0:T(8,128)(2,1)}), bf16[16,400,128]{2,1,0:T(8,128)(2,1)S(1)}, u32[]{:S(2)}, u32[]{:S(2)}) async-start(bf16[16,400,128]{2,1,0:T(8,128)(2,1)} %bitcast.5), calls=%async_computation.2 | async-start | bytes 3276800 | tf_op jit(solution)/shard_map/all_to_all | solution.py:474
  111.2 5.2 %shard_map.69.value_ref = bf16[6144,256]{1,0:T(8,128)(2,1)} custom-call(s32[1]{0:T(128)} %bitcast.4.member_ref, s32[16]{0:T(128)} %count_ref.9, bf16[4,784,128]{2,1,0:T(8,128)(2,1)} %copy-done.2, bf16[4,784,128]{2,1,0:T(8,128)(2,1)} %collective-permute-done.1.rest_1_, bf16[4,784,128]{2,1,0:T(8,128)(2,1)} %copy-done.6, bf16[4,784,128]{2,1,0:T(8,128)(2,1)} %copy-done.7), custom_call_target="tpu_custom_call" | custom-call | flops 6291456 | bytes 6291456 | tf_op jit(solution)/shard_map/pallas_call | solution.py:196
  116.4 21.0 %shard_map.70 = bf16[16,192,128]{2,1,0:T(8,128)(2,1)} custom-call(s32[1]{0:T(128)} %constant.64.clone.1.cls_ref, s32[16]{0:T(128)} %count_ref.9, bf16[16,400,128]{2,1,0:T(8,128)(2,1)} %copy-done.5, bf16[128,6144]{1,0:T(8,128)(2,1)} %shard_map.68.key_ref, bf16[6144,256]{1,0:T(8,128)(2,1)} %shard_map.69.value_ref), custom_call_target="tpu_custom_call" | custom-call | flops 9663676416 | bytes 6291456 | tf_op jit(solution)/shard_map/pallas_call | solution.py:330
  139.6 9.4 %all-to-all-start.4 = ((bf16[16,192,128]{2,1,0:T(8,128)(2,1)}), bf16[16,192,128]{2,1,0:T(8,128)(2,1)S(1)}, u32[]{:S(2)}, u32[]{:S(2)}) async-start(bf16[16,192,128]{2,1,0:T(8,128)(2,1)} %shard_map.70), calls=%async_computation.4 | async-start | bytes 1572864 | tf_op jit(solution)/shard_map/all_to_all | solution.py:505
  149.0 21.1 %shard_map.71 = bf16[16,192,128]{2,1,0:T(8,128)(2,1)} custom-call(s32[1]{0:T(128)} %constant.65.clone.1.cls_ref, s32[16]{0:T(128)} %count_ref.9, bf16[16,400,128]{2,1,0:T(8,128)(2,1)} %copy-done.4, bf16[128,6144]{1,0:T(8,128)(2,1)} %shard_map.68.key_ref, bf16[6144,256]{1,0:T(8,128)(2,1)} %shard_map.69.value_ref), custom_call_target="tpu_custom_call" | custom-call | flops 9663676416 | bytes 6291456 | tf_op jit(solution)/shard_map/pallas_call | solution.py:330
  171.0 6.4 %shard_map.72 = bf16[192,2048]{1,0:T(8,128)(2,1)} custom-call(s32[1]{0:T(128)} %bitcast.7.column_ref, bf16[16,192,128]{2,1,0:T(8,128)(2,1)} %copy-done, bf16[2048,8192]{1,0:T(8,128)(2,1)} %rest_1_.7), custom_call_target="tpu_custom_call" | custom-call | flops 1610612736 | bytes 8388608 | tf_op jit(solution)/shard_map/pallas_call | solution.py:372
  177.4 6.0 %all-to-all-start.5 = ((bf16[16,192,128]{2,1,0:T(8,128)(2,1)}), bf16[16,192,128]{2,1,0:T(8,128)(2,1)S(1)}, u32[]{:S(2)}, u32[]{:S(2)}) async-start(bf16[16,192,128]{2,1,0:T(8,128)(2,1)} %shard_map.71), calls=%async_computation.5 | async-start | bytes 1572864 | tf_op jit(solution)/shard_map/all_to_all | solution.py:527
  185.0 6.4 %shard_map.73 = bf16[192,2048]{1,0:T(8,128)(2,1)} custom-call(s32[1]{0:T(128)} %bitcast.8.column_ref, bf16[16,192,128]{2,1,0:T(8,128)(2,1)} %copy-done, bf16[2048,8192]{1,0:T(8,128)(2,1)} %rest_1_.7), custom_call_target="tpu_custom_call" | custom-call | flops 1610612736 | bytes 8388608 | tf_op jit(solution)/shard_map/pallas_call | solution.py:372
  191.4 10.7 %all-to-all-done.5.rest_1_.rest_0_ = bf16[16,192,128]{2,1,0:T(8,128)(2,1)S(1)} async-done(((bf16[16,192,128]{2,1,0:T(8,128)(2,1)}), bf16[16,192,128]{2,1,0:T(8,128)(2,1)S(1)}, u32[]{:S(2)}, u32[]{:S(2)}) %all-to-all-start.5) | async-done | bytes 786464 | tf_op jit(solution)/shard_map/all_to_all | solution.py:527
  203.7 6.4 %shard_map.77 = bf16[192,2048]{1,0:T(8,128)(2,1)} custom-call(s32[1]{0:T(128)} %bitcast.7.column_ref, bf16[16,192,128]{2,1,0:T(8,128)(2,1)} %copy-done.1, bf16[2048,8192]{1,0:T(8,128)(2,1)} %rest_1_.7), custom_call_target="tpu_custom_call" | custom-call | flops 1610612736 | bytes 8388608 | tf_op jit(solution)/shard_map/pallas_call | solution.py:372
  211.0 6.4 %shard_map.79 = bf16[192,2048]{1,0:T(8,128)(2,1)} custom-call(s32[1]{0:T(128)} %bitcast.8.column_ref, bf16[16,192,128]{2,1,0:T(8,128)(2,1)} %copy-done.1, bf16[2048,8192]{1,0:T(8,128)(2,1)} %rest_1_.7), custom_call_target="tpu_custom_call" | custom-call | flops 1610612736 | bytes 8388608 | tf_op jit(solution)/shard_map/pallas_call | solution.py:372
  218.5 13.8 %shard_map.74.sum_ref = bf16[384,4096]{1,0:T(8,128)(2,1)} custom-call(s32[1]{0:T(128)} %bitcast.column_ref, bf16[16,192,128]{2,1,0:T(8,128)(2,1)} %copy-done, bf16[16,192,128]{2,1,0:T(8,128)(2,1)} %copy-done.1, bf16[2048,8192]{1,0:T(8,128)(2,1)} %rest_1_.7), custom_call_target="tpu_custom_call" | custom-call | flops 6442450944 | bytes 16777216 | tf_op jit(solution)/shard_map/pallas_call | solution.py:372
  242.6 13.1 %collective-permute-done.9.part_ref = bf16[192,2048]{1,0:T(8,128)(2,1)S(1)} collective-permute-done((bf16[192,2048]{1,0:T(8,128)(2,1)}, bf16[192,2048]{1,0:T(8,128)(2,1)S(1)}, u32[]{:S(2)}, u32[]{:S(2)}) %collective-permute-start.9) | collective-permute-done | bytes 786464 | tf_op jit(solution)/shard_map/ppermute | solution.py:521
  (53 shorter events, 35.5 us)
Async XLA Ops:
  7.6 26.8 %all-to-all-start = ((bf16[4,784,128]{2,1,0:T(8,128)(2,1)}), bf16[4,784,128]{2,1,0:T(8,128)(2,1)S(1)}, u32[]{:S(2)}, u32[]{:S(2)}) async-start(bf16[4,784,128]{2,1,0:T(8,128)(2,1)} %bitcast.10), calls=%async_computation | async-start | bytes 1605632 | tf_op jit(solution)/shard_map/all_to_all | solution.py:460
  34.4 28.3 %copy-start.3 = (bf16[4,784,128]{2,1,0:T(8,128)(2,1)}, bf16[4,784,128]{2,1,0:T(8,128)(2,1)S(1)}, u32[]{:S(2)}) copy-start(bf16[4,784,128]{2,1,0:T(8,128)(2,1)S(1)} %all-to-all-done.rest_0_) | copy-start | bytes 2408452
  34.4 23.4 %all-to-all-start.1 = ((bf16[4,784,128]{2,1,0:T(8,128)(2,1)}), bf16[4,784,128]{2,1,0:T(8,128)(2,1)S(1)}, u32[]{:S(2)}, u32[]{:S(2)}) async-start(bf16[4,784,128]{2,1,0:T(8,128)(2,1)} %bitcast.9), calls=%async_computation.1 | async-start | bytes 1605632 | tf_op jit(solution)/shard_map/all_to_all | solution.py:460
  37.9 19.0 %collective-permute-start = (bf16[4,784,128]{2,1,0:T(8,128)(2,1)S(1)}, bf16[4,784,128]{2,1,0:T(8,128)(2,1)}, u32[]{:S(2)}, u32[]{:S(2)}) collective-permute-start(bf16[4,784,128]{2,1,0:T(8,128)(2,1)S(1)} %all-to-all-done.rest_0_), channel_id=1, source_target_pairs={{0,4},{2,6},{4,0},{6,2},{8,12},{10,14},{12,8},{14,10},{16,20},{18,... | collective-permute-start | bytes 2408456 | tf_op jit(solution)/shard_map/ppermute | solution.py:466
  57.8 48.7 %copy-start.2 = (bf16[4,784,128]{2,1,0:T(8,128)(2,1)}, bf16[4,784,128]{2,1,0:T(8,128)(2,1)S(1)}, u32[]{:S(2)}) copy-start(bf16[4,784,128]{2,1,0:T(8,128)(2,1)S(1)} %all-to-all-done.1.rest_0_) | copy-start | bytes 2408452
  57.8 42.9 %all-to-all-start.3 = ((bf16[16,400,128]{2,1,0:T(8,128)(2,1)}), bf16[16,400,128]{2,1,0:T(8,128)(2,1)S(1)}, u32[]{:S(2)}, u32[]{:S(2)}) async-start(bf16[16,400,128]{2,1,0:T(8,128)(2,1)} %bitcast.11), calls=%async_computation.3 | async-start | bytes 3276800 | tf_op jit(solution)/shard_map/all_to_all | solution.py:474
  62.7 2.6 %collective-permute-start.2 = (bf16[4,784,128]{2,1,0:T(8,128)(2,1)S(1)}, bf16[4,784,128]{2,1,0:T(8,128)(2,1)}, u32[]{:S(2)}, u32[]{:S(2)}) collective-permute-start(bf16[4,784,128]{2,1,0:T(8,128)(2,1)S(1)} %all-to-all-done.rest_0_), channel_id=1, source_target_pairs={{0,2},{2,0},{4,6},{6,4},{8,10},{10,8},{12,14},{14,12},{16,18},{18,... | collective-permute-start | bytes 2408456 | tf_op jit(solution)/shard_map/ppermute | solution.py:466
  63.1 3.4 %collective-permute-start.3 = (bf16[4,784,128]{2,1,0:T(8,128)(2,1)}, bf16[4,784,128]{2,1,0:T(8,128)(2,1)}, u32[]{:S(2)}, u32[]{:S(2)}) collective-permute-start(bf16[4,784,128]{2,1,0:T(8,128)(2,1)} %collective-permute-done.rest_1_), channel_id=1, source_target_pairs={{0,2},{2,0},{4,6},{6,4},{8,10},{10,8},{12,14},{14,12},{16,18},{18,... | collective-permute-start | bytes 2408456 | tf_op jit(solution)/shard_map/ppermute | solution.py:466
  63.2 37.4 %collective-permute-start.1 = (bf16[4,784,128]{2,1,0:T(8,128)(2,1)S(1)}, bf16[4,784,128]{2,1,0:T(8,128)(2,1)}, u32[]{:S(2)}, u32[]{:S(2)}) collective-permute-start(bf16[4,784,128]{2,1,0:T(8,128)(2,1)S(1)} %all-to-all-done.1.rest_0_), channel_id=1, source_target_pairs={{0,4},{2,6},{4,0},{6,2},{8,12},{10,14},{12,8},{14,10},{16,20},{18,... | collective-permute-start | bytes 2408456 | tf_op jit(solution)/shard_map/ppermute | solution.py:466
  100.7 1.2 copy-start.5
  101.8 37.8 %all-to-all-start.2 = ((bf16[16,400,128]{2,1,0:T(8,128)(2,1)}), bf16[16,400,128]{2,1,0:T(8,128)(2,1)S(1)}, u32[]{:S(2)}, u32[]{:S(2)}) async-start(bf16[16,400,128]{2,1,0:T(8,128)(2,1)} %bitcast.5), calls=%async_computation.2 | async-start | bytes 3276800 | tf_op jit(solution)/shard_map/all_to_all | solution.py:474
  106.5 2.5 collective-permute-start.4
  107.0 3.3 %collective-permute-start.5 = (bf16[4,784,128]{2,1,0:T(8,128)(2,1)}, bf16[4,784,128]{2,1,0:T(8,128)(2,1)S(1)}, u32[]{:S(2)}, u32[]{:S(2)}) collective-permute-start(bf16[4,784,128]{2,1,0:T(8,128)(2,1)} %collective-permute-done.1.rest_1_), channel_id=1, source_target_pairs={{0,2},{2,0},{4,6},{6,4},{8,10},{10,8},{12,14},{14,12},{16,18},{18,... | collective-permute-start | bytes 2408456 | tf_op jit(solution)/shard_map/ppermute | solution.py:466
  109.0 1.3 copy-start.6
  110.3 1.0 copy-start.7
  139.6 9.4 %copy-start.4 = (bf16[16,400,128]{2,1,0:T(8,128)(2,1)}, bf16[16,400,128]{2,1,0:T(8,128)(2,1)S(1)}, u32[]{:S(2)}) copy-start(bf16[16,400,128]{2,1,0:T(8,128)(2,1)S(1)} %all-to-all-done.2.got_ref) | copy-start | bytes 4915204
  139.6 30.5 %all-to-all-start.4 = ((bf16[16,192,128]{2,1,0:T(8,128)(2,1)}), bf16[16,192,128]{2,1,0:T(8,128)(2,1)S(1)}, u32[]{:S(2)}, u32[]{:S(2)}) async-start(bf16[16,192,128]{2,1,0:T(8,128)(2,1)} %shard_map.70), calls=%async_computation.4 | async-start | bytes 1572864 | tf_op jit(solution)/shard_map/all_to_all | solution.py:505
  177.4 24.7 %all-to-all-start.5 = ((bf16[16,192,128]{2,1,0:T(8,128)(2,1)}), bf16[16,192,128]{2,1,0:T(8,128)(2,1)S(1)}, u32[]{:S(2)}, u32[]{:S(2)}) async-start(bf16[16,192,128]{2,1,0:T(8,128)(2,1)} %shard_map.71), calls=%async_computation.5 | async-start | bytes 1572864 | tf_op jit(solution)/shard_map/all_to_all | solution.py:527
  183.4 48.9 %collective-permute-start.6 = (bf16[192,2048]{1,0:T(8,128)(2,1)}, bf16[192,2048]{1,0:T(8,128)(2,1)S(1)}, u32[]{:S(2)}, u32[]{:S(2)}) collective-permute-start(bf16[192,2048]{1,0:T(8,128)(2,1)} %shard_map.72), channel_id=1, source_target_pairs={{0,1},{1,0},{2,3},{3,2},{4,5},{5,4},{6,7},{7,6},{8,9},{9,8},{10,11... | collective-permute-start | bytes 2359304 | tf_op jit(solution)/shard_map/ppermute | solution.py:521
  202.1 1.5 copy-start.1
  202.1 33.2 %collective-permute-start.7 = (bf16[192,2048]{1,0:T(8,128)(2,1)}, bf16[192,2048]{1,0:T(8,128)(2,1)S(1)}, u32[]{:S(2)}, u32[]{:S(2)}) collective-permute-start(bf16[192,2048]{1,0:T(8,128)(2,1)} %shard_map.73), channel_id=1, source_target_pairs={{0,1},{1,0},{2,3},{3,2},{4,5},{5,4},{6,7},{7,6},{8,9},{9,8},{10,11... | collective-permute-start | bytes 2359304 | tf_op jit(solution)/shard_map/ppermute | solution.py:521
  210.1 29.5 %collective-permute-start.8 = (bf16[192,2048]{1,0:T(8,128)(2,1)}, bf16[192,2048]{1,0:T(8,128)(2,1)S(1)}, u32[]{:S(2)}, u32[]{:S(2)}) collective-permute-start(bf16[192,2048]{1,0:T(8,128)(2,1)} %shard_map.77), channel_id=1, source_target_pairs={{0,1},{1,0},{2,3},{3,2},{4,5},{5,4},{6,7},{7,6},{8,9},{9,8},{10,11... | collective-permute-start | bytes 2359304 | tf_op jit(solution)/shard_map/ppermute | solution.py:521
  217.3 38.4 %collective-permute-start.9 = (bf16[192,2048]{1,0:T(8,128)(2,1)}, bf16[192,2048]{1,0:T(8,128)(2,1)S(1)}, u32[]{:S(2)}, u32[]{:S(2)}) collective-permute-start(bf16[192,2048]{1,0:T(8,128)(2,1)} %shard_map.79), channel_id=1, source_target_pairs={{0,1},{1,0},{2,3},{3,2},{4,5},{5,4},{6,7},{7,6},{8,9},{9,8},{10,11... | collective-permute-start | bytes 2359304 | tf_op jit(solution)/shard_map/ppermute | solution.py:521
  235.4 0.9 copy-start.11
  (4 other events, 3.5 us)

commit v16 on v15

--- a/solution.py
+++ b/solution.py
@@ -187,8 +187,7 @@
                 all_rows[first : first + 2 * TOK_DEV, :]
             )
     else:
-        out[:, :HD] = all_rows[:total, :]
-        out[:, HD:] = jnp.ones((total, HD), jnp.bfloat16)
+        out[...] = all_rows[:total, :]
 
 
 def compact(member, counts, parts, offsets, total, as_keys):
@@ -198,7 +197,7 @@
         in_specs=[whole_smem(), whole_smem()] + [whole_vmem()] * len(parts),
         out_specs=whole_vmem(),
         out_shape=jax.ShapeDtypeStruct(
-            (HD, total) if as_keys else (total, 2 * HD), jnp.bfloat16
+            (HD, total) if as_keys else (total, HD), jnp.bfloat16
         ),
         scratch_shapes=[
             pltpu.VMEM((total + PAD, HD), jnp.bfloat16),
@@ -278,7 +277,13 @@
         weights = jnp.exp2(
             (scores[part, :] - jnp.concatenate([after] * (span // HD), axis=1)) * exp2_scale
         )
-        values = value_ref[pl.ds(pl.multiple_of(k * span, TILE), span), :]
+        values = jnp.concatenate(
+            [
+                value_ref[pl.ds(pl.multiple_of(k * span, TILE), span), :],
+                jnp.ones((span, HD), jnp.bfloat16),
+            ],
+            axis=1,
+        )
         run_acc[part, :] = run_acc[part, :] * jnp.concatenate([rescale, rescale], axis=1) + jnp.dot(
             weights.astype(jnp.bfloat16), values, preferred_element_type=jnp.float32
         )
@@ -393,11 +398,11 @@
     ).astype(jnp.bfloat16)
 
 
-def add_piece(total_sum, part, j, n):
+def add_piece(total_sum, part, j, first):
     rows, width = part.shape
-    step = min(1024, width)
+    step = 512
     steps = width // step
-    here = pl.BlockSpec((rows, step), lambda i: (j, n * steps + i))
+    here = pl.BlockSpec((rows, step), lambda i: (j, first // step + i))
     return pl.pallas_call(
         add_piece_kernel,
         grid=(steps,),
@@ -509,12 +514,13 @@
         if j + 2 < chunks:
             packed_q[j + 2], done = lax.optimization_barrier((packed_q[j + 2], done))
             got_q.append(send_query(packed_q[j + 2]))
-    half = columns // 2
-
-    def for_peer(one):
+    quarter = columns // 4
+    widths = [(quarter, 3 * quarter), (3 * quarter, quarter)]
+
+    def for_peer(one, j):
         return [
-            project((1 - tp_me) * columns + n * half, [one], out_weight, half, classes)
-            for n in range(2)
+            project((1 - tp_me) * columns + first, [one], out_weight, width, classes)
+            for first, width in zip((0, widths[j][0]), widths[j])
         ]
 
     def trade(parts):
@@ -522,16 +528,16 @@
 
     paired = tp_size == 2 and chunks == 2
     if paired:
-        first = for_peer(got[0])
+        first = for_peer(got[0], 0)
         done, first[0] = lax.optimization_barrier((done, first[0]))
     last = lax.all_to_all(done, "ctx", split_axis=0, concat_axis=0, tiled=True)
     if paired:
         last, first[1] = lax.optimization_barrier((last, first[1]))
-        came = [trade(first), trade(for_peer(last))]
+        came = [trade(first), trade(for_peer(last, 1))]
         total_sum = project(tp_me * columns, got + [last], out_weight, columns, classes)
         for j, parts in enumerate(came):
-            for n, part in enumerate(parts):
-                total_sum = add_piece(total_sum, part, j, n)
+            total_sum = add_piece(total_sum, parts[0], j, 0)
+            total_sum = add_piece(total_sum, parts[1], j, widths[j][0])
         return total_sum
     got.append(last)
     full = project(jnp.int32(0) * tp_me, got, out_weight, columns * tp_size, classes)

time: 260 us -> 280 us (1.077)
  waiting for transfers between devices: 88.1 us -> 107 us
    ppermute x4, waiting for transfers between devices: 14.2 us -> 31.8 us  [trade(): return [lax.ppermute(part, 'tp', [(0, 1), (1, 0)]) for part in parts]]
    pallas_call x4, Pallas kernels: 8.77 us -> 13.4 us  [add_piece(): pl.pallas_call(add_piece_kernel, grid=(steps,), in_specs=[here, pl.BlockS...]
    unnamed x24 -> x26, local copies, waits for them, and re-layouts: 6.6 us -> 6.6 us
  transfers between devices with their start and end apart: 16 -> 16, of which waited for: 12 -> 11; matrix products, arithmetic and copies ran while one was open for 0% -> 0% of each run, Pallas kernels for 40% -> 39%
where the time goes in v16:
time: 280 us; the launch traced here: 278 us
  Pallas kernels  119 us (42%)
  waiting for transfers between devices  107 us (38%)
  starting transfers between devices  43.7 us (16%)
  local copies, waits for them, and re-layouts  6.6 us (2%)
    ppermute x6, waiting for transfers between devices, swap(): return parts + [lax.ppermute(part, 'ctx', pairs) for part in parts]  42.8 us
    pallas_call x2, Pallas kernels, attend(): pl.pallas_call(functools.partial(attend_kernel, ctx_size, block), in_spec...  40.1 us
    pallas_call x5, Pallas kernels, project(): pl.pallas_call(functools.partial(project_kernel, classes, len(got)), grid...  39.2 us
    ppermute x4, waiting for transfers between devices, trade(): return [lax.ppermute(part, 'tp', [(0, 1), (1, 0)]) for part in parts]  31.8 us
    all_to_all x2, waiting for transfers between devices, send_across(): lax.all_to_all(packed, 'ctx', split_axis=0, concat_axis=0, tiled=True, ax...  18.2 us
    pallas_call x3, Pallas kernels, pack(): pl.pallas_call(functools.partial(pack_kernel, turned, classes, cap, width...  15.4 us
    pallas_call x4, Pallas kernels, add_piece(): pl.pallas_call(add_piece_kernel, grid=(steps,), in_specs=[here, pl.BlockS...  13.4 us
    all_to_all x1, waiting for transfers between devices, local(): last = lax.all_to_all(done, 'ctx', split_axis=0, concat_axis=0, tiled=True)  9.86 us
  transfers between devices with their start and end apart: 16, of which 11 were waited for; matrix products, arithmetic and copies ran while one was open for 0% of the time, Pallas kernels for 39%

profile of v16, /device:TPU:0, one launch (start us, length us, event | category | flops | bytes accessed | tf_op | source)
XLA Modules:
  0.0 278.3 jit_solution(3113803483572975406)
XLA Ops:
  7.6 6.3 %all-to-all-start = ((bf16[4,784,128]{2,1,0:T(8,128)(2,1)}), bf16[4,784,128]{2,1,0:T(8,128)(2,1)S(1)}, u32[]{:S(2)}, u32[]{:S(2)}) async-start(bf16[4,784,128]{2,1,0:T(8,128)(2,1)} %bitcast.11), calls=%async_computation | async-start | bytes 1605632 | tf_op jit(solution)/shard_map/all_to_all | solution.py:465
  17.1 17.3 %all-to-all-done.rest_0_ = bf16[4,784,128]{2,1,0:T(8,128)(2,1)S(1)} async-done(((bf16[4,784,128]{2,1,0:T(8,128)(2,1)}), bf16[4,784,128]{2,1,0:T(8,128)(2,1)S(1)}, u32[]{:S(2)}, u32[]{:S(2)}) %all-to-all-start) | async-done | bytes 802848 | tf_op jit(solution)/shard_map/all_to_all | solution.py:465
  34.4 3.5 %all-to-all-start.1 = ((bf16[4,784,128]{2,1,0:T(8,128)(2,1)}), bf16[4,784,128]{2,1,0:T(8,128)(2,1)S(1)}, u32[]{:S(2)}, u32[]{:S(2)}) async-start(bf16[4,784,128]{2,1,0:T(8,128)(2,1)} %bitcast.10), calls=%async_computation.1 | async-start | bytes 1605632 | tf_op jit(solution)/shard_map/all_to_all | solution.py:465
  39.4 8.7 %shard_map.65 = (bf16[16,1,400,128]{3,2,1,0:T(8,128)(2,1)}, bf16[16,1,400,128]{3,2,1,0:T(8,128)(2,1)}) custom-call(s32[1,768]{1,0:T(1,128)} %get-tuple-element.25.slot_ref, f32[768,128]{1,0:T(8,128)} %get-tuple-element.46.cos_ref, f32[768,128]{1,0:T(8,128)} %get-tuple-element.45.sin_ref, bf16[768,2048]{1,0:T(8,128)(2,1)} %row_ref.3), custom_call_target="tpu_custom_call" | custom-call | flops 2516582400 | bytes 6291456 | tf_op jit(solution)/shard_map/pallas_call | solution.py:124
  48.1 8.8 %collective-permute-done.rest_1_ = bf16[4,784,128]{2,1,0:T(8,128)(2,1)} collective-permute-done((bf16[4,784,128]{2,1,0:T(8,128)(2,1)S(1)}, bf16[4,784,128]{2,1,0:T(8,128)(2,1)}, u32[]{:S(2)}, u32[]{:S(2)}) %collective-permute-start) | collective-permute-done | bytes 802848 | tf_op jit(solution)/shard_map/ppermute | solution.py:471
  57.8 4.9 %all-to-all-start.3 = ((bf16[16,400,128]{2,1,0:T(8,128)(2,1)}), bf16[16,400,128]{2,1,0:T(8,128)(2,1)S(1)}, u32[]{:S(2)}, u32[]{:S(2)}) async-start(bf16[16,400,128]{2,1,0:T(8,128)(2,1)} %bitcast.12), calls=%async_computation.3 | async-start | bytes 3276800 | tf_op jit(solution)/shard_map/all_to_all | solution.py:479
  66.6 4.7 %shard_map.68.key_ref = bf16[128,6144]{1,0:T(8,128)(2,1)} custom-call(s32[1]{0:T(128)} %bitcast.4.member_ref, s32[16]{0:T(128)} %count_ref.9, bf16[4,784,128]{2,1,0:T(8,128)(2,1)} %copy-done.3, bf16[4,784,128]{2,1,0:T(8,128)(2,1)} %collective-permute-done.rest_1_, bf16[4,784,128]{2,1,0:T(8,128)(2,1)} %collective-permute-done.2.rest_2_, ...), custom_call_target="tpu_custom_call" | custom-call | flops 6291456 | bytes 6291456 | tf_op jit(solution)/shard_map/pallas_call | solution.py:195
  71.2 29.4 %collective-permute-done.1.rest_1_ = bf16[4,784,128]{2,1,0:T(8,128)(2,1)} collective-permute-done((bf16[4,784,128]{2,1,0:T(8,128)(2,1)S(1)}, bf16[4,784,128]{2,1,0:T(8,128)(2,1)}, u32[]{:S(2)}, u32[]{:S(2)}) %collective-permute-start.1) | collective-permute-done | bytes 802848 | tf_op jit(solution)/shard_map/ppermute | solution.py:471
  101.8 4.6 %all-to-all-start.2 = ((bf16[16,400,128]{2,1,0:T(8,128)(2,1)}), bf16[16,400,128]{2,1,0:T(8,128)(2,1)S(1)}, u32[]{:S(2)}, u32[]{:S(2)}) async-start(bf16[16,400,128]{2,1,0:T(8,128)(2,1)} %bitcast.5), calls=%async_computation.2 | async-start | bytes 3276800 | tf_op jit(solution)/shard_map/all_to_all | solution.py:479
  111.2 4.3 %shard_map.69.value_ref = bf16[6144,128]{1,0:T(8,128)(2,1)} custom-call(s32[1]{0:T(128)} %bitcast.4.member_ref, s32[16]{0:T(128)} %count_ref.9, bf16[4,784,128]{2,1,0:T(8,128)(2,1)} %copy-done.2, bf16[4,784,128]{2,1,0:T(8,128)(2,1)} %collective-permute-done.1.rest_1_, bf16[4,784,128]{2,1,0:T(8,128)(2,1)} %copy-done.8, bf16[4,784,128]{2,1,0:T(8,128)(2,1)} %copy-done.9), custom_call_target="tpu_custom_call" | custom-call | flops 6291456 | bytes 6291456 | tf_op jit(solution)/shard_map/pallas_call | solution.py:195
  115.5 20.0 %shard_map.70 = bf16[16,192,128]{2,1,0:T(8,128)(2,1)} custom-call(s32[1]{0:T(128)} %constant.70.clone.1.cls_ref, s32[16]{0:T(128)} %count_ref.9, bf16[16,400,128]{2,1,0:T(8,128)(2,1)} %copy-done.5, bf16[128,6144]{1,0:T(8,128)(2,1)} %shard_map.68.key_ref, bf16[6144,128]{1,0:T(8,128)(2,1)} %shard_map.69.value_ref), custom_call_target="tpu_custom_call" | custom-call | flops 9663676416 | bytes 6291456 | tf_op jit(solution)/shard_map/pallas_call | solution.py:335
  135.5 4.1 %all-to-all-done.2.got_ref = bf16[16,400,128]{2,1,0:T(8,128)(2,1)S(1)} async-done(((bf16[16,400,128]{2,1,0:T(8,128)(2,1)}), bf16[16,400,128]{2,1,0:T(8,128)(2,1)S(1)}, u32[]{:S(2)}, u32[]{:S(2)}) %all-to-all-start.2) | async-done | bytes 1638432 | tf_op jit(solution)/shard_map/all_to_all | solution.py:479
  139.6 9.4 %all-to-all-start.4 = ((bf16[16,192,128]{2,1,0:T(8,128)(2,1)}), bf16[16,192,128]{2,1,0:T(8,128)(2,1)S(1)}, u32[]{:S(2)}, u32[]{:S(2)}) async-start(bf16[16,192,128]{2,1,0:T(8,128)(2,1)} %shard_map.70), calls=%async_computation.4 | async-start | bytes 1572864 | tf_op jit(solution)/shard_map/all_to_all | solution.py:510
  149.0 20.2 %shard_map.71 = bf16[16,192,128]{2,1,0:T(8,128)(2,1)} custom-call(s32[1]{0:T(128)} %constant.71.clone.1.cls_ref, s32[16]{0:T(128)} %count_ref.9, bf16[16,400,128]{2,1,0:T(8,128)(2,1)} %copy-done.4, bf16[128,6144]{1,0:T(8,128)(2,1)} %shard_map.68.key_ref, bf16[6144,128]{1,0:T(8,128)(2,1)} %shard_map.69.value_ref), custom_call_target="tpu_custom_call" | custom-call | flops 9663676416 | bytes 6291456 | tf_op jit(solution)/shard_map/pallas_call | solution.py:335
  170.0 3.9 %shard_map.72 = bf16[192,1024]{1,0:T(8,128)(2,1)} custom-call(s32[1]{0:T(128)} %bitcast.7.column_ref, bf16[16,192,128]{2,1,0:T(8,128)(2,1)} %copy-done, bf16[2048,8192]{1,0:T(8,128)(2,1)} %rest_1_.7), custom_call_target="tpu_custom_call" | custom-call | flops 805306368 | bytes 4194304 | tf_op jit(solution)/shard_map/pallas_call | solution.py:377
  173.9 6.0 %all-to-all-start.5 = ((bf16[16,192,128]{2,1,0:T(8,128)(2,1)}), bf16[16,192,128]{2,1,0:T(8,128)(2,1)S(1)}, u32[]{:S(2)}, u32[]{:S(2)}) async-start(bf16[16,192,128]{2,1,0:T(8,128)(2,1)} %shard_map.71), calls=%async_computation.5 | async-start | bytes 1572864 | tf_op jit(solution)/shard_map/all_to_all | solution.py:533
  179.9 8.8 %shard_map.73 = bf16[192,3072]{1,0:T(8,128)(2,1)} custom-call(s32[1]{0:T(128)} %bitcast.8.column_ref, bf16[16,192,128]{2,1,0:T(8,128)(2,1)} %copy-done, bf16[2048,8192]{1,0:T(8,128)(2,1)} %rest_1_.7), custom_call_target="tpu_custom_call" | custom-call | flops 2415919104 | bytes 12582912 | tf_op jit(solution)/shard_map/pallas_call | solution.py:377
  188.7 9.9 %all-to-all-done.5.rest_1_.rest_0_ = bf16[16,192,128]{2,1,0:T(8,128)(2,1)S(1)} async-done(((bf16[16,192,128]{2,1,0:T(8,128)(2,1)}), bf16[16,192,128]{2,1,0:T(8,128)(2,1)S(1)}, u32[]{:S(2)}, u32[]{:S(2)}) %all-to-all-start.5) | async-done | bytes 786464 | tf_op jit(solution)/shard_map/all_to_all | solution.py:533
  200.1 8.8 %shard_map.77 = bf16[192,3072]{1,0:T(8,128)(2,1)} custom-call(s32[1]{0:T(128)} %bitcast.7.column_ref, bf16[16,192,128]{2,1,0:T(8,128)(2,1)} %copy-done.1, bf16[2048,8192]{1,0:T(8,128)(2,1)} %rest_1_.7), custom_call_target="tpu_custom_call" | custom-call | flops 2415919104 | bytes 12582912 | tf_op jit(solution)/shard_map/pallas_call | solution.py:377
  211.0 3.9 %shard_map.79 = bf16[192,1024]{1,0:T(8,128)(2,1)} custom-call(s32[1]{0:T(128)} %bitcast.9.column_ref, bf16[16,192,128]{2,1,0:T(8,128)(2,1)} %copy-done.1, bf16[2048,8192]{1,0:T(8,128)(2,1)} %rest_1_.7), custom_call_target="tpu_custom_call" | custom-call | flops 805306368 | bytes 4194304 | tf_op jit(solution)/shard_map/pallas_call | solution.py:377
  215.8 13.8 %shard_map.74.sum_ref = bf16[384,4096]{1,0:T(8,128)(2,1)} custom-call(s32[1]{0:T(128)} %bitcast.column_ref, bf16[16,192,128]{2,1,0:T(8,128)(2,1)} %copy-done, bf16[16,192,128]{2,1,0:T(8,128)(2,1)} %copy-done.1, bf16[2048,8192]{1,0:T(8,128)(2,1)} %rest_1_.7), custom_call_target="tpu_custom_call" | custom-call | flops 6442450944 | bytes 16777216 | tf_op jit(solution)/shard_map/pallas_call | solution.py:377
  229.6 31.8 %collective-permute-done.6.part_ref = bf16[192,1024]{1,0:T(8,128)(2,1)S(1)} collective-permute-done((bf16[192,1024]{1,0:T(8,128)(2,1)S(1)}, bf16[192,1024]{1,0:T(8,128)(2,1)S(1)}, u32[]{:S(2)}, u32[]{:S(2)}) %collective-permute-start.6) | collective-permute-done | bytes 393248 | tf_op jit(solution)/shard_map/ppermute | solution.py:527
  265.1 4.7 %shard_map.76.sum_ref = bf16[384,4096]{1,0:T(8,128)(2,1)} custom-call(bf16[384,4096]{1,0:T(8,128)(2,1)} %shard_map.75.sum_ref, bf16[192,3072]{1,0:T(8,128)(2,1)} %copy-done.7), custom_call_target="tpu_custom_call", output_to_operand_aliasing={{}: (0, {})} | custom-call | flops 589824 | bytes 3538944 | tf_op jit(solution)/shard_map/pallas_call | solution.py:406
  270.9 4.7 %shard_map.78.sum_ref = bf16[384,4096]{1,0:T(8,128)(2,1)} custom-call(bf16[384,4096]{1,0:T(8,128)(2,1)} %shard_map.76.sum_ref, bf16[192,3072]{1,0:T(8,128)(2,1)} %copy-done.6), custom_call_target="tpu_custom_call", output_to_operand_aliasing={{}: (0, {})} | custom-call | flops 589824 | bytes 3538944 | tf_op jit(solution)/shard_map/pallas_call | solution.py:406
  (55 shorter events, 35.8 us)
Async XLA Ops:
  7.6 26.8 %all-to-all-start = ((bf16[4,784,128]{2,1,0:T(8,128)(2,1)}), bf16[4,784,128]{2,1,0:T(8,128)(2,1)S(1)}, u32[]{:S(2)}, u32[]{:S(2)}) async-start(bf16[4,784,128]{2,1,0:T(8,128)(2,1)} %bitcast.11), calls=%async_computation | async-start | bytes 1605632 | tf_op jit(solution)/shard_map/all_to_all | solution.py:465
  34.4 28.3 %copy-start.3 = (bf16[4,784,128]{2,1,0:T(8,128)(2,1)}, bf16[4,784,128]{2,1,0:T(8,128)(2,1)S(1)}, u32[]{:S(2)}) copy-start(bf16[4,784,128]{2,1,0:T(8,128)(2,1)S(1)} %all-to-all-done.rest_0_) | copy-start | bytes 2408452
  34.4 23.4 %all-to-all-start.1 = ((bf16[4,784,128]{2,1,0:T(8,128)(2,1)}), bf16[4,784,128]{2,1,0:T(8,128)(2,1)S(1)}, u32[]{:S(2)}, u32[]{:S(2)}) async-start(bf16[4,784,128]{2,1,0:T(8,128)(2,1)} %bitcast.10), calls=%async_computation.1 | async-start | bytes 1605632 | tf_op jit(solution)/shard_map/all_to_all | solution.py:465
  37.9 19.0 %collective-permute-start = (bf16[4,784,128]{2,1,0:T(8,128)(2,1)S(1)}, bf16[4,784,128]{2,1,0:T(8,128)(2,1)}, u32[]{:S(2)}, u32[]{:S(2)}) collective-permute-start(bf16[4,784,128]{2,1,0:T(8,128)(2,1)S(1)} %all-to-all-done.rest_0_), channel_id=1, source_target_pairs={{0,4},{2,6},{4,0},{6,2},{8,12},{10,14},{12,8},{14,10},{16,20},{18,... | collective-permute-start | bytes 2408456 | tf_op jit(solution)/shard_map/ppermute | solution.py:471
  57.8 48.7 %copy-start.2 = (bf16[4,784,128]{2,1,0:T(8,128)(2,1)}, bf16[4,784,128]{2,1,0:T(8,128)(2,1)S(1)}, u32[]{:S(2)}) copy-start(bf16[4,784,128]{2,1,0:T(8,128)(2,1)S(1)} %all-to-all-done.1.rest_0_) | copy-start | bytes 2408452
  57.8 42.9 %all-to-all-start.3 = ((bf16[16,400,128]{2,1,0:T(8,128)(2,1)}), bf16[16,400,128]{2,1,0:T(8,128)(2,1)S(1)}, u32[]{:S(2)}, u32[]{:S(2)}) async-start(bf16[16,400,128]{2,1,0:T(8,128)(2,1)} %bitcast.12), calls=%async_computation.3 | async-start | bytes 3276800 | tf_op jit(solution)/shard_map/all_to_all | solution.py:479
  62.7 2.6 collective-permute-start.2
  63.1 3.4 %collective-permute-start.3 = (bf16[4,784,128]{2,1,0:T(8,128)(2,1)}, bf16[4,784,128]{2,1,0:T(8,128)(2,1)}, u32[]{:S(2)}, u32[]{:S(2)}) collective-permute-start(bf16[4,784,128]{2,1,0:T(8,128)(2,1)} %collective-permute-done.rest_1_), channel_id=1, source_target_pairs={{0,2},{2,0},{4,6},{6,4},{8,10},{10,8},{12,14},{14,12},{16,18},{18,... | collective-permute-start | bytes 2408456 | tf_op jit(solution)/shard_map/ppermute | solution.py:471
  63.2 37.4 %collective-permute-start.1 = (bf16[4,784,128]{2,1,0:T(8,128)(2,1)S(1)}, bf16[4,784,128]{2,1,0:T(8,128)(2,1)}, u32[]{:S(2)}, u32[]{:S(2)}) collective-permute-start(bf16[4,784,128]{2,1,0:T(8,128)(2,1)S(1)} %all-to-all-done.1.rest_0_), channel_id=1, source_target_pairs={{0,4},{2,6},{4,0},{6,2},{8,12},{10,14},{12,8},{14,10},{16,20},{18,... | collective-permute-start | bytes 2408456 | tf_op jit(solution)/shard_map/ppermute | solution.py:471
  100.6 1.2 copy-start.5
  101.8 37.8 %all-to-all-start.2 = ((bf16[16,400,128]{2,1,0:T(8,128)(2,1)}), bf16[16,400,128]{2,1,0:T(8,128)(2,1)S(1)}, u32[]{:S(2)}, u32[]{:S(2)}) async-start(bf16[16,400,128]{2,1,0:T(8,128)(2,1)} %bitcast.5), calls=%async_computation.2 | async-start | bytes 3276800 | tf_op jit(solution)/shard_map/all_to_all | solution.py:479
  106.5 2.5 collective-permute-start.4
  107.0 3.3 %collective-permute-start.5 = (bf16[4,784,128]{2,1,0:T(8,128)(2,1)}, bf16[4,784,128]{2,1,0:T(8,128)(2,1)S(1)}, u32[]{:S(2)}, u32[]{:S(2)}) collective-permute-start(bf16[4,784,128]{2,1,0:T(8,128)(2,1)} %collective-permute-done.1.rest_1_), channel_id=1, source_target_pairs={{0,2},{2,0},{4,6},{6,4},{8,10},{10,8},{12,14},{14,12},{16,18},{18,... | collective-permute-start | bytes 2408456 | tf_op jit(solution)/shard_map/ppermute | solution.py:471
  109.0 1.3 copy-start.8
  139.6 9.4 %copy-start.4 = (bf16[16,400,128]{2,1,0:T(8,128)(2,1)}, bf16[16,400,128]{2,1,0:T(8,128)(2,1)S(1)}, u32[]{:S(2)}) copy-start(bf16[16,400,128]{2,1,0:T(8,128)(2,1)S(1)} %all-to-all-done.2.got_ref) | copy-start | bytes 4915204
  139.6 29.6 %all-to-all-start.4 = ((bf16[16,192,128]{2,1,0:T(8,128)(2,1)}), bf16[16,192,128]{2,1,0:T(8,128)(2,1)S(1)}, u32[]{:S(2)}, u32[]{:S(2)}) async-start(bf16[16,192,128]{2,1,0:T(8,128)(2,1)} %shard_map.70), calls=%async_computation.4 | async-start | bytes 1572864 | tf_op jit(solution)/shard_map/all_to_all | solution.py:510
  173.9 24.7 %all-to-all-start.5 = ((bf16[16,192,128]{2,1,0:T(8,128)(2,1)}), bf16[16,192,128]{2,1,0:T(8,128)(2,1)S(1)}, u32[]{:S(2)}, u32[]{:S(2)}) async-start(bf16[16,192,128]{2,1,0:T(8,128)(2,1)} %shard_map.71), calls=%async_computation.5 | async-start | bytes 1572864 | tf_op jit(solution)/shard_map/all_to_all | solution.py:533
  188.7 21.1 %copy-start.10 = (bf16[192,1024]{1,0:T(8,128)(2,1)S(1)}, bf16[192,1024]{1,0:T(8,128)(2,1)}, u32[]{:S(2)}) copy-start(bf16[192,1024]{1,0:T(8,128)(2,1)} %shard_map.72) | copy-start | bytes 1179652
  198.6 1.5 copy-start.1
  198.6 65.4 %collective-permute-start.7 = (bf16[192,3072]{1,0:T(8,128)(2,1)}, bf16[192,3072]{1,0:T(8,128)(2,1)S(1)}, u32[]{:S(2)}, u32[]{:S(2)}) collective-permute-start(bf16[192,3072]{1,0:T(8,128)(2,1)} %shard_map.73), channel_id=1, source_target_pairs={{0,1},{1,0},{2,3},{3,2},{4,5},{5,4},{6,7},{7,6},{8,9},{9,8},{10,11... | collective-permute-start | bytes 3538952 | tf_op jit(solution)/shard_map/ppermute | solution.py:527
  209.0 60.9 %collective-permute-start.8 = (bf16[192,3072]{1,0:T(8,128)(2,1)}, bf16[192,3072]{1,0:T(8,128)(2,1)S(1)}, u32[]{:S(2)}, u32[]{:S(2)}) collective-permute-start(bf16[192,3072]{1,0:T(8,128)(2,1)} %shard_map.77), channel_id=1, source_target_pairs={{0,1},{1,0},{2,3},{3,2},{4,5},{5,4},{6,7},{7,6},{8,9},{9,8},{10,11... | collective-permute-start | bytes 3538952 | tf_op jit(solution)/shard_map/ppermute | solution.py:527
  209.9 51.5 %collective-permute-start.6 = (bf16[192,1024]{1,0:T(8,128)(2,1)S(1)}, bf16[192,1024]{1,0:T(8,128)(2,1)S(1)}, u32[]{:S(2)}, u32[]{:S(2)}) collective-permute-start(bf16[192,1024]{1,0:T(8,128)(2,1)S(1)} %copy-done.10), channel_id=1, source_target_pairs={{0,1},{1,0},{2,3},{3,2},{4,5},{5,4},{6,7},{7,6},{8,9},{9,8},{10,11... | collective-permute-start | bytes 1179656 | tf_op jit(solution)/shard_map/ppermute | solution.py:527
  214.9 60.7 %collective-permute-start.9 = (bf16[192,1024]{1,0:T(8,128)(2,1)}, bf16[192,1024]{1,0:T(8,128)(2,1)S(1)}, u32[]{:S(2)}, u32[]{:S(2)}) collective-permute-start(bf16[192,1024]{1,0:T(8,128)(2,1)} %shard_map.79), channel_id=1, source_target_pairs={{0,1},{1,0},{2,3},{3,2},{4,5},{5,4},{6,7},{7,6},{8,9},{9,8},{10,11... | collective-permute-start | bytes 1179656 | tf_op jit(solution)/shard_map/ppermute | solution.py:527
  269.8 1.0 copy-start.6
  (5 other events, 4.4 us)

commit v17 on v15

--- a/solution.py
+++ b/solution.py
@@ -187,8 +187,7 @@
                 all_rows[first : first + 2 * TOK_DEV, :]
             )
     else:
-        out[:, :HD] = all_rows[:total, :]
-        out[:, HD:] = jnp.ones((total, HD), jnp.bfloat16)
+        out[...] = all_rows[:total, :]
 
 
 def compact(member, counts, parts, offsets, total, as_keys):
@@ -198,7 +197,7 @@
         in_specs=[whole_smem(), whole_smem()] + [whole_vmem()] * len(parts),
         out_specs=whole_vmem(),
         out_shape=jax.ShapeDtypeStruct(
-            (HD, total) if as_keys else (total, 2 * HD), jnp.bfloat16
+            (HD, total) if as_keys else (total, HD), jnp.bfloat16
         ),
         scratch_shapes=[
             pltpu.VMEM((total + PAD, HD), jnp.bfloat16),
@@ -278,7 +277,13 @@
         weights = jnp.exp2(
             (scores[part, :] - jnp.concatenate([after] * (span // HD), axis=1)) * exp2_scale
         )
-        values = value_ref[pl.ds(pl.multiple_of(k * span, TILE), span), :]
+        values = jnp.concatenate(
+            [
+                value_ref[pl.ds(pl.multiple_of(k * span, TILE), span), :],
+                jnp.ones((span, HD), jnp.bfloat16),
+            ],
+            axis=1,
+        )
         run_acc[part, :] = run_acc[part, :] * jnp.concatenate([rescale, rescale], axis=1) + jnp.dot(
             weights.astype(jnp.bfloat16), values, preferred_element_type=jnp.float32
         )

time: 260 us -> 259 us (level)
  Pallas kernels: 117 us -> 114 us
  transfers between devices with their start and end apart: 16 -> 16, of which waited for: 12 -> 12; matrix products, arithmetic and copies ran while one was open for 0% -> 0% of each run, Pallas kernels for 40% -> 39%
where the time goes in v17:
time: 259 us; the launch traced here: 258 us
  Pallas kernels  114 us (44%)
  waiting for transfers between devices  90 us (35%)
  starting transfers between devices  44.4 us (17%)
  local copies, waits for them, and re-layouts  6.55 us (3%)
    ppermute x6, waiting for transfers between devices, swap(): return parts + [lax.ppermute(part, 'ctx', pairs) for part in parts]  42.8 us
    pallas_call x2, Pallas kernels, attend(): pl.pallas_call(functools.partial(attend_kernel, ctx_size, block), in_spec...  40.1 us
    pallas_call x5, Pallas kernels, project(): pl.pallas_call(functools.partial(project_kernel, classes, len(got)), grid...  39.4 us
    all_to_all x2, waiting for transfers between devices, send_across(): lax.all_to_all(packed, 'ctx', split_axis=0, concat_axis=0, tiled=True, ax...  18.2 us
    pallas_call x3, Pallas kernels, pack(): pl.pallas_call(functools.partial(pack_kernel, turned, classes, cap, width...  15.4 us
    ppermute x4, waiting for transfers between devices, trade(): return [lax.ppermute(part, 'tp', [(0, 1), (1, 0)]) for part in parts]  14.2 us
    all_to_all x1, waiting for transfers between devices, local(): last = lax.all_to_all(done, 'ctx', split_axis=0, concat_axis=0, tiled=True)  10.7 us
    all_to_all x2, starting transfers between devices, send_across(): lax.all_to_all(packed, 'ctx', split_axis=0, concat_axis=0, tiled=True, ax...  9.82 us
  transfers between devices with their start and end apart: 16, of which 12 were waited for; matrix products, arithmetic and copies ran while one was open for 0% of the time, Pallas kernels for 39%

profile of v17, /device:TPU:0, one launch (start us, length us, event | category | flops | bytes accessed | tf_op | source)
XLA Modules:
  0.0 257.8 jit_solution(7206689645914195416)
XLA Ops:
  4.1 3.5 %shard_map.67 = bf16[4,1,784,128]{3,2,1,0:T(8,128)(2,1)} custom-call(s32[1,768]{1,0:T(1,128)} %get-tuple-element.28.slot_ref, f32[768,128]{1,0:T(8,128)} %get-tuple-element.46.cos_ref, f32[768,128]{1,0:T(8,128)} %get-tuple-element.45.sin_ref, bf16[768,512]{1,0:T(8,128)(2,1)} %row_ref.5), custom_call_target="tpu_custom_call" | custom-call | flops 616562688 | bytes 1572864 | tf_op jit(solution)/shard_map/pallas_call | solution.py:124
  7.6 6.3 %all-to-all-start = ((bf16[4,784,128]{2,1,0:T(8,128)(2,1)}), bf16[4,784,128]{2,1,0:T(8,128)(2,1)S(1)}, u32[]{:S(2)}, u32[]{:S(2)}) async-start(bf16[4,784,128]{2,1,0:T(8,128)(2,1)} %bitcast.10), calls=%async_computation | async-start | bytes 1605632 | tf_op jit(solution)/shard_map/all_to_all | solution.py:465
  13.9 3.2 %shard_map.66 = bf16[4,1,784,128]{3,2,1,0:T(8,128)(2,1)} custom-call(s32[1,768]{1,0:T(1,128)} %get-tuple-element.28.slot_ref, f32[768,128]{1,0:T(8,128)} %get-tuple-element.46.cos_ref, f32[768,128]{1,0:T(8,128)} %get-tuple-element.45.sin_ref, bf16[768,512]{1,0:T(8,128)(2,1)} %row_ref.4), custom_call_target="tpu_custom_call" | custom-call | flops 616562688 | bytes 1572864 | tf_op jit(solution)/shard_map/pallas_call | solution.py:124
  17.1 17.3 %all-to-all-done.rest_0_ = bf16[4,784,128]{2,1,0:T(8,128)(2,1)S(1)} async-done(((bf16[4,784,128]{2,1,0:T(8,128)(2,1)}), bf16[4,784,128]{2,1,0:T(8,128)(2,1)S(1)}, u32[]{:S(2)}, u32[]{:S(2)}) %all-to-all-start) | async-done | bytes 802848 | tf_op jit(solution)/shard_map/all_to_all | solution.py:465
  34.4 3.5 %all-to-all-start.1 = ((bf16[4,784,128]{2,1,0:T(8,128)(2,1)}), bf16[4,784,128]{2,1,0:T(8,128)(2,1)S(1)}, u32[]{:S(2)}, u32[]{:S(2)}) async-start(bf16[4,784,128]{2,1,0:T(8,128)(2,1)} %bitcast.9), calls=%async_computation.1 | async-start | bytes 1605632 | tf_op jit(solution)/shard_map/all_to_all | solution.py:465
  39.4 8.7 %shard_map.65 = (bf16[16,1,400,128]{3,2,1,0:T(8,128)(2,1)}, bf16[16,1,400,128]{3,2,1,0:T(8,128)(2,1)}) custom-call(s32[1,768]{1,0:T(1,128)} %get-tuple-element.25.slot_ref, f32[768,128]{1,0:T(8,128)} %get-tuple-element.46.cos_ref, f32[768,128]{1,0:T(8,128)} %get-tuple-element.45.sin_ref, bf16[768,2048]{1,0:T(8,128)(2,1)} %row_ref.3), custom_call_target="tpu_custom_call" | custom-call | flops 2516582400 | bytes 6291456 | tf_op jit(solution)/shard_map/pallas_call | solution.py:124
  48.1 8.8 %collective-permute-done.rest_1_ = bf16[4,784,128]{2,1,0:T(8,128)(2,1)} collective-permute-done((bf16[4,784,128]{2,1,0:T(8,128)(2,1)S(1)}, bf16[4,784,128]{2,1,0:T(8,128)(2,1)}, u32[]{:S(2)}, u32[]{:S(2)}) %collective-permute-start) | collective-permute-done | bytes 802848 | tf_op jit(solution)/shard_map/ppermute | solution.py:471
  57.8 4.9 %all-to-all-start.3 = ((bf16[16,400,128]{2,1,0:T(8,128)(2,1)}), bf16[16,400,128]{2,1,0:T(8,128)(2,1)S(1)}, u32[]{:S(2)}, u32[]{:S(2)}) async-start(bf16[16,400,128]{2,1,0:T(8,128)(2,1)} %bitcast.11), calls=%async_computation.3 | async-start | bytes 3276800 | tf_op jit(solution)/shard_map/all_to_all | solution.py:479
  66.6 4.7 %shard_map.68.key_ref = bf16[128,6144]{1,0:T(8,128)(2,1)} custom-call(s32[1]{0:T(128)} %bitcast.4.member_ref, s32[16]{0:T(128)} %count_ref.9, bf16[4,784,128]{2,1,0:T(8,128)(2,1)} %copy-done.3, bf16[4,784,128]{2,1,0:T(8,128)(2,1)} %collective-permute-done.rest_1_, bf16[4,784,128]{2,1,0:T(8,128)(2,1)} %collective-permute-done.2.rest_2_, ...), custom_call_target="tpu_custom_call" | custom-call | flops 6291456 | bytes 6291456 | tf_op jit(solution)/shard_map/pallas_call | solution.py:195
  71.3 29.4 %collective-permute-done.1.rest_1_ = bf16[4,784,128]{2,1,0:T(8,128)(2,1)} collective-permute-done((bf16[4,784,128]{2,1,0:T(8,128)(2,1)S(1)}, bf16[4,784,128]{2,1,0:T(8,128)(2,1)}, u32[]{:S(2)}, u32[]{:S(2)}) %collective-permute-start.1) | collective-permute-done | bytes 802848 | tf_op jit(solution)/shard_map/ppermute | solution.py:471
  101.8 4.6 %all-to-all-start.2 = ((bf16[16,400,128]{2,1,0:T(8,128)(2,1)}), bf16[16,400,128]{2,1,0:T(8,128)(2,1)S(1)}, u32[]{:S(2)}, u32[]{:S(2)}) async-start(bf16[16,400,128]{2,1,0:T(8,128)(2,1)} %bitcast.5), calls=%async_computation.2 | async-start | bytes 3276800 | tf_op jit(solution)/shard_map/all_to_all | solution.py:479
  111.2 4.3 %shard_map.69.value_ref = bf16[6144,128]{1,0:T(8,128)(2,1)} custom-call(s32[1]{0:T(128)} %bitcast.4.member_ref, s32[16]{0:T(128)} %count_ref.9, bf16[4,784,128]{2,1,0:T(8,128)(2,1)} %copy-done.2, bf16[4,784,128]{2,1,0:T(8,128)(2,1)} %collective-permute-done.1.rest_1_, bf16[4,784,128]{2,1,0:T(8,128)(2,1)} %copy-done.6, bf16[4,784,128]{2,1,0:T(8,128)(2,1)} %copy-done.7), custom_call_target="tpu_custom_call" | custom-call | flops 6291456 | bytes 6291456 | tf_op jit(solution)/shard_map/pallas_call | solution.py:195
  115.5 20.0 %shard_map.70 = bf16[16,192,128]{2,1,0:T(8,128)(2,1)} custom-call(s32[1]{0:T(128)} %constant.64.clone.1.cls_ref, s32[16]{0:T(128)} %count_ref.9, bf16[16,400,128]{2,1,0:T(8,128)(2,1)} %copy-done.5, bf16[128,6144]{1,0:T(8,128)(2,1)} %shard_map.68.key_ref, bf16[6144,128]{1,0:T(8,128)(2,1)} %shard_map.69.value_ref), custom_call_target="tpu_custom_call" | custom-call | flops 9663676416 | bytes 6291456 | tf_op jit(solution)/shard_map/pallas_call | solution.py:335
  135.5 4.1 %all-to-all-done.2.got_ref = bf16[16,400,128]{2,1,0:T(8,128)(2,1)S(1)} async-done(((bf16[16,400,128]{2,1,0:T(8,128)(2,1)}), bf16[16,400,128]{2,1,0:T(8,128)(2,1)S(1)}, u32[]{:S(2)}, u32[]{:S(2)}) %all-to-all-start.2) | async-done | bytes 1638432 | tf_op jit(solution)/shard_map/all_to_all | solution.py:479
  139.6 9.4 %all-to-all-start.4 = ((bf16[16,192,128]{2,1,0:T(8,128)(2,1)}), bf16[16,192,128]{2,1,0:T(8,128)(2,1)S(1)}, u32[]{:S(2)}, u32[]{:S(2)}) async-start(bf16[16,192,128]{2,1,0:T(8,128)(2,1)} %shard_map.70), calls=%async_computation.4 | async-start | bytes 1572864 | tf_op jit(solution)/shard_map/all_to_all | solution.py:510
  149.0 20.1 %shard_map.71 = bf16[16,192,128]{2,1,0:T(8,128)(2,1)} custom-call(s32[1]{0:T(128)} %constant.65.clone.1.cls_ref, s32[16]{0:T(128)} %count_ref.9, bf16[16,400,128]{2,1,0:T(8,128)(2,1)} %copy-done.4, bf16[128,6144]{1,0:T(8,128)(2,1)} %shard_map.68.key_ref, bf16[6144,128]{1,0:T(8,128)(2,1)} %shard_map.69.value_ref), custom_call_target="tpu_custom_call" | custom-call | flops 9663676416 | bytes 6291456 | tf_op jit(solution)/shard_map/pallas_call | solution.py:335
  170.0 6.4 %shard_map.72 = bf16[192,2048]{1,0:T(8,128)(2,1)} custom-call(s32[1]{0:T(128)} %bitcast.7.column_ref, bf16[16,192,128]{2,1,0:T(8,128)(2,1)} %copy-done, bf16[2048,8192]{1,0:T(8,128)(2,1)} %rest_1_.7), custom_call_target="tpu_custom_call" | custom-call | flops 1610612736 | bytes 8388608 | tf_op jit(solution)/shard_map/pallas_call | solution.py:377
  176.4 6.0 %all-to-all-start.5 = ((bf16[16,192,128]{2,1,0:T(8,128)(2,1)}), bf16[16,192,128]{2,1,0:T(8,128)(2,1)S(1)}, u32[]{:S(2)}, u32[]{:S(2)}) async-start(bf16[16,192,128]{2,1,0:T(8,128)(2,1)} %shard_map.71), calls=%async_computation.5 | async-start | bytes 1572864 | tf_op jit(solution)/shard_map/all_to_all | solution.py:532
  184.0 6.4 %shard_map.73 = bf16[192,2048]{1,0:T(8,128)(2,1)} custom-call(s32[1]{0:T(128)} %bitcast.8.column_ref, bf16[16,192,128]{2,1,0:T(8,128)(2,1)} %copy-done, bf16[2048,8192]{1,0:T(8,128)(2,1)} %rest_1_.7), custom_call_target="tpu_custom_call" | custom-call | flops 1610612736 | bytes 8388608 | tf_op jit(solution)/shard_map/pallas_call | solution.py:377
  190.4 10.7 %all-to-all-done.5.rest_1_.rest_0_ = bf16[16,192,128]{2,1,0:T(8,128)(2,1)S(1)} async-done(((bf16[16,192,128]{2,1,0:T(8,128)(2,1)}), bf16[16,192,128]{2,1,0:T(8,128)(2,1)S(1)}, u32[]{:S(2)}, u32[]{:S(2)}) %all-to-all-start.5) | async-done | bytes 786464 | tf_op jit(solution)/shard_map/all_to_all | solution.py:532
  202.6 6.4 %shard_map.77 = bf16[192,2048]{1,0:T(8,128)(2,1)} custom-call(s32[1]{0:T(128)} %bitcast.7.column_ref, bf16[16,192,128]{2,1,0:T(8,128)(2,1)} %copy-done.1, bf16[2048,8192]{1,0:T(8,128)(2,1)} %rest_1_.7), custom_call_target="tpu_custom_call" | custom-call | flops 1610612736 | bytes 8388608 | tf_op jit(solution)/shard_map/pallas_call | solution.py:377
  209.9 6.4 %shard_map.79 = bf16[192,2048]{1,0:T(8,128)(2,1)} custom-call(s32[1]{0:T(128)} %bitcast.8.column_ref, bf16[16,192,128]{2,1,0:T(8,128)(2,1)} %copy-done.1, bf16[2048,8192]{1,0:T(8,128)(2,1)} %rest_1_.7), custom_call_target="tpu_custom_call" | custom-call | flops 1610612736 | bytes 8388608 | tf_op jit(solution)/shard_map/pallas_call | solution.py:377
  217.5 13.8 %shard_map.74.sum_ref = bf16[384,4096]{1,0:T(8,128)(2,1)} custom-call(s32[1]{0:T(128)} %bitcast.column_ref, bf16[16,192,128]{2,1,0:T(8,128)(2,1)} %copy-done, bf16[16,192,128]{2,1,0:T(8,128)(2,1)} %copy-done.1, bf16[2048,8192]{1,0:T(8,128)(2,1)} %rest_1_.7), custom_call_target="tpu_custom_call" | custom-call | flops 6442450944 | bytes 16777216 | tf_op jit(solution)/shard_map/pallas_call | solution.py:377
  241.6 13.1 %collective-permute-done.9.part_ref = bf16[192,2048]{1,0:T(8,128)(2,1)S(1)} collective-permute-done((bf16[192,2048]{1,0:T(8,128)(2,1)}, bf16[192,2048]{1,0:T(8,128)(2,1)S(1)}, u32[]{:S(2)}, u32[]{:S(2)}) %collective-permute-start.9) | collective-permute-done | bytes 786464 | tf_op jit(solution)/shard_map/ppermute | solution.py:526
  (53 shorter events, 35.8 us)
Async XLA Ops:
  7.6 26.8 %all-to-all-start = ((bf16[4,784,128]{2,1,0:T(8,128)(2,1)}), bf16[4,784,128]{2,1,0:T(8,128)(2,1)S(1)}, u32[]{:S(2)}, u32[]{:S(2)}) async-start(bf16[4,784,128]{2,1,0:T(8,128)(2,1)} %bitcast.10), calls=%async_computation | async-start | bytes 1605632 | tf_op jit(solution)/shard_map/all_to_all | solution.py:465
  34.4 28.3 %copy-start.3 = (bf16[4,784,128]{2,1,0:T(8,128)(2,1)}, bf16[4,784,128]{2,1,0:T(8,128)(2,1)S(1)}, u32[]{:S(2)}) copy-start(bf16[4,784,128]{2,1,0:T(8,128)(2,1)S(1)} %all-to-all-done.rest_0_) | copy-start | bytes 2408452
  34.4 23.4 %all-to-all-start.1 = ((bf16[4,784,128]{2,1,0:T(8,128)(2,1)}), bf16[4,784,128]{2,1,0:T(8,128)(2,1)S(1)}, u32[]{:S(2)}, u32[]{:S(2)}) async-start(bf16[4,784,128]{2,1,0:T(8,128)(2,1)} %bitcast.9), calls=%async_computation.1 | async-start | bytes 1605632 | tf_op jit(solution)/shard_map/all_to_all | solution.py:465
  37.9 19.0 %collective-permute-start = (bf16[4,784,128]{2,1,0:T(8,128)(2,1)S(1)}, bf16[4,784,128]{2,1,0:T(8,128)(2,1)}, u32[]{:S(2)}, u32[]{:S(2)}) collective-permute-start(bf16[4,784,128]{2,1,0:T(8,128)(2,1)S(1)} %all-to-all-done.rest_0_), channel_id=1, source_target_pairs={{0,4},{2,6},{4,0},{6,2},{8,12},{10,14},{12,8},{14,10},{16,20},{18,... | collective-permute-start | bytes 2408456 | tf_op jit(solution)/shard_map/ppermute | solution.py:471
  57.8 48.7 %copy-start.2 = (bf16[4,784,128]{2,1,0:T(8,128)(2,1)}, bf16[4,784,128]{2,1,0:T(8,128)(2,1)S(1)}, u32[]{:S(2)}) copy-start(bf16[4,784,128]{2,1,0:T(8,128)(2,1)S(1)} %all-to-all-done.1.rest_0_) | copy-start | bytes 2408452
  57.8 42.9 %all-to-all-start.3 = ((bf16[16,400,128]{2,1,0:T(8,128)(2,1)}), bf16[16,400,128]{2,1,0:T(8,128)(2,1)S(1)}, u32[]{:S(2)}, u32[]{:S(2)}) async-start(bf16[16,400,128]{2,1,0:T(8,128)(2,1)} %bitcast.11), calls=%async_computation.3 | async-start | bytes 3276800 | tf_op jit(solution)/shard_map/all_to_all | solution.py:479
  62.7 2.6 %collective-permute-start.2 = (bf16[4,784,128]{2,1,0:T(8,128)(2,1)S(1)}, bf16[4,784,128]{2,1,0:T(8,128)(2,1)}, u32[]{:S(2)}, u32[]{:S(2)}) collective-permute-start(bf16[4,784,128]{2,1,0:T(8,128)(2,1)S(1)} %all-to-all-done.rest_0_), channel_id=1, source_target_pairs={{0,2},{2,0},{4,6},{6,4},{8,10},{10,8},{12,14},{14,12},{16,18},{18,... | collective-permute-start | bytes 2408456 | tf_op jit(solution)/shard_map/ppermute | solution.py:471
  63.1 3.4 %collective-permute-start.3 = (bf16[4,784,128]{2,1,0:T(8,128)(2,1)}, bf16[4,784,128]{2,1,0:T(8,128)(2,1)}, u32[]{:S(2)}, u32[]{:S(2)}) collective-permute-start(bf16[4,784,128]{2,1,0:T(8,128)(2,1)} %collective-permute-done.rest_1_), channel_id=1, source_target_pairs={{0,2},{2,0},{4,6},{6,4},{8,10},{10,8},{12,14},{14,12},{16,18},{18,... | collective-permute-start | bytes 2408456 | tf_op jit(solution)/shard_map/ppermute | solution.py:471
  63.2 37.4 %collective-permute-start.1 = (bf16[4,784,128]{2,1,0:T(8,128)(2,1)S(1)}, bf16[4,784,128]{2,1,0:T(8,128)(2,1)}, u32[]{:S(2)}, u32[]{:S(2)}) collective-permute-start(bf16[4,784,128]{2,1,0:T(8,128)(2,1)S(1)} %all-to-all-done.1.rest_0_), channel_id=1, source_target_pairs={{0,4},{2,6},{4,0},{6,2},{8,12},{10,14},{12,8},{14,10},{16,20},{18,... | collective-permute-start | bytes 2408456 | tf_op jit(solution)/shard_map/ppermute | solution.py:471
  100.7 1.2 copy-start.5
  101.8 37.8 %all-to-all-start.2 = ((bf16[16,400,128]{2,1,0:T(8,128)(2,1)}), bf16[16,400,128]{2,1,0:T(8,128)(2,1)S(1)}, u32[]{:S(2)}, u32[]{:S(2)}) async-start(bf16[16,400,128]{2,1,0:T(8,128)(2,1)} %bitcast.5), calls=%async_computation.2 | async-start | bytes 3276800 | tf_op jit(solution)/shard_map/all_to_all | solution.py:479
  106.5 2.5 collective-permute-start.4
  107.0 3.3 %collective-permute-start.5 = (bf16[4,784,128]{2,1,0:T(8,128)(2,1)}, bf16[4,784,128]{2,1,0:T(8,128)(2,1)S(1)}, u32[]{:S(2)}, u32[]{:S(2)}) collective-permute-start(bf16[4,784,128]{2,1,0:T(8,128)(2,1)} %collective-permute-done.1.rest_1_), channel_id=1, source_target_pairs={{0,2},{2,0},{4,6},{6,4},{8,10},{10,8},{12,14},{14,12},{16,18},{18,... | collective-permute-start | bytes 2408456 | tf_op jit(solution)/shard_map/ppermute | solution.py:471
  109.0 1.3 copy-start.6
  110.3 0.9 copy-start.7
  139.6 9.4 %copy-start.4 = (bf16[16,400,128]{2,1,0:T(8,128)(2,1)}, bf16[16,400,128]{2,1,0:T(8,128)(2,1)S(1)}, u32[]{:S(2)}) copy-start(bf16[16,400,128]{2,1,0:T(8,128)(2,1)S(1)} %all-to-all-done.2.got_ref) | copy-start | bytes 4915204
  139.6 29.5 %all-to-all-start.4 = ((bf16[16,192,128]{2,1,0:T(8,128)(2,1)}), bf16[16,192,128]{2,1,0:T(8,128)(2,1)S(1)}, u32[]{:S(2)}, u32[]{:S(2)}) async-start(bf16[16,192,128]{2,1,0:T(8,128)(2,1)} %shard_map.70), calls=%async_computation.4 | async-start | bytes 1572864 | tf_op jit(solution)/shard_map/all_to_all | solution.py:510
  176.4 24.7 %all-to-all-start.5 = ((bf16[16,192,128]{2,1,0:T(8,128)(2,1)}), bf16[16,192,128]{2,1,0:T(8,128)(2,1)S(1)}, u32[]{:S(2)}, u32[]{:S(2)}) async-start(bf16[16,192,128]{2,1,0:T(8,128)(2,1)} %shard_map.71), calls=%async_computation.5 | async-start | bytes 1572864 | tf_op jit(solution)/shard_map/all_to_all | solution.py:532
  182.4 48.8 %collective-permute-start.6 = (bf16[192,2048]{1,0:T(8,128)(2,1)}, bf16[192,2048]{1,0:T(8,128)(2,1)S(1)}, u32[]{:S(2)}, u32[]{:S(2)}) collective-permute-start(bf16[192,2048]{1,0:T(8,128)(2,1)} %shard_map.72), channel_id=1, source_target_pairs={{0,1},{1,0},{2,3},{3,2},{4,5},{5,4},{6,7},{7,6},{8,9},{9,8},{10,11... | collective-permute-start | bytes 2359304 | tf_op jit(solution)/shard_map/ppermute | solution.py:526
  201.1 1.5 copy-start.1
  201.1 33.2 %collective-permute-start.7 = (bf16[192,2048]{1,0:T(8,128)(2,1)}, bf16[192,2048]{1,0:T(8,128)(2,1)S(1)}, u32[]{:S(2)}, u32[]{:S(2)}) collective-permute-start(bf16[192,2048]{1,0:T(8,128)(2,1)} %shard_map.73), channel_id=1, source_target_pairs={{0,1},{1,0},{2,3},{3,2},{4,5},{5,4},{6,7},{7,6},{8,9},{9,8},{10,11... | collective-permute-start | bytes 2359304 | tf_op jit(solution)/shard_map/ppermute | solution.py:526
  209.1 29.5 %collective-permute-start.8 = (bf16[192,2048]{1,0:T(8,128)(2,1)}, bf16[192,2048]{1,0:T(8,128)(2,1)S(1)}, u32[]{:S(2)}, u32[]{:S(2)}) collective-permute-start(bf16[192,2048]{1,0:T(8,128)(2,1)} %shard_map.77), channel_id=1, source_target_pairs={{0,1},{1,0},{2,3},{3,2},{4,5},{5,4},{6,7},{7,6},{8,9},{9,8},{10,11... | collective-permute-start | bytes 2359304 | tf_op jit(solution)/shard_map/ppermute | solution.py:526
  216.3 38.4 %collective-permute-start.9 = (bf16[192,2048]{1,0:T(8,128)(2,1)}, bf16[192,2048]{1,0:T(8,128)(2,1)S(1)}, u32[]{:S(2)}, u32[]{:S(2)}) collective-permute-start(bf16[192,2048]{1,0:T(8,128)(2,1)} %shard_map.79), channel_id=1, source_target_pairs={{0,1},{1,0},{2,3},{3,2},{4,5},{5,4},{6,7},{7,6},{8,9},{9,8},{10,11... | collective-permute-start | bytes 2359304 | tf_op jit(solution)/shard_map/ppermute | solution.py:526
  234.3 0.9 copy-start.11
  (4 other events, 3.5 us)

commit v18 on v17

--- a/solution.py
+++ b/solution.py
@@ -490,14 +490,18 @@
         (packed_q[0], key_parts, value_parts)
     )
     got_q = [send_query(packed_q[0])]
+    early = swap(value_parts, bits[1])[1:] if len(bits) == 2 else []
     value_parts = swap(value_parts, bits[0])
     for bit in bits[1:]:
         key_parts = swap(key_parts, bit)
     keys = compact(member, kept_count, key_parts, offsets, total, True)
     if chunks > 1:
         packed_q[1], value_parts, keys = lax.optimization_barrier((packed_q[1], value_parts, keys))
-    for bit in bits[1:]:
-        value_parts = swap(value_parts, bit)
+    if len(bits) == 2:
+        value_parts = value_parts + early + swap(value_parts[1:], bits[1])[1:]
+    else:
+        for bit in bits[1:]:
+            value_parts = swap(value_parts, bit)
     if chunks > 1:
         got_q.append(send_query(packed_q[1]))
     values = compact(member, kept_count, value_parts, offsets, total, False)

time: 259 us -> 259 us (level)
  no operation moved by 1% of the time
where the time goes in v18:
time: 259 us; the launch traced here: 258 us
  Pallas kernels  114 us (44%)
  waiting for transfers between devices  90 us (35%)
  starting transfers between devices  44.4 us (17%)
  local copies, waits for them, and re-layouts  6.55 us (3%)
    ppermute x6, waiting for transfers between devices, swap(): return parts + [lax.ppermute(part, 'ctx', pairs) for part in parts]  42.8 us
    pallas_call x2, Pallas kernels, attend(): pl.pallas_call(functools.partial(attend_kernel, ctx_size, block), in_spec...  40.1 us
    pallas_call x5, Pallas kernels, project(): pl.pallas_call(functools.partial(project_kernel, classes, len(got)), grid...  39.4 us
    all_to_all x2, waiting for transfers between devices, send_across(): lax.all_to_all(packed, 'ctx', split_axis=0, concat_axis=0, tiled=True, ax...  18.2 us
    pallas_call x3, Pallas kernels, pack(): pl.pallas_call(functools.partial(pack_kernel, turned, classes, cap, width...  15.4 us
    ppermute x4, waiting for transfers between devices, trade(): return [lax.ppermute(part, 'tp', [(0, 1), (1, 0)]) for part in parts]  14.2 us
    all_to_all x1, waiting for transfers between devices, local(): last = lax.all_to_all(done, 'ctx', split_axis=0, concat_axis=0, tiled=True)  10.7 us
    all_to_all x2, starting transfers between devices, send_across(): lax.all_to_all(packed, 'ctx', split_axis=0, concat_axis=0, tiled=True, ax...  9.82 us
  transfers between devices with their start and end apart: 16, of which 12 were waited for; matrix products, arithmetic and copies ran while one was open for 0% of the time, Pallas kernels for 39%

profile of v18, /device:TPU:0, one launch (start us, length us, event | category | flops | bytes accessed | tf_op | source)
XLA Modules:
  0.0 257.8 jit_solution(7206689645914195416)
XLA Ops:
  4.1 3.5 %shard_map.67 = bf16[4,1,784,128]{3,2,1,0:T(8,128)(2,1)} custom-call(s32[1,768]{1,0:T(1,128)} %get-tuple-element.28.slot_ref, f32[768,128]{1,0:T(8,128)} %get-tuple-element.46.cos_ref, f32[768,128]{1,0:T(8,128)} %get-tuple-element.45.sin_ref, bf16[768,512]{1,0:T(8,128)(2,1)} %row_ref.5), custom_call_target="tpu_custom_call" | custom-call | flops 616562688 | bytes 1572864 | tf_op jit(solution)/shard_map/pallas_call | solution.py:124
  7.6 6.3 %all-to-all-start = ((bf16[4,784,128]{2,1,0:T(8,128)(2,1)}), bf16[4,784,128]{2,1,0:T(8,128)(2,1)S(1)}, u32[]{:S(2)}, u32[]{:S(2)}) async-start(bf16[4,784,128]{2,1,0:T(8,128)(2,1)} %bitcast.10), calls=%async_computation | async-start | bytes 1605632 | tf_op jit(solution)/shard_map/all_to_all | solution.py:465
  13.9 3.2 %shard_map.66 = bf16[4,1,784,128]{3,2,1,0:T(8,128)(2,1)} custom-call(s32[1,768]{1,0:T(1,128)} %get-tuple-element.28.slot_ref, f32[768,128]{1,0:T(8,128)} %get-tuple-element.46.cos_ref, f32[768,128]{1,0:T(8,128)} %get-tuple-element.45.sin_ref, bf16[768,512]{1,0:T(8,128)(2,1)} %row_ref.4), custom_call_target="tpu_custom_call" | custom-call | flops 616562688 | bytes 1572864 | tf_op jit(solution)/shard_map/pallas_call | solution.py:124
  17.1 17.3 %all-to-all-done.rest_0_ = bf16[4,784,128]{2,1,0:T(8,128)(2,1)S(1)} async-done(((bf16[4,784,128]{2,1,0:T(8,128)(2,1)}), bf16[4,784,128]{2,1,0:T(8,128)(2,1)S(1)}, u32[]{:S(2)}, u32[]{:S(2)}) %all-to-all-start) | async-done | bytes 802848 | tf_op jit(solution)/shard_map/all_to_all | solution.py:465
  34.4 3.5 %all-to-all-start.1 = ((bf16[4,784,128]{2,1,0:T(8,128)(2,1)}), bf16[4,784,128]{2,1,0:T(8,128)(2,1)S(1)}, u32[]{:S(2)}, u32[]{:S(2)}) async-start(bf16[4,784,128]{2,1,0:T(8,128)(2,1)} %bitcast.9), calls=%async_computation.1 | async-start | bytes 1605632 | tf_op jit(solution)/shard_map/all_to_all | solution.py:465
  39.4 8.7 %shard_map.65 = (bf16[16,1,400,128]{3,2,1,0:T(8,128)(2,1)}, bf16[16,1,400,128]{3,2,1,0:T(8,128)(2,1)}) custom-call(s32[1,768]{1,0:T(1,128)} %get-tuple-element.25.slot_ref, f32[768,128]{1,0:T(8,128)} %get-tuple-element.46.cos_ref, f32[768,128]{1,0:T(8,128)} %get-tuple-element.45.sin_ref, bf16[768,2048]{1,0:T(8,128)(2,1)} %row_ref.3), custom_call_target="tpu_custom_call" | custom-call | flops 2516582400 | bytes 6291456 | tf_op jit(solution)/shard_map/pallas_call | solution.py:124
  48.1 8.8 %collective-permute-done.rest_1_ = bf16[4,784,128]{2,1,0:T(8,128)(2,1)} collective-permute-done((bf16[4,784,128]{2,1,0:T(8,128)(2,1)S(1)}, bf16[4,784,128]{2,1,0:T(8,128)(2,1)}, u32[]{:S(2)}, u32[]{:S(2)}) %collective-permute-start) | collective-permute-done | bytes 802848 | tf_op jit(solution)/shard_map/ppermute | solution.py:471
  57.8 4.9 %all-to-all-start.3 = ((bf16[16,400,128]{2,1,0:T(8,128)(2,1)}), bf16[16,400,128]{2,1,0:T(8,128)(2,1)S(1)}, u32[]{:S(2)}, u32[]{:S(2)}) async-start(bf16[16,400,128]{2,1,0:T(8,128)(2,1)} %bitcast.11), calls=%async_computation.3 | async-start | bytes 3276800 | tf_op jit(solution)/shard_map/all_to_all | solution.py:479
  66.6 4.7 %shard_map.68.key_ref = bf16[128,6144]{1,0:T(8,128)(2,1)} custom-call(s32[1]{0:T(128)} %bitcast.4.member_ref, s32[16]{0:T(128)} %count_ref.9, bf16[4,784,128]{2,1,0:T(8,128)(2,1)} %copy-done.3, bf16[4,784,128]{2,1,0:T(8,128)(2,1)} %collective-permute-done.rest_1_, bf16[4,784,128]{2,1,0:T(8,128)(2,1)} %collective-permute-done.2.rest_2_, ...), custom_call_target="tpu_custom_call" | custom-call | flops 6291456 | bytes 6291456 | tf_op jit(solution)/shard_map/pallas_call | solution.py:195
  71.2 29.4 %collective-permute-done.1.rest_1_ = bf16[4,784,128]{2,1,0:T(8,128)(2,1)} collective-permute-done((bf16[4,784,128]{2,1,0:T(8,128)(2,1)S(1)}, bf16[4,784,128]{2,1,0:T(8,128)(2,1)}, u32[]{:S(2)}, u32[]{:S(2)}) %collective-permute-start.1) | collective-permute-done | bytes 802848 | tf_op jit(solution)/shard_map/ppermute | solution.py:471
  101.8 4.6 %all-to-all-start.2 = ((bf16[16,400,128]{2,1,0:T(8,128)(2,1)}), bf16[16,400,128]{2,1,0:T(8,128)(2,1)S(1)}, u32[]{:S(2)}, u32[]{:S(2)}) async-start(bf16[16,400,128]{2,1,0:T(8,128)(2,1)} %bitcast.5), calls=%async_computation.2 | async-start | bytes 3276800 | tf_op jit(solution)/shard_map/all_to_all | solution.py:479
  111.2 4.3 %shard_map.69.value_ref = bf16[6144,128]{1,0:T(8,128)(2,1)} custom-call(s32[1]{0:T(128)} %bitcast.4.member_ref, s32[16]{0:T(128)} %count_ref.9, bf16[4,784,128]{2,1,0:T(8,128)(2,1)} %copy-done.2, bf16[4,784,128]{2,1,0:T(8,128)(2,1)} %collective-permute-done.1.rest_1_, bf16[4,784,128]{2,1,0:T(8,128)(2,1)} %copy-done.6, bf16[4,784,128]{2,1,0:T(8,128)(2,1)} %copy-done.7), custom_call_target="tpu_custom_call" | custom-call | flops 6291456 | bytes 6291456 | tf_op jit(solution)/shard_map/pallas_call | solution.py:195
  115.5 20.0 %shard_map.70 = bf16[16,192,128]{2,1,0:T(8,128)(2,1)} custom-call(s32[1]{0:T(128)} %constant.64.clone.1.cls_ref, s32[16]{0:T(128)} %count_ref.9, bf16[16,400,128]{2,1,0:T(8,128)(2,1)} %copy-done.5, bf16[128,6144]{1,0:T(8,128)(2,1)} %shard_map.68.key_ref, bf16[6144,128]{1,0:T(8,128)(2,1)} %shard_map.69.value_ref), custom_call_target="tpu_custom_call" | custom-call | flops 9663676416 | bytes 6291456 | tf_op jit(solution)/shard_map/pallas_call | solution.py:335
  135.5 4.1 %all-to-all-done.2.got_ref = bf16[16,400,128]{2,1,0:T(8,128)(2,1)S(1)} async-done(((bf16[16,400,128]{2,1,0:T(8,128)(2,1)}), bf16[16,400,128]{2,1,0:T(8,128)(2,1)S(1)}, u32[]{:S(2)}, u32[]{:S(2)}) %all-to-all-start.2) | async-done | bytes 1638432 | tf_op jit(solution)/shard_map/all_to_all | solution.py:479
  139.6 9.4 %all-to-all-start.4 = ((bf16[16,192,128]{2,1,0:T(8,128)(2,1)}), bf16[16,192,128]{2,1,0:T(8,128)(2,1)S(1)}, u32[]{:S(2)}, u32[]{:S(2)}) async-start(bf16[16,192,128]{2,1,0:T(8,128)(2,1)} %shard_map.70), calls=%async_computation.4 | async-start | bytes 1572864 | tf_op jit(solution)/shard_map/all_to_all | solution.py:514
  149.0 20.1 %shard_map.71 = bf16[16,192,128]{2,1,0:T(8,128)(2,1)} custom-call(s32[1]{0:T(128)} %constant.65.clone.1.cls_ref, s32[16]{0:T(128)} %count_ref.9, bf16[16,400,128]{2,1,0:T(8,128)(2,1)} %copy-done.4, bf16[128,6144]{1,0:T(8,128)(2,1)} %shard_map.68.key_ref, bf16[6144,128]{1,0:T(8,128)(2,1)} %shard_map.69.value_ref), custom_call_target="tpu_custom_call" | custom-call | flops 9663676416 | bytes 6291456 | tf_op jit(solution)/shard_map/pallas_call | solution.py:335
  170.0 6.4 %shard_map.72 = bf16[192,2048]{1,0:T(8,128)(2,1)} custom-call(s32[1]{0:T(128)} %bitcast.7.column_ref, bf16[16,192,128]{2,1,0:T(8,128)(2,1)} %copy-done, bf16[2048,8192]{1,0:T(8,128)(2,1)} %rest_1_.7), custom_call_target="tpu_custom_call" | custom-call | flops 1610612736 | bytes 8388608 | tf_op jit(solution)/shard_map/pallas_call | solution.py:377
  176.4 6.0 %all-to-all-start.5 = ((bf16[16,192,128]{2,1,0:T(8,128)(2,1)}), bf16[16,192,128]{2,1,0:T(8,128)(2,1)S(1)}, u32[]{:S(2)}, u32[]{:S(2)}) async-start(bf16[16,192,128]{2,1,0:T(8,128)(2,1)} %shard_map.71), calls=%async_computation.5 | async-start | bytes 1572864 | tf_op jit(solution)/shard_map/all_to_all | solution.py:536
  184.0 6.4 %shard_map.73 = bf16[192,2048]{1,0:T(8,128)(2,1)} custom-call(s32[1]{0:T(128)} %bitcast.8.column_ref, bf16[16,192,128]{2,1,0:T(8,128)(2,1)} %copy-done, bf16[2048,8192]{1,0:T(8,128)(2,1)} %rest_1_.7), custom_call_target="tpu_custom_call" | custom-call | flops 1610612736 | bytes 8388608 | tf_op jit(solution)/shard_map/pallas_call | solution.py:377
  190.4 10.7 %all-to-all-done.5.rest_1_.rest_0_ = bf16[16,192,128]{2,1,0:T(8,128)(2,1)S(1)} async-done(((bf16[16,192,128]{2,1,0:T(8,128)(2,1)}), bf16[16,192,128]{2,1,0:T(8,128)(2,1)S(1)}, u32[]{:S(2)}, u32[]{:S(2)}) %all-to-all-start.5) | async-done | bytes 786464 | tf_op jit(solution)/shard_map/all_to_all | solution.py:536
  202.6 6.4 %shard_map.77 = bf16[192,2048]{1,0:T(8,128)(2,1)} custom-call(s32[1]{0:T(128)} %bitcast.7.column_ref, bf16[16,192,128]{2,1,0:T(8,128)(2,1)} %copy-done.1, bf16[2048,8192]{1,0:T(8,128)(2,1)} %rest_1_.7), custom_call_target="tpu_custom_call" | custom-call | flops 1610612736 | bytes 8388608 | tf_op jit(solution)/shard_map/pallas_call | solution.py:377
  209.9 6.4 %shard_map.79 = bf16[192,2048]{1,0:T(8,128)(2,1)} custom-call(s32[1]{0:T(128)} %bitcast.8.column_ref, bf16[16,192,128]{2,1,0:T(8,128)(2,1)} %copy-done.1, bf16[2048,8192]{1,0:T(8,128)(2,1)} %rest_1_.7), custom_call_target="tpu_custom_call" | custom-call | flops 1610612736 | bytes 8388608 | tf_op jit(solution)/shard_map/pallas_call | solution.py:377
  217.5 13.8 %shard_map.74.sum_ref = bf16[384,4096]{1,0:T(8,128)(2,1)} custom-call(s32[1]{0:T(128)} %bitcast.column_ref, bf16[16,192,128]{2,1,0:T(8,128)(2,1)} %copy-done, bf16[16,192,128]{2,1,0:T(8,128)(2,1)} %copy-done.1, bf16[2048,8192]{1,0:T(8,128)(2,1)} %rest_1_.7), custom_call_target="tpu_custom_call" | custom-call | flops 6442450944 | bytes 16777216 | tf_op jit(solution)/shard_map/pallas_call | solution.py:377
  241.6 13.1 %collective-permute-done.9.part_ref = bf16[192,2048]{1,0:T(8,128)(2,1)S(1)} collective-permute-done((bf16[192,2048]{1,0:T(8,128)(2,1)}, bf16[192,2048]{1,0:T(8,128)(2,1)S(1)}, u32[]{:S(2)}, u32[]{:S(2)}) %collective-permute-start.9) | collective-permute-done | bytes 786464 | tf_op jit(solution)/shard_map/ppermute | solution.py:530
  (53 shorter events, 35.8 us)
Async XLA Ops:
  7.6 26.8 %all-to-all-start = ((bf16[4,784,128]{2,1,0:T(8,128)(2,1)}), bf16[4,784,128]{2,1,0:T(8,128)(2,1)S(1)}, u32[]{:S(2)}, u32[]{:S(2)}) async-start(bf16[4,784,128]{2,1,0:T(8,128)(2,1)} %bitcast.10), calls=%async_computation | async-start | bytes 1605632 | tf_op jit(solution)/shard_map/all_to_all | solution.py:465
  34.4 28.3 %copy-start.3 = (bf16[4,784,128]{2,1,0:T(8,128)(2,1)}, bf16[4,784,128]{2,1,0:T(8,128)(2,1)S(1)}, u32[]{:S(2)}) copy-start(bf16[4,784,128]{2,1,0:T(8,128)(2,1)S(1)} %all-to-all-done.rest_0_) | copy-start | bytes 2408452
  34.4 23.4 %all-to-all-start.1 = ((bf16[4,784,128]{2,1,0:T(8,128)(2,1)}), bf16[4,784,128]{2,1,0:T(8,128)(2,1)S(1)}, u32[]{:S(2)}, u32[]{:S(2)}) async-start(bf16[4,784,128]{2,1,0:T(8,128)(2,1)} %bitcast.9), calls=%async_computation.1 | async-start | bytes 1605632 | tf_op jit(solution)/shard_map/all_to_all | solution.py:465
  37.9 19.0 %collective-permute-start = (bf16[4,784,128]{2,1,0:T(8,128)(2,1)S(1)}, bf16[4,784,128]{2,1,0:T(8,128)(2,1)}, u32[]{:S(2)}, u32[]{:S(2)}) collective-permute-start(bf16[4,784,128]{2,1,0:T(8,128)(2,1)S(1)} %all-to-all-done.rest_0_), channel_id=1, source_target_pairs={{0,4},{2,6},{4,0},{6,2},{8,12},{10,14},{12,8},{14,10},{16,20},{18,... | collective-permute-start | bytes 2408456 | tf_op jit(solution)/shard_map/ppermute | solution.py:471
  57.8 48.7 %copy-start.2 = (bf16[4,784,128]{2,1,0:T(8,128)(2,1)}, bf16[4,784,128]{2,1,0:T(8,128)(2,1)S(1)}, u32[]{:S(2)}) copy-start(bf16[4,784,128]{2,1,0:T(8,128)(2,1)S(1)} %all-to-all-done.1.rest_0_) | copy-start | bytes 2408452
  57.8 42.9 %all-to-all-start.3 = ((bf16[16,400,128]{2,1,0:T(8,128)(2,1)}), bf16[16,400,128]{2,1,0:T(8,128)(2,1)S(1)}, u32[]{:S(2)}, u32[]{:S(2)}) async-start(bf16[16,400,128]{2,1,0:T(8,128)(2,1)} %bitcast.11), calls=%async_computation.3 | async-start | bytes 3276800 | tf_op jit(solution)/shard_map/all_to_all | solution.py:479
  62.7 2.6 %collective-permute-start.2 = (bf16[4,784,128]{2,1,0:T(8,128)(2,1)S(1)}, bf16[4,784,128]{2,1,0:T(8,128)(2,1)}, u32[]{:S(2)}, u32[]{:S(2)}) collective-permute-start(bf16[4,784,128]{2,1,0:T(8,128)(2,1)S(1)} %all-to-all-done.rest_0_), channel_id=1, source_target_pairs={{0,2},{2,0},{4,6},{6,4},{8,10},{10,8},{12,14},{14,12},{16,18},{18,... | collective-permute-start | bytes 2408456 | tf_op jit(solution)/shard_map/ppermute | solution.py:471
  63.1 3.4 %collective-permute-start.3 = (bf16[4,784,128]{2,1,0:T(8,128)(2,1)}, bf16[4,784,128]{2,1,0:T(8,128)(2,1)}, u32[]{:S(2)}, u32[]{:S(2)}) collective-permute-start(bf16[4,784,128]{2,1,0:T(8,128)(2,1)} %collective-permute-done.rest_1_), channel_id=1, source_target_pairs={{0,2},{2,0},{4,6},{6,4},{8,10},{10,8},{12,14},{14,12},{16,18},{18,... | collective-permute-start | bytes 2408456 | tf_op jit(solution)/shard_map/ppermute | solution.py:471
  63.2 37.4 %collective-permute-start.1 = (bf16[4,784,128]{2,1,0:T(8,128)(2,1)S(1)}, bf16[4,784,128]{2,1,0:T(8,128)(2,1)}, u32[]{:S(2)}, u32[]{:S(2)}) collective-permute-start(bf16[4,784,128]{2,1,0:T(8,128)(2,1)S(1)} %all-to-all-done.1.rest_0_), channel_id=1, source_target_pairs={{0,4},{2,6},{4,0},{6,2},{8,12},{10,14},{12,8},{14,10},{16,20},{18,... | collective-permute-start | bytes 2408456 | tf_op jit(solution)/shard_map/ppermute | solution.py:471
  100.7 1.2 copy-start.5
  101.8 37.8 %all-to-all-start.2 = ((bf16[16,400,128]{2,1,0:T(8,128)(2,1)}), bf16[16,400,128]{2,1,0:T(8,128)(2,1)S(1)}, u32[]{:S(2)}, u32[]{:S(2)}) async-start(bf16[16,400,128]{2,1,0:T(8,128)(2,1)} %bitcast.5), calls=%async_computation.2 | async-start | bytes 3276800 | tf_op jit(solution)/shard_map/all_to_all | solution.py:479
  106.5 2.5 collective-permute-start.4
  107.0 3.3 %collective-permute-start.5 = (bf16[4,784,128]{2,1,0:T(8,128)(2,1)}, bf16[4,784,128]{2,1,0:T(8,128)(2,1)S(1)}, u32[]{:S(2)}, u32[]{:S(2)}) collective-permute-start(bf16[4,784,128]{2,1,0:T(8,128)(2,1)} %collective-permute-done.1.rest_1_), channel_id=1, source_target_pairs={{0,2},{2,0},{4,6},{6,4},{8,10},{10,8},{12,14},{14,12},{16,18},{18,... | collective-permute-start | bytes 2408456 | tf_op jit(solution)/shard_map/ppermute | solution.py:471
  109.0 1.3 copy-start.6
  110.3 0.9 copy-start.7
  139.6 9.4 %copy-start.4 = (bf16[16,400,128]{2,1,0:T(8,128)(2,1)}, bf16[16,400,128]{2,1,0:T(8,128)(2,1)S(1)}, u32[]{:S(2)}) copy-start(bf16[16,400,128]{2,1,0:T(8,128)(2,1)S(1)} %all-to-all-done.2.got_ref) | copy-start | bytes 4915204
  139.6 29.5 %all-to-all-start.4 = ((bf16[16,192,128]{2,1,0:T(8,128)(2,1)}), bf16[16,192,128]{2,1,0:T(8,128)(2,1)S(1)}, u32[]{:S(2)}, u32[]{:S(2)}) async-start(bf16[16,192,128]{2,1,0:T(8,128)(2,1)} %shard_map.70), calls=%async_computation.4 | async-start | bytes 1572864 | tf_op jit(solution)/shard_map/all_to_all | solution.py:514
  176.4 24.7 %all-to-all-start.5 = ((bf16[16,192,128]{2,1,0:T(8,128)(2,1)}), bf16[16,192,128]{2,1,0:T(8,128)(2,1)S(1)}, u32[]{:S(2)}, u32[]{:S(2)}) async-start(bf16[16,192,128]{2,1,0:T(8,128)(2,1)} %shard_map.71), calls=%async_computation.5 | async-start | bytes 1572864 | tf_op jit(solution)/shard_map/all_to_all | solution.py:536
  182.4 48.8 %collective-permute-start.6 = (bf16[192,2048]{1,0:T(8,128)(2,1)}, bf16[192,2048]{1,0:T(8,128)(2,1)S(1)}, u32[]{:S(2)}, u32[]{:S(2)}) collective-permute-start(bf16[192,2048]{1,0:T(8,128)(2,1)} %shard_map.72), channel_id=1, source_target_pairs={{0,1},{1,0},{2,3},{3,2},{4,5},{5,4},{6,7},{7,6},{8,9},{9,8},{10,11... | collective-permute-start | bytes 2359304 | tf_op jit(solution)/shard_map/ppermute | solution.py:530
  201.1 1.5 copy-start.1
  201.1 33.2 %collective-permute-start.7 = (bf16[192,2048]{1,0:T(8,128)(2,1)}, bf16[192,2048]{1,0:T(8,128)(2,1)S(1)}, u32[]{:S(2)}, u32[]{:S(2)}) collective-permute-start(bf16[192,2048]{1,0:T(8,128)(2,1)} %shard_map.73), channel_id=1, source_target_pairs={{0,1},{1,0},{2,3},{3,2},{4,5},{5,4},{6,7},{7,6},{8,9},{9,8},{10,11... | collective-permute-start | bytes 2359304 | tf_op jit(solution)/shard_map/ppermute | solution.py:530
  209.0 29.5 %collective-permute-start.8 = (bf16[192,2048]{1,0:T(8,128)(2,1)}, bf16[192,2048]{1,0:T(8,128)(2,1)S(1)}, u32[]{:S(2)}, u32[]{:S(2)}) collective-permute-start(bf16[192,2048]{1,0:T(8,128)(2,1)} %shard_map.77), channel_id=1, source_target_pairs={{0,1},{1,0},{2,3},{3,2},{4,5},{5,4},{6,7},{7,6},{8,9},{9,8},{10,11... | collective-permute-start | bytes 2359304 | tf_op jit(solution)/shard_map/ppermute | solution.py:530
  216.3 38.4 %collective-permute-start.9 = (bf16[192,2048]{1,0:T(8,128)(2,1)}, bf16[192,2048]{1,0:T(8,128)(2,1)S(1)}, u32[]{:S(2)}, u32[]{:S(2)}) collective-permute-start(bf16[192,2048]{1,0:T(8,128)(2,1)} %shard_map.79), channel_id=1, source_target_pairs={{0,1},{1,0},{2,3},{3,2},{4,5},{5,4},{6,7},{7,6},{8,9},{9,8},{10,11... | collective-permute-start | bytes 2359304 | tf_op jit(solution)/shard_map/ppermute | solution.py:530
  234.3 0.9 copy-start.11
  (4 other events, 3.5 us)
